TPU v7x, 32 devices: a whole 2x2x4 slice. The times are simulated.
32 devices in a mesh: orb: 2 (over y), grid: 16 (over z, x, core).
Axes of the slice: x: 2, y: 2, z: 4, core: 2. Of those that a mesh axis runs over, the one named last changes fastest.
Arguments:
- random_orbitals: float32 [2, 256, 256, 256], P('orb', 'grid'), may hold values from -6 to 6
- potential: float32 [256, 256, 256], P('grid'), may hold values from -1.5 to 0.5
- sphere_cells: int32 [256, 2, 128], P('grid'), may hold values from 0 to 65535, as said below
- projectors: float32 [256, 4, 128], P('grid'), may hold values from -0.9 to 0.9
- kb_energy: float32 [4], replicated, may hold values from 0.5 to 1.5
- cheb_coef: float32 [3], replicated, may hold values from 0.5 to 1.5
Outputs:
- density: float32 [256, 256, 256], P('grid')
Inputs may be any that keep to these rules, and one draw needn't show every extreme that they name: `sphere_cells`: for each atom a the 128 points are distinct cells: the 128 offsets (dz, dy, dx) with |dz|, |dy|, |dx| <= 3 nearest to the atom's centre, ties broken by the order of (dz, dy, dx) from smallest to largest, added to the centre with periodic wrap along each dimension; row 0 holds the z-plane and row 1 the cell y * 256 + x. The centre's z lies in the slab of planes (a // 16) * 16 to (a // 16) * 16 + 15. Spheres of different atoms may share cells.
All inputs are finite; a program needn't handle non-finite values.
Results may differ from a plain program's by a relative error of at most 0.0002.
Values sent between devices are 32-bit elements; how exact they have to be, the bound alone decides.
No kernel may reach another device: no remote copies, remote signals or barrier semaphores. Data moves between devices by JAX's collectives and lax.ppermute only.
A program may use at most 64 MiB of HBM per device.

v0:
```python
import math

import jax
import jax.numpy as jnp
from jax import lax
from jax.sharding import PartitionSpec as P

REACH = 3


PRECISE = lax.Precision.HIGHEST
CENTRE = 2.0
HALF_RANGE = 4.0


def with_halo(cells, sides, width):
    for axis, dim in sides:
        count = lax.axis_size(axis)
        head = lax.slice_in_dim(cells, 0, width, axis=dim)
        tail = lax.slice_in_dim(cells, cells.shape[dim] - width, cells.shape[dim], axis=dim)
        cells = jnp.concatenate(
            [
                lax.ppermute(tail, axis, [(i, (i + 1) % count) for i in range(count)]),
                cells,
                lax.ppermute(head, axis, [((i + 1) % count, i) for i in range(count)]),
            ],
            axis=dim,
        )
    return cells


def from_behind(block, axis, distance):
    devices = range(lax.axis_size(axis))
    route = [((i - distance) % len(devices), i) for i in devices]
    return lax.ppermute(block, axis, route)


def kinetic_table(length):
    places = jnp.arange(length)
    offset = places[:, None] - places[None, :]
    parity = jnp.where(offset % 2 == 0, 1.0, -1.0).astype(jnp.float32)
    angle_half = offset.astype(jnp.float32) * (math.pi / length)
    sine = jnp.where(offset == 0, 1.0, jnp.sin(angle_half))
    off_diag = parity / (2.0 * sine * sine)
    on_diag = jnp.float32(length * length / 12.0 + 1.0 / 6.0)
    return jnp.where(offset == 0, on_diag, off_diag) * (4.0 / (length * length))


def local(random_orbitals, potential, sphere_cells, projectors, kb_energy, cheb_coef):
    grid_count = lax.axis_size("grid")
    grid_pos = lax.axis_index("grid")
    planes = potential.shape[0]
    rows_y = potential.shape[1]
    cols_x = potential.shape[2]
    all_planes = planes * grid_count
    plane_cells = rows_y * cols_x
    first_plane = grid_pos * planes
    orb_count = random_orbitals.shape[0]
    per_dev = sphere_cells.shape[0]
    kinetic_x = kinetic_table(cols_x)
    kinetic_y = kinetic_table(rows_y)
    kinetic_z = kinetic_table(all_planes)

    def along_z(columns):
        turned = jnp.einsum("ozyx,zw->owyx", columns, kinetic_z, precision=PRECISE)
        return lax.all_to_all(turned, "grid", split_axis=1, concat_axis=2, tiled=True)

    z_glob = sphere_cells[:, 0, :]
    in_plane = sphere_cells[:, 1, :]
    local_plane = (z_glob - first_plane + REACH) % all_planes
    ghost_index = (local_plane * plane_cells + in_plane).reshape(-1)

    def nonlocal_term(vector):
        extended = with_halo(vector, (("grid", 1),), REACH)
        flattened = extended.reshape(orb_count, -1)
        values = flattened[:, ghost_index].reshape(orb_count, per_dev, -1)
        coeffs = jnp.einsum("oaj,apj->oap", values, projectors, precision=PRECISE) * kb_energy
        spread = jnp.einsum("oap,apj->oaj", coeffs, projectors, precision=PRECISE).reshape(
            orb_count, -1
        )
        placed = jnp.zeros_like(flattened).at[:, ghost_index].add(spread).reshape(extended.shape)
        lower_rim = placed[:, :REACH]
        upper_rim = placed[:, REACH + planes :]
        from_above = from_behind(lower_rim, "grid", -1)
        from_below = from_behind(upper_rim, "grid", 1)
        interior = placed[:, REACH : REACH + planes]
        interior = interior.at[:, :REACH].add(from_below)
        interior = interior.at[:, planes - REACH :].add(from_above)
        return interior

    def apply_hamiltonian(vector):
        kinetic = jnp.dot(vector.reshape(-1, cols_x), kinetic_x, precision=PRECISE).reshape(
            vector.shape
        )
        kinetic = kinetic + jnp.einsum("ozyx,yw->ozwx", vector, kinetic_y, precision=PRECISE)
        kinetic = kinetic + along_z(
            lax.all_to_all(vector, "grid", split_axis=2, concat_axis=1, tiled=True)
        )
        summed = kinetic + potential * vector + nonlocal_term(vector)
        return (summed - CENTRE * vector) / HALF_RANGE

    first_term = apply_hamiltonian(random_orbitals)
    second_term = 2.0 * apply_hamiltonian(first_term) - random_orbitals
    filtered = (
        cheb_coef[0] * random_orbitals + cheb_coef[1] * first_term + cheb_coef[2] * second_term
    )
    group_density = jnp.sum(filtered * filtered, axis=0)
    density = lax.psum(group_density, "orb")
    return density / (orb_count * lax.axis_size("orb"))


def solution(mesh):
    in_specs = (
        P("orb", "grid", None, None),
        P("grid", None, None),
        P("grid", None, None),
        P("grid", None, None),
        P(),
        P(),
    )
    out_specs = P("grid", None, None)
    return jax.shard_map(local, mesh=mesh, in_specs=in_specs, out_specs=out_specs, check_vma=False)
```

profile of v0, /device:TPU:0, one launch (start us, length us, event | category | flops | bytes accessed | tf_op | source)
XLA Modules:
  0.0 781.7 jit_solution(6812235059067261994)
XLA Ops:
  6.5 4.6 copy.20
  11.2 99.4 %all_to_all.66 = f32[1,16,256,256]{3,1,0,2:T(8,128)S(1)} all-to-all(f32[1,16,256,256]{3,1,0,2:T(8,128)S(1)} %copy.20), channel_id=1, replica_groups=mesh['orb'=2,'grid'=16] {'grid'}, dimensions={2} | all-to-all | bytes 8388608 | tf_op jit(solution)/shard_map/all_to_all | solution.py:97
  110.6 0.6 copy.21
  111.2 4.8 convolution_bitcast_fusion.2
  116.0 4.4 copy.22
  120.4 5.5 all-to-all-start.1
  125.9 1.5 fusion.114
  127.4 4.4 collective-permute-start.1
  131.7 0.4 collective-permute-start
  132.2 0.1 compare_select_fusion
  132.3 70.7 %collective-permute-done.1 = f32[1,3,256,256]{3,2,1,0:T(8,128)S(1)} collective-permute-done((f32[1,3,256,256]{3,2,1,0:T(8,128)S(1)}, f32[1,3,256,256]{3,2,1,0:T(8,128)S(1)}, u32[]{:S(2)}, u32[]{:S(2)}) %collective-permute-start.1) | collective-permute-done | bytes 786464 | tf_op jit(solution)/shard_map/ppermute | solution.py:25
  203.0 4.9 collective-permute-done
  207.9 2.6 pad_maximum_fusion
  210.5 5.4 copy.40
  215.9 35.7 %gather_fusion = f32[2048]{0:T(1024)S(1)} fusion(f32[1441792]{0:T(1024)} %bitcast.166, s32[2048]{0:T(1024)S(1)} %broadcast_clamp_fusion), kind=kCustom, calls=%fused_computation | custom fusion | bytes 24576 | tf_op jit(solution)/shard_map/gather | solution.py:76
  251.7 0.2 fusion.116
  251.9 0.3 fusion.117
  252.2 14.2 %scatter_custom_fusion = f32[1441792]{0:T(1024)} fusion(s32[2048]{0:T(1024)S(1)} %bitcast.177, f32[2048]{0:T(1024)S(1)} %bitcast.186, f32[]{:T(128)} %constant.158.clone.1), kind=kCustom, calls=%fused_computation.32 | custom fusion | flops 2048 | bytes 5767172 | tf_op jit(solution)/shard_map/scatter-add | solution.py:81
  266.4 7.4 reshape.291
  273.7 1.5 fusion.112
  275.2 0.1 collective-permute-start.2
  275.3 4.6 collective-permute-start.3
  279.9 13.2 %convolution_bitcast_fusion = f32[4096,256]{0,1:T(8,128)} fusion(f32[4096,256]{1,0:T(8,128)} %bitcast.164), kind=kOutput, calls=%fused_computation.6 | convolution fusion | flops 3222732800 | bytes 8388608 | tf_op jit(solution)/shard_map/dot_general | solution.py:92
  293.1 5.6 copy.38
  298.7 4.6 slice.186
  303.3 2.1 fusion.31
  305.4 2.1 fusion.30
  307.5 2.8 copy.23
  310.3 0.6 copy-done.1
  310.9 1.3 copy-done.5
  312.2 10.9 %broadcast_multiply_fusion.1 = (f32[1,16,256,256]{3,2,1,0:T(8,128)S(1)}, f32[1,16,256,256]{3,2,1,0:T(8,128)}) fusion(f32[1,16,256,256]{3,2,1,0:T(8,128)S(1)} %copy-done.1, f32[1,16,256,256]{3,2,1,0:T(8,128)} %fusion.30, f32[16,256,256]{2,1,0:T(8,128)S(1)} %copy-done.5, f32[1,16,16,16,256]{4,3,1,2,0:T(8,128)S(1)} %copy.23, f32[1,16,256,256]{3,2,1,0:T(8,128)} %bitcast.171), kind=kOutput, calls=%fused_computation.37 | convolution fusion | flops 3231121408 | bytes 29360128 | tf_op jit(solution)/shard_map/ozyx,yw->ozwx/dot_general | solution.py:95
  323.2 2.4 copy.25
  325.6 114.7 %all_to_all.67 = f32[1,16,256,256]{3,1,0,2:T(8,128)S(1)} all-to-all(f32[1,16,256,256]{3,1,0,2:T(8,128)S(1)} %copy.25), channel_id=1, replica_groups=mesh['orb'=2,'grid'=16] {'grid'}, dimensions={2} | all-to-all | bytes 8388608 | tf_op jit(solution)/shard_map/all_to_all | solution.py:97
  440.3 0.6 copy.26
  441.0 4.8 convolution_bitcast_fusion.1
  445.8 4.4 copy.27
  450.1 5.3 all-to-all-start.3
  455.5 0.0 all-reduce.2.cloned.1.call-start
  455.5 1.5 fusion.113
  457.0 4.4 collective-permute-start.5
  461.4 0.2 collective-permute-start.4
  461.6 70.9 %collective-permute-done.5 = f32[1,3,256,256]{3,2,1,0:T(8,128)S(1)} collective-permute-done((f32[1,3,256,256]{3,2,1,0:T(8,128)S(1)}, f32[1,3,256,256]{3,2,1,0:T(8,128)S(1)}, u32[]{:S(2)}, u32[]{:S(2)}) %collective-permute-start.5) | collective-permute-done | bytes 786464 | tf_op jit(solution)/shard_map/ppermute | solution.py:25
  532.5 4.9 collective-permute-done.4
  537.5 2.6 pad_maximum_fusion.1
  540.1 5.4 copy.41
  545.5 35.7 %gather_fusion.1 = f32[2048]{0:T(1024)S(1)} fusion(f32[1441792]{0:T(1024)} %bitcast.165, s32[2048]{0:T(1024)S(1)} %broadcast_clamp_fusion), kind=kCustom, calls=%fused_computation.1 | custom fusion | bytes 24576 | tf_op jit(solution)/shard_map/gather | solution.py:76
  581.3 0.2 fusion.118
  581.5 0.2 fusion.119
  581.8 14.2 %scatter_custom_fusion.1 = f32[1441792]{0:T(1024)} fusion(s32[2048]{0:T(1024)S(1)} %bitcast.178, f32[2048]{0:T(1024)S(1)} %bitcast.185, f32[]{:T(128)} %constant.158.clone.1), kind=kCustom, calls=%fused_computation.30 | custom fusion | flops 2048 | bytes 5767172 | tf_op jit(solution)/shard_map/scatter-add | solution.py:81
  596.0 7.4 reshape.296
  603.4 1.6 fusion.111
  605.0 0.1 collective-permute-start.6
  605.1 4.7 collective-permute-start.7
  609.8 0.6 fusion.115
  611.0 9.7 %fusion.11 = f32[256,16,256]{2,0,1:T(8,128)} fusion(f32[1,16,256,256]{3,2,1,0:T(8,128)} %get-tuple-element.65), kind=kOutput, calls=%fused_computation.22 | convolution fusion | flops 3223781376 | bytes 8388608 | tf_op jit(solution)/shard_map/ozyx,yw->ozwx/dot_general | solution.py:95
  620.7 2.4 slice.193
  623.0 1.0 fusion.29
  624.0 2.1 fusion.28
  626.1 2.8 copy.28
  629.0 0.6 copy-done.2
  629.6 1.3 copy-done.4
  630.9 13.2 %fusion.25 = f32[16,256,256]{2,1,0:T(8,128)} fusion(f32[1,16,256,256]{3,2,1,0:T(8,128)S(1)} %copy-done.2, f32[1,16,256,256]{3,2,1,0:T(8,128)S(1)} %copy-done.4, f32[1,16,256,256]{3,2,1,0:T(8,128)} %fusion.28, f32[16,256,256]{2,1,0:T(8,128)} %param.15, f32[1,16,16,16,256]{4,3,1,2,0:T(8,128)S(1)} %copy.28, f32[256,16,256]{2,0,1:T(8,128)} %fusion.11, ...), kind=kOutput, calls=%fused_computation.38 | convolution fusion | flops 3240558592 | bytes 29360140 | tf_op jit(solution)/shard_map/dot_general | solution.py:92
  644.0 125.8 %all-reduce.2.cloned.1.call-done = f32[16,256,256]{2,1,0:T(8,128)} async-done(((f32[16,256,256]{2,1,0:T(8,128)}), f32[16,256,256]{2,1,0:T(8,128)}) %all-reduce.2.cloned.1.call-update) | async-done | bytes 4194320 | tf_op jit(solution)/shard_map/psum | solution.py:108
  769.9 4.5 broadcast_multiply_fusion
  (29 shorter events, 0.1 us)
Async XLA Ops:
  6.5 245.1 %copy-start = (f32[16,4,128]{2,1,0:T(4,128)S(1)}, f32[16,4,128]{2,1,0:T(4,128)}, u32[]{:S(2)}) copy-start(f32[16,4,128]{2,1,0:T(4,128)} %param.17) | copy-start | bytes 98308
  120.4 11.8 %copy-start.6 = (s32[16,2,128]{2,1,0:T(2,128)S(1)}, s32[16,2,128]{2,1,0:T(2,128)}, u32[]{:S(2)}) copy-start(s32[16,2,128]{2,1,0:T(2,128)} %param.16) | copy-start | bytes 49156
  120.4 187.1 %all-to-all-start.1 = ((f32[1,256,16,256]{3,2,0,1:T(8,128)}), f32[1,256,16,256]{3,2,0,1:T(8,128)}, u32[]{:S(2)}, u32[]{:S(2)}) async-start(f32[1,256,16,256]{3,2,0,1:T(8,128)} %copy.22), calls=%async_computation.1 | async-start | bytes 8388608 | tf_op jit(solution)/shard_map/all_to_all | solution.py:66
  127.4 75.6 %collective-permute-start.1 = (f32[1,3,256,256]{3,2,1,0:T(8,128)S(1)}, f32[1,3,256,256]{3,2,1,0:T(8,128)S(1)}, u32[]{:S(2)}, u32[]{:S(2)}) collective-permute-start(f32[1,3,256,256]{3,2,1,0:T(8,128)S(1)} %get-tuple-element.60), channel_id=1, source_target_pairs={{1,0},{2,1},{3,2},{4,3},{5,4},{6,5},{7,6},{8,7},{9,8},{10,9},{11,1... | collective-permute-start | bytes 2359304 | tf_op jit(solution)/shard_map/ppermute | solution.py:25
  131.7 76.1 %collective-permute-start = (f32[1,3,256,256]{3,2,1,0:T(8,128)S(1)}, f32[1,3,256,256]{3,2,1,0:T(8,128)S(1)}, u32[]{:S(2)}, u32[]{:S(2)}) collective-permute-start(f32[1,3,256,256]{3,2,1,0:T(8,128)S(1)} %get-tuple-element.59), channel_id=1, source_target_pairs={{0,1},{1,2},{2,3},{3,4},{4,5},{5,6},{6,7},{7,8},{8,9},{9,10},{10,1... | collective-permute-start | bytes 2359304 | tf_op jit(solution)/shard_map/ppermute | solution.py:23
  215.9 36.0 %copy-start.8 = (f32[4]{0:T(128)S(1)}, f32[4]{0:T(128)}, u32[]{:S(2)}) copy-start(f32[4]{0:T(128)} %param.18) | copy-start | bytes 52
  275.2 28.0 %collective-permute-start.2 = (f32[1,3,256,256]{3,2,1,0:T(8,128)S(1)}, f32[1,3,256,256]{3,2,1,0:T(8,128)S(1)}, u32[]{:S(2)}, u32[]{:S(2)}) collective-permute-start(f32[1,3,256,256]{3,2,1,0:T(8,128)S(1)} %get-tuple-element.56), channel_id=1, source_target_pairs={{15,0},{0,1},{1,2},{2,3},{3,4},{4,5},{5,6},{6,7},{7,8},{8,9},{9,10... | collective-permute-start | bytes 2359304 | tf_op jit(solution)/shard_map/ppermute | solution.py:35
  275.3 30.1 %collective-permute-start.3 = (f32[1,3,256,256]{3,2,1,0:T(8,128)S(1)}, f32[1,3,256,256]{3,2,1,0:T(8,128)S(1)}, u32[]{:S(2)}, u32[]{:S(2)}) collective-permute-start(f32[1,3,256,256]{3,2,1,0:T(8,128)S(1)} %get-tuple-element.55), channel_id=1, source_target_pairs={{1,0},{2,1},{3,2},{4,3},{5,4},{6,5},{7,6},{8,7},{9,8},{10,9},{11,1... | collective-permute-start | bytes 2359304 | tf_op jit(solution)/shard_map/ppermute | solution.py:35
  307.5 3.5 copy-start.1
  307.5 4.7 copy-start.5
  323.2 2.4 copy-start.3
  450.1 176.0 %all-to-all-start.3 = ((f32[1,256,16,256]{3,2,0,1:T(8,128)}), f32[1,256,16,256]{3,2,0,1:T(8,128)}, u32[]{:S(2)}, u32[]{:S(2)}) async-start(f32[1,256,16,256]{3,2,0,1:T(8,128)} %copy.27), calls=%async_computation.3 | async-start | bytes 8388608 | tf_op jit(solution)/shard_map/all_to_all | solution.py:66
  455.5 314.4 %all-reduce.2.cloned.1.call-start = ((), (), s32[]{:S(2)}) async-start(), calls=%async_computation.4 | async-start | bytes 8388608 | tf_op jit(solution)/shard_map/psum | solution.py:108
  457.0 75.5 %collective-permute-start.5 = (f32[1,3,256,256]{3,2,1,0:T(8,128)S(1)}, f32[1,3,256,256]{3,2,1,0:T(8,128)S(1)}, u32[]{:S(2)}, u32[]{:S(2)}) collective-permute-start(f32[1,3,256,256]{3,2,1,0:T(8,128)S(1)} %get-tuple-element.58), channel_id=1, source_target_pairs={{1,0},{2,1},{3,2},{4,3},{5,4},{6,5},{7,6},{8,7},{9,8},{10,9},{11,1... | collective-permute-start | bytes 2359304 | tf_op jit(solution)/shard_map/ppermute | solution.py:25
  461.4 76.1 %collective-permute-start.4 = (f32[1,3,256,256]{3,2,1,0:T(8,128)S(1)}, f32[1,3,256,256]{3,2,1,0:T(8,128)S(1)}, u32[]{:S(2)}, u32[]{:S(2)}) collective-permute-start(f32[1,3,256,256]{3,2,1,0:T(8,128)S(1)} %get-tuple-element.57), channel_id=1, source_target_pairs={{0,1},{1,2},{2,3},{3,4},{4,5},{5,6},{6,7},{7,8},{8,9},{9,10},{10,1... | collective-permute-start | bytes 2359304 | tf_op jit(solution)/shard_map/ppermute | solution.py:23
  596.0 13.8 %copy-start.7 = (f32[3]{0:T(128)S(1)}, f32[3]{0:T(128)}, u32[]{:S(2)}) copy-start(f32[3]{0:T(128)} %param.19) | copy-start | bytes 40
  603.4 17.3 %slice-start = ((s8[5767168]{0:T(1024)(128)(4,1)}), s8[4194304]{0:T(1024)(128)(4,1)S(1)}, s32[]{:S(2)}) async-start(s8[5767168]{0:T(1024)(128)(4,1)} %bitcast.167), calls=%async_computation.5 | async-start | bytes 8388608
  605.0 18.0 %collective-permute-start.6 = (f32[1,3,256,256]{3,2,1,0:T(8,128)S(1)}, f32[1,3,256,256]{3,2,1,0:T(8,128)S(1)}, u32[]{:S(2)}, u32[]{:S(2)}) collective-permute-start(f32[1,3,256,256]{3,2,1,0:T(8,128)S(1)} %get-tuple-element.54), channel_id=1, source_target_pairs={{15,0},{0,1},{1,2},{2,3},{3,4},{4,5},{5,6},{6,7},{7,8},{8,9},{9,10... | collective-permute-start | bytes 2359304 | tf_op jit(solution)/shard_map/ppermute | solution.py:35
  605.1 18.9 %collective-permute-start.7 = (f32[1,3,256,256]{3,2,1,0:T(8,128)S(1)}, f32[1,3,256,256]{3,2,1,0:T(8,128)S(1)}, u32[]{:S(2)}, u32[]{:S(2)}) collective-permute-start(f32[1,3,256,256]{3,2,1,0:T(8,128)S(1)} %get-tuple-element.53), channel_id=1, source_target_pairs={{1,0},{2,1},{3,2},{4,3},{5,4},{6,5},{7,6},{8,7},{9,8},{10,9},{11,1... | collective-permute-start | bytes 2359304 | tf_op jit(solution)/shard_map/ppermute | solution.py:35
  611.0 9.7 %slice-start.1 = ((s8[5767168]{0:T(1024)(128)(4,1)}), s8[1572864]{0:T(1024)(128)(4,1)S(1)}, s32[]{:S(2)}) async-start(s8[5767168]{0:T(1024)(128)(4,1)} %bitcast.167), calls=%async_computation.6 | async-start | bytes 3145728
  626.1 3.5 copy-start.2
  626.1 4.7 copy-start.4
Sparse Core Ops, SparseCore 0:
  644.2 125.6 all-reduce.1
where the time goes:
time: 792 us; the launch traced here: 782 us
  waiting for transfers between devices  277 us (35%)
  blocking collectives  214 us (27%)
  local copies, waits for them, and re-layouts  143 us (18%)
  matrix products  57.5 us (7%)
  other arithmetic  45.5 us (6%)
  starting transfers between devices  29.7 us (4%)
  between operations  14.8 us (2%)
    all_to_all x2, blocking collectives, apply_hamiltonian(): lax.all_to_all(vector, 'grid', split_axis=2, concat_axis=1, tiled=True)  214 us
    ppermute x2, waiting for transfers between devices, with_halo(): lax.ppermute(head, axis, [((i + 1) % count, i) for i in range(count)])  142 us
    psum x1, waiting for transfers between devices, local(): density = lax.psum(group_density, 'orb')  126 us
    gather x2, local copies, waits for them, and re-layouts, nonlocal_term(): values = flattened[:, ghost_index].reshape(orb_count, per_dev, -1)  71.4 us
    scatter-add x2, other arithmetic, nonlocal_term(): jnp.zeros_like(flattened).at[:, ghost_index].add(spread)  28.4 us
    dot_general x2, matrix products, apply_hamiltonian(): jnp.dot(vector.reshape(-1, cols_x), kinetic_x, precision=PRECISE)  26.4 us
    dot_general x2, matrix products, apply_hamiltonian(): jnp.einsum('ozyx,yw->ozwx', vector, kinetic_y, precision=PRECISE)  20.6 us
    unnamed x25, local copies, waits for them, and re-layouts  19.3 us
  transfers between devices with their start and end apart: 11, of which 5 were waited for; matrix products, arithmetic and copies ran while one was open for 23% of the time, Pallas kernels for 0%

commit v1 on v0

v1 whole, which is shorter than its diff:
```python
import functools
import math

import jax
import jax.numpy as jnp
from jax import lax
from jax.experimental import pallas as pl
from jax.experimental.pallas import tpu as pltpu
from jax.sharding import PartitionSpec as P

REACH = 3
WIDE = 2 * REACH + 1
STRIDE = 16
PRECISE = lax.Precision.HIGHEST
CHUNKS = 2


def kinetic_table(length):
    places = jnp.arange(length)
    offset = places[:, None] - places[None, :]
    parity = jnp.where(offset % 2 == 0, 1.0, -1.0).astype(jnp.float32)
    angle_half = offset.astype(jnp.float32) * (math.pi / length)
    sine = jnp.where(offset == 0, 1.0, jnp.sin(angle_half))
    off_diag = parity / (2.0 * sine * sine)
    on_diag = jnp.float32(length * length / 12.0 + 1.0 / 6.0)
    return jnp.where(offset == 0, on_diag, off_diag) * (4.0 / (length * length))


def xor_route(size, bit):
    return [(i, i ^ bit) for i in range(size)]


def xor_bits(size):
    bits = []
    bit = size // 2
    while bit:
        bits.append(bit)
        bit //= 2
    return bits


def sum_over(block, axis):
    size = lax.axis_size(axis)
    for bit in xor_bits(size):
        block = block + lax.ppermute(block, axis, xor_route(size, bit))
    return block


def gather_over(block, axis):
    size = lax.axis_size(axis)
    place = lax.axis_index(axis)
    shape = block.shape
    bits = xor_bits(size)
    for bit in bits:
        other = lax.ppermute(block, axis, xor_route(size, bit))
        upper = (place & bit) != 0
        block = jnp.stack([jnp.where(upper, other, block), jnp.where(upper, block, other)])
    count = len(bits)
    block = jnp.transpose(block, tuple(range(count))[::-1] + tuple(range(count, block.ndim)))
    return block.reshape((size * shape[0],) + shape[1:])


def exchange(block, axis):
    return lax.all_to_all(block, axis, split_axis=0, concat_axis=0, tiled=True)


def window_tiles(starts, corner, atom, total, field_shape):
    planes, tiles = field_shape[0], field_shape[1]
    all_planes, all_tiles = total
    z_start, y_start, x_start = starts[atom, 0], starts[atom, 1], starts[atom, 2]
    z_ahead = lax.rem(z_start - corner[0] + all_planes, all_planes)
    z_behind = lax.rem(corner[0] - z_start + all_planes, all_planes)
    first = lax.rem(y_start // 8 - corner[1] + all_tiles, all_tiles)
    second = lax.rem(first + 1, all_tiles)
    rows = [(jnp.minimum(t, tiles - 1), t < tiles) for t in (first, second)]
    here = ((z_ahead < planes) | (z_behind < WIDE)) & (rows[0][1] | rows[1][1])
    depth = []
    for dz in range(WIDE):
        z = lax.rem(z_ahead + dz, all_planes)
        depth.append((jnp.minimum(z, planes - 1), z < planes))
    return here, depth, rows, y_start % 8, x_start


def pick_kernel(total, starts, corner, spots, field, values):
    values[...] = jnp.zeros_like(values)
    columns = field.shape[3]
    lane = lax.broadcasted_iota(jnp.int32, (8, 128), 1)
    row = lax.broadcasted_iota(jnp.int32, (8, 128), 0)
    slot = lax.broadcasted_iota(jnp.int32, (128, 128), 0)

    def one(atom, carry):
        here, depth, rows, shift, x_start = window_tiles(starts, corner, atom, total, field.shape)

        @pl.when(here)
        def _():
            halves = []
            for tile, row_in in rows:
                half = jnp.zeros((8, 128), jnp.float32)
                for dz, (z, z_in) in enumerate(depth):
                    turn = lax.rem(STRIDE * dz - x_start + columns, columns)
                    turned = pltpu.roll(field[z, tile], turn, 1)[:, :128]
                    mine = (lane >= STRIDE * dz) & (lane < STRIDE * dz + WIDE)
                    half = jnp.where(mine & (row_in & z_in), turned, half)
                halves.append(half)
            both = pltpu.roll(jnp.concatenate(halves, axis=0), lax.rem(16 - shift, 16), 0)[:8]
            spot = spots[atom]
            chosen = (slot == spot[1:2]).astype(jnp.float32)
            found = jnp.dot(both, chosen, precision=PRECISE, preferred_element_type=jnp.float32)
            found = jnp.where(row == spot[0:1], found, 0.0)
            values[pl.ds(atom, 1)] = jnp.sum(found, axis=0, keepdims=True)[None]

        return carry

    lax.fori_loop(0, values.shape[0], one, 0)


def put_kernel(total, starts, corner, spots, spread, base, field):
    field[...] = base[...]
    columns = field.shape[3]
    lane = lax.broadcasted_iota(jnp.int32, (8, 128), 1)
    row = lax.broadcasted_iota(jnp.int32, (8, 128), 0)
    slot = lax.broadcasted_iota(jnp.int32, (128, 128), 0)
    empty = jnp.zeros((8, columns - 128), jnp.float32)

    def one(atom, carry):
        here, depth, rows, shift, x_start = window_tiles(starts, corner, atom, total, field.shape)

        @pl.when(here)
        def _():
            spot = spots[atom]
            chosen = (slot == spot[1:2]).astype(jnp.float32)
            amounts = jnp.where(row == spot[0:1], spread[atom], 0.0)
            window = lax.dot_general(
                amounts,
                chosen,
                (((1,), (1,)), ((), ())),
                precision=PRECISE,
                preferred_element_type=jnp.float32,
            )
            both = pltpu.roll(jnp.concatenate([window, jnp.zeros_like(window)], axis=0), shift, 0)
            for half, (tile, row_in) in enumerate(rows):
                part = both[8 * half : 8 * half + 8]
                for dz, (z, z_in) in enumerate(depth):

                    @pl.when(row_in & z_in)
                    def _():
                        mine = (lane >= STRIDE * dz) & (lane < STRIDE * dz + WIDE)
                        piece = jnp.concatenate([jnp.where(mine, part, 0.0), empty], axis=1)
                        turn = lax.rem(x_start - STRIDE * dz + columns, columns)
                        field[z, tile] += pltpu.roll(piece, turn, 1)

        return carry

    lax.fori_loop(0, spread.shape[0], one, 0)


def tiled(field):
    return field.reshape(field.shape[0], field.shape[1] // 8, 8, field.shape[2])


SMEM = pl.BlockSpec(memory_space=pltpu.SMEM)
VMEM = pl.BlockSpec(memory_space=pltpu.VMEM)
PARAMS = pltpu.CompilerParams(vmem_limit_bytes=48 * 2**20)


def pick(total, starts, corner, spots, field):
    return pl.pallas_call(
        functools.partial(pick_kernel, total),
        out_shape=jax.ShapeDtypeStruct((starts.shape[0], 1, 128), jnp.float32),
        in_specs=[SMEM, SMEM, VMEM, VMEM],
        out_specs=VMEM,
        compiler_params=PARAMS,
        cost_estimate=pl.CostEstimate(flops=1 << 24, bytes_accessed=1 << 23, transcendentals=0),
        name="pick",
    )(starts, corner, spots, tiled(field))


def put(total, starts, corner, spots, spread, base):
    shaped = tiled(base)
    return pl.pallas_call(
        functools.partial(put_kernel, total),
        out_shape=jax.ShapeDtypeStruct(shaped.shape, jnp.float32),
        in_specs=[SMEM, SMEM, VMEM, VMEM, VMEM],
        out_specs=VMEM,
        compiler_params=PARAMS,
        cost_estimate=pl.CostEstimate(flops=1 << 24, bytes_accessed=1 << 23, transcendentals=0),
        name="put",
    )(starts, corner, spots, spread, shaped).reshape(base.shape)


def atom_windows(cells, all_planes, rows_y, cols_x):
    parts = []
    for coords, size in (
        (cells[:, 0], all_planes),
        (cells[:, 1] // cols_x, rows_y),
        (cells[:, 1] % cols_x, cols_x),
    ):
        anchor = coords[:, :1]
        apart = (coords - anchor + size // 2) % size - size // 2
        least = jnp.min(apart, axis=1, keepdims=True)
        parts.append(((anchor + least) % size, apart - least))
    starts = jnp.concatenate([start for start, _ in parts], axis=1)
    (_, off_z), (_, off_y), (_, off_x) = parts
    spots = jnp.stack([off_y, off_z * STRIDE + off_x], axis=1)
    return starts.astype(jnp.int32), spots.astype(jnp.int32)


def local(random_orbitals, potential, sphere_cells, projectors, kb_energy, cheb_coef):
    grid_count = lax.axis_size("grid")
    grid_pos = lax.axis_index("grid")
    orb_groups = lax.axis_size("orb")
    orb_pos = lax.axis_index("orb")
    planes, rows_y, cols_x = potential.shape
    all_planes = planes * grid_count
    rows = rows_y // grid_count
    orb_count = random_orbitals.shape[0]
    kinetic_x = kinetic_table(cols_x)
    kinetic_y = kinetic_table(rows_y)
    kinetic_z = kinetic_table(all_planes)
    c0, c1, c2 = cheb_coef[0], cheb_coef[1], cheb_coef[2]
    c1_4 = c1 / 4.0
    c2_8 = c2 / 8.0

    def to_blocks(field):
        wide = field.shape[2]
        parts = field.reshape(planes, grid_count, rows, wide).transpose(1, 0, 2, 3)
        return exchange(parts, "grid").reshape(all_planes, rows, wide)

    def to_slab(field):
        wide = field.shape[2]
        parts = exchange(field.reshape(grid_count, planes, rows, wide), "grid")
        return parts.transpose(1, 0, 2, 3).reshape(planes, rows_y, wide)

    def in_plane(field):
        along_x = jnp.dot(field.reshape(-1, cols_x), kinetic_x, precision=PRECISE).reshape(field.shape)
        return along_x + jnp.einsum("zyx,yw->zwx", field, kinetic_y, precision=PRECISE)

    def along_z(field):
        return jnp.einsum("wz,zyx->wyx", kinetic_z, field, precision=PRECISE)

    raw = jnp.concatenate([sphere_cells.astype(jnp.float32), projectors], axis=1)
    raw = gather_over(raw, "grid")
    cells = raw[:, :2].astype(jnp.int32)
    projs = raw[:, 2:]
    starts, spots = atom_windows(cells, all_planes, rows_y, cols_x)
    total = (all_planes, rows_y // 8)
    slab_corner = jnp.stack([grid_pos * planes, jnp.zeros_like(grid_pos)]).astype(jnp.int32)
    first_row = grid_pos * rows
    block_corner = jnp.stack([jnp.zeros_like(grid_pos), first_row // 8]).astype(jnp.int32)

    def pick_slab(field):
        return pick(total, starts, slab_corner, spots, field)

    def pick_block(field):
        if rows % 8:
            padded = jnp.zeros((all_planes, -(-rows // 8) * 8, cols_x), jnp.float32)
            field = lax.dynamic_update_slice(padded, field, (0, first_row % 8, 0))
        return pick(total, starts, block_corner, spots, field)

    def amounts(values):
        coeffs = jnp.einsum("aj,apj->ap", values[:, 0], projs, precision=PRECISE)
        coeffs = sum_over(coeffs, "grid") * kb_energy
        return jnp.einsum("ap,apj->aj", coeffs, projs, precision=PRECISE)[:, None]

    def put_slab(spread, base):
        return put(total, starts, slab_corner, spots, spread, base)

    part = cols_x // orb_groups

    def shared_blocks(after):
        mine = lax.dynamic_slice_in_dim(potential, orb_pos * part, part, axis=2)
        mine, after = lax.optimization_barrier((mine, after))
        got = to_blocks(mine)
        got = gather_over(got[None], "orb")
        return jnp.moveaxis(got, 0, 2).reshape(all_planes, rows, cols_x), after

    wide = cols_x // CHUNKS
    pieces = [[] for _ in range(CHUNKS)]
    block_potential = None
    for orb in range(orb_count):
        v = random_orbitals[orb]
        v_block = to_blocks(v)
        if block_potential is None:
            block_potential, v_block = shared_blocks(v_block)
        pv = in_plane(v)
        u = put_slab(amounts(pick_slab(v)), pv + (potential - 2.0) * v)
        g = pv + u
        a = along_z(v_block)
        bu = in_plane(u) + (potential - 2.0) * u
        base = (c0 - c2) * v + c1_4 * u + c2_8 * bu
        q = put_slab(c2_8 * amounts(pick_slab(u) + pick_block(a)), base)
        for i in range(CHUNKS):
            cols = slice(i * wide, (i + 1) * wide)
            g_block = to_blocks(g[:, :, cols])
            a_i = a[:, :, cols]
            m = along_z(c1_4 * v_block[:, :, cols] + c2_8 * (g_block + a_i))
            m = m + c2_8 * (block_potential[:, :, cols] - 2.0) * a_i
            filtered = q[:, :, cols] + to_slab(m)
            pieces[i].append(filtered * filtered)
    out = []
    for parts in pieces:
        own = functools.reduce(jnp.add, parts)
        out.append(sum_over(own, "orb") * (1.0 / (orb_count * orb_groups)))
    return jnp.concatenate(out, axis=2)


def solution(mesh):
    in_specs = (
        P("orb", "grid", None, None),
        P("grid", None, None),
        P("grid", None, None),
        P("grid", None, None),
        P(),
        P(),
    )
    out_specs = P("grid", None, None)
    return jax.shard_map(local, mesh=mesh, in_specs=in_specs, out_specs=out_specs, check_vma=False)
```

time: 792 us -> 665 us (0.84)
  blocking collectives: 214 us -> 0 us
  Pallas kernels: 0 us -> 135 us
  local copies, waits for them, and re-layouts: 143 us -> 56.8 us
  starting transfers between devices: 29.7 us -> 70.7 us
  waiting for transfers between devices: 277 us -> 308 us
  other arithmetic: 45.5 us -> 30.1 us
  between operations: 14.8 us -> 3.48 us
    all_to_all x2 -> x0, blocking collectives: 214 us -> none  [apply_hamiltonian(): lax.all_to_all(vector, 'grid', split_axis=2, concat_axis=1, tiled=True)]
    all_to_all x2 -> x6, waiting for transfers between devices: 0.01 us -> 137 us  [exchange(): return lax.all_to_all(block, axis, split_axis=0, concat_axis=0, tiled=True)]
    pallas_call x0 -> x5, Pallas kernels: none -> 135 us  [the longest x2 77.5 us: put(): pl.pallas_call(functools.partial(put_kernel, total), out_shape=jax.ShapeD...]
    psum x1 -> x0, waiting for transfers between devices: 126 us -> none  [local(): density = lax.psum(group_density, 'orb')]
    gather x2 -> x0, local copies, waits for them, and re-layouts: 71.4 us -> none  [nonlocal_term(): values = flattened[:, ghost_index].reshape(orb_count, per_dev, -1)]
    all_to_all x2 -> x6, starting transfers between devices: 10.8 us -> 55.1 us  [exchange(): return lax.all_to_all(block, axis, split_axis=0, concat_axis=0, tiled=True)]
    scatter-add x6 -> x0, other arithmetic: 35.7 us -> none  [the longest x2 28.4 us: nonlocal_term(): jnp.zeros_like(flattened).at[:, ghost_index].add(spread)]
    ppermute x8 -> x15, waiting for transfers between devices: 151 us -> 171 us  [the longest x10 136 us: sum_over(): block = block + lax.ppermute(block, axis, xor_route(size, bit))]
  transfers between devices with their start and end apart: 11 -> 21, of which waited for: 5 -> 12; matrix products, arithmetic and copies ran while one was open for 23% -> 16% of each run, Pallas kernels for 0% -> 20%
where the time goes in v1:
time: 665 us; the launch traced here: 661 us
  waiting for transfers between devices  308 us (46%)
  Pallas kernels  135 us (20%)
  starting transfers between devices  70.7 us (11%)
  matrix products  57.1 us (9%)
  local copies, waits for them, and re-layouts  56.8 us (9%)
  other arithmetic  30.1 us (5%)
    all_to_all x6, waiting for transfers between devices, exchange(): return lax.all_to_all(block, axis, split_axis=0, concat_axis=0, tiled=True)  137 us
    ppermute x10, waiting for transfers between devices, sum_over(): block = block + lax.ppermute(block, axis, xor_route(size, bit))  136 us
    pallas_call x2, Pallas kernels, put(): pl.pallas_call(functools.partial(put_kernel, total), out_shape=jax.ShapeD...  77.5 us
    pallas_call x3, Pallas kernels, pick(): pl.pallas_call(functools.partial(pick_kernel, total), out_shape=jax.Shape...  57.3 us
    all_to_all x6, starting transfers between devices, exchange(): return lax.all_to_all(block, axis, split_axis=0, concat_axis=0, tiled=True)  55.1 us
    ppermute x5, waiting for transfers between devices, gather_over(): other = lax.ppermute(block, axis, xor_route(size, bit))  35.5 us
    dot_general x2, matrix products, in_plane(): jnp.dot(field.reshape(-1, cols_x), kinetic_x, precision=PRECISE)  18.4 us
    dot_general x3, matrix products, along_z(): return jnp.einsum('wz,zyx->wyx', kinetic_z, field, precision=PRECISE)  15.9 us
  transfers between devices with their start and end apart: 21, of which 12 were waited for; matrix products, arithmetic and copies ran while one was open for 16% of the time, Pallas kernels for 20%

profile of v1, /device:TPU:0, one launch (start us, length us, event | category | flops | bytes accessed | tf_op | source)
XLA Modules:
  0.0 660.7 jit_solution(8721685029296968025)
XLA Ops:
  1.5 4.1 collective-permute-start
  5.6 3.6 collective-permute-done
  10.7 6.6 copy.149
  17.3 5.9 all-to-all-start
  23.3 2.1 collective-permute-start.2
  25.4 30.0 %collective-permute-done.2 = f32[2,2,16,6,128]{4,3,2,1,0:T(8,128)S(1)} collective-permute-done((f32[2,2,16,6,128]{4,3,2,1,0:T(8,128)S(1)}, f32[2,2,16,6,128]{4,3,2,1,0:T(8,128)S(1)}, u32[]{:S(2)}, u32[]{:S(2)}) %collective-permute-start.2) | collective-permute-done | bytes 196640 | tf_op jit(solution)/shard_map/ppermute | solution.py:55
  55.7 1.8 collective-permute-done.3
  60.1 3.9 fusion.84
  64.2 20.0 %pick.3 = f32[256,1,128]{2,1,0:T(1,128)S(1)} custom-call(s32[256,3]{1,0:T(8,128)S(1)} %pad_add_fusion.1.starts, s32[2]{0:T(128)S(1)} %get-tuple-element.43.corner, s32[256,2,128]{2,1,0:T(2,128)S(1)} %pad_add_fusion.spots, f32[16,32,8,256]{3,2,1,0:T(8,128)S(1)} %bitcast.215), custom_call_target="tpu_custom_call" | custom-call | flops 16777216 | bytes 8388608 | tf_op jit(solution)/shard_map/pick/pallas_call | solution.py:167
  84.3 2.0 fusion.37
  86.6 36.2 %collective-permute-done.4 = f32[256,4]{1,0:T(8,128)S(1)} collective-permute-done((f32[256,4]{1,0:T(8,128)S(1)}, f32[256,4]{1,0:T(8,128)S(1)}, u32[]{:S(2)}, u32[]{:S(2)}) %collective-permute-start.4) | collective-permute-done | bytes 4128 | tf_op jit(solution)/shard_map/ppermute | solution.py:45
  122.9 10.4 %convolution_bitcast_fusion = f32[4096,256]{0,1:T(8,128)} fusion(f32[4096,256]{1,0:T(8,128)S(1)} %bitcast.216), kind=kOutput, calls=%fused_computation | convolution fusion | flops 3222732800 | bytes 8388608 | tf_op jit(solution)/shard_map/dot_general | solution.py:235
  133.3 5.7 copy.177
  139.0 1.5 collective-permute-start.6
  140.6 9.4 %bitcast_add_fusion.2 = f32[16,256,256]{2,1,0:T(8,128)S(1)} fusion(f32[16,256,256]{2,1,0:T(8,128)} %bitcast.224, f32[1,16,256,256]{3,2,1,0:T(8,128)} %param.6), kind=kOutput, calls=%fused_computation.16 | convolution fusion | flops 3223781376 | bytes 12582912 | tf_op jit(solution)/shard_map/zyx,yw->zwx/dot_general | solution.py:236
  150.1 2.8 fusion.12.base
  153.0 2.0 fusion.35.spread
  155.0 38.7 %put.2.field = f32[16,32,8,256]{3,2,1,0:T(8,128)S(1)} custom-call(s32[256,3]{1,0:T(8,128)S(1)} %pad_add_fusion.1.starts, s32[2]{0:T(128)S(1)} %get-tuple-element.43.corner, s32[256,2,128]{2,1,0:T(2,128)S(1)} %pad_add_fusion.spots, f32[256,1,128]{2,1,0:T(1,128)S(1)} %fusion.35.spread, f32[16,32,8,256]{3,2,1,0:T(8,128)} %fusion.12.base), custom_call_target="tpu_custom_call" | custom-call | flops 16777216 | bytes 8388608 | tf_op jit(solution)/shard_map/put/pallas_call | solution.py:180
  195.9 1.8 fusion.152
  197.7 1.6 copy.208
  199.3 3.7 all-to-all-start.1
  203.1 1.7 constant_dynamic-slice_fusion
  204.8 4.8 copy.150
  209.6 1.6 copy.155
  211.2 32.9 %all-to-all-done.1 = f32[16,16,16,128]{3,2,1,0:T(8,128)S(1)} async-done(((f32[16,16,16,128]{3,2,1,0:T(8,128)}), f32[16,16,16,128]{3,2,1,0:T(8,128)S(1)}, u32[]{:S(2)}, u32[]{:S(2)}) %all-to-all-start.1) | async-done | bytes 2097184 | tf_op jit(solution)/shard_map/all_to_all | solution.py:64
  245.5 11.2 %all-to-all-start.2 = ((f32[16,16,16,128]{3,2,1,0:T(8,128)}), f32[16,16,16,128]{3,2,1,0:T(8,128)S(1)}, u32[]{:S(2)}, u32[]{:S(2)}) async-start(f32[16,16,16,128]{3,2,1,0:T(8,128)} %copy.155), calls=%async_computation.2 | async-start | bytes 4194304 | tf_op jit(solution)/shard_map/all_to_all | solution.py:64
  256.6 3.2 copy.207
  259.9 37.9 %all-to-all-done.2 = f32[16,16,16,128]{3,2,1,0:T(8,128)S(1)} async-done(((f32[16,16,16,128]{3,2,1,0:T(8,128)}), f32[16,16,16,128]{3,2,1,0:T(8,128)S(1)}, u32[]{:S(2)}, u32[]{:S(2)}) %all-to-all-start.2) | async-done | bytes 2097184 | tf_op jit(solution)/shard_map/all_to_all | solution.py:64
  297.8 11.7 %all-to-all-start.4 = ((f32[16,16,16,128]{3,2,1,0:T(8,128)}), f32[16,16,16,128]{3,2,1,0:T(8,128)}, u32[]{:S(2)}, u32[]{:S(2)}) async-start(f32[16,16,16,128]{3,2,1,0:T(8,128)} %bitcast.227), calls=%async_computation.4 | async-start | bytes 4194304 | tf_op jit(solution)/shard_map/all_to_all | solution.py:64
  309.4 2.0 copy.156
  311.5 1.5 collective-permute-start.12
  314.9 3.6 copy.154
  318.5 31.7 %all-to-all-done.4 = f32[16,16,16,128]{3,2,1,0:T(8,128)} async-done(((f32[16,16,16,128]{3,2,1,0:T(8,128)}), f32[16,16,16,128]{3,2,1,0:T(8,128)}, u32[]{:S(2)}, u32[]{:S(2)}) %all-to-all-start.4) | async-done | bytes 2097184 | tf_op jit(solution)/shard_map/all_to_all | solution.py:64
  350.2 2.4 copy.163
  353.0 5.2 fusion.48
  358.2 3.1 fusion.28
  361.4 2.3 broadcast_select_fusion.1
  363.7 6.0 maximum_bitcast_fusion
  369.7 6.7 %reshape.115 = f32[256,16,256]{2,0,1:T(8,128)} reshape(f32[256,16,2,128]{3,2,0,1:T(2,128)} %maximum_bitcast_fusion) | data formatting | bytes 8388608 | tf_op jit(solution)/shard_map/reshape | solution.py:275
  376.3 5.4 fusion.19
  381.7 1.6 copy.164
  383.3 11.4 %all-to-all-start.5 = ((f32[16,16,16,128]{3,1,2,0:T(8,128)}), f32[16,16,16,128]{3,1,2,0:T(8,128)}, u32[]{:S(2)}, u32[]{:S(2)}) async-start(f32[16,16,16,128]{3,1,2,0:T(8,128)} %copy.164), calls=%async_computation.5 | async-start | bytes 4194304 | tf_op jit(solution)/shard_map/all_to_all | solution.py:64
  394.8 5.4 fusion.23
  400.1 1.6 copy.160
  401.7 34.2 %all-to-all-done.5 = f32[16,16,16,128]{3,1,2,0:T(8,128)} async-done(((f32[16,16,16,128]{3,1,2,0:T(8,128)}), f32[16,16,16,128]{3,1,2,0:T(8,128)}, u32[]{:S(2)}, u32[]{:S(2)}) %all-to-all-start.5) | async-done | bytes 2097184 | tf_op jit(solution)/shard_map/all_to_all | solution.py:64
  435.9 11.2 %all-to-all-start.3 = ((f32[16,16,16,128]{3,1,2,0:T(8,128)}), f32[16,16,16,128]{3,1,2,0:T(8,128)S(1)}, u32[]{:S(2)}, u32[]{:S(2)}) async-start(f32[16,16,16,128]{3,1,2,0:T(8,128)} %copy.160), calls=%async_computation.3 | async-start | bytes 4194304 | tf_op jit(solution)/shard_map/all_to_all | solution.py:64
  447.1 2.2 copy-done.4
  449.3 20.0 %pick.4 = f32[256,1,128]{2,1,0:T(1,128)S(1)} custom-call(s32[256,3]{1,0:T(8,128)S(1)} %pad_add_fusion.1.starts, s32[2]{0:T(128)S(1)} %get-tuple-element.43.corner, s32[256,2,128]{2,1,0:T(2,128)S(1)} %pad_add_fusion.spots, f32[16,32,8,256]{3,2,1,0:T(8,128)S(1)} %copy-done.4), custom_call_target="tpu_custom_call" | custom-call | flops 16777216 | bytes 8388608 | tf_op jit(solution)/shard_map/pick/pallas_call | solution.py:167
  469.4 2.4 copy.206
  471.8 17.3 %pick.5 = f32[256,1,128]{2,1,0:T(1,128)S(1)} custom-call(s32[256,3]{1,0:T(8,128)S(1)} %pad_add_fusion.1.starts, s32[2]{0:T(128)S(1)} %get-tuple-element.44.corner, s32[256,2,128]{2,1,0:T(2,128)S(1)} %pad_add_fusion.spots, f32[256,2,8,256]{3,2,1,0:T(8,128)S(1)} %bitcast.218), custom_call_target="tpu_custom_call" | custom-call | flops 16777216 | bytes 8388608 | tf_op jit(solution)/shard_map/pick/pallas_call | solution.py:167
  489.1 2.1 fusion.33
  492.2 9.6 %collective-permute-done.8 = f32[256,4]{1,0:T(8,128)S(1)} collective-permute-done((f32[256,4]{1,0:T(8,128)S(1)}, f32[256,4]{1,0:T(8,128)S(1)}, u32[]{:S(2)}, u32[]{:S(2)}) %collective-permute-start.8) | collective-permute-done | bytes 4128 | tf_op jit(solution)/shard_map/ppermute | solution.py:45
  503.1 3.8 collective-permute-done.9
  507.0 1.8 collective-permute-start.10
  508.8 5.2 fusion.4
  514.1 8.0 %fusion.3.base = f32[16,32,8,256]{3,2,1,0:T(8,128)} fusion(f32[256,16,256]{2,0,1:T(8,128)S(1)} %fusion.4, f32[16,32,8,256]{3,2,1,0:T(8,128)S(1)} %copy-done.5, f32[1,16,256,256]{3,2,1,0:T(8,128)S(1)} %copy-done.2, f32[16,256,256]{2,1,0:T(8,128)S(1)} %copy-done.11, f32[]{:T(128)} %bitcast.28, f32[]{:T(128)} %bitcast.63, f32[]{:T(128)} %bitcast.62), kind=kOutput, calls=%fused_computation.7 | convolution fusion | flops 3232169984 | bytes 20971532 | tf_op jit(solution)/shard_map/dot_general | solution.py:235
  522.1 2.1 fusion.31
  524.2 38.7 %put.3 = f32[16,32,8,256]{3,2,1,0:T(8,128)S(1)} custom-call(s32[256,3]{1,0:T(8,128)S(1)} %pad_add_fusion.1.starts, s32[2]{0:T(128)S(1)} %get-tuple-element.43.corner, s32[256,2,128]{2,1,0:T(2,128)S(1)} %pad_add_fusion.spots, f32[256,1,128]{2,1,0:T(1,128)S(1)} %bitcast.219, f32[16,32,8,256]{3,2,1,0:T(8,128)} %fusion.3.base), custom_call_target="tpu_custom_call" | custom-call | flops 16777216 | bytes 8388608 | tf_op jit(solution)/shard_map/put/pallas_call | solution.py:180
  563.0 2.1 copy-done.6
  565.0 4.3 fusion.24
  569.3 1.6 collective-permute-start.13
  571.4 46.5 %collective-permute-done.13 = f32[16,256,128]{2,1,0:T(8,128)S(1)} collective-permute-done((f32[16,256,128]{2,1,0:T(8,128)S(1)}, f32[16,256,128]{2,1,0:T(8,128)S(1)}, u32[]{:S(2)}, u32[]{:S(2)}) %collective-permute-start.13) | collective-permute-done | bytes 2097184 | tf_op jit(solution)/shard_map/ppermute | solution.py:45
  618.3 39.5 %collective-permute-done.14 = f32[16,256,128]{2,1,0:T(8,128)S(1)} collective-permute-done((f32[16,256,128]{2,1,0:T(8,128)S(1)}, f32[16,256,128]{2,1,0:T(8,128)S(1)}, u32[]{:S(2)}, u32[]{:S(2)}) %collective-permute-start.14) | collective-permute-done | bytes 2097184 | tf_op jit(solution)/shard_map/ppermute | solution.py:45
  658.1 2.3 pad_maximum_fusion
  (100 shorter events, 13.6 us)
Async XLA Ops:
  1.5 7.8 %collective-permute-start = (f32[16,6,128]{2,1,0:T(8,128)S(1)}, f32[16,6,128]{2,1,0:T(8,128)S(1)}, u32[]{:S(2)}, u32[]{:S(2)}) collective-permute-start(f32[16,6,128]{2,1,0:T(8,128)S(1)} %pad_maximum_fusion.4), channel_id=1, source_target_pairs={{0,8},{1,9},{2,10},{3,11},{4,12},{5,13},{6,14},{7,15},{8,0},{9,1},... | collective-permute-start | bytes 147464 | tf_op jit(solution)/shard_map/ppermute | solution.py:55
  10.1 13.2 %collective-permute-start.1 = (f32[2,16,6,128]{3,2,1,0:T(8,128)S(1)}, f32[2,16,6,128]{3,2,1,0:T(8,128)S(1)}, u32[]{:S(2)}, u32[]{:S(2)}) collective-permute-start(f32[2,16,6,128]{3,2,1,0:T(8,128)S(1)} %pad_maximum_fusion.3), channel_id=1, source_target_pairs={{0,4},{1,5},{2,6},{3,7},{4,0},{5,1},{6,2},{7,3},{8,12},{9,13},{10,... | collective-permute-start | bytes 294920 | tf_op jit(solution)/shard_map/ppermute | solution.py:55
  17.3 182.0 %all-to-all-start = ((f32[16,16,16,256]{3,1,2,0:T(8,128)}), f32[16,16,16,256]{3,1,2,0:T(8,128)}, u32[]{:S(2)}, u32[]{:S(2)}) async-start(f32[16,16,16,256]{3,1,2,0:T(8,128)} %bitcast.225), calls=%async_computation | async-start | bytes 8388608 | tf_op jit(solution)/shard_map/all_to_all | solution.py:64
  23.3 32.1 %collective-permute-start.2 = (f32[2,2,16,6,128]{4,3,2,1,0:T(8,128)S(1)}, f32[2,2,16,6,128]{4,3,2,1,0:T(8,128)S(1)}, u32[]{:S(2)}, u32[]{:S(2)}) collective-permute-start(f32[2,2,16,6,128]{4,3,2,1,0:T(8,128)S(1)} %pad_maximum_fusion.2), channel_id=1, source_target_pairs={{0,2},{1,3},{2,0},{3,1},{4,6},{5,7},{6,4},{7,5},{8,10},{9,11},{10,... | collective-permute-start | bytes 589832 | tf_op jit(solution)/shard_map/ppermute | solution.py:55
  55.5 2.0 collective-permute-start.3
  59.6 4.6 copy-start
  86.3 36.6 %collective-permute-start.4 = (f32[256,4]{1,0:T(8,128)S(1)}, f32[256,4]{1,0:T(8,128)S(1)}, u32[]{:S(2)}, u32[]{:S(2)}) collective-permute-start(f32[256,4]{1,0:T(8,128)S(1)} %bitcast.250), channel_id=1, source_target_pairs={{0,8},{1,9},{2,10},{3,11},{4,12},{5,13},{6,14},{7,15},{8,0},{9,1},... | collective-permute-start | bytes 12296 | tf_op jit(solution)/shard_map/ppermute | solution.py:45
  122.9 16.1 %collective-permute-start.5 = (f32[256,4]{1,0:T(8,128)S(1)}, f32[256,4]{1,0:T(8,128)S(1)}, u32[]{:S(2)}, u32[]{:S(2)}) collective-permute-start(f32[256,4]{1,0:T(8,128)S(1)} %add.211), channel_id=1, source_target_pairs={{0,4},{1,5},{2,6},{3,7},{4,0},{5,1},{6,2},{7,3},{8,12},{9,13},{10,... | collective-permute-start | bytes 12296 | tf_op jit(solution)/shard_map/ppermute | solution.py:45
  139.0 11.0 %collective-permute-start.6 = (f32[256,4]{1,0:T(8,128)S(1)}, f32[256,4]{1,0:T(8,128)S(1)}, u32[]{:S(2)}, u32[]{:S(2)}) collective-permute-start(f32[256,4]{1,0:T(8,128)S(1)} %add.212), channel_id=1, source_target_pairs={{0,2},{1,3},{2,0},{3,1},{4,6},{5,7},{6,4},{7,5},{8,10},{9,11},{10,... | collective-permute-start | bytes 12296 | tf_op jit(solution)/shard_map/ppermute | solution.py:45
  140.6 9.5 %copy-start.1 = (f32[1,16,256,256]{3,2,1,0:T(8,128)S(1)}, f32[1,16,256,256]{3,2,1,0:T(8,128)}, u32[]{:S(2)}) copy-start(f32[1,16,256,256]{3,2,1,0:T(8,128)} %param.6) | copy-start | bytes 12582916
  140.6 9.5 %copy-start.10 = (f32[16,256,256]{2,1,0:T(8,128)S(1)}, f32[16,256,256]{2,1,0:T(8,128)}, u32[]{:S(2)}) copy-start(f32[16,256,256]{2,1,0:T(8,128)} %param.7) | copy-start | bytes 12582916
  150.0 3.0 copy-start.17
  150.0 2.9 collective-permute-start.7
  193.8 2.2 copy-start.3
  199.3 44.8 %all-to-all-start.1 = ((f32[16,16,16,128]{3,2,1,0:T(8,128)}), f32[16,16,16,128]{3,2,1,0:T(8,128)S(1)}, u32[]{:S(2)}, u32[]{:S(2)}) async-start(f32[16,16,16,128]{3,2,1,0:T(8,128)} %bitcast.226), calls=%async_computation.1 | async-start | bytes 4194304 | tf_op jit(solution)/shard_map/all_to_all | solution.py:64
  244.1 1.4 copy-start.13
  245.5 52.3 %all-to-all-start.2 = ((f32[16,16,16,128]{3,2,1,0:T(8,128)}), f32[16,16,16,128]{3,2,1,0:T(8,128)S(1)}, u32[]{:S(2)}, u32[]{:S(2)}) async-start(f32[16,16,16,128]{3,2,1,0:T(8,128)} %copy.155), calls=%async_computation.2 | async-start | bytes 4194304 | tf_op jit(solution)/shard_map/all_to_all | solution.py:64
  297.8 52.4 %all-to-all-start.4 = ((f32[16,16,16,128]{3,2,1,0:T(8,128)}), f32[16,16,16,128]{3,2,1,0:T(8,128)}, u32[]{:S(2)}, u32[]{:S(2)}) async-start(f32[16,16,16,128]{3,2,1,0:T(8,128)} %bitcast.227), calls=%async_computation.4 | async-start | bytes 4194304 | tf_op jit(solution)/shard_map/all_to_all | solution.py:64
  309.4 3.5 copy-start.16
  311.5 49.9 %collective-permute-start.12 = (f32[1,256,16,128]{3,1,2,0:T(8,128)}, f32[1,256,16,128]{3,1,2,0:T(8,128)}, u32[]{:S(2)}, u32[]{:S(2)}) collective-permute-start(f32[1,256,16,128]{3,1,2,0:T(8,128)} %copy.156), channel_id=1, source_target_pairs={{0,16},{16,0},{1,17},{17,1},{2,18},{18,2},{3,19},{19,3},{4,20},{20... | collective-permute-start | bytes 6291464 | tf_op jit(solution)/shard_map/ppermute | solution.py:55
  350.2 2.8 copy-start.9
  353.0 5.2 copy-start.12
  358.2 3.2 copy-start.7
  369.7 6.7 %copy-start.15 = (f32[256,16,128]{2,0,1:T(8,128)S(1)}, f32[256,16,128]{2,0,1:T(8,128)}, u32[]{:S(2)}) copy-start(f32[256,16,128]{2,0,1:T(8,128)} %get-tuple-element.17) | copy-start | bytes 6291460
  383.3 11.4 %copy-start.14 = (f32[256,16,128]{2,0,1:T(8,128)S(1)}, f32[256,16,128]{2,0,1:T(8,128)}, u32[]{:S(2)}) copy-start(f32[256,16,128]{2,0,1:T(8,128)} %get-tuple-element.16) | copy-start | bytes 6291460
  383.3 52.6 %all-to-all-start.5 = ((f32[16,16,16,128]{3,1,2,0:T(8,128)}), f32[16,16,16,128]{3,1,2,0:T(8,128)}, u32[]{:S(2)}, u32[]{:S(2)}) async-start(f32[16,16,16,128]{3,1,2,0:T(8,128)} %copy.164), calls=%async_computation.5 | async-start | bytes 4194304 | tf_op jit(solution)/shard_map/all_to_all | solution.py:64
  435.9 129.1 %all-to-all-start.3 = ((f32[16,16,16,128]{3,1,2,0:T(8,128)}), f32[16,16,16,128]{3,1,2,0:T(8,128)S(1)}, u32[]{:S(2)}, u32[]{:S(2)}) async-start(f32[16,16,16,128]{3,1,2,0:T(8,128)} %copy.160), calls=%async_computation.3 | async-start | bytes 4194304 | tf_op jit(solution)/shard_map/all_to_all | solution.py:64
  447.1 2.2 copy-start.4
  449.3 20.0 %copy-start.8 = (f32[256,16,256]{2,0,1:T(8,128)S(1)}, f32[256,16,256]{2,0,1:T(8,128)}, u32[]{:S(2)}) copy-start(f32[256,16,256]{2,0,1:T(8,128)} %copy-done.7) | copy-start | bytes 12582916
  471.8 37.0 %copy-start.5 = (f32[16,32,8,256]{3,2,1,0:T(8,128)S(1)}, f32[16,32,8,256]{3,2,1,0:T(8,128)}, u32[]{:S(2)}) copy-start(f32[16,32,8,256]{3,2,1,0:T(8,128)} %copy-done.3) | copy-start | bytes 12582916
  491.1 10.7 %collective-permute-start.8 = (f32[256,4]{1,0:T(8,128)S(1)}, f32[256,4]{1,0:T(8,128)S(1)}, u32[]{:S(2)}, u32[]{:S(2)}) collective-permute-start(f32[256,4]{1,0:T(8,128)S(1)} %bitcast.248), channel_id=1, source_target_pairs={{0,8},{1,9},{2,10},{3,11},{4,12},{5,13},{6,14},{7,15},{8,0},{9,1},... | collective-permute-start | bytes 12296 | tf_op jit(solution)/shard_map/ppermute | solution.py:45
  501.8 5.1 collective-permute-start.9
  507.0 7.0 %collective-permute-start.10 = (f32[256,4]{1,0:T(8,128)S(1)}, f32[256,4]{1,0:T(8,128)S(1)}, u32[]{:S(2)}, u32[]{:S(2)}) collective-permute-start(f32[256,4]{1,0:T(8,128)S(1)} %add.221), channel_id=1, source_target_pairs={{0,2},{1,3},{2,0},{3,1},{4,6},{5,7},{6,4},{7,5},{8,10},{9,11},{10,... | collective-permute-start | bytes 12296 | tf_op jit(solution)/shard_map/ppermute | solution.py:45
  508.8 5.3 copy-start.2
  508.8 5.3 copy-start.11
  514.0 8.1 %collective-permute-start.11 = (f32[256,4]{1,0:T(8,128)S(1)}, f32[256,4]{1,0:T(8,128)S(1)}, u32[]{:S(2)}, u32[]{:S(2)}) collective-permute-start(f32[256,4]{1,0:T(8,128)S(1)} %add.222), channel_id=1, source_target_pairs={{0,1},{1,0},{2,3},{3,2},{4,5},{5,4},{6,7},{7,6},{8,9},{9,8},{10,11... | collective-permute-start | bytes 12296 | tf_op jit(solution)/shard_map/ppermute | solution.py:45
  563.0 2.1 copy-start.6
  569.3 48.6 %collective-permute-start.13 = (f32[16,256,128]{2,1,0:T(8,128)S(1)}, f32[16,256,128]{2,1,0:T(8,128)S(1)}, u32[]{:S(2)}, u32[]{:S(2)}) collective-permute-start(f32[16,256,128]{2,1,0:T(8,128)S(1)} %get-tuple-element.18), channel_id=1, source_target_pairs={{0,16},{16,0},{1,17},{17,1},{2,18},{18,2},{3,19},{19,3},{4,20},{20... | collective-permute-start | bytes 6291464 | tf_op jit(solution)/shard_map/ppermute | solution.py:45
  570.9 86.9 %collective-permute-start.14 = (f32[16,256,128]{2,1,0:T(8,128)S(1)}, f32[16,256,128]{2,1,0:T(8,128)S(1)}, u32[]{:S(2)}, u32[]{:S(2)}) collective-permute-start(f32[16,256,128]{2,1,0:T(8,128)S(1)} %get-tuple-element.19), channel_id=1, source_target_pairs={{0,16},{16,0},{1,17},{17,1},{2,18},{18,2},{3,19},{19,3},{4,20},{20... | collective-permute-start | bytes 6291464 | tf_op jit(solution)/shard_map/ppermute | solution.py:45

commit v2 on v1

v2 whole, which is shorter than its diff:
```python
import functools
import math

import jax
import jax.numpy as jnp
from jax import lax
from jax.experimental import pallas as pl
from jax.experimental.pallas import tpu as pltpu
from jax.sharding import PartitionSpec as P

REACH = 3
WIDE = 2 * REACH + 1
STRIDE = 16
PRECISE = lax.Precision.HIGHEST
TOGETHER = 4


def kinetic_table(length):
    places = jnp.arange(length)
    offset = places[:, None] - places[None, :]
    parity = jnp.where(offset % 2 == 0, 1.0, -1.0).astype(jnp.float32)
    angle_half = offset.astype(jnp.float32) * (math.pi / length)
    sine = jnp.where(offset == 0, 1.0, jnp.sin(angle_half))
    off_diag = parity / (2.0 * sine * sine)
    on_diag = jnp.float32(length * length / 12.0 + 1.0 / 6.0)
    return jnp.where(offset == 0, on_diag, off_diag) * (4.0 / (length * length))


def xor_route(size, bit):
    return [(i, i ^ bit) for i in range(size)]


def xor_bits(size):
    bits = []
    bit = size // 2
    while bit:
        bits.append(bit)
        bit //= 2
    return bits


def sum_over(block, axis):
    size = lax.axis_size(axis)
    for bit in xor_bits(size):
        block = block + lax.ppermute(block, axis, xor_route(size, bit))
    return block


def gather_over(block, axis):
    size = lax.axis_size(axis)
    place = lax.axis_index(axis)
    shape = block.shape
    bits = xor_bits(size)
    for bit in bits:
        other = lax.ppermute(block, axis, xor_route(size, bit))
        upper = (place & bit) != 0
        block = jnp.stack([jnp.where(upper, other, block), jnp.where(upper, block, other)])
    count = len(bits)
    block = jnp.transpose(block, tuple(range(count))[::-1] + tuple(range(count, block.ndim)))
    return block.reshape((size * shape[0],) + shape[1:])


def trade(blocks, axis):
    size = lax.axis_size(axis)
    place = lax.axis_index(axis)
    out = blocks
    for apart in range(1, size):
        sent = lax.dynamic_index_in_dim(blocks, place ^ apart, 0)
        got = lax.ppermute(sent, axis, xor_route(size, apart))
        out = lax.dynamic_update_slice_in_dim(out, got, place ^ apart, 0)
    return out


def exchange(block, axis):
    return lax.all_to_all(block, axis, split_axis=0, concat_axis=0, tiled=True)


def listed(starts, corner, first, limit, total, planes, tiles, listing):
    all_planes, all_tiles = total

    def one(k, count):
        atom = lax.rem(first + k, starts.shape[0])
        ahead = lax.rem(starts[atom, 0] - corner[0] + all_planes, all_planes)
        behind = lax.rem(corner[0] - starts[atom, 0] + all_planes, all_planes)
        tile = lax.rem(starts[atom, 1] // 8 - corner[1] + all_tiles, all_tiles)
        here = ((ahead < planes) | (behind < WIDE)) & ((tile < tiles) | (tile == all_tiles - 1))
        listing[count] = atom
        return count + here.astype(jnp.int32)

    return lax.fori_loop(0, limit, one, jnp.int32(0))


def split3(block):
    high = block.astype(jnp.bfloat16).astype(jnp.float32)
    rest = block - high
    middle = rest.astype(jnp.bfloat16).astype(jnp.float32)
    return jnp.concatenate([high, middle, rest - middle], axis=0).astype(jnp.bfloat16)


def placed(starts, corner, total, atom, planes, tiles, columns, lane):
    all_planes, all_tiles = total
    z_start, y_start, x_start = starts[atom, 0], starts[atom, 1], starts[atom, 2]
    ahead = lax.rem(z_start - corner[0] + all_planes, all_planes)
    depth = [jnp.minimum(lax.rem(ahead + dz, all_planes), planes - 1) for dz in range(WIDE)]
    z_in = lax.rem(ahead + lane // STRIDE, all_planes) < planes
    first = lax.rem(y_start // 8 - corner[1] + all_tiles, all_tiles)
    tile_pair = (first, lax.rem(first + 1, all_tiles))
    lane_pair = (x_start // 128, lax.rem(x_start // 128 + 1, columns // 128))
    return depth, z_in, tile_pair, lane_pair, lax.rem(y_start, 8), lax.rem(x_start, 128)


def corner_of(z, tile, group):
    return z, tile, slice(None), pl.ds(pl.multiple_of(group * 128, 128), 128)


def pick_kernel(total, limit, first, starts, corner, spots, field, values, listing):
    values[...] = jnp.zeros_like(values)
    planes, tiles, _, columns = field.shape
    lane = lax.broadcasted_iota(jnp.int32, (8, 128), 1)
    row = lax.broadcasted_iota(jnp.int32, (8, 128), 0)
    slot = lax.broadcasted_iota(jnp.int32, (128, 128), 0)
    count = listed(starts, corner, first[0], limit, total, planes, tiles, listing)

    def some(group, carry):
        for k in range(TOGETHER):
            atom = listing[jnp.minimum(group * TOGETHER + k, count - 1)]
            depth, z_in, tile_pair, groups, down, right = placed(
                starts, corner, total, atom, planes, tiles, columns, lane
            )
            t0, t1 = (jnp.minimum(t, tiles - 1) for t in tile_pair)
            window = jnp.zeros((8, 128), jnp.float32)
            for dz, z in enumerate(depth):
                upper = jnp.where(lane >= right, field[corner_of(z, t0, groups[0])], field[corner_of(z, t0, groups[1])])
                lower = jnp.where(lane >= right, field[corner_of(z, t1, groups[0])], field[corner_of(z, t1, groups[1])])
                met = jnp.where(row >= down, upper, lower)
                met = pltpu.roll(met, lax.rem(STRIDE * dz - right + 128, 128), 1)
                window = jnp.where(lane // STRIDE == dz, met, window)
            window = pltpu.roll(window, lax.rem(8 - down, 8), 0)
            tile_of = jnp.where(row < 8 - down, tile_pair[0], tile_pair[1])
            window = jnp.where(z_in & (tile_of < tiles), window, 0.0)
            spot = spots[atom]
            chosen = (slot == spot[1:2]).astype(jnp.float32).astype(jnp.bfloat16)
            found = jnp.dot(split3(window), chosen, preferred_element_type=jnp.float32)
            found = found[0:8] + found[8:16] + found[16:24]
            found = jnp.where(row == spot[0:1], found, 0.0)
            values[pl.ds(atom, 1)] = jnp.sum(found, axis=0, keepdims=True)[None]
        return carry

    lax.fori_loop(0, (count + TOGETHER - 1) // TOGETHER, some, 0)


def put_kernel(total, limit, first, starts, corner, spots, spread, base, field, listing):
    field[...] = base[...]
    planes, tiles, _, columns = field.shape
    lane = lax.broadcasted_iota(jnp.int32, (8, 128), 1)
    row = lax.broadcasted_iota(jnp.int32, (8, 128), 0)
    slot = lax.broadcasted_iota(jnp.int32, (128, 128), 0)
    count = listed(starts, corner, first[0], limit, total, planes, tiles, listing)

    def some(group, carry):
        for k in range(TOGETHER):
            at = group * TOGETHER + k
            atom = listing[jnp.minimum(at, count - 1)]
            depth, z_in, (t0, t1), groups, down, right = placed(
                starts, corner, total, atom, planes, tiles, columns, lane
            )
            spot = spots[atom]
            chosen = (slot == spot[1:2]).astype(jnp.float32).astype(jnp.bfloat16)
            amounts = jnp.where(row == spot[0:1], spread[atom], 0.0)
            window = lax.dot_general(
                split3(amounts), chosen, (((1,), (1,)), ((), ())), preferred_element_type=jnp.float32
            )
            window = window[0:8] + window[8:16] + window[16:24]
            window = jnp.where(z_in & (at < count), window, 0.0)
            window = pltpu.roll(window, down, 0)
            for dz, z in enumerate(depth):
                part = jnp.where(lane // STRIDE == dz, window, 0.0)
                part = pltpu.roll(part, lax.rem(right - STRIDE * dz + 128, 128), 1)
                places = [corner_of(z, t, g) for t in (t0, t1) for g in groups]
                before = [field[place] for place in places]
                for i, place in enumerate(places):
                    inside = ((row >= down) if i < 2 else (row < down)) & (
                        (lane >= right) if i % 2 == 0 else (lane < right)
                    )
                    field[place] = before[i] + jnp.where(inside, part, 0.0)
        return carry

    lax.fori_loop(0, (count + TOGETHER - 1) // TOGETHER, some, 0)


def planar_kernel(weights, field, extra, potential, table, low_table, first_out, second_out):
    block = field[0]
    high = block.astype(jnp.bfloat16)
    low = (block - high.astype(jnp.float32)).astype(jnp.bfloat16)

    def times(left, right):
        return jnp.dot(left, right, preferred_element_type=jnp.float32)

    kin = times(high, table[0]) + (times(high, low_table[0]) + times(low, table[0]))
    kin = kin + (times(table[1], high) + (times(low_table[1], high) + times(table[1], low)))
    total = kin + (potential[0] - 2.0) * block
    first_out[0] = weights[0] * kin + weights[1] * block + weights[2] * extra[0]
    second_out[0] = weights[3] * total + weights[4] * block + weights[5] * extra[0]


def tiled(field):
    return field.reshape(field.shape[0], field.shape[1] // 8, 8, field.shape[2])


SMEM = pl.BlockSpec(memory_space=pltpu.SMEM)
VMEM = pl.BlockSpec(memory_space=pltpu.VMEM)
PARAMS = pltpu.CompilerParams(vmem_limit_bytes=48 * 2**20)


def pick(total, limit, first, starts, corner, spots, field):
    return pl.pallas_call(
        functools.partial(pick_kernel, total, limit),
        out_shape=jax.ShapeDtypeStruct((starts.shape[0], 1, 128), jnp.float32),
        in_specs=[SMEM, SMEM, SMEM, VMEM, VMEM],
        out_specs=VMEM,
        scratch_shapes=[pltpu.SMEM((limit + 1,), jnp.int32)],
        compiler_params=PARAMS,
        cost_estimate=pl.CostEstimate(flops=1 << 24, bytes_accessed=1 << 24, transcendentals=0),
        name="pick",
    )(first, starts, corner, spots, tiled(field))


def put(total, limit, first, starts, corner, spots, spread, base):
    shaped = tiled(base)
    return pl.pallas_call(
        functools.partial(put_kernel, total, limit),
        out_shape=jax.ShapeDtypeStruct(shaped.shape, jnp.float32),
        in_specs=[SMEM, SMEM, SMEM, VMEM, VMEM, VMEM],
        out_specs=VMEM,
        scratch_shapes=[pltpu.SMEM((limit + 1,), jnp.int32)],
        compiler_params=PARAMS,
        cost_estimate=pl.CostEstimate(flops=1 << 24, bytes_accessed=1 << 24, transcendentals=0),
        name="put",
    )(first, starts, corner, spots, spread, shaped).reshape(base.shape)


def halves_of(table):
    high = lax.reduce_precision(table, 8, 7)
    return high.astype(jnp.bfloat16), (table - high).astype(jnp.bfloat16)


def planar(weights, field, extra, potential, kinetic_x, kinetic_y):
    planes, rows_y, cols_x = field.shape
    assert rows_y == cols_x
    highs, lows = zip(halves_of(kinetic_x), halves_of(kinetic_y))
    plane = pl.BlockSpec((1, rows_y, cols_x), lambda z: (z, 0, 0))
    tables = pl.BlockSpec((2, rows_y, cols_x), lambda z: (0, 0, 0))
    return pl.pallas_call(
        planar_kernel,
        grid=(planes,),
        out_shape=[jax.ShapeDtypeStruct(field.shape, jnp.float32)] * 2,
        in_specs=[SMEM, plane, plane, plane, tables, tables],
        out_specs=[plane, plane],
        compiler_params=PARAMS,
        cost_estimate=pl.CostEstimate(
            flops=12 * planes * rows_y * cols_x * (rows_y + cols_x) // 2,
            bytes_accessed=20 * planes * rows_y * cols_x,
            transcendentals=0,
        ),
        name="planar",
    )(weights, field, extra, potential, jnp.stack(highs), jnp.stack(lows))


def atom_windows(cells, all_planes, rows_y, cols_x):
    parts = []
    for coords, size in (
        (cells[:, 0], all_planes),
        (cells[:, 1] // cols_x, rows_y),
        (cells[:, 1] % cols_x, cols_x),
    ):
        anchor = coords[:, :1]
        apart = (coords - anchor + size // 2) % size - size // 2
        least = jnp.min(apart, axis=1, keepdims=True)
        parts.append(((anchor + least) % size, apart - least))
    starts = jnp.concatenate([start for start, _ in parts], axis=1)
    (_, off_z), (_, off_y), (_, off_x) = parts
    spots = jnp.stack([off_y, off_z * STRIDE + off_x], axis=1)
    return starts.astype(jnp.int32), spots.astype(jnp.int32)


def after(value, *others):
    return lax.optimization_barrier((value,) + others)[0]


def local(random_orbitals, potential, sphere_cells, projectors, kb_energy, cheb_coef):
    grid_count = lax.axis_size("grid")
    grid_pos = lax.axis_index("grid")
    orb_groups = lax.axis_size("orb")
    orb_pos = lax.axis_index("orb")
    planes, rows_y, cols_x = potential.shape
    all_planes = planes * grid_count
    rows = rows_y // grid_count
    orb_count = random_orbitals.shape[0]
    per_dev = sphere_cells.shape[0]
    atoms = per_dev * grid_count
    chunks = 2 if rows % 16 == 0 else 1
    some_rows = rows // chunks
    part = cols_x // orb_groups
    kinetic_x = kinetic_table(cols_x)
    kinetic_y = kinetic_table(rows_y)
    kinetic_z = kinetic_table(all_planes)
    c0, c1, c2 = cheb_coef[0], cheb_coef[1], cheb_coef[2]
    c1_4 = c1 / 4.0
    c2_8 = c2 / 8.0

    def to_blocks(field):
        got = exchange(field.transpose(1, 0, 2, 3), "grid")
        return got.reshape((all_planes,) + field.shape[2:])

    def along_z(field):
        return jnp.einsum("wz,zyx->wyx", kinetic_z, field, precision=PRECISE)

    raw = jnp.concatenate([sphere_cells.astype(jnp.float32), projectors], axis=1)
    raw = gather_over(raw, "grid")
    cells = raw[:, :2].astype(jnp.int32)
    projs = raw[:, 2:]
    starts, spots = atom_windows(cells, all_planes, rows_y, cols_x)
    total = (all_planes, rows_y // 8)
    zero = jnp.zeros_like(grid_pos)
    slab_corner = jnp.stack([grid_pos * planes, zero])
    first_row = grid_pos * rows
    block_corner = jnp.stack([zero, first_row // 8])
    near = min(3 * per_dev, atoms)
    near_first = ((grid_pos + grid_count - 1) * per_dev % atoms)[None]

    def pick_slab(field):
        return pick(total, near, near_first, starts, slab_corner, spots, field)

    def pick_block(field):
        if rows % 8:
            padded = jnp.zeros((all_planes, -(-rows // 8) * 8, cols_x), jnp.float32)
            field = lax.dynamic_update_slice(padded, field, (0, first_row % 8, 0))
        return pick(total, atoms, zero[None], starts, block_corner, spots, field)

    def amounts(values):
        coeffs = jnp.einsum("aj,apj->ap", values[:, 0], projs, precision=PRECISE)
        coeffs = sum_over(coeffs, "grid") * kb_energy
        return jnp.einsum("ap,apj->aj", coeffs, projs, precision=PRECISE)[:, None]

    def put_slab(spread, base):
        return put(total, near, near_first, starts, slab_corner, spots, spread, base)

    def cut(field):
        return field.reshape(planes, grid_count, rows, field.shape[2])

    block_potential = None
    sums = [0.0] * chunks
    for orb in range(orb_count):
        v = random_orbitals[orb]
        v_block = to_blocks(cut(v))
        if block_potential is None:
            mine = lax.dynamic_slice_in_dim(potential, orb_pos * part, part, axis=2)
            got = to_blocks(cut(after(mine, v_block)))
            got = gather_over(got[None], "orb")
            block_potential = jnp.moveaxis(got, 0, 2).reshape(all_planes, rows, cols_x)
        one = jnp.ones((), jnp.float32)
        none = jnp.zeros((), jnp.float32)
        pv, t = planar(jnp.stack([one, none, none, one, none, none]), v, v, potential, kinetic_x, kinetic_y)
        u = put_slab(amounts(pick_slab(v)), t)
        g = pv + u
        a = along_z(v_block)
        _, base = planar(jnp.stack([none, none, none, c2_8, c1_4, c0 - c2]), u, v, potential, kinetic_x, kinetic_y)
        q = put_slab(c2_8 * amounts(pick_slab(u) + pick_block(a)), base)
        q = q.reshape(planes, rows_y, orb_groups, part)
        q_all = trade(jnp.moveaxis(q, 2, 0), "orb")
        q_all = q_all.reshape(orb_groups, planes, grid_count, chunks, some_rows, part)
        c_block = c1_4 * v_block + c2_8 * a
        b_block = c2_8 * (block_potential - 2.0) * a
        ms = []
        for i in range(chunks):
            lines = slice(i * some_rows, (i + 1) * some_rows)
            send = cut(g)[:, :, lines]
            if i == 0:
                send = after(send, c_block)
            g_block = to_blocks(send)
            ms.append(along_z(c_block[:, lines] + c2_8 * g_block) + b_block[:, lines])
        for i in range(chunks):
            m = ms[i]
            if i > 0:
                m = after(m, q_all)
            m = m.reshape(grid_count, planes, some_rows, orb_groups, part).transpose(3, 0, 1, 2, 4)
            m = m.reshape((orb_groups * grid_count,) + m.shape[2:])
            m = exchange(m, ("orb", "grid")).reshape(orb_groups, grid_count, planes, some_rows, part)
            filtered = q_all[:, :, :, i] + m.transpose(0, 2, 1, 3, 4)
            sums[i] = sums[i] + jnp.sum(filtered * filtered, axis=0)
    out = []
    for own in sums:
        own = own * (1.0 / (orb_count * orb_groups))
        out.append(jnp.moveaxis(gather_over(own[None], "orb"), 0, 3))
    return jnp.stack(out, axis=2).reshape(planes, rows_y, cols_x)


def solution(mesh):
    in_specs = (
        P("orb", "grid", None, None),
        P("grid", None, None),
        P("grid", None, None),
        P("grid", None, None),
        P(),
        P(),
    )
    out_specs = P("grid", None, None)
    return jax.shard_map(local, mesh=mesh, in_specs=in_specs, out_specs=out_specs, check_vma=False)
```

time: 665 us -> 640 us (0.962)
  Pallas kernels: 135 us -> 71.4 us
  blocking collectives: 0 us -> 52.4 us
  starting transfers between devices: 70.7 us -> 42.5 us
  matrix products: 57.1 us -> 29.4 us
  local copies, waits for them, and re-layouts: 56.8 us -> 77.3 us
  waiting for transfers between devices: 308 us -> 320 us
    ppermute x5 -> x7, waiting for transfers between devices: 35.5 us -> 182 us  [gather_over(): other = lax.ppermute(block, axis, xor_route(size, bit))]
    all_to_all x6 -> x5, waiting for transfers between devices: 137 us -> 33.5 us  [exchange(): return lax.all_to_all(block, axis, split_axis=0, concat_axis=0, tiled=True)]
    ppermute x10 -> x8, waiting for transfers between devices: 136 us -> 70.8 us  [sum_over(): block = block + lax.ppermute(block, axis, xor_route(size, bit))]
    pallas_call x5 -> x7, Pallas kernels: 135 us -> 71.4 us  [the longest x2 30.2 us: planar(): pl.pallas_call(planar_kernel, grid=(planes,), out_shape=[jax.ShapeDtypeSt...]
    all_to_all x0 -> x1, blocking collectives: none -> 52.4 us  [exchange(): return lax.all_to_all(block, axis, split_axis=0, concat_axis=0, tiled=True)]
    ppermute x0 -> x1, waiting for transfers between devices: none -> 34.2 us  [trade(): got = lax.ppermute(sent, axis, xor_route(size, apart))]
    dot_general x4 -> x0, matrix products: 33 us -> none  [the longest x2 18.4 us: in_plane(): jnp.dot(field.reshape(-1, cols_x), kinetic_x, precision=PRECISE)]
    all_to_all x6 -> x5, starting transfers between devices: 55.1 us -> 24.7 us  [exchange(): return lax.all_to_all(block, axis, split_axis=0, concat_axis=0, tiled=True)]
  transfers between devices with their start and end apart: 21 -> 21, of which waited for: 12 -> 15; matrix products, arithmetic and copies ran while one was open for 16% -> 17% of each run, Pallas kernels for 20% -> 11%
where the time goes in v2:
time: 640 us; the launch traced here: 632 us
  waiting for transfers between devices  320 us (50%)
  local copies, waits for them, and re-layouts  77.3 us (12%)
  Pallas kernels  71.4 us (11%)
  blocking collectives  52.4 us (8%)
  starting transfers between devices  42.5 us (7%)
  other arithmetic  34.8 us (5%)
  matrix products  29.4 us (5%)
    ppermute x7, waiting for transfers between devices, gather_over(): other = lax.ppermute(block, axis, xor_route(size, bit))  182 us
    ppermute x8, waiting for transfers between devices, sum_over(): block = block + lax.ppermute(block, axis, xor_route(size, bit))  70.8 us
    all_to_all x1, blocking collectives, exchange(): return lax.all_to_all(block, axis, split_axis=0, concat_axis=0, tiled=True)  52.4 us
    ppermute x1, waiting for transfers between devices, trade(): got = lax.ppermute(sent, axis, xor_route(size, apart))  34.2 us
    all_to_all x5, waiting for transfers between devices, exchange(): return lax.all_to_all(block, axis, split_axis=0, concat_axis=0, tiled=True)  33.5 us
    pallas_call x2, Pallas kernels, planar(): pl.pallas_call(planar_kernel, grid=(planes,), out_shape=[jax.ShapeDtypeSt...  30.2 us
    pallas_call x3, Pallas kernels, pick(): pl.pallas_call(functools.partial(pick_kernel, total, limit), out_shape=ja...  26.4 us
    all_to_all x5, starting transfers between devices, exchange(): return lax.all_to_all(block, axis, split_axis=0, concat_axis=0, tiled=True)  24.7 us
  transfers between devices with their start and end apart: 21, of which 15 were waited for; matrix products, arithmetic and copies ran while one was open for 17% of the time, Pallas kernels for 11%

profile of v2, /device:TPU:0, one launch (start us, length us, event | category | flops | bytes accessed | tf_op | source)
XLA Modules:
  0.0 631.6 jit_solution(6633089111652556352)
XLA Ops:
  0.0 6.6 %copy.162 = f32[1,16,256,256]{3,1,2,0:T(8,128)} copy(f32[1,16,256,256]{3,2,1,0:T(8,128)} %param.6) | data formatting | bytes 8388608 | tf_op args[0]
  6.6 7.5 %all-to-all-start = ((f32[16,16,16,256]{3,1,2,0:T(8,128)}), f32[16,16,16,256]{3,1,2,0:T(8,128)}, u32[]{:S(2)}, u32[]{:S(2)}) async-start(f32[16,16,16,256]{3,1,2,0:T(8,128)} %bitcast.226), calls=%async_computation | async-start | bytes 8388608 | tf_op jit(solution)/shard_map/all_to_all | solution.py:75
  14.2 2.8 collective-permute-start
  17.1 93.9 %collective-permute-done = f32[16,6,128]{2,1,0:T(8,128)S(1)} collective-permute-done((f32[16,6,128]{2,1,0:T(8,128)S(1)}, f32[16,6,128]{2,1,0:T(8,128)S(1)}, u32[]{:S(2)}, u32[]{:S(2)}) %collective-permute-start) | collective-permute-done | bytes 49184 | tf_op jit(solution)/shard_map/ppermute | solution.py:55
  111.1 5.0 collective-permute-done.1
  117.7 5.5 collective-permute-done.2
  124.2 1.7 constant_dynamic-slice_fusion
  128.6 4.8 copy.163
  135.0 3.8 all-to-all-start.2
  138.8 1.6 fusion.49
  145.1 5.6 fusion.93
  151.0 7.2 %pick.3 = f32[256,1,128]{2,1,0:T(1,128)S(1)} custom-call(s32[1]{0:T(128)} %bitcast.first, s32[256,3]{1,0:T(8,128)S(1)} %pad_add_fusion.1.starts, s32[2]{0:T(128)S(1)} %get-tuple-element.55.corner, s32[256,2,128]{2,1,0:T(2,128)S(1)} %pad_add_fusion.spots, f32[16,32,8,256]{3,2,1,0:T(8,128)S(1)} %bitcast.218), custom_call_target="tpu_custom_call" | custom-call | flops 16777216 | bytes 16777216 | tf_op jit(solution)/shard_map/pick/pallas_call | solution.py:216
  158.2 2.0 fusion.18
  160.2 2.3 collective-permute-start.4
  163.6 29.8 %collective-permute-done.4 = f32[256,4]{1,0:T(8,128)S(1)} collective-permute-done((f32[256,4]{1,0:T(8,128)S(1)}, f32[256,4]{1,0:T(8,128)S(1)}, u32[]{:S(2)}, u32[]{:S(2)}) %collective-permute-start.4) | collective-permute-done | bytes 4128 | tf_op jit(solution)/shard_map/ppermute | solution.py:45
  194.6 4.0 collective-permute-done.5
  200.2 3.4 collective-permute-done.6
  203.7 14.8 %planar.2 = (f32[16,256,256]{2,1,0:T(8,128)S(1)}, f32[16,256,256]{2,1,0:T(8,128)}) custom-call(f32[6]{0:T(128)S(1)} %copy-done.4, f32[16,256,256]{2,1,0:T(8,128)} %bitcast.215, f32[16,256,256]{2,1,0:T(8,128)} %bitcast.216, f32[16,256,256]{2,1,0:T(8,128)} %potential.3, bf16[2,256,256]{2,1,0:T(8,128)(2,1)S(1)} %get-tuple-element.58.table, ...), custom_call_target="tpu_custom_call" | custom-call | flops 3221225472 | bytes 20971520 | tf_op jit(solution)/shard_map/planar/pallas_call | solution.py:253
  218.5 2.0 fusion.16.spread
  220.6 7.3 %put.2.field = f32[16,32,8,256]{3,2,1,0:T(8,128)S(1)} custom-call(s32[1]{0:T(128)} %bitcast.first, s32[256,3]{1,0:T(8,128)S(1)} %pad_add_fusion.1.starts, s32[2]{0:T(128)S(1)} %get-tuple-element.55.corner, s32[256,2,128]{2,1,0:T(2,128)S(1)} %pad_add_fusion.spots, f32[256,1,128]{2,1,0:T(1,128)S(1)} %fusion.16.spread, f32[16,32,8,256]{3,2,1,0:T(8,128)} %bitcast.238), custom_call_target="tpu_custom_call" | custom-call | flops 16777216 | bytes 16777216 | tf_op jit(solution)/shard_map/put/pallas_call | solution.py:230
  227.9 2.6 bitcast_add_fusion
  230.5 2.0 copy-done.1
  232.5 2.0 copy.169
  236.0 1.9 fusion.125
  239.5 4.8 all-to-all-start.4
  246.2 3.2 copy.191
  249.3 32.4 %collective-permute-done.13 = f32[1,256,16,128]{3,1,2,0:T(8,128)} collective-permute-done((f32[1,256,16,128]{3,1,2,0:T(8,128)}, f32[1,256,16,128]{3,1,2,0:T(8,128)}, u32[]{:S(2)}, u32[]{:S(2)}) %collective-permute-start.13) | collective-permute-done | bytes 2097184 | tf_op jit(solution)/shard_map/ppermute | solution.py:55
  281.8 2.3 broadcast_select_fusion.1
  284.1 5.2 fusion.1
  289.2 6.4 %mul.259 = f32[256,16,256]{2,0,1:T(8,128)} reshape(f32[256,16,2,128]{3,2,0,1:T(2,128)} %fusion.1) | data formatting | bytes 8388608 | tf_op jit(solution)/shard_map/mul | solution.py:373
  295.7 12.5 %multiply_add_fusion = (f32[256,16,256]{2,0,1:T(8,128)}, f32[256,16,256]{2,0,1:T(8,128)}, f32[256,16,256]{2,0,1:T(8,128)}) fusion(f32[]{:T(128)} %bitcast.29, f32[]{:T(128)} %bitcast.64, f32[16,16,16,256]{3,1,0,2:T(8,128)} %copy.163, f32[256,16,256]{2,0,1:T(8,128)} %mul.259, f32[256,16,256]{2,0,1:T(8,128)} %bitcast.222), kind=kOutput, calls=%fused_computation.6 | convolution fusion | flops 3226927104 | bytes 25165832 | tf_op jit(solution)/shard_map/wz,zyx->wyx/dot_general | solution.py:316
  308.2 4.2 all-to-all-start.1
  312.4 2.2 copy-done.2
  314.6 7.0 %pick.4 = f32[256,1,128]{2,1,0:T(1,128)S(1)} custom-call(s32[1]{0:T(128)} %bitcast.first, s32[256,3]{1,0:T(8,128)S(1)} %pad_add_fusion.1.starts, s32[2]{0:T(128)S(1)} %get-tuple-element.55.corner, s32[256,2,128]{2,1,0:T(2,128)S(1)} %pad_add_fusion.spots, f32[16,32,8,256]{3,2,1,0:T(8,128)S(1)} %copy-done.2), custom_call_target="tpu_custom_call" | custom-call | flops 16777216 | bytes 16777216 | tf_op jit(solution)/shard_map/pick/pallas_call | solution.py:216
  321.6 2.4 copy.221
  324.0 12.1 %pick.5 = f32[256,1,128]{2,1,0:T(1,128)S(1)} custom-call(s32[1]{0:T(128)} %constant.160.clone.1.first, s32[256,3]{1,0:T(8,128)S(1)} %pad_add_fusion.1.starts, s32[2]{0:T(128)S(1)} %get-tuple-element.56.corner, s32[256,2,128]{2,1,0:T(2,128)S(1)} %pad_add_fusion.spots, f32[256,2,8,256]{3,2,1,0:T(8,128)S(1)} %bitcast.220), custom_call_target="tpu_custom_call" | custom-call | flops 16777216 | bytes 16777216 | tf_op jit(solution)/shard_map/pick/pallas_call | solution.py:216
  336.2 2.1 fusion.14
  338.3 2.4 collective-permute-start.8
  340.6 26.4 %collective-permute-done.8 = f32[256,4]{1,0:T(8,128)S(1)} collective-permute-done((f32[256,4]{1,0:T(8,128)S(1)}, f32[256,4]{1,0:T(8,128)S(1)}, u32[]{:S(2)}, u32[]{:S(2)}) %collective-permute-start.8) | collective-permute-done | bytes 4128 | tf_op jit(solution)/shard_map/ppermute | solution.py:45
  367.2 5.0 collective-permute-done.9
  375.1 2.1 collective-permute-done.10
  377.3 15.4 %planar.3 = (f32[16,256,256]{2,1,0:T(8,128)}, f32[16,256,256]{2,1,0:T(8,128)}) custom-call(f32[6]{0:T(128)S(1)} %stack.130.weights, f32[16,256,256]{2,1,0:T(8,128)} %bitcast.219, f32[16,256,256]{2,1,0:T(8,128)} %bitcast.217, f32[16,256,256]{2,1,0:T(8,128)} %potential.3, bf16[2,256,256]{2,1,0:T(8,128)(2,1)S(1)} %get-tuple-element.58.table, ...), custom_call_target="tpu_custom_call" | custom-call | flops 3221225472 | bytes 20971520 | tf_op jit(solution)/shard_map/planar/pallas_call | solution.py:253
  392.8 2.0 fusion.12
  394.9 7.5 %put.3 = f32[16,32,8,256]{3,2,1,0:T(8,128)S(1)} custom-call(s32[1]{0:T(128)} %bitcast.first, s32[256,3]{1,0:T(8,128)S(1)} %pad_add_fusion.1.starts, s32[2]{0:T(128)S(1)} %get-tuple-element.55.corner, s32[256,2,128]{2,1,0:T(2,128)S(1)} %pad_add_fusion.spots, f32[256,1,128]{2,1,0:T(1,128)S(1)} %bitcast.221, f32[16,32,8,256]{3,2,1,0:T(8,128)} %bitcast.237), custom_call_target="tpu_custom_call" | custom-call | flops 16777216 | bytes 16777216 | tf_op jit(solution)/shard_map/put/pallas_call | solution.py:230
  402.4 2.0 copy-done.3
  404.4 5.7 reshape_reshape.3
  410.2 4.4 constant_dynamic-slice_fusion.1
  416.1 1.9 broadcast_multiply_fusion
  420.5 4.3 slice_add_fusion
  424.8 2.5 copy.220
  427.4 34.2 %collective-permute-done.12 = f32[1,16,256,128]{3,2,1,0:T(8,128)S(1)} collective-permute-done((f32[1,16,256,128]{3,2,1,0:T(8,128)S(1)}, f32[1,16,256,128]{3,2,1,0:T(8,128)S(1)}, u32[]{:S(2)}, u32[]{:S(2)}) %collective-permute-start.12) | collective-permute-done | bytes 2097184 | tf_op jit(solution)/shard_map/ppermute | solution.py:69
  463.0 3.2 reshape.253
  466.3 4.1 copy.177
  471.8 4.3 all-to-all-start.5
  476.1 2.0 broadcast_multiply_fusion.1
  480.5 4.4 slice_add_fusion.3
  484.9 3.2 reshape.249
  488.1 4.2 copy.173
  492.3 33.5 %all-to-all-done.5 = f32[32,16,8,128]{3,2,1,0:T(8,128)S(1)} async-done(((f32[32,16,8,128]{3,2,1,0:T(8,128)}), f32[32,16,8,128]{3,2,1,0:T(8,128)S(1)}, u32[]{:S(2)}, u32[]{:S(2)}) %all-to-all-start.5) | async-done | bytes 2097184 | tf_op jit(solution)/shard_map/all_to_all | solution.py:75
  525.8 52.4 %all_to_all.30 = f32[32,16,8,128]{3,2,1,0:T(8,128)S(1)} all-to-all(f32[32,16,8,128]{3,2,1,0:T(8,128)} %bitcast.232), channel_id=1, replica_groups=mesh['orb'=2,'grid'=16] {'orb','grid'}, dimensions={0} | all-to-all | bytes 4194304 | tf_op jit(solution)/shard_map/all_to_all | solution.py:75
  578.2 3.3 fusion.9
  583.8 23.9 %collective-permute-done.15 = f32[1,16,16,8,128]{4,3,2,1,0:T(8,128)S(1)} collective-permute-done((f32[1,16,16,8,128]{4,3,2,1,0:T(8,128)S(1)}, f32[1,16,16,8,128]{4,3,2,1,0:T(8,128)S(1)}, u32[]{:S(2)}, u32[]{:S(2)}) %collective-permute-start.15) | collective-permute-done | bytes 1048608 | tf_op jit(solution)/shard_map/ppermute | solution.py:55
  608.1 20.7 %collective-permute-done.14 = f32[1,16,16,8,128]{4,3,2,1,0:T(8,128)S(1)} collective-permute-done((f32[1,16,16,8,128]{4,3,2,1,0:T(8,128)S(1)}, f32[1,16,16,8,128]{4,3,2,1,0:T(8,128)S(1)}, u32[]{:S(2)}, u32[]{:S(2)}) %collective-permute-start.14) | collective-permute-done | bytes 1048608 | tf_op jit(solution)/shard_map/ppermute | solution.py:55
  629.0 2.4 pad_maximum_fusion
  (130 shorter events, 33.4 us)
Async XLA Ops:
  6.6 7.6 %copy-start.20 = (s32[16,2,128]{2,1,0:T(2,128)S(1)}, s32[16,2,128]{2,1,0:T(2,128)}, u32[]{:S(2)}) copy-start(s32[16,2,128]{2,1,0:T(2,128)} %param.8) | copy-start | bytes 49156
  6.6 7.6 %copy-start.19 = (f32[16,4,128]{2,1,0:T(4,128)S(1)}, f32[16,4,128]{2,1,0:T(4,128)}, u32[]{:S(2)}) copy-start(f32[16,4,128]{2,1,0:T(4,128)} %param.9) | copy-start | bytes 98308
  6.6 122.0 %all-to-all-start = ((f32[16,16,16,256]{3,1,2,0:T(8,128)}), f32[16,16,16,256]{3,1,2,0:T(8,128)}, u32[]{:S(2)}, u32[]{:S(2)}) async-start(f32[16,16,16,256]{3,1,2,0:T(8,128)} %bitcast.226), calls=%async_computation | async-start | bytes 8388608 | tf_op jit(solution)/shard_map/all_to_all | solution.py:75
  14.2 96.7 %collective-permute-start = (f32[16,6,128]{2,1,0:T(8,128)S(1)}, f32[16,6,128]{2,1,0:T(8,128)S(1)}, u32[]{:S(2)}, u32[]{:S(2)}) collective-permute-start(f32[16,6,128]{2,1,0:T(8,128)S(1)} %pad_maximum_fusion.6), channel_id=1, source_target_pairs={{0,8},{1,9},{2,10},{3,11},{4,12},{5,13},{6,14},{7,15},{8,0},{9,1},... | collective-permute-start | bytes 147464 | tf_op jit(solution)/shard_map/ppermute | solution.py:55
  111.0 5.1 collective-permute-start.1
  116.2 7.0 %collective-permute-start.2 = (f32[2,2,16,6,128]{4,3,2,1,0:T(8,128)S(1)}, f32[2,2,16,6,128]{4,3,2,1,0:T(8,128)S(1)}, u32[]{:S(2)}, u32[]{:S(2)}) collective-permute-start(f32[2,2,16,6,128]{4,3,2,1,0:T(8,128)S(1)} %pad_maximum_fusion.2), channel_id=1, source_target_pairs={{0,2},{1,3},{2,0},{3,1},{4,6},{5,7},{6,4},{7,5},{8,10},{9,11},{10,... | collective-permute-start | bytes 589832 | tf_op jit(solution)/shard_map/ppermute | solution.py:55
  124.1 2.1 collective-permute-start.3
  126.7 6.8 %copy-start.13 = (f32[2,2,2,2,16,6,128]{6,4,3,2,1,0,5:T(8,128)}, f32[2,2,2,2,16,6,128]{6,4,3,2,1,0,5:T(8,128)S(1)}, u32[]{:S(2)}) copy-start(f32[2,2,2,2,16,6,128]{6,4,3,2,1,0,5:T(8,128)S(1)} %copy.143) | copy-start | bytes 2359300
  127.7 5.7 copy-start.15
  135.0 5.5 copy-start.14
  135.0 97.5 %all-to-all-start.2 = ((f32[16,16,16,128]{3,2,1,0:T(8,128)}), f32[16,16,16,128]{3,2,1,0:T(8,128)S(1)}, u32[]{:S(2)}, u32[]{:S(2)}) async-start(f32[16,16,16,128]{3,2,1,0:T(8,128)} %copy.168), calls=%async_computation.2 | async-start | bytes 4194304 | tf_op jit(solution)/shard_map/all_to_all | solution.py:75
  141.3 3.8 copy-start.18
  141.4 1.1 copy-start.21
  141.6 0.9 copy-start.23
  143.3 1.7 copy-start.22
  143.3 1.7 copy-start.24
  143.4 7.5 %copy-start = (f32[1,16,256,256]{3,2,1,0:T(8,128)S(1)}, f32[1,16,256,256]{3,2,1,0:T(8,128)}, u32[]{:S(2)}) copy-start(f32[1,16,256,256]{3,2,1,0:T(8,128)} %param.6) | copy-start | bytes 12582916
  150.9 7.3 %copy-start.16 = (f32[256,4,128]{2,0,1:T(8,128)S(1)}, f32[256,4,128]{2,0,1:T(8,128)}, u32[]{:S(2)}) copy-start(f32[256,4,128]{2,0,1:T(8,128)} %slice.79) | copy-start | bytes 1572868
  158.2 45.5 %copy-start.4 = (f32[6]{0:T(128)S(1)}, f32[6]{0:T(128)}, u32[]{:S(2)}) copy-start(f32[6]{0:T(128)} %constant.162.clone.1.weights) | copy-start | bytes 76
  160.2 33.2 %collective-permute-start.4 = (f32[256,4]{1,0:T(8,128)S(1)}, f32[256,4]{1,0:T(8,128)S(1)}, u32[]{:S(2)}, u32[]{:S(2)}) collective-permute-start(f32[256,4]{1,0:T(8,128)S(1)} %bitcast.252), channel_id=1, source_target_pairs={{0,8},{1,9},{2,10},{3,11},{4,12},{5,13},{6,14},{7,15},{8,0},{9,1},... | collective-permute-start | bytes 12296 | tf_op jit(solution)/shard_map/ppermute | solution.py:45
  193.5 5.1 collective-permute-start.5
  198.6 5.0 collective-permute-start.6
  203.6 14.9 %collective-permute-start.7 = (f32[256,4]{1,0:T(8,128)S(1)}, f32[256,4]{1,0:T(8,128)S(1)}, u32[]{:S(2)}, u32[]{:S(2)}) collective-permute-start(f32[256,4]{1,0:T(8,128)S(1)} %add.212), channel_id=1, source_target_pairs={{0,1},{1,0},{2,3},{3,2},{4,5},{5,4},{6,7},{7,6},{8,9},{9,8},{10,11... | collective-permute-start | bytes 12296 | tf_op jit(solution)/shard_map/ppermute | solution.py:45
  203.7 14.8 %copy-start.26 = (f32[4]{0:T(128)S(1)}, f32[4]{0:T(128)}, u32[]{:S(2)}) copy-start(f32[4]{0:T(128)} %param.10) | copy-start | bytes 52
  230.5 2.0 copy-start.1
  232.5 3.5 copy-start.7
  234.5 47.3 %collective-permute-start.13 = (f32[1,256,16,128]{3,1,2,0:T(8,128)}, f32[1,256,16,128]{3,1,2,0:T(8,128)}, u32[]{:S(2)}, u32[]{:S(2)}) collective-permute-start(f32[1,256,16,128]{3,1,2,0:T(8,128)} %copy.169), channel_id=1, source_target_pairs={{0,16},{16,0},{1,17},{17,1},{2,18},{18,2},{3,19},{19,3},{4,20},{20... | collective-permute-start | bytes 6291464 | tf_op jit(solution)/shard_map/ppermute | solution.py:55
  239.5 4.8 copy-start.25
  239.5 68.7 %all-to-all-start.4 = ((f32[16,16,8,256]{3,2,1,0:T(8,128)}), f32[16,16,8,256]{3,2,1,0:T(8,128)}, u32[]{:S(2)}, u32[]{:S(2)}) async-start(f32[16,16,8,256]{3,2,1,0:T(8,128)} %bitcast.229), calls=%async_computation.4 | async-start | bytes 4194304 | tf_op jit(solution)/shard_map/all_to_all | solution.py:75
  308.2 162.2 %all-to-all-start.1 = ((f32[16,16,8,256]{3,2,1,0:T(8,128)}), f32[16,16,8,256]{3,2,1,0:T(8,128)S(1)}, u32[]{:S(2)}, u32[]{:S(2)}) async-start(f32[16,16,8,256]{3,2,1,0:T(8,128)} %bitcast.66), calls=%async_computation.1 | async-start | bytes 4194304 | tf_op jit(solution)/shard_map/all_to_all | solution.py:75
  312.4 2.2 copy-start.2
  314.6 7.0 %copy-start.6 = (f32[256,16,256]{2,0,1:T(8,128)S(1)}, f32[256,16,256]{2,0,1:T(8,128)}, u32[]{:S(2)}) copy-start(f32[256,16,256]{2,0,1:T(8,128)} %get-tuple-element.54) | copy-start | bytes 12582916
  338.3 28.8 %collective-permute-start.8 = (f32[256,4]{1,0:T(8,128)S(1)}, f32[256,4]{1,0:T(8,128)S(1)}, u32[]{:S(2)}, u32[]{:S(2)}) collective-permute-start(f32[256,4]{1,0:T(8,128)S(1)} %bitcast.254), channel_id=1, source_target_pairs={{0,8},{1,9},{2,10},{3,11},{4,12},{5,13},{6,14},{7,15},{8,0},{9,1},... | collective-permute-start | bytes 12296 | tf_op jit(solution)/shard_map/ppermute | solution.py:45
  367.1 5.1 collective-permute-start.9
  372.2 5.0 collective-permute-start.10
  377.3 15.5 %collective-permute-start.11 = (f32[256,4]{1,0:T(8,128)S(1)}, f32[256,4]{1,0:T(8,128)S(1)}, u32[]{:S(2)}, u32[]{:S(2)}) collective-permute-start(f32[256,4]{1,0:T(8,128)S(1)} %add.219), channel_id=1, source_target_pairs={{0,1},{1,0},{2,3},{3,2},{4,5},{5,4},{6,7},{7,6},{8,9},{9,8},{10,11... | collective-permute-start | bytes 12296 | tf_op jit(solution)/shard_map/ppermute | solution.py:45
  377.3 15.5 %copy-start.17 = (f32[256,4,128]{2,0,1:T(8,128)S(1)}, f32[256,4,128]{2,0,1:T(8,128)}, u32[]{:S(2)}) copy-start(f32[256,4,128]{2,0,1:T(8,128)} %slice.79) | copy-start | bytes 1572868
  402.4 2.0 copy-start.3
  414.5 47.0 %collective-permute-start.12 = (f32[1,16,256,128]{3,2,1,0:T(8,128)S(1)}, f32[1,16,256,128]{3,2,1,0:T(8,128)S(1)}, u32[]{:S(2)}, u32[]{:S(2)}) collective-permute-start(f32[1,16,256,128]{3,2,1,0:T(8,128)S(1)} %bitcast.241), channel_id=1, source_target_pairs={{0,16},{16,0},{1,17},{17,1},{2,18},{18,2},{3,19},{19,3},{4,20},{20... | collective-permute-start | bytes 6291464 | tf_op jit(solution)/shard_map/ppermute | solution.py:69
  416.1 2.8 copy-start.10
  418.1 2.4 copy-start.8
  420.5 4.3 copy-start.5
  470.4 1.3 copy-start.12
  471.8 54.0 %all-to-all-start.5 = ((f32[32,16,8,128]{3,2,1,0:T(8,128)}), f32[32,16,8,128]{3,2,1,0:T(8,128)S(1)}, u32[]{:S(2)}, u32[]{:S(2)}) async-start(f32[32,16,8,128]{3,2,1,0:T(8,128)} %bitcast.231), calls=%async_computation.5 | async-start | bytes 4194304 | tf_op jit(solution)/shard_map/all_to_all | solution.py:75
  476.1 2.8 copy-start.11
  478.1 2.4 copy-start.9
  581.5 26.1 %collective-permute-start.15 = (f32[1,16,16,8,128]{4,3,2,1,0:T(8,128)S(1)}, f32[1,16,16,8,128]{4,3,2,1,0:T(8,128)S(1)}, u32[]{:S(2)}, u32[]{:S(2)}) collective-permute-start(f32[1,16,16,8,128]{4,3,2,1,0:T(8,128)S(1)} %multiply_bitcast_fusion), channel_id=1, source_target_pairs={{0,16},{16,0},{1,17},{17,1},{2,18},{18,2},{3,19},{19,3},{4,20},{20... | collective-permute-start | bytes 3145736 | tf_op jit(solution)/shard_map/ppermute | solution.py:55
  582.7 46.0 %collective-permute-start.14 = (f32[1,16,16,8,128]{4,3,2,1,0:T(8,128)S(1)}, f32[1,16,16,8,128]{4,3,2,1,0:T(8,128)S(1)}, u32[]{:S(2)}, u32[]{:S(2)}) collective-permute-start(f32[1,16,16,8,128]{4,3,2,1,0:T(8,128)S(1)} %multiply_bitcast_fusion.1), channel_id=1, source_target_pairs={{0,16},{16,0},{1,17},{17,1},{2,18},{18,2},{3,19},{19,3},{4,20},{20... | collective-permute-start | bytes 3145736 | tf_op jit(solution)/shard_map/ppermute | solution.py:55

commit v3 on v2

v3 whole, which is shorter than its diff:
```python
import functools
import math

import jax
import jax.numpy as jnp
from jax import lax
from jax.experimental import pallas as pl
from jax.experimental.pallas import tpu as pltpu
from jax.sharding import PartitionSpec as P

REACH = 3
WIDE = 2 * REACH + 1
STRIDE = 16
PRECISE = lax.Precision.HIGHEST
TOGETHER = 4


def kinetic_table(length):
    places = jnp.arange(length)
    offset = places[:, None] - places[None, :]
    parity = jnp.where(offset % 2 == 0, 1.0, -1.0).astype(jnp.float32)
    angle_half = offset.astype(jnp.float32) * (math.pi / length)
    sine = jnp.where(offset == 0, 1.0, jnp.sin(angle_half))
    off_diag = parity / (2.0 * sine * sine)
    on_diag = jnp.float32(length * length / 12.0 + 1.0 / 6.0)
    return jnp.where(offset == 0, on_diag, off_diag) * (4.0 / (length * length))


def xor_route(size, bit):
    return [(i, i ^ bit) for i in range(size)]


def xor_bits(size):
    bits = []
    bit = size // 2
    while bit:
        bits.append(bit)
        bit //= 2
    return bits


def after(value, *others):
    return lax.optimization_barrier((value,) + others)[0]


def gather_steps(block, axis, waits=()):
    size = lax.axis_size(axis)
    place = lax.axis_index(axis)
    shape = block.shape
    bits = xor_bits(size)
    for i, bit in enumerate(bits):
        if i < len(waits) and waits[i] is not None:
            block = after(block, waits[i])
        other = lax.ppermute(block, axis, xor_route(size, bit))
        upper = (place & bit) != 0
        block = jnp.stack([jnp.where(upper, other, block), jnp.where(upper, block, other)])
    count = len(bits)
    block = jnp.transpose(block, tuple(range(count))[::-1] + tuple(range(count, block.ndim)))
    return block.reshape((size * shape[0],) + shape[1:])


def trade(blocks, axis):
    size = lax.axis_size(axis)
    place = lax.axis_index(axis)
    out = blocks
    for apart in range(1, size):
        sent = lax.dynamic_index_in_dim(blocks, place ^ apart, 0)
        got = lax.ppermute(sent, axis, xor_route(size, apart))
        out = lax.dynamic_update_slice_in_dim(out, got, place ^ apart, 0)
    return out


def exchange(block, axis):
    return lax.all_to_all(block, axis, split_axis=0, concat_axis=0, tiled=True)


def listed(starts, corner, total, planes, tiles, listing):
    all_planes, all_tiles, _ = total

    def one(atom, count):
        ahead = lax.rem(starts[atom, 0] - corner[0] + all_planes, all_planes)
        behind = lax.rem(corner[0] - starts[atom, 0] + all_planes, all_planes)
        tile = lax.rem(starts[atom, 1] // 8 - corner[1] + all_tiles, all_tiles)
        here = ((ahead < planes) | (behind < WIDE)) & ((tile < tiles) | (tile == all_tiles - 1))
        listing[count] = atom
        return count + here.astype(jnp.int32)

    return lax.fori_loop(0, starts.shape[0], one, jnp.int32(0))


def split3(block):
    high = block.astype(jnp.bfloat16).astype(jnp.float32)
    rest = block - high
    middle = rest.astype(jnp.bfloat16).astype(jnp.float32)
    return jnp.concatenate([high, middle, rest - middle], axis=0).astype(jnp.bfloat16)


def placed(starts, corner, total, atom, planes, tiles, lane):
    all_planes, all_tiles, all_groups = total
    z_start, y_start, x_start = starts[atom, 0], starts[atom, 1], starts[atom, 2]
    ahead = lax.rem(z_start - corner[0] + all_planes, all_planes)
    depth = [jnp.minimum(lax.rem(ahead + dz, all_planes), planes - 1) for dz in range(WIDE)]
    z_in = lax.rem(ahead + lane // STRIDE, all_planes) < planes
    first = lax.rem(y_start // 8 - corner[1] + all_tiles, all_tiles)
    tile_pair = (first, lax.rem(first + 1, all_tiles))
    lane_pair = (x_start // 128, lax.rem(x_start // 128 + 1, all_groups))
    return depth, z_in, tile_pair, lane_pair, lax.rem(y_start, 8), lax.rem(x_start, 128)


def corner_of(z, tile, group):
    return z, tile, slice(None), pl.ds(pl.multiple_of(group * 128, 128), 128)


def pick_kernel(total, grouped, starts, corner, spots, field, values, listing):
    values[...] = jnp.zeros_like(values)
    planes, tiles = (field.shape[1], 1) if grouped else field.shape[:2]

    def at(z, tile, group):
        return field[group, z] if grouped else field[corner_of(z, tile, group)]

    lane = lax.broadcasted_iota(jnp.int32, (8, 128), 1)
    row = lax.broadcasted_iota(jnp.int32, (8, 128), 0)
    slot = lax.broadcasted_iota(jnp.int32, (128, 128), 0)
    count = listed(starts, corner, total, planes, tiles, listing)

    def some(group, carry):
        for k in range(TOGETHER):
            atom = listing[jnp.minimum(group * TOGETHER + k, count - 1)]
            depth, z_in, tile_pair, groups, down, right = placed(
                starts, corner, total, atom, planes, tiles, lane
            )
            t0, t1 = (jnp.minimum(t, tiles - 1) for t in tile_pair)
            window = jnp.zeros((8, 128), jnp.float32)
            for dz, z in enumerate(depth):
                upper = jnp.where(lane >= right, at(z, t0, groups[0]), at(z, t0, groups[1]))
                lower = jnp.where(lane >= right, at(z, t1, groups[0]), at(z, t1, groups[1]))
                met = jnp.where(row >= down, upper, lower)
                met = pltpu.roll(met, lax.rem(STRIDE * dz - right + 128, 128), 1)
                window = jnp.where(lane // STRIDE == dz, met, window)
            window = pltpu.roll(window, lax.rem(8 - down, 8), 0)
            tile_of = jnp.where(row < 8 - down, tile_pair[0], tile_pair[1])
            window = jnp.where(z_in & (tile_of < tiles), window, 0.0)
            spot = spots[atom]
            chosen = (slot == spot[1:2]).astype(jnp.float32).astype(jnp.bfloat16)
            found = jnp.dot(split3(window), chosen, preferred_element_type=jnp.float32)
            found = found[0:8] + found[8:16] + found[16:24]
            found = jnp.where(row == spot[0:1], found, 0.0)
            values[pl.ds(atom, 1)] = jnp.sum(found, axis=0, keepdims=True)[None]
        return carry

    lax.fori_loop(0, (count + TOGETHER - 1) // TOGETHER, some, 0)


def put_kernel(total, starts, corner, spots, spread, base, field, listing):
    field[...] = base[...]
    planes, tiles = field.shape[:2]
    lane = lax.broadcasted_iota(jnp.int32, (8, 128), 1)
    row = lax.broadcasted_iota(jnp.int32, (8, 128), 0)
    slot = lax.broadcasted_iota(jnp.int32, (128, 128), 0)
    count = listed(starts, corner, total, planes, tiles, listing)

    def some(group, carry):
        for k in range(TOGETHER):
            at = group * TOGETHER + k
            atom = listing[jnp.minimum(at, count - 1)]
            depth, z_in, (t0, t1), groups, down, right = placed(
                starts, corner, total, atom, planes, tiles, lane
            )
            spot = spots[atom]
            chosen = (slot == spot[1:2]).astype(jnp.float32).astype(jnp.bfloat16)
            amounts = jnp.where(row == spot[0:1], spread[atom], 0.0)
            window = lax.dot_general(
                split3(amounts), chosen, (((1,), (1,)), ((), ())), preferred_element_type=jnp.float32
            )
            window = window[0:8] + window[8:16] + window[16:24]
            window = jnp.where(z_in & (at < count), window, 0.0)
            window = pltpu.roll(window, down, 0)
            for dz, z in enumerate(depth):
                part = jnp.where(lane // STRIDE == dz, window, 0.0)
                part = pltpu.roll(part, lax.rem(right - STRIDE * dz + 128, 128), 1)
                spans = range(field.shape[3] // 128)
                places = [(i, g, corner_of(z, t, g)) for i, t in enumerate((t0, t1)) for g in spans]
                before = [field[place] for _, _, place in places]
                for old, (i, g, place) in zip(before, places):
                    inside = (row < down) if i else (row >= down)
                    inside = inside & (jnp.where(lane >= right, groups[0], groups[1]) == g + corner[2])
                    field[place] = old + jnp.where(inside, part, 0.0)
        return carry

    lax.fori_loop(0, (count + TOGETHER - 1) // TOGETHER, some, 0)


def bf16_pair(block):
    high = block.astype(jnp.bfloat16)
    return high, (block - high.astype(jnp.float32)).astype(jnp.bfloat16)


def times(left, right):
    return jnp.dot(left, right, preferred_element_type=jnp.float32)


def in_plane(block, high_tables, low_tables):
    high, low = bf16_pair(block)
    kin = times(high, high_tables[0]) + (times(high, low_tables[0]) + times(low, high_tables[0]))
    return kin + (times(high_tables[1], high) + (times(low_tables[1], high) + times(high_tables[1], low)))


def first_kernel(field, potential, high_tables, low_tables, kin_out, all_out):
    block = field[0]
    kin = in_plane(block, high_tables, low_tables)
    kin_out[0] = kin
    all_out[0] = kin + (potential[0] - 2.0) * block


def second_kernel(weights, field, extra, potential, high_tables, low_tables, out):
    block = field[0]
    total = in_plane(block, high_tables, low_tables) + (potential[0] - 2.0) * block
    total = weights[0] * total + weights[1] * block + weights[2] * extra[0]
    part = out.shape[3]
    for i in range(out.shape[0]):
        out[i, 0] = total[:, i * part : (i + 1) * part]


def depth_times(high_table, low_table, block):
    high, low = bf16_pair(block)
    return times(high_table[...], high) + (times(low_table[...], high) + times(high_table[...], low))


def lines_of(ref, group, start, rows, planes, r):
    line = pl.ds(start + group * planes * rows + r, planes, stride=rows)
    return jnp.concatenate([ref[d, line, :] for d in range(ref.shape[0])], axis=0)


def out_kernel(rows, weights, field, potential, high_table, low_table, a_out, c_out, b_out):
    groups, everywhere = a_out.shape[0], high_table.shape[0]
    planes = everywhere // field.shape[0]

    def one(r, carry):
        v = jnp.concatenate([lines_of(field, g, 0, rows, planes, r) for g in range(groups)], axis=1)
        a = depth_times(high_table, low_table, v)
        for g in range(groups):
            cols = slice(128 * g, 128 * g + 128)
            well = lines_of(potential.at[g], 0, 0, rows, planes, r) - 2.0
            line = pl.ds(r, everywhere, stride=rows)
            a_out[g, line, :] = a[:, cols]
            c_out[g, line, :] = weights[0] * v[:, cols] + weights[1] * a[:, cols]
            b_out[g, line, :] = weights[1] * well * a[:, cols]
        return carry

    lax.fori_loop(0, rows, one, 0)


def back_kernel(rows, weights, g_in, c_in, b_in, high_table, low_table, out):
    groups, everywhere = out.shape[0], high_table.shape[0]
    planes = everywhere // g_in.shape[0]

    def one(r, carry):
        line = pl.ds(r, everywhere, stride=rows)
        parts = [
            c_in[g, line, :] + weights[1] * lines_of(g_in, g, 0, rows, planes, r) for g in range(groups)
        ]
        m = depth_times(high_table, low_table, jnp.concatenate(parts, axis=1))
        for g in range(groups):
            out[g, line, :] = m[:, 128 * g : 128 * g + 128] + b_in[g, line, :]
        return carry

    lax.fori_loop(0, rows, one, 0)


def tiled(field):
    return field.reshape(field.shape[0], field.shape[1] // 8, 8, field.shape[2])


SMEM = pl.BlockSpec(memory_space=pltpu.SMEM)
VMEM = pl.BlockSpec(memory_space=pltpu.VMEM)
PARAMS = pltpu.CompilerParams(vmem_limit_bytes=48 * 2**20)


def pick(total, starts, corner, spots, field, grouped=False):
    return pl.pallas_call(
        functools.partial(pick_kernel, total, grouped),
        out_shape=jax.ShapeDtypeStruct((starts.shape[0], 1, 128), jnp.float32),
        in_specs=[SMEM, SMEM, VMEM, VMEM],
        out_specs=VMEM,
        scratch_shapes=[pltpu.SMEM((starts.shape[0] + 1,), jnp.int32)],
        compiler_params=PARAMS,
        cost_estimate=pl.CostEstimate(flops=1 << 24, bytes_accessed=1 << 24, transcendentals=0),
        name="pick",
    )(starts, corner, spots, field if grouped else tiled(field))


def put(total, starts, corner, spots, spread, base):
    shaped = tiled(base)
    return pl.pallas_call(
        functools.partial(put_kernel, total),
        out_shape=jax.ShapeDtypeStruct(shaped.shape, jnp.float32),
        in_specs=[SMEM, SMEM, VMEM, VMEM, VMEM],
        out_specs=VMEM,
        scratch_shapes=[pltpu.SMEM((starts.shape[0] + 1,), jnp.int32)],
        compiler_params=PARAMS,
        cost_estimate=pl.CostEstimate(flops=1 << 24, bytes_accessed=1 << 24, transcendentals=0),
        name="put",
    )(starts, corner, spots, spread, shaped).reshape(base.shape)


def halves_of(table):
    high = lax.reduce_precision(table, 8, 7)
    return high.astype(jnp.bfloat16), (table - high).astype(jnp.bfloat16)


def plane_specs(shape):
    plane = pl.BlockSpec((1,) + shape[1:], lambda z: (z, 0, 0))
    return plane, pl.BlockSpec((2,) + shape[1:], lambda z: (0, 0, 0))


def cost(flops, numbers):
    return pl.CostEstimate(flops=flops, bytes_accessed=4 * numbers, transcendentals=0)


def planar_first(field, potential, tables):
    plane, pair = plane_specs(field.shape)
    return pl.pallas_call(
        first_kernel,
        grid=field.shape[:1],
        out_shape=[jax.ShapeDtypeStruct(field.shape, jnp.float32)] * 2,
        in_specs=[plane, plane, pair, pair],
        out_specs=[plane, plane],
        compiler_params=PARAMS,
        cost_estimate=cost(12 * field.shape[2] * field.size, 4 * field.size),
        name="planar_first",
    )(field, potential, *tables)


def planar_second(weights, field, extra, potential, tables, parts):
    plane, pair = plane_specs(field.shape)
    planes, rows_y, cols_x = field.shape
    shape = (parts, planes, rows_y, cols_x // parts)
    return pl.pallas_call(
        second_kernel,
        grid=field.shape[:1],
        out_shape=jax.ShapeDtypeStruct(shape, jnp.float32),
        in_specs=[SMEM, plane, plane, plane, pair, pair],
        out_specs=pl.BlockSpec((parts, 1) + shape[2:], lambda z: (0, z, 0, 0)),
        compiler_params=PARAMS,
        cost_estimate=cost(12 * field.shape[2] * field.size, 4 * field.size),
        name="planar_second",
    )(weights, field, extra, potential, *tables)


def depth_out(weights, field, potential, rows, tables):
    groups = potential.shape[0]
    lines = tables[0].shape[0] * rows
    return pl.pallas_call(
        functools.partial(out_kernel, rows),
        out_shape=[jax.ShapeDtypeStruct((groups, lines, 128), jnp.float32)] * 3,
        in_specs=[SMEM, VMEM, VMEM, VMEM, VMEM],
        out_specs=[VMEM] * 3,
        compiler_params=PARAMS,
        cost_estimate=cost(6 * tables[0].size * rows * groups * 128, 5 * groups * lines * 128),
        name="depth_out",
    )(weights, field, potential, *tables)


def depth_back(weights, g, c, b, rows, tables):
    return pl.pallas_call(
        functools.partial(back_kernel, rows),
        out_shape=jax.ShapeDtypeStruct(c.shape, jnp.float32),
        in_specs=[SMEM] + [VMEM] * 5,
        out_specs=VMEM,
        compiler_params=PARAMS,
        cost_estimate=cost(6 * tables[0].shape[0] * c.size, 4 * c.size),
        name="depth_back",
    )(weights, g, c, b, *tables)


def atom_windows(cells, all_planes, rows_y, cols_x):
    parts = []
    for coords, size in (
        (cells[:, 0], all_planes),
        (cells[:, 1] // cols_x, rows_y),
        (cells[:, 1] % cols_x, cols_x),
    ):
        anchor = coords[:, :1]
        apart = (coords - anchor + size // 2) % size - size // 2
        least = jnp.min(apart, axis=1, keepdims=True)
        parts.append(((anchor + least) % size, apart - least))
    starts = jnp.concatenate([start for start, _ in parts], axis=1)
    (_, off_z), (_, off_y), (_, off_x) = parts
    spots = jnp.stack([off_y, off_z * STRIDE + off_x], axis=1)
    return starts.astype(jnp.int32), spots.astype(jnp.int32)


def local(random_orbitals, potential, sphere_cells, projectors, kb_energy, cheb_coef):
    grid_count = lax.axis_size("grid")
    grid_pos = lax.axis_index("grid")
    orb_groups = lax.axis_size("orb")
    orb_pos = lax.axis_index("orb")
    planes, rows_y, cols_x = potential.shape
    all_planes = planes * grid_count
    rows = rows_y // grid_count
    orb_count = random_orbitals.shape[0]
    per_dev, projs_each = projectors.shape[:2]
    atoms = per_dev * grid_count
    chunks = 2 if rows % 16 == 0 else 1
    some = rows // chunks
    part = cols_x // orb_groups
    put_late = part % 128 == 0
    c0, c1, c2 = cheb_coef[0], cheb_coef[1], cheb_coef[2]
    c1_4 = c1 / 4.0
    c2_8 = c2 / 8.0
    planar_tables = [jnp.stack(pair) for pair in zip(halves_of(kinetic_table(cols_x)), halves_of(kinetic_table(rows_y)))]
    depth_tables = halves_of(kinetic_table(all_planes))
    total = (all_planes, rows_y // 8, cols_x // 128)

    groups = cols_x // 128
    lines = groups * planes * some

    def pieces(field):
        field = field.reshape(planes, grid_count, chunks, some, groups, 128)
        return [field[:, :, i].transpose(1, 3, 0, 2, 4).reshape(grid_count, lines, 128) for i in range(chunks)]

    def exchange_with(piece, numbers, *others):
        more = -(-numbers.size // 1024) * 8
        extra = jnp.pad(numbers.reshape(-1), (0, more * 128 - numbers.size)).reshape(1, more, 128)
        send = jnp.concatenate([piece, jnp.broadcast_to(extra, (grid_count, more, 128))], axis=1)
        got = exchange(after(send, *others), "grid")
        summed = jnp.sum(got[:, lines:], axis=0).reshape(-1)[: numbers.size].reshape(numbers.shape)
        return got, summed

    def exchange_alone(piece, *others):
        return exchange(after(piece, *others), "grid")

    def joined(got):
        if planes % 8 == 0 and some % 8 == 0:
            return got
        got = got[:, :lines].reshape(grid_count, groups, planes * some, 128)
        return got.transpose(1, 0, 2, 3).reshape(1, grid_count * lines, 128)

    raw = jnp.concatenate([sphere_cells.astype(jnp.float32), projectors], axis=1)
    here = [(grid_pos + grid_count + step) % grid_count for step in (-1, 0, 1)]
    ahead = [(i, (i + 1) % grid_count) for i in range(grid_count)]
    behind = [(j, i) for i, j in ahead]
    near = jnp.concatenate([lax.ppermute(raw, "grid", ahead), raw, lax.ppermute(raw, "grid", behind)])
    near_projs = near[:, 2:]
    near_starts, near_spots = atom_windows(near[:, :2].astype(jnp.int32), all_planes, rows_y, cols_x)
    zero = jnp.zeros_like(grid_pos)
    slab_corner = jnp.stack([grid_pos * planes, zero, zero])

    def partial_slab(field):
        values = pick(total, near_starts, slab_corner, near_spots, field)
        coeffs = jnp.einsum("aj,apj->ap", values[:, 0], near_projs, precision=PRECISE)
        coeffs = coeffs.reshape(3, per_dev, projs_each)
        out = jnp.zeros((grid_count, per_dev, projs_each), jnp.float32)
        for i, slab in enumerate(here):
            out = lax.dynamic_update_slice_in_dim(out, coeffs[i : i + 1], slab, 0)
        return out.reshape(atoms, projs_each)

    def amounts(coeffs):
        coeffs = coeffs.reshape(grid_count, per_dev, projs_each)
        coeffs = jnp.concatenate([lax.dynamic_index_in_dim(coeffs, slab, 0, keepdims=False) for slab in here])
        return jnp.einsum("ap,apj->aj", coeffs * kb_energy, near_projs, precision=PRECISE)[:, None]

    def put_near(coeffs, base, corner=slab_corner):
        return put(total, near_starts, corner, near_spots, amounts(coeffs), base)

    mine = lax.dynamic_slice_in_dim(potential, orb_pos * part, part, axis=2)
    mine = mine.reshape(planes, grid_count, rows, part).transpose(1, 0, 2, 3)
    mine = after(mine, near_starts)
    got_potential = exchange_alone(mine)
    shared = gather_steps(got_potential[None], "orb")
    shared = jnp.moveaxis(shared.reshape(orb_groups, all_planes, rows, part), 0, 2)
    shared = jnp.moveaxis(shared.reshape(all_planes, rows, groups, 128), 2, 0)
    shared = shared.reshape(groups, grid_count, planes, chunks, some, 128)
    wells = [shared[:, :, :, i].reshape(groups, grid_count, planes * some, 128) for i in range(chunks)]
    if joined(jnp.zeros((grid_count, lines, 128))).shape[0] == 1:
        wells = [well.reshape(groups, 1, all_planes * some, 128) for well in wells]

    every = None
    sums = [0.0] * chunks
    for orb in range(orb_count):
        v = random_orbitals[orb]
        v_here = after(v, mine)
        v_sends = pieces(v_here)
        first = partial_slab(v_here)
        pv, t = planar_first(v_here, potential, planar_tables)
        v0, first = exchange_with(v_sends[0], first, got_potential)
        v_blocks = [v0]
        if every is None:
            every = gather_steps(raw, "grid", (None, mine, got_potential, v0))
            every_projs = every[:, 2:]
            every_starts, every_spots = atom_windows(every[:, :2].astype(jnp.int32), all_planes, rows_y, cols_x)
        for piece in v_sends[1:]:
            v_blocks.append(exchange_alone(piece, v_blocks[-1], pv, t))
        u = put_near(first, t)
        g_sends = pieces(pv + u)
        base = planar_second(
            jnp.stack([c2_8, c1_4, c0 - c2]), u, v, potential, planar_tables, orb_groups
        )
        second = partial_slab(u)

        abc = []
        weights = jnp.stack([c1_4, c2_8])
        for i in range(chunks):
            a, c, b = depth_out(weights, joined(v_blocks[i]), wells[i], some, depth_tables)
            abc.append((a, c, b))
            field = a.reshape(groups, all_planes, some, 128)
            first_row = grid_pos * rows + i * some
            if some % 8:
                padded = jnp.zeros((groups, all_planes, 8, 128), jnp.float32)
                field = lax.dynamic_update_slice(padded, field, (0, 0, first_row % 8, 0))
            corner = jnp.stack([zero, first_row // 8, zero])
            values = pick(total, every_starts, corner, every_spots, field, grouped=True)
            second = second + jnp.einsum("aj,apj->ap", values[:, 0], every_projs, precision=PRECISE)
        second = c2_8 * second
        if put_late:
            second = gather_steps(second[None], "orb")
            base_all = trade(base, "orb")

        g_blocks = []
        for i in range(chunks):
            waits = [v_blocks[-1], base] + g_blocks[-1:] + [x[1] for x in abc[:i]]
            if i < chunks - 1:
                g_blocks.append(exchange_alone(g_sends[i], *waits))
            else:
                g_last, second = exchange_with(g_sends[i], second, *waits)
                g_blocks.append(g_last)
        if put_late:
            corner = slab_corner + jnp.stack([zero, zero, orb_pos * (part // 128)])
            q_all = jnp.stack([put_near(second[o], base_all[o], corner) for o in range(orb_groups)])
        else:
            base = jnp.moveaxis(base, 0, 2).reshape(planes, rows_y, cols_x)
            q = put_near(second, base).reshape(planes, rows_y, orb_groups, part)
            q_all = trade(jnp.moveaxis(q, 2, 0), "orb")
        q_all = q_all.reshape(orb_groups, planes, grid_count, chunks, some, part)

        last = None
        for i in range(chunks):
            m = depth_back(weights, joined(g_blocks[i]), abc[i][1], abc[i][2], some, depth_tables)
            if part != 128:
                m = jnp.moveaxis(m.reshape(groups, all_planes * some, 128), 0, 1)
                m = jnp.moveaxis(m.reshape(all_planes * some, orb_groups, part), 1, 0)
            m = m.reshape(orb_groups * grid_count, planes, some, part)
            m = after(m, g_blocks[-1]) if last is None else after(m, last, q_all)
            last = exchange(m, ("orb", "grid"))
            m = last.reshape(orb_groups, grid_count, planes, some, part)
            filtered = q_all[:, :, :, i] + m.transpose(0, 2, 1, 3, 4)
            sums[i] = sums[i] + jnp.sum(filtered * filtered, axis=0)
    out = []
    for own in sums:
        own = own * (1.0 / (orb_count * orb_groups))
        out.append(jnp.moveaxis(gather_steps(own[None], "orb"), 0, 3))
    return jnp.stack(out, axis=2).reshape(planes, rows_y, cols_x)


def solution(mesh):
    in_specs = (
        P("orb", "grid", None, None),
        P("grid", None, None),
        P("grid", None, None),
        P("grid", None, None),
        P(),
        P(),
    )
    out_specs = P("grid", None, None)
    return jax.shard_map(local, mesh=mesh, in_specs=in_specs, out_specs=out_specs, check_vma=False)
```

time: 640 us -> 518 us (0.81)
  waiting for transfers between devices: 320 us -> 265 us
  blocking collectives: 52.4 us -> 0 us
  local copies, waits for them, and re-layouts: 77.3 us -> 45.4 us
  Pallas kernels: 71.4 us -> 94.7 us
  matrix products: 29.4 us -> 6.25 us
  starting transfers between devices: 42.5 us -> 65.4 us
    ppermute x15 -> x10, waiting for transfers between devices: 252 us -> 92.2 us  [the longest x8 87.8 us: gather_steps(): other = lax.ppermute(block, axis, xor_route(size, bit))]
    all_to_all x5 -> x7, waiting for transfers between devices: 33.5 us -> 106 us  [exchange(): return lax.all_to_all(block, axis, split_axis=0, concat_axis=0, tiled=True)]
    all_to_all x1 -> x0, blocking collectives: 52.4 us -> none  [exchange(): return lax.all_to_all(block, axis, split_axis=0, concat_axis=0, tiled=True)]
    ppermute x1, waiting for transfers between devices: 34.2 us -> 66.4 us  [trade(): got = lax.ppermute(sent, axis, xor_route(size, apart))]
    all_to_all x5 -> x7, starting transfers between devices: 24.7 us -> 48.4 us  [exchange(): return lax.all_to_all(block, axis, split_axis=0, concat_axis=0, tiled=True)]
    pallas_call x7 -> x13, Pallas kernels: 71.4 us -> 94.7 us  [the longest x4 27.1 us: pick(): pl.pallas_call(functools.partial(pick_kernel, total, grouped), out_shape=...]
    dot_general x7, matrix products: 29.4 us -> 6.25 us  [the longest x2 3.99 us: local(): jnp.einsum('aj,apj->ap', values[:, 0], every_projs, precision=PRECISE)]
    reshape x4 -> x1, local copies, waits for them, and re-layouts: 14.8 us -> 0.09 us  [partial_slab(): return out.reshape(atoms, projs_each)]
  transfers between devices with their start and end apart: 21 -> 18, of which waited for: 15 -> 9; matrix products, arithmetic and copies ran while one was open for 17% -> 12% of each run, Pallas kernels for 11% -> 18%
where the time goes in v3:
time: 518 us; the launch traced here: 516 us
  waiting for transfers between devices  265 us (51%)
  Pallas kernels  94.7 us (18%)
  starting transfers between devices  65.4 us (13%)
  local copies, waits for them, and re-layouts  45.4 us (9%)
  other arithmetic  36.1 us (7%)
  matrix products  6.25 us (1%)
    all_to_all x7, waiting for transfers between devices, exchange(): return lax.all_to_all(block, axis, split_axis=0, concat_axis=0, tiled=True)  106 us
    ppermute x8, waiting for transfers between devices, gather_steps(): other = lax.ppermute(block, axis, xor_route(size, bit))  87.8 us
    ppermute x1, waiting for transfers between devices, trade(): got = lax.ppermute(sent, axis, xor_route(size, apart))  66.4 us
    all_to_all x7, starting transfers between devices, exchange(): return lax.all_to_all(block, axis, split_axis=0, concat_axis=0, tiled=True)  48.4 us
    pallas_call x4, Pallas kernels, pick(): pl.pallas_call(functools.partial(pick_kernel, total, grouped), out_shape=...  27.1 us
    unnamed x51, local copies, waits for them, and re-layouts  20.8 us
    pallas_call x2, Pallas kernels, depth_out(): pl.pallas_call(functools.partial(out_kernel, rows), out_shape=[jax.ShapeD...  14.6 us
    pallas_call x3, Pallas kernels, put(): pl.pallas_call(functools.partial(put_kernel, total), out_shape=jax.ShapeD...  14.2 us
  transfers between devices with their start and end apart: 18, of which 9 were waited for; matrix products, arithmetic and copies ran while one was open for 12% of the time, Pallas kernels for 18%

profile of v3, /device:TPU:0, one launch (start us, length us, event | category | flops | bytes accessed | tf_op | source)
XLA Modules:
  0.0 515.9 jit_solution(16431643883207709799)
XLA Ops:
  1.5 5.4 %collective-permute-start.1 = (f32[16,6,128]{2,0,1:T(8,128)S(1)}, f32[16,6,128]{2,0,1:T(8,128)S(1)}, u32[]{:S(2)}, u32[]{:S(2)}) collective-permute-start(f32[16,6,128]{2,0,1:T(8,128)S(1)} %pad_maximum_fusion.13), channel_id=1, source_target_pairs={{1,0},{2,1},{3,2},{4,3},{5,4},{6,5},{7,6},{8,7},{9,8},{10,9},{11,1... | collective-permute-start | bytes 147464 | tf_op jit(solution)/shard_map/ppermute | solution.py:443
  6.9 1.7 constant_dynamic-slice_fusion.10
  8.7 4.5 collective-permute-done
  14.6 1.6 copy.223
  16.2 4.4 all-to-all-start
  21.5 2.2 copy-done.1
  23.7 4.6 pick.4
  29.3 4.0 slice_bitcast_fusion.2
  33.6 1.6 pad_maximum_fusion.3
  35.2 26.5 %all-to-all-done = f32[16,16,16,128]{3,2,1,0:T(8,128)} async-done(((f32[16,16,16,128]{3,2,1,0:T(8,128)}), f32[16,16,16,128]{3,2,1,0:T(8,128)}, u32[]{:S(2)}, u32[]{:S(2)}) %all-to-all-start) | async-done | bytes 2097184 | tf_op jit(solution)/shard_map/all_to_all | solution.py:74
  61.7 11.2 %all-to-all-start.1 = ((f32[16,264,128]{2,1,0:T(8,128)}), f32[16,264,128]{2,1,0:T(8,128)}, u32[]{:S(2)}, u32[]{:S(2)}) async-start(f32[16,264,128]{2,1,0:T(8,128)} %pad_maximum_fusion.3), calls=%async_computation.1 | async-start | bytes 4325376 | tf_op jit(solution)/shard_map/all_to_all | solution.py:74
  72.9 2.8 collective-permute-start.2
  76.3 1.5 collective-permute-start.6
  83.6 41.8 %collective-permute-done.2 = f32[16,6,128]{2,0,1:T(8,128)S(1)} collective-permute-done((f32[16,6,128]{2,0,1:T(8,128)S(1)}, f32[16,6,128]{2,0,1:T(8,128)S(1)}, u32[]{:S(2)}, u32[]{:S(2)}) %collective-permute-start.2) | collective-permute-done | bytes 49184 | tf_op jit(solution)/shard_map/ppermute | solution.py:54
  125.6 3.1 copy.250
  128.8 1.4 collective-permute-done.3
  130.2 1.6 collective-permute-start.4
  131.8 13.6 %planar_first.1 = (f32[16,256,256]{2,1,0:T(8,128)S(1)}, f32[16,256,256]{2,1,0:T(8,128)}) custom-call(f32[16,256,256]{2,1,0:T(8,128)} %bitcast.312, f32[16,256,256]{2,1,0:T(8,128)} %potential.3, bf16[2,256,256]{2,1,0:T(8,128)(2,1)S(1)} %get-tuple-element.123.high_tables, bf16[2,256,256]{2,1,0:T(8,128)(2,1)S(1)} %get-tuple-element.124.low_tables), custom_call_target="tpu_custom_call" | custom-call | flops 3221225472 | bytes 16777216 | tf_op jit(solution)/shard_map/planar_first/pallas_call | solution.py:322
  145.4 2.0 copy-done.8
  147.4 4.4 all-to-all-start.2
  151.9 2.6 select_bitcast_fusion.1
  154.5 2.6 fusion.1
  159.3 5.7 %put.3.field = f32[16,32,8,256]{3,2,1,0:T(8,128)S(1)} custom-call(s32[48,3]{1,0:T(8,128)S(1)} %pad_add_fusion.3.starts, s32[3]{0:T(128)S(1)} %stack.144.corner, s32[48,2,128]{2,1,0:T(2,128)S(1)} %pad_add_fusion.2.spots, f32[48,1,128]{2,1,0:T(1,128)S(1)} %fusion.71.spread, f32[16,32,8,256]{3,2,1,0:T(8,128)} %bitcast.326), custom_call_target="tpu_custom_call" | custom-call | flops 16777216 | bytes 16777216 | tf_op jit(solution)/shard_map/put/pallas_call | solution.py:294
  165.0 4.7 pick.5
  170.3 4.1 bitcast_add_fusion.2
  174.4 1.8 fusion.108
  176.3 1.6 copy.282
  178.1 7.4 %depth_out.2 = (f32[2,2048,128]{2,1,0:T(8,128)S(1)}, f32[2,2048,128]{2,1,0:T(8,128)S(1)}, f32[2,2048,128]{2,1,0:T(8,128)}) custom-call(f32[2]{0:T(128)S(1)} %pad_maximum_fusion.15.weights, f32[16,264,128]{2,1,0:T(8,128)} %all-to-all-done.1.field, f32[2,16,128,128]{3,2,1,0:T(8,128)} %get-tuple-element.63.potential, ...), custom_call_target="tpu_custom_call" | custom-call | flops 805306368 | bytes 10485760 | tf_op jit(solution)/shard_map/depth_out/pallas_call | solution.py:353
  185.5 1.4 copy-done.9
  186.8 1.4 copy-done.12
  188.2 13.0 %planar_second.1 = f32[2,16,256,128]{3,2,1,0:T(8,128)S(1)} custom-call(f32[3]{0:T(128)S(1)} %pad_maximum_fusion.16.weights, f32[16,256,256]{2,1,0:T(8,128)} %bitcast.310, f32[16,256,256]{2,1,0:T(8,128)} %bitcast.313, f32[16,256,256]{2,1,0:T(8,128)} %potential.3, bf16[2,256,256]{2,1,0:T(8,128)(2,1)S(1)} %get-tuple-element.123.high_tables, ...), custom_call_target="tpu_custom_call" | custom-call | flops 3221225472 | bytes 16777216 | tf_op jit(solution)/shard_map/planar_second/pallas_call | solution.py:338
  201.5 1.7 copy-done.2
  204.4 6.8 %all-to-all-start.3 = ((f32[16,256,128]{2,1,0:T(8,128)}), f32[16,256,128]{2,1,0:T(8,128)S(1)}, u32[]{:S(2)}, u32[]{:S(2)}) async-start(f32[16,256,128]{2,1,0:T(8,128)} %bitcast.321), calls=%async_computation.3 | async-start | bytes 4194304 | tf_op jit(solution)/shard_map/all_to_all | solution.py:74
  211.4 1.9 slice.192
  217.7 3.9 fusion.60
  221.8 9.3 %pick.6 = f32[256,1,128]{2,1,0:T(1,128)S(1)} custom-call(s32[256,3]{1,0:T(8,128)S(1)} %pad_add_fusion.1.starts, s32[3]{0:T(128)S(1)} %get-tuple-element.120.corner, s32[256,2,128]{2,1,0:T(2,128)S(1)} %pad_add_fusion.spots, f32[2,256,8,128]{3,2,1,0:T(8,128)S(1)} %bitcast.318), custom_call_target="tpu_custom_call" | custom-call | flops 16777216 | bytes 16777216 | tf_op jit(solution)/shard_map/pick/pallas_call | solution.py:280
  231.0 2.0 fusion.17
  233.1 7.3 %depth_out.3 = (f32[2,2048,128]{2,1,0:T(8,128)S(1)}, f32[2,2048,128]{2,1,0:T(8,128)S(1)}, f32[2,2048,128]{2,1,0:T(8,128)}) custom-call(f32[2]{0:T(128)S(1)} %pad_maximum_fusion.15.weights, f32[16,256,128]{2,1,0:T(8,128)} %all-to-all-done.2.field, f32[2,16,128,128]{3,2,1,0:T(8,128)} %get-tuple-element.64.potential, ...), custom_call_target="tpu_custom_call" | custom-call | flops 805306368 | bytes 10485760 | tf_op jit(solution)/shard_map/depth_out/pallas_call | solution.py:353
  240.4 1.4 copy-done.10
  241.7 8.5 %pick.7 = f32[256,1,128]{2,1,0:T(1,128)S(1)} custom-call(s32[256,3]{1,0:T(8,128)S(1)} %pad_add_fusion.1.starts, s32[3]{0:T(128)S(1)} %get-tuple-element.119.corner, s32[256,2,128]{2,1,0:T(2,128)S(1)} %pad_add_fusion.spots, f32[2,256,8,128]{3,2,1,0:T(8,128)S(1)} %bitcast.319), custom_call_target="tpu_custom_call" | custom-call | flops 16777216 | bytes 16777216 | tf_op jit(solution)/shard_map/pick/pallas_call | solution.py:280
  250.2 2.0 fusion.15
  252.3 1.6 collective-permute-start.7
  253.9 3.1 copy.280
  257.4 3.1 pad_maximum_fusion.2
  260.5 7.2 %all-to-all-start.4 = ((f32[16,272,128]{2,1,0:T(8,128)}), f32[16,272,128]{2,1,0:T(8,128)}, u32[]{:S(2)}, u32[]{:S(2)}) async-start(f32[16,272,128]{2,1,0:T(8,128)} %pad_maximum_fusion.2), calls=%async_computation.4 | async-start | bytes 4456448 | tf_op jit(solution)/shard_map/all_to_all | solution.py:74
  267.8 5.4 %depth_back.2 = f32[2,2048,128]{2,1,0:T(8,128)S(1)} custom-call(f32[2]{0:T(128)S(1)} %pad_maximum_fusion.15.weights, f32[16,256,128]{2,1,0:T(8,128)S(1)} %all-to-all-done.3.g_in, f32[2,2048,128]{2,1,0:T(8,128)} %copy-done.9, f32[2,2048,128]{2,1,0:T(8,128)} %get-tuple-element.38.b_in, bf16[256,256]{1,0:T(8,128)(2,1)S(1)} %get-tuple-element.125.high_table, ...), custom_call_target="tpu_custom_call" | custom-call | flops 805306368 | bytes 8388608 | tf_op jit(solution)/shard_map/depth_back/pallas_call | solution.py:365
  273.2 1.4 copy-done.4
  274.5 36.7 %all-to-all-done.4.g_in = f32[16,272,128]{2,1,0:T(8,128)} async-done(((f32[16,272,128]{2,1,0:T(8,128)}), f32[16,272,128]{2,1,0:T(8,128)}, u32[]{:S(2)}, u32[]{:S(2)}) %all-to-all-start.4) | async-done | bytes 2228256 | tf_op jit(solution)/shard_map/all_to_all | solution.py:74
  311.2 10.9 %all-to-all-start.5 = ((f32[32,16,8,128]{3,2,1,0:T(8,128)}), f32[32,16,8,128]{3,2,1,0:T(8,128)}, u32[]{:S(2)}, u32[]{:S(2)}) async-start(f32[32,16,8,128]{3,2,1,0:T(8,128)} %bitcast.316), calls=%async_computation.5 | async-start | bytes 4194304 | tf_op jit(solution)/shard_map/all_to_all | solution.py:74
  322.1 6.8 %depth_back.3 = f32[2,2048,128]{2,1,0:T(8,128)} custom-call(f32[2]{0:T(128)S(1)} %pad_maximum_fusion.15.weights, f32[16,272,128]{2,1,0:T(8,128)} %all-to-all-done.4.g_in, f32[2,2048,128]{2,1,0:T(8,128)S(1)} %copy-done.11, f32[2,2048,128]{2,1,0:T(8,128)} %get-tuple-element.41.b_in, bf16[256,256]{1,0:T(8,128)(2,1)S(1)} %get-tuple-element.125.high_table, ...), custom_call_target="tpu_custom_call" | custom-call | flops 805306368 | bytes 8388608 | tf_op jit(solution)/shard_map/depth_back/pallas_call | solution.py:365
  328.9 42.9 %all-to-all-done.5 = f32[32,16,8,128]{3,2,1,0:T(8,128)} async-done(((f32[32,16,8,128]{3,2,1,0:T(8,128)}), f32[32,16,8,128]{3,2,1,0:T(8,128)}, u32[]{:S(2)}, u32[]{:S(2)}) %all-to-all-start.5) | async-done | bytes 2097184 | tf_op jit(solution)/shard_map/all_to_all | solution.py:74
  371.8 3.5 all-to-all-start.6
  375.2 1.9 constant_dynamic-slice_fusion.3
  377.1 1.6 collective-permute-start.8
  378.9 66.4 %collective-permute-done.8 = f32[1,16,256,128]{3,2,1,0:T(8,128)S(1)} collective-permute-done((f32[1,16,256,128]{3,2,1,0:T(8,128)S(1)}, f32[1,16,256,128]{3,2,1,0:T(8,128)S(1)}, u32[]{:S(2)}, u32[]{:S(2)}) %collective-permute-start.8) | collective-permute-done | bytes 2097184 | tf_op jit(solution)/shard_map/ppermute | solution.py:68
  445.5 2.3 slice_bitcast_fusion
  450.3 1.6 copy-done.7
  451.9 4.2 put.5
  456.6 4.2 put.4
  462.1 3.7 fusion.6
  466.4 1.8 collective-permute-start.9
  468.2 23.9 %collective-permute-done.10 = f32[1,16,16,8,128]{4,3,2,1,0:T(8,128)S(1)} collective-permute-done((f32[1,16,16,8,128]{4,3,2,1,0:T(8,128)S(1)}, f32[1,16,16,8,128]{4,3,2,1,0:T(8,128)S(1)}, u32[]{:S(2)}, u32[]{:S(2)}) %collective-permute-start.10) | collective-permute-done | bytes 1048608 | tf_op jit(solution)/shard_map/ppermute | solution.py:54
  492.5 20.7 %collective-permute-done.9 = f32[1,16,16,8,128]{4,3,2,1,0:T(8,128)S(1)} collective-permute-done((f32[1,16,16,8,128]{4,3,2,1,0:T(8,128)S(1)}, f32[1,16,16,8,128]{4,3,2,1,0:T(8,128)S(1)}, u32[]{:S(2)}, u32[]{:S(2)}) %collective-permute-start.9) | collective-permute-done | bytes 1048608 | tf_op jit(solution)/shard_map/ppermute | solution.py:54
  513.4 2.4 pad_maximum_fusion.1
  (181 shorter events, 24.4 us)
Async XLA Ops:
  1.5 7.2 %collective-permute-start.1 = (f32[16,6,128]{2,0,1:T(8,128)S(1)}, f32[16,6,128]{2,0,1:T(8,128)S(1)}, u32[]{:S(2)}, u32[]{:S(2)}) collective-permute-start(f32[16,6,128]{2,0,1:T(8,128)S(1)} %pad_maximum_fusion.13), channel_id=1, source_target_pairs={{1,0},{2,1},{3,2},{4,3},{5,4},{6,5},{7,6},{8,7},{9,8},{10,9},{11,1... | collective-permute-start | bytes 147464 | tf_op jit(solution)/shard_map/ppermute | solution.py:443
  6.9 6.2 %collective-permute-start = (f32[16,6,128]{2,0,1:T(8,128)S(1)}, f32[16,6,128]{2,0,1:T(8,128)S(1)}, u32[]{:S(2)}, u32[]{:S(2)}) collective-permute-start(f32[16,6,128]{2,0,1:T(8,128)S(1)} %pad_maximum_fusion.13), channel_id=1, source_target_pairs={{0,1},{1,2},{2,3},{3,4},{4,5},{5,6},{6,7},{7,8},{8,9},{9,10},{10,1... | collective-permute-start | bytes 147464 | tf_op jit(solution)/shard_map/ppermute | solution.py:443
  16.2 45.5 %all-to-all-start = ((f32[16,16,16,128]{3,2,1,0:T(8,128)}), f32[16,16,16,128]{3,2,1,0:T(8,128)}, u32[]{:S(2)}, u32[]{:S(2)}) async-start(f32[16,16,16,128]{3,2,1,0:T(8,128)} %copy.223), calls=%async_computation | async-start | bytes 4194304 | tf_op jit(solution)/shard_map/all_to_all | solution.py:74
  21.5 2.2 copy-start.1
  28.3 141.4 %copy-start.19 = (f32[48,4,128]{2,0,1:T(8,128)}, f32[48,4,128]{2,0,1:T(8,128)S(1)}, u32[]{:S(2)}) copy-start(f32[48,4,128]{2,0,1:T(8,128)S(1)} %pad_maximum_fusion.9) | copy-start | bytes 294916
  35.2 40.5 %copy-start.21 = (f32[3]{0:T(128)S(1)}, f32[3]{0:T(128)}, u32[]{:S(2)}) copy-start(f32[3]{0:T(128)} %param.11) | copy-start | bytes 40
  61.7 85.8 %all-to-all-start.1 = ((f32[16,264,128]{2,1,0:T(8,128)}), f32[16,264,128]{2,1,0:T(8,128)}, u32[]{:S(2)}, u32[]{:S(2)}) async-start(f32[16,264,128]{2,1,0:T(8,128)} %pad_maximum_fusion.3), calls=%async_computation.1 | async-start | bytes 4325376 | tf_op jit(solution)/shard_map/all_to_all | solution.py:74
  72.9 52.5 %collective-permute-start.2 = (f32[16,6,128]{2,0,1:T(8,128)S(1)}, f32[16,6,128]{2,0,1:T(8,128)S(1)}, u32[]{:S(2)}, u32[]{:S(2)}) collective-permute-start(f32[16,6,128]{2,0,1:T(8,128)S(1)} %pad_maximum_fusion.13), channel_id=1, source_target_pairs={{0,8},{1,9},{2,10},{3,11},{4,12},{5,13},{6,14},{7,15},{8,0},{9,1},... | collective-permute-start | bytes 147464 | tf_op jit(solution)/shard_map/ppermute | solution.py:54
  76.3 75.6 %collective-permute-start.6 = (f32[1,16,16,16,128]{4,3,2,1,0:T(8,128)}, f32[1,16,16,16,128]{4,3,2,1,0:T(8,128)}, u32[]{:S(2)}, u32[]{:S(2)}) collective-permute-start(f32[1,16,16,16,128]{4,3,2,1,0:T(8,128)} %bitcast.88), channel_id=1, source_target_pairs={{0,16},{16,0},{1,17},{17,1},{2,18},{18,2},{3,19},{19,3},{4,20},{20... | collective-permute-start | bytes 6291464 | tf_op jit(solution)/shard_map/ppermute | solution.py:54
  125.5 4.7 collective-permute-start.3
  130.2 17.2 %collective-permute-start.4 = (f32[2,2,16,6,128]{4,2,3,1,0:T(8,128)S(1)}, f32[2,2,16,6,128]{4,2,3,1,0:T(8,128)S(1)}, u32[]{:S(2)}, u32[]{:S(2)}) collective-permute-start(f32[2,2,16,6,128]{4,2,3,1,0:T(8,128)S(1)} %pad_maximum_fusion.8), channel_id=1, source_target_pairs={{0,2},{1,3},{2,0},{3,1},{4,6},{5,7},{6,4},{7,5},{8,10},{9,11},{10,... | collective-permute-start | bytes 589832 | tf_op jit(solution)/shard_map/ppermute | solution.py:54
  145.4 2.0 copy-start.8
  147.4 57.0 %all-to-all-start.2 = ((f32[16,256,128]{2,1,0:T(8,128)}), f32[16,256,128]{2,1,0:T(8,128)}, u32[]{:S(2)}, u32[]{:S(2)}) async-start(f32[16,256,128]{2,1,0:T(8,128)} %bitcast.322), calls=%async_computation.2 | async-start | bytes 4194304 | tf_op jit(solution)/shard_map/all_to_all | solution.py:74
  154.5 3.9 copy-start.22
  158.6 42.7 %collective-permute-start.5 = (f32[2,2,2,16,6,128]{5,3,4,2,1,0:T(8,128)S(1)}, f32[2,2,2,16,6,128]{5,3,4,2,1,0:T(8,128)S(1)}, u32[]{:S(2)}, u32[]{:S(2)}) collective-permute-start(f32[2,2,2,16,6,128]{5,3,4,2,1,0:T(8,128)S(1)} %pad_maximum_fusion.5), channel_id=1, source_target_pairs={{0,1},{1,0},{2,3},{3,2},{4,5},{5,4},{6,7},{7,6},{8,9},{9,8},{10,11... | collective-permute-start | bytes 1179656 | tf_op jit(solution)/shard_map/ppermute | solution.py:54
  165.0 4.8 copy-start
  185.5 1.4 copy-start.9
  186.8 1.4 copy-start.12
  201.2 2.0 copy-start.2
  203.3 0.9 copy-start.14
  204.4 56.1 %all-to-all-start.3 = ((f32[16,256,128]{2,1,0:T(8,128)}), f32[16,256,128]{2,1,0:T(8,128)S(1)}, u32[]{:S(2)}, u32[]{:S(2)}) async-start(f32[16,256,128]{2,1,0:T(8,128)} %bitcast.321), calls=%async_computation.3 | async-start | bytes 4194304 | tf_op jit(solution)/shard_map/all_to_all | solution.py:74
  215.9 1.7 copy-start.16
  215.9 1.7 copy-start.17
  216.0 1.7 copy-start.18
  216.1 5.6 %copy-start.13 = (f32[2,2048,128]{2,1,0:T(8,128)S(1)}, f32[2,2048,128]{2,1,0:T(8,128)}, u32[]{:S(2)}) copy-start(f32[2,2048,128]{2,1,0:T(8,128)} %copy-done.12) | copy-start | bytes 6291460
  217.7 13.4 %copy-start.15 = (f32[256,4,128]{2,0,1:T(8,128)S(1)}, f32[256,4,128]{2,0,1:T(8,128)}, u32[]{:S(2)}) copy-start(f32[256,4,128]{2,0,1:T(8,128)} %slice.192) | copy-start | bytes 1572868
  240.4 1.4 copy-start.10
  252.3 4.7 collective-permute-start.7
  260.5 50.7 %all-to-all-start.4 = ((f32[16,272,128]{2,1,0:T(8,128)}), f32[16,272,128]{2,1,0:T(8,128)}, u32[]{:S(2)}, u32[]{:S(2)}) async-start(f32[16,272,128]{2,1,0:T(8,128)} %pad_maximum_fusion.2), calls=%async_computation.4 | async-start | bytes 4456448 | tf_op jit(solution)/shard_map/all_to_all | solution.py:74
  273.2 1.4 copy-start.4
  311.2 10.9 %copy-start.11 = (f32[2,2048,128]{2,1,0:T(8,128)S(1)}, f32[2,2048,128]{2,1,0:T(8,128)}, u32[]{:S(2)}) copy-start(f32[2,2048,128]{2,1,0:T(8,128)} %copy-done.10) | copy-start | bytes 6291460
  311.2 60.5 %all-to-all-start.5 = ((f32[32,16,8,128]{3,2,1,0:T(8,128)}), f32[32,16,8,128]{3,2,1,0:T(8,128)}, u32[]{:S(2)}, u32[]{:S(2)}) async-start(f32[32,16,8,128]{3,2,1,0:T(8,128)} %bitcast.316), calls=%async_computation.5 | async-start | bytes 4194304 | tf_op jit(solution)/shard_map/all_to_all | solution.py:74
  371.8 90.4 %all-to-all-start.6 = ((f32[32,16,8,128]{3,2,1,0:T(8,128)}), f32[32,16,8,128]{3,2,1,0:T(8,128)}, u32[]{:S(2)}, u32[]{:S(2)}) async-start(f32[32,16,8,128]{3,2,1,0:T(8,128)} %bitcast.140), calls=%async_computation.6 | async-start | bytes 4194304 | tf_op jit(solution)/shard_map/all_to_all | solution.py:74
  375.2 70.0 %copy-start.3 = (f32[2,16,256,128]{3,2,1,0:T(8,128)S(1)}, f32[2,16,256,128]{3,2,1,0:T(8,128)}, u32[]{:S(2)}) copy-start(f32[2,16,256,128]{3,2,1,0:T(8,128)} %copy-done.2) | copy-start | bytes 12582916
  377.1 68.1 %collective-permute-start.8 = (f32[1,16,256,128]{3,2,1,0:T(8,128)S(1)}, f32[1,16,256,128]{3,2,1,0:T(8,128)S(1)}, u32[]{:S(2)}, u32[]{:S(2)}) collective-permute-start(f32[1,16,256,128]{3,2,1,0:T(8,128)S(1)} %constant_dynamic-slice_fusion.3), channel_id=1, source_target_pairs={{0,16},{16,0},{1,17},{17,1},{2,18},{18,2},{3,19},{19,3},{4,20},{20... | collective-permute-start | bytes 6291464 | tf_op jit(solution)/shard_map/ppermute | solution.py:68
  445.5 4.1 copy-start.23
  445.5 4.3 copy-start.20
  450.3 1.6 copy-start.7
  451.9 4.7 copy-start.6
  460.8 1.3 copy-start.5
  465.9 26.1 %collective-permute-start.10 = (f32[1,16,16,8,128]{4,3,2,1,0:T(8,128)S(1)}, f32[1,16,16,8,128]{4,3,2,1,0:T(8,128)S(1)}, u32[]{:S(2)}, u32[]{:S(2)}) collective-permute-start(f32[1,16,16,8,128]{4,3,2,1,0:T(8,128)S(1)} %multiply_bitcast_fusion), channel_id=1, source_target_pairs={{0,16},{16,0},{1,17},{17,1},{2,18},{18,2},{3,19},{19,3},{4,20},{20... | collective-permute-start | bytes 3145736 | tf_op jit(solution)/shard_map/ppermute | solution.py:54
  466.4 46.7 %collective-permute-start.9 = (f32[1,16,16,8,128]{4,3,2,1,0:T(8,128)S(1)}, f32[1,16,16,8,128]{4,3,2,1,0:T(8,128)S(1)}, u32[]{:S(2)}, u32[]{:S(2)}) collective-permute-start(f32[1,16,16,8,128]{4,3,2,1,0:T(8,128)S(1)} %multiply_bitcast_fusion.1), channel_id=1, source_target_pairs={{0,16},{16,0},{1,17},{17,1},{2,18},{18,2},{3,19},{19,3},{4,20},{20... | collective-permute-start | bytes 3145736 | tf_op jit(solution)/shard_map/ppermute | solution.py:54

commit v4 on v3

--- a/solution.py
+++ b/solution.py
@@ -13,6 +13,7 @@
 STRIDE = 16
 PRECISE = lax.Precision.HIGHEST
 TOGETHER = 4
+EARLY = True
 
 
 def kinetic_table(length):
@@ -250,9 +251,12 @@
     lax.fori_loop(0, rows, one, 0)
 
 
-def back_kernel(rows, weights, g_in, c_in, b_in, high_table, low_table, out):
-    groups, everywhere = out.shape[0], high_table.shape[0]
+def back_kernel(rows, weights, g_in, c_in, b_in, high_table, low_table, *numbers_out):
+    out = numbers_out[-1]
+    groups, everywhere = c_in.shape[0], high_table.shape[0]
     planes = everywhere // g_in.shape[0]
+    devices = out.shape[1]
+    mine = everywhere // devices
 
     def one(r, carry):
         line = pl.ds(r, everywhere, stride=rows)
@@ -261,10 +265,16 @@
         ]
         m = depth_times(high_table, low_table, jnp.concatenate(parts, axis=1))
         for g in range(groups):
-            out[g, line, :] = m[:, 128 * g : 128 * g + 128] + b_in[g, line, :]
+            m_g = m[:, 128 * g : 128 * g + 128] + b_in[g, line, :]
+            for d in range(devices):
+                out[g, d, pl.ds(r, mine, stride=rows), :] = m_g[mine * d : mine * d + mine]
         return carry
 
     lax.fori_loop(0, rows, one, 0)
+    for numbers in numbers_out[:-1]:
+        for g in range(groups):
+            for d in range(devices):
+                out[g, d, mine * rows :, :] = numbers[...]
 
 
 def tiled(field):
@@ -361,16 +371,18 @@
     )(weights, field, potential, *tables)
 
 
-def depth_back(weights, g, c, b, rows, tables):
+def depth_back(weights, g, c, b, rows, devices, tables, *numbers):
+    groups, lines = c.shape[:2]
+    shape = (groups, devices, lines // devices + sum(n.shape[0] for n in numbers), 128)
     return pl.pallas_call(
         functools.partial(back_kernel, rows),
-        out_shape=jax.ShapeDtypeStruct(c.shape, jnp.float32),
-        in_specs=[SMEM] + [VMEM] * 5,
+        out_shape=jax.ShapeDtypeStruct(shape, jnp.float32),
+        in_specs=[SMEM] + [VMEM] * (5 + len(numbers)),
         out_specs=VMEM,
         compiler_params=PARAMS,
         cost_estimate=cost(6 * tables[0].shape[0] * c.size, 4 * c.size),
         name="depth_back",
-    )(weights, g, c, b, *tables)
+    )(weights, g, c, b, *tables, *numbers)
 
 
 def atom_windows(cells, all_planes, rows_y, cols_x):
@@ -414,95 +426,106 @@
 
     groups = cols_x // 128
     lines = groups * planes * some
+    whole_tiles = planes % 8 == 0 and some % 8 == 0
 
     def pieces(field):
         field = field.reshape(planes, grid_count, chunks, some, groups, 128)
         return [field[:, :, i].transpose(1, 3, 0, 2, 4).reshape(grid_count, lines, 128) for i in range(chunks)]
 
-    def exchange_with(piece, numbers, *others):
-        more = -(-numbers.size // 1024) * 8
-        extra = jnp.pad(numbers.reshape(-1), (0, more * 128 - numbers.size)).reshape(1, more, 128)
-        send = jnp.concatenate([piece, jnp.broadcast_to(extra, (grid_count, more, 128))], axis=1)
-        got = exchange(after(send, *others), "grid")
-        summed = jnp.sum(got[:, lines:], axis=0).reshape(-1)[: numbers.size].reshape(numbers.shape)
-        return got, summed
-
-    def exchange_alone(piece, *others):
+    def exchange_after(piece, *others):
         return exchange(after(piece, *others), "grid")
 
     def joined(got):
-        if planes % 8 == 0 and some % 8 == 0:
+        if whole_tiles:
             return got
         got = got[:, :lines].reshape(grid_count, groups, planes * some, 128)
         return got.transpose(1, 0, 2, 3).reshape(1, grid_count * lines, 128)
 
     raw = jnp.concatenate([sphere_cells.astype(jnp.float32), projectors], axis=1)
     here = [(grid_pos + grid_count + step) % grid_count for step in (-1, 0, 1)]
-    ahead = [(i, (i + 1) % grid_count) for i in range(grid_count)]
-    behind = [(j, i) for i, j in ahead]
-    near = jnp.concatenate([lax.ppermute(raw, "grid", ahead), raw, lax.ppermute(raw, "grid", behind)])
+
+    def shifted(block, step):
+        return lax.ppermute(block, "grid", [(i, (i + step) % grid_count) for i in range(grid_count)])
+
+    near = jnp.concatenate([shifted(raw, 1), raw, shifted(raw, -1)])
     near_projs = near[:, 2:]
     near_starts, near_spots = atom_windows(near[:, :2].astype(jnp.int32), all_planes, rows_y, cols_x)
     zero = jnp.zeros_like(grid_pos)
     slab_corner = jnp.stack([grid_pos * planes, zero, zero])
 
-    def partial_slab(field):
+    def partial_near(field):
         values = pick(total, near_starts, slab_corner, near_spots, field)
         coeffs = jnp.einsum("aj,apj->ap", values[:, 0], near_projs, precision=PRECISE)
-        coeffs = coeffs.reshape(3, per_dev, projs_each)
+        return coeffs.reshape(3, per_dev, projs_each)
+
+    def whole_near(coeffs):
+        steps = 1 if planes >= WIDE else 2
+        whole = coeffs
+        for step in [s for s in range(-steps, steps + 1) if s]:
+            got = shifted(coeffs, step)
+            moved = jnp.zeros_like(coeffs)
+            for i in range(3):
+                if 0 <= i - step < 3:
+                    moved = moved.at[i - step].set(got[i])
+            whole = whole + moved
+        return whole.reshape(3 * per_dev, projs_each)
+
+    def everywhere(coeffs):
         out = jnp.zeros((grid_count, per_dev, projs_each), jnp.float32)
         for i, slab in enumerate(here):
             out = lax.dynamic_update_slice_in_dim(out, coeffs[i : i + 1], slab, 0)
         return out.reshape(atoms, projs_each)
 
-    def amounts(coeffs):
+    def nearby(coeffs):
         coeffs = coeffs.reshape(grid_count, per_dev, projs_each)
-        coeffs = jnp.concatenate([lax.dynamic_index_in_dim(coeffs, slab, 0, keepdims=False) for slab in here])
-        return jnp.einsum("ap,apj->aj", coeffs * kb_energy, near_projs, precision=PRECISE)[:, None]
+        return jnp.concatenate([lax.dynamic_index_in_dim(coeffs, slab, 0, keepdims=False) for slab in here])
 
     def put_near(coeffs, base, corner=slab_corner):
-        return put(total, near_starts, corner, near_spots, amounts(coeffs), base)
+        spread = jnp.einsum("ap,apj->aj", coeffs * kb_energy, near_projs, precision=PRECISE)
+        return put(total, near_starts, corner, near_spots, spread[:, None], base)
 
     mine = lax.dynamic_slice_in_dim(potential, orb_pos * part, part, axis=2)
     mine = mine.reshape(planes, grid_count, rows, part).transpose(1, 0, 2, 3)
-    mine = after(mine, near_starts)
-    got_potential = exchange_alone(mine)
+    if EARLY:
+        mine = after(mine, near_starts)
+    got_potential = exchange(mine, "grid")
     shared = gather_steps(got_potential[None], "orb")
     shared = jnp.moveaxis(shared.reshape(orb_groups, all_planes, rows, part), 0, 2)
     shared = jnp.moveaxis(shared.reshape(all_planes, rows, groups, 128), 2, 0)
     shared = shared.reshape(groups, grid_count, planes, chunks, some, 128)
     wells = [shared[:, :, :, i].reshape(groups, grid_count, planes * some, 128) for i in range(chunks)]
-    if joined(jnp.zeros((grid_count, lines, 128))).shape[0] == 1:
+    if not whole_tiles:
         wells = [well.reshape(groups, 1, all_planes * some, 128) for well in wells]
 
     every = None
     sums = [0.0] * chunks
+    weights = jnp.stack([c1_4, c2_8])
     for orb in range(orb_count):
         v = random_orbitals[orb]
-        v_here = after(v, mine)
-        v_sends = pieces(v_here)
-        first = partial_slab(v_here)
-        pv, t = planar_first(v_here, potential, planar_tables)
-        v0, first = exchange_with(v_sends[0], first, got_potential)
-        v_blocks = [v0]
+        first = whole_near(partial_near(v))
+        pv, t = planar_first(v, potential, planar_tables)
+        v_send = jnp.concatenate(pieces(v), axis=1)
+        v_got = exchange_after(v_send, got_potential, pv, t, first)
+        v_blocks = [v_got[:, i * lines : (i + 1) * lines] for i in range(chunks)]
         if every is None:
-            every = gather_steps(raw, "grid", (None, mine, got_potential, v0))
+            every = gather_steps(raw, "grid", (None, mine, got_potential, got_potential))
             every_projs = every[:, 2:]
             every_starts, every_spots = atom_windows(every[:, :2].astype(jnp.int32), all_planes, rows_y, cols_x)
-        for piece in v_sends[1:]:
-            v_blocks.append(exchange_alone(piece, v_blocks[-1], pv, t))
         u = put_near(first, t)
-        g_sends = pieces(pv + u)
+        g_send = jnp.concatenate(pieces(pv + u), axis=1)
         base = planar_second(
             jnp.stack([c2_8, c1_4, c0 - c2]), u, v, potential, planar_tables, orb_groups
         )
-        second = partial_slab(u)
-
-        abc = []
-        weights = jnp.stack([c1_4, c2_8])
+        second = everywhere(partial_near(u))
+        if put_late:
+            base = trade(base, "orb")
+        g_got = exchange_after(g_send, v_got, base, second, every_starts, every_spots)
+        g_blocks = [g_got[:, i * lines : (i + 1) * lines] for i in range(chunks)]
+
+        cb = []
         for i in range(chunks):
             a, c, b = depth_out(weights, joined(v_blocks[i]), wells[i], some, depth_tables)
-            abc.append((a, c, b))
+            cb.append((c, b))
             field = a.reshape(groups, all_planes, some, 128)
             first_row = grid_pos * rows + i * some
             if some % 8:
@@ -511,38 +534,41 @@
             corner = jnp.stack([zero, first_row // 8, zero])
             values = pick(total, every_starts, corner, every_spots, field, grouped=True)
             second = second + jnp.einsum("aj,apj->ap", values[:, 0], every_projs, precision=PRECISE)
-        second = c2_8 * second
-        if put_late:
-            second = gather_steps(second[None], "orb")
-            base_all = trade(base, "orb")
-
-        g_blocks = []
-        for i in range(chunks):
-            waits = [v_blocks[-1], base] + g_blocks[-1:] + [x[1] for x in abc[:i]]
-            if i < chunks - 1:
-                g_blocks.append(exchange_alone(g_sends[i], *waits))
-            else:
-                g_last, second = exchange_with(g_sends[i], second, *waits)
-                g_blocks.append(g_last)
-        if put_late:
-            corner = slab_corner + jnp.stack([zero, zero, orb_pos * (part // 128)])
-            q_all = jnp.stack([put_near(second[o], base_all[o], corner) for o in range(orb_groups)])
-        else:
-            base = jnp.moveaxis(base, 0, 2).reshape(planes, rows_y, cols_x)
-            q = put_near(second, base).reshape(planes, rows_y, orb_groups, part)
-            q_all = trade(jnp.moveaxis(q, 2, 0), "orb")
-        q_all = q_all.reshape(orb_groups, planes, grid_count, chunks, some, part)
+        second = (c2_8 * second).reshape(-1)
+        more = -(-second.size // 1024) * 8
+        extra = jnp.pad(second, (0, more * 128 - second.size)).reshape(more, 128)
 
         last = None
         for i in range(chunks):
-            m = depth_back(weights, joined(g_blocks[i]), abc[i][1], abc[i][2], some, depth_tables)
-            if part != 128:
+            if part == 128:
+                tail = [extra] if i == 0 else []
+                m = depth_back(weights, joined(g_blocks[i]), *cb[i], some, grid_count, depth_tables, *tail)
+                m = m.reshape(orb_groups * grid_count, -1, 128)
+            else:
+                m = depth_back(weights, joined(g_blocks[i]), *cb[i], some, 1, depth_tables)
                 m = jnp.moveaxis(m.reshape(groups, all_planes * some, 128), 0, 1)
                 m = jnp.moveaxis(m.reshape(all_planes * some, orb_groups, part), 1, 0)
-            m = m.reshape(orb_groups * grid_count, planes, some, part)
-            m = after(m, g_blocks[-1]) if last is None else after(m, last, q_all)
+                m = m.reshape(orb_groups * grid_count, planes * some * part // 128, 128)
+                if i == 0:
+                    tail = jnp.broadcast_to(extra, (orb_groups * grid_count, more, 128))
+                    m = jnp.concatenate([m, tail], axis=1)
+            if last is not None:
+                m = after(m, last)
             last = exchange(m, ("orb", "grid"))
-            m = last.reshape(orb_groups, grid_count, planes, some, part)
+            length = planes * some * part // 128
+            m = last[:, :length].reshape(orb_groups, grid_count, planes, some, part)
+            if i == 0:
+                sent = last[:, length:].reshape(orb_groups, grid_count, more * 128)
+                second = jnp.sum(sent, axis=1)[:, : atoms * projs_each]
+                if put_late:
+                    corner = slab_corner + jnp.stack([zero, zero, orb_pos * (part // 128)])
+                    q_all = jnp.stack([put_near(nearby(second[o]), base[o], corner) for o in range(orb_groups)])
+                else:
+                    base = jnp.moveaxis(base, 0, 2).reshape(planes, rows_y, cols_x)
+                    own = lax.dynamic_index_in_dim(second, orb_pos, 0, keepdims=False)
+                    q = put_near(nearby(own), base).reshape(planes, rows_y, orb_groups, part)
+                    q_all = trade(jnp.moveaxis(q, 2, 0), "orb")
+                q_all = q_all.reshape(orb_groups, planes, grid_count, chunks, some, part)
             filtered = q_all[:, :, :, i] + m.transpose(0, 2, 1, 3, 4)
             sums[i] = sums[i] + jnp.sum(filtered * filtered, axis=0)
     out = []

time: 518 us -> 452 us (0.87)
  waiting for transfers between devices: 265 us -> 209 us
  starting transfers between devices: 65.4 us -> 48.8 us
    ppermute x1, waiting for transfers between devices: 66.4 us -> 0.01 us  [trade(): got = lax.ppermute(sent, axis, xor_route(size, apart))]
    ppermute x8 -> x7, waiting for transfers between devices: 87.8 us -> 127 us  [gather_steps(): other = lax.ppermute(block, axis, xor_route(size, bit))]
    all_to_all x7 -> x5, waiting for transfers between devices: 106 us -> 75.4 us  [exchange(): return lax.all_to_all(block, axis, split_axis=0, concat_axis=0, tiled=True)]
    all_to_all x7 -> x5, starting transfers between devices: 48.4 us -> 28.9 us  [exchange(): return lax.all_to_all(block, axis, split_axis=0, concat_axis=0, tiled=True)]
    slice x2 -> x10, local copies, waits for them, and re-layouts: 0.15 us -> 10.5 us  [the longest x1 4.67 us: local(): v_blocks = [v_got[:, i * lines:(i + 1) * lines] for i in range(chunks)]]
    transpose x3 -> x0, local copies, waits for them, and re-layouts: 7.4 us -> none  [pieces(): field[:, :, i].transpose(1, 3, 0, 2, 4).reshape(grid_count, lines, 128)]
    unnamed x51 -> x37, local copies, waits for them, and re-layouts: 20.8 us -> 18.2 us
  transfers between devices with their start and end apart: 18 -> 17, of which waited for: 9 -> 11; matrix products, arithmetic and copies ran while one was open for 12% -> 15% of each run, Pallas kernels for 18% -> 20%
where the time goes in v4:
time: 452 us; the launch traced here: 451 us
  waiting for transfers between devices  209 us (46%)
  Pallas kernels  96.6 us (21%)
  local copies, waits for them, and re-layouts  50.5 us (11%)
  starting transfers between devices  48.8 us (11%)
  other arithmetic  36.4 us (8%)
  matrix products  6.25 us (1%)
    ppermute x7, waiting for transfers between devices, gather_steps(): other = lax.ppermute(block, axis, xor_route(size, bit))  127 us
    all_to_all x5, waiting for transfers between devices, exchange(): return lax.all_to_all(block, axis, split_axis=0, concat_axis=0, tiled=True)  75.4 us
    all_to_all x5, starting transfers between devices, exchange(): return lax.all_to_all(block, axis, split_axis=0, concat_axis=0, tiled=True)  28.9 us
    pallas_call x4, Pallas kernels, pick(): pl.pallas_call(functools.partial(pick_kernel, total, grouped), out_shape=...  27.9 us
    unnamed x37, local copies, waits for them, and re-layouts  18.2 us
    pallas_call x2, Pallas kernels, depth_out(): pl.pallas_call(functools.partial(out_kernel, rows), out_shape=[jax.ShapeD...  14.6 us
    pallas_call x3, Pallas kernels, put(): pl.pallas_call(functools.partial(put_kernel, total), out_shape=jax.ShapeD...  14.4 us
    pallas_call x1, Pallas kernels, planar_first(): pl.pallas_call(first_kernel, grid=field.shape[:1], out_shape=[jax.ShapeDt...  13.8 us
  transfers between devices with their start and end apart: 17, of which 11 were waited for; matrix products, arithmetic and copies ran while one was open for 15% of the time, Pallas kernels for 20%

profile of v4, /device:TPU:0, one launch (start us, length us, event | category | flops | bytes accessed | tf_op | source)
XLA Modules:
  0.0 450.7 jit_solution(4696923451330114339)
XLA Ops:
  1.5 5.4 %collective-permute-start.1 = (f32[16,6,128]{2,0,1:T(8,128)S(1)}, f32[16,6,128]{2,0,1:T(8,128)S(1)}, u32[]{:S(2)}, u32[]{:S(2)}) collective-permute-start(f32[16,6,128]{2,0,1:T(8,128)S(1)} %pad_maximum_fusion.13), channel_id=1, source_target_pairs={{0,15},{1,0},{2,1},{3,2},{4,3},{5,4},{6,5},{7,6},{8,7},{9,8},{10,9... | collective-permute-start | bytes 147464 | tf_op jit(solution)/shard_map/ppermute | solution.py:448
  6.9 1.7 constant_dynamic-slice_fusion.7
  8.7 4.5 collective-permute-done
  14.6 1.6 copy.230
  16.1 3.7 all-to-all-start
  19.9 2.6 fusion.104
  22.5 1.7 copy.283
  24.2 1.7 copy.284
  25.8 1.1 fusion.16
  28.0 13.8 %planar_first.1 = (f32[16,256,256]{2,1,0:T(8,128)S(1)}, f32[16,256,256]{2,1,0:T(8,128)}) custom-call(f32[16,256,256]{2,1,0:T(8,128)} %bitcast.283, f32[16,256,256]{2,1,0:T(8,128)} %potential.3, bf16[2,256,256]{2,1,0:T(8,128)(2,1)S(1)} %get-tuple-element.159.high_tables, bf16[2,256,256]{2,1,0:T(8,128)(2,1)S(1)} %get-tuple-element.160.low_tables), custom_call_target="tpu_custom_call" | custom-call | flops 3221225472 | bytes 16777216 | tf_op jit(solution)/shard_map/planar_first/pallas_call | solution.py:332
  41.8 1.9 copy-done.7
  44.6 4.6 %pick.4 = f32[48,1,128]{2,1,0:T(1,128)S(1)} custom-call(s32[48,3]{1,0:T(8,128)S(1)} %pad_add_fusion.3.starts, s32[3]{0:T(128)S(1)} %stack.135.corner, s32[48,2,128]{2,1,0:T(2,128)S(1)} %pad_add_fusion.2.spots, f32[16,32,8,256]{3,2,1,0:T(8,128)S(1)} %bitcast.285), custom_call_target="tpu_custom_call" | custom-call | flops 16777216 | bytes 16777216 | tf_op jit(solution)/shard_map/pick/pallas_call | solution.py:290
  50.2 4.6 %pad_maximum_fusion.1 = f32[16,512,128]{2,1,0:T(8,128)} fusion(f32[16,256,128]{2,1,0:T(8,128)} %bitcast.296, f32[16,256,128]{2,1,0:T(8,128)} %bitcast.295), kind=kLoop, calls=%fused_computation.1 | loop fusion | flops 1048576 | bytes 8388608 | tf_op jit(solution)/shard_map/concatenate | solution.py:507
  54.7 4.2 collective-permute-start.2
  61.1 11.3 %all-to-all-start.1 = ((f32[16,512,128]{2,1,0:T(8,128)}), f32[16,512,128]{2,1,0:T(8,128)}, u32[]{:S(2)}, u32[]{:S(2)}) async-start(f32[16,512,128]{2,1,0:T(8,128)} %pad_maximum_fusion.1), calls=%async_computation.1 | async-start | bytes 8388608 | tf_op jit(solution)/shard_map/all_to_all | solution.py:75
  72.4 2.8 collective-permute-start.5
  79.1 5.9 %put.3.field = f32[16,32,8,256]{3,2,1,0:T(8,128)S(1)} custom-call(s32[48,3]{1,0:T(8,128)S(1)} %pad_add_fusion.3.starts, s32[3]{0:T(128)S(1)} %stack.135.corner, s32[48,2,128]{2,1,0:T(2,128)S(1)} %pad_add_fusion.2.spots, f32[48,1,128]{2,1,0:T(1,128)S(1)} %fusion.68.spread, f32[16,32,8,256]{3,2,1,0:T(8,128)} %bitcast.299), custom_call_target="tpu_custom_call" | custom-call | flops 16777216 | bytes 16777216 | tf_op jit(solution)/shard_map/put/pallas_call | solution.py:304
  85.1 2.0 copy-done
  87.1 13.1 %planar_second.1 = f32[2,16,256,128]{3,2,1,0:T(8,128)S(1)} custom-call(f32[3]{0:T(128)S(1)} %pad_maximum_fusion.15.weights, f32[16,256,256]{2,1,0:T(8,128)} %bitcast.281, f32[16,256,256]{2,1,0:T(8,128)} %bitcast.284, f32[16,256,256]{2,1,0:T(8,128)} %potential.3, bf16[2,256,256]{2,1,0:T(8,128)(2,1)S(1)} %get-tuple-element.159.high_tables, ...), custom_call_target="tpu_custom_call" | custom-call | flops 3221225472 | bytes 16777216 | tf_op jit(solution)/shard_map/planar_second/pallas_call | solution.py:348
  100.2 1.7 constant_dynamic-slice_fusion.6
  102.9 1.5 collective-permute-start.4
  104.4 64.1 %collective-permute-done.5 = f32[16,6,128]{2,0,1:T(8,128)S(1)} collective-permute-done((f32[16,6,128]{2,0,1:T(8,128)S(1)}, f32[16,6,128]{2,0,1:T(8,128)S(1)}, u32[]{:S(2)}, u32[]{:S(2)}) %collective-permute-start.5) | collective-permute-done | bytes 49184 | tf_op jit(solution)/shard_map/ppermute | solution.py:55
  168.6 4.6 %collective-permute-done.6 = f32[2,16,6,128]{3,1,2,0:T(8,128)S(1)} collective-permute-done((f32[2,16,6,128]{3,1,2,0:T(8,128)S(1)}, f32[2,16,6,128]{3,1,2,0:T(8,128)S(1)}, u32[]{:S(2)}, u32[]{:S(2)}) %collective-permute-start.6) | collective-permute-done | bytes 98336 | tf_op jit(solution)/shard_map/ppermute | solution.py:55
  173.2 1.5 collective-permute-start.7
  174.8 4.0 bitcast_add_fusion
  180.2 2.5 pad_maximum_fusion
  182.8 1.2 copy-done.4
  183.9 1.8 constant_dynamic-update-slice_fusion.3
  186.0 1.7 copy-done.5
  191.7 5.4 %fusion.57 = (s32[256,1,128]{2,1,0:T(1,128)S(1)}, s32[256,1,128]{2,1,0:T(1,128)S(1)}) fusion(s32[256,1,128]{2,1,0:T(1,128)S(1)} %bitcast.306, s32[256,1,128]{2,1,0:T(1,128)} %bitcast.309, s32[256,1,128]{2,1,0:T(1,128)} %bitcast.310, s32[256,1,128]{2,1,0:T(1,128)S(1)} %bitcast.302, pred[256,1,128]{2,0,1:T(8,128)(4,1)S(1)} %get-tuple-element.125, ...), kind=kLoop, calls=%fused_computation.148 | loop fusion | flops 1703936 | bytes 1120256 | tf_op jit(solution)/shard_map/sub | solution.py:398
  197.3 4.6 %all-to-all-start.2 = ((f32[16,512,128]{2,1,0:T(8,128)}), f32[16,512,128]{2,1,0:T(8,128)}, u32[]{:S(2)}, u32[]{:S(2)}) async-start(f32[16,512,128]{2,1,0:T(8,128)} %pad_maximum_fusion), calls=%async_computation.2 | async-start | bytes 8388608 | tf_op jit(solution)/shard_map/all_to_all | solution.py:75
  201.9 1.6 collective-permute-start.9
  203.6 1.1 reduce-precision_convert_fusion
  204.7 2.2 copy-done.1
  206.9 4.6 %pick.5 = f32[48,1,128]{2,1,0:T(1,128)S(1)} custom-call(s32[48,3]{1,0:T(8,128)S(1)} %pad_add_fusion.3.starts, s32[3]{0:T(128)S(1)} %stack.135.corner, s32[48,2,128]{2,1,0:T(2,128)S(1)} %pad_add_fusion.2.spots, f32[16,32,8,256]{3,2,1,0:T(8,128)S(1)} %copy-done.1), custom_call_target="tpu_custom_call" | custom-call | flops 16777216 | bytes 16777216 | tf_op jit(solution)/shard_map/pick/pallas_call | solution.py:290
  212.4 1.1 slice.283
  213.5 36.5 %collective-permute-done.9 = f32[1,16,16,16,128]{4,3,2,1,0:T(8,128)} collective-permute-done((f32[1,16,16,16,128]{4,3,2,1,0:T(8,128)S(1)}, f32[1,16,16,16,128]{4,3,2,1,0:T(8,128)}, u32[]{:S(2)}, u32[]{:S(2)}) %collective-permute-start.9) | collective-permute-done | bytes 2097184 | tf_op jit(solution)/shard_map/ppermute | solution.py:55
  250.0 2.2 select_bitcast_fusion.1
  252.2 2.6 fusion.2
  254.8 4.7 %fusion.102 = (f32[16,256,128]{2,1,0:T(8,128)}, f32[16,256,128]{2,1,0:T(8,128)}) fusion(f32[16,512,128]{2,1,0:T(8,128)} %all-to-all-done.1), kind=kLoop, calls=%fused_computation.286 | loop fusion | bytes 8388608 | tf_op jit(solution)/shard_map/slice | solution.py:509
  259.5 7.3 %depth_out.2 = (f32[2,2048,128]{2,1,0:T(8,128)S(1)}, f32[2,2048,128]{2,1,0:T(8,128)S(1)}, f32[2,2048,128]{2,1,0:T(8,128)}) custom-call(f32[2]{0:T(128)S(1)} %pad_maximum_fusion.14.weights, f32[16,256,128]{2,1,0:T(8,128)} %get-tuple-element.105.field, f32[2,16,128,128]{3,2,1,0:T(8,128)} %get-tuple-element.103.potential, ...), custom_call_target="tpu_custom_call" | custom-call | flops 805306368 | bytes 10485760 | tf_op jit(solution)/shard_map/depth_out/pallas_call | solution.py:363
  266.8 1.3 copy-done.9
  268.1 9.3 %pick.6 = f32[256,1,128]{2,1,0:T(1,128)S(1)} custom-call(s32[256,3]{1,0:T(8,128)S(1)} %pad_add_fusion.1.starts, s32[3]{0:T(128)S(1)} %get-tuple-element.162.corner, s32[256,2,128]{2,1,0:T(2,128)S(1)} %pad_add_fusion.spots, f32[2,256,8,128]{3,2,1,0:T(8,128)S(1)} %bitcast.289), custom_call_target="tpu_custom_call" | custom-call | flops 16777216 | bytes 16777216 | tf_op jit(solution)/shard_map/pick/pallas_call | solution.py:290
  277.4 7.3 %depth_out.3 = (f32[2,2048,128]{2,1,0:T(8,128)S(1)}, f32[2,2048,128]{2,1,0:T(8,128)S(1)}, f32[2,2048,128]{2,1,0:T(8,128)}) custom-call(f32[2]{0:T(128)S(1)} %pad_maximum_fusion.14.weights, f32[16,256,128]{2,1,0:T(8,128)} %get-tuple-element.106.field, f32[2,16,128,128]{3,2,1,0:T(8,128)} %get-tuple-element.104.potential, ...), custom_call_target="tpu_custom_call" | custom-call | flops 805306368 | bytes 10485760 | tf_op jit(solution)/shard_map/depth_out/pallas_call | solution.py:363
  284.7 1.3 copy-done.8
  286.0 9.5 %pick.7 = f32[256,1,128]{2,1,0:T(1,128)S(1)} custom-call(s32[256,3]{1,0:T(8,128)S(1)} %pad_add_fusion.1.starts, s32[3]{0:T(128)S(1)} %get-tuple-element.161.corner, s32[256,2,128]{2,1,0:T(2,128)S(1)} %pad_add_fusion.spots, f32[2,256,8,128]{3,2,1,0:T(8,128)S(1)} %bitcast.288), custom_call_target="tpu_custom_call" | custom-call | flops 16777216 | bytes 16777216 | tf_op jit(solution)/shard_map/pick/pallas_call | solution.py:290
  295.5 2.0 fusion.14
  297.5 2.0 fusion.12
  299.6 2.7 fusion.103
  302.5 6.1 %depth_back.2 = f32[2,16,136,128]{3,2,1,0:T(8,128)} custom-call(f32[2]{0:T(128)S(1)} %pad_maximum_fusion.14.weights, f32[16,256,128]{2,1,0:T(8,128)S(1)} %get-tuple-element.107.g_in, f32[2,2048,128]{2,1,0:T(8,128)S(1)} %copy-done.10, f32[2,2048,128]{2,1,0:T(8,128)} %get-tuple-element.77.b_in, bf16[256,256]{1,0:T(8,128)(2,1)S(1)} %get-tuple-element.165.high_table, ...), custom_call_target="tpu_custom_call" | custom-call | flops 805306368 | bytes 8388608 | tf_op jit(solution)/shard_map/depth_back/pallas_call | solution.py:377
  308.6 5.8 %all-to-all-start.3 = ((f32[32,136,128]{2,1,0:T(8,128)}), f32[32,136,128]{2,1,0:T(8,128)}, u32[]{:S(2)}, u32[]{:S(2)}) async-start(f32[32,136,128]{2,1,0:T(8,128)} %bitcast.291), calls=%async_computation.3 | async-start | bytes 4456448 | tf_op jit(solution)/shard_map/all_to_all | solution.py:75
  314.5 6.8 %depth_back.3 = f32[2,16,128,128]{3,2,1,0:T(8,128)} custom-call(f32[2]{0:T(128)S(1)} %pad_maximum_fusion.14.weights, f32[16,256,128]{2,1,0:T(8,128)S(1)} %get-tuple-element.108.g_in, f32[2,2048,128]{2,1,0:T(8,128)} %copy-done.8, f32[2,2048,128]{2,1,0:T(8,128)} %get-tuple-element.81.b_in, bf16[256,256]{1,0:T(8,128)(2,1)S(1)} %get-tuple-element.165.high_table, ...), custom_call_target="tpu_custom_call" | custom-call | flops 805306368 | bytes 8388608 | tf_op jit(solution)/shard_map/depth_back/pallas_call | solution.py:377
  321.3 45.7 %all-to-all-done.3 = f32[32,136,128]{2,1,0:T(8,128)} async-done(((f32[32,136,128]{2,1,0:T(8,128)}), f32[32,136,128]{2,1,0:T(8,128)}, u32[]{:S(2)}, u32[]{:S(2)}) %all-to-all-start.3) | async-done | bytes 2228256 | tf_op jit(solution)/shard_map/all_to_all | solution.py:75
  367.0 3.5 all-to-all-start.4
  370.6 4.0 slice_bitcast_fusion.1
  376.6 1.9 slice.292
  379.0 4.2 put.4
  383.7 4.2 put.5
  389.7 1.6 collective-permute-start.10
  391.3 29.0 %all-to-all-done.4 = f32[32,128,128]{2,1,0:T(8,128)} async-done(((f32[32,128,128]{2,1,0:T(8,128)}), f32[32,128,128]{2,1,0:T(8,128)}, u32[]{:S(2)}, u32[]{:S(2)}) %all-to-all-start.4) | async-done | bytes 2097184 | tf_op jit(solution)/shard_map/all_to_all | solution.py:75
  420.3 2.1 fusion.6
  423.3 1.5 select_bitcast_fusion.5
  425.1 22.0 %collective-permute-done.11 = f32[1,16,16,8,128]{4,3,1,2,0:T(8,128)S(1)} collective-permute-done((f32[1,16,16,8,128]{4,3,1,2,0:T(8,128)S(1)}, f32[1,16,16,8,128]{4,3,1,2,0:T(8,128)S(1)}, u32[]{:S(2)}, u32[]{:S(2)}) %collective-permute-start.11) | collective-permute-done | bytes 1048608 | tf_op jit(solution)/shard_map/ppermute | solution.py:55
  448.1 2.6 copy.262
  (163 shorter events, 24.4 us)
Async XLA Ops:
  1.5 7.2 %collective-permute-start.1 = (f32[16,6,128]{2,0,1:T(8,128)S(1)}, f32[16,6,128]{2,0,1:T(8,128)S(1)}, u32[]{:S(2)}, u32[]{:S(2)}) collective-permute-start(f32[16,6,128]{2,0,1:T(8,128)S(1)} %pad_maximum_fusion.13), channel_id=1, source_target_pairs={{0,15},{1,0},{2,1},{3,2},{4,3},{5,4},{6,5},{7,6},{8,7},{9,8},{10,9... | collective-permute-start | bytes 147464 | tf_op jit(solution)/shard_map/ppermute | solution.py:448
  6.9 6.2 %collective-permute-start = (f32[16,6,128]{2,0,1:T(8,128)S(1)}, f32[16,6,128]{2,0,1:T(8,128)S(1)}, u32[]{:S(2)}, u32[]{:S(2)}) collective-permute-start(f32[16,6,128]{2,0,1:T(8,128)S(1)} %pad_maximum_fusion.13), channel_id=1, source_target_pairs={{0,1},{1,2},{2,3},{3,4},{4,5},{5,6},{6,7},{7,8},{8,9},{9,10},{10,1... | collective-permute-start | bytes 147464 | tf_op jit(solution)/shard_map/ppermute | solution.py:448
  16.1 44.9 %all-to-all-start = ((f32[16,16,16,128]{3,2,1,0:T(8,128)}), f32[16,16,16,128]{3,2,1,0:T(8,128)S(1)}, u32[]{:S(2)}, u32[]{:S(2)}) async-start(f32[16,16,16,128]{3,2,1,0:T(8,128)} %copy.230), calls=%async_computation | async-start | bytes 4194304 | tf_op jit(solution)/shard_map/all_to_all | solution.py:75
  28.0 16.6 %copy-start.2 = (f32[1,16,256,256]{3,2,1,0:T(8,128)S(1)}, f32[1,16,256,256]{3,2,1,0:T(8,128)}, u32[]{:S(2)}) copy-start(f32[1,16,256,256]{3,2,1,0:T(8,128)} %param.14) | copy-start | bytes 12582916
  41.8 1.9 copy-start.7
  49.2 29.4 %copy-start.12 = (f32[48,4,128]{2,0,1:T(8,128)}, f32[48,4,128]{2,0,1:T(8,128)S(1)}, u32[]{:S(2)}) copy-start(f32[48,4,128]{2,0,1:T(8,128)S(1)} %pad_maximum_fusion.9) | copy-start | bytes 294916
  49.9 9.5 %collective-permute-start.3 = (f32[3,16,4]{1,0,2:T(4,128)S(1)}, f32[3,16,4]{1,0,2:T(4,128)S(1)}, u32[]{:S(2)}, u32[]{:S(2)}) collective-permute-start(f32[3,16,4]{1,0,2:T(4,128)S(1)} %reshape.401), channel_id=1, source_target_pairs={{0,1},{1,2},{2,3},{3,4},{4,5},{5,6},{6,7},{7,8},{8,9},{9,10},{10,1... | collective-permute-start | bytes 2312 | tf_op jit(solution)/shard_map/ppermute | solution.py:448
  54.7 5.5 %collective-permute-start.2 = (f32[3,16,4]{1,0,2:T(4,128)S(1)}, f32[3,16,4]{1,0,2:T(4,128)S(1)}, u32[]{:S(2)}, u32[]{:S(2)}) collective-permute-start(f32[3,16,4]{1,0,2:T(4,128)S(1)} %reshape.401), channel_id=1, source_target_pairs={{0,15},{1,0},{2,1},{3,2},{4,3},{5,4},{6,5},{7,6},{8,7},{9,8},{10,9... | collective-permute-start | bytes 2312 | tf_op jit(solution)/shard_map/ppermute | solution.py:448
  61.1 14.1 %copy-start.14 = (f32[3]{0:T(128)S(1)}, f32[3]{0:T(128)}, u32[]{:S(2)}) copy-start(f32[3]{0:T(128)} %param.19) | copy-start | bytes 40
  61.1 17.4 %copy-start.15 = (f32[4]{0:T(128)S(1)}, f32[4]{0:T(128)}, u32[]{:S(2)}) copy-start(f32[4]{0:T(128)} %param.18) | copy-start | bytes 52
  61.1 136.2 %all-to-all-start.1 = ((f32[16,512,128]{2,1,0:T(8,128)}), f32[16,512,128]{2,1,0:T(8,128)}, u32[]{:S(2)}, u32[]{:S(2)}) async-start(f32[16,512,128]{2,1,0:T(8,128)} %pad_maximum_fusion.1), calls=%async_computation.1 | async-start | bytes 8388608 | tf_op jit(solution)/shard_map/all_to_all | solution.py:75
  72.4 96.1 %collective-permute-start.5 = (f32[16,6,128]{2,0,1:T(8,128)S(1)}, f32[16,6,128]{2,0,1:T(8,128)S(1)}, u32[]{:S(2)}, u32[]{:S(2)}) collective-permute-start(f32[16,6,128]{2,0,1:T(8,128)S(1)} %pad_maximum_fusion.13), channel_id=1, source_target_pairs={{0,8},{1,9},{2,10},{3,11},{4,12},{5,13},{6,14},{7,15},{8,0},{9,1},... | collective-permute-start | bytes 147464 | tf_op jit(solution)/shard_map/ppermute | solution.py:55
  85.0 2.0 copy-start
  100.1 2.7 copy-start.3
  102.9 79.9 %collective-permute-start.4 = (f32[1,16,256,128]{3,2,1,0:T(8,128)}, f32[1,16,256,128]{3,2,1,0:T(8,128)}, u32[]{:S(2)}, u32[]{:S(2)}) collective-permute-start(f32[1,16,256,128]{3,2,1,0:T(8,128)} %constant_dynamic-slice_fusion.6), channel_id=1, source_target_pairs={{0,16},{16,0},{1,17},{17,1},{2,18},{18,2},{3,19},{19,3},{4,20},{20... | collective-permute-start | bytes 6291464 | tf_op jit(solution)/shard_map/ppermute | solution.py:69
  168.5 4.7 %collective-permute-start.6 = (f32[2,16,6,128]{3,1,2,0:T(8,128)S(1)}, f32[2,16,6,128]{3,1,2,0:T(8,128)S(1)}, u32[]{:S(2)}, u32[]{:S(2)}) collective-permute-start(f32[2,16,6,128]{3,1,2,0:T(8,128)S(1)} %pad_maximum_fusion.12), channel_id=1, source_target_pairs={{0,4},{1,5},{2,6},{3,7},{4,0},{5,1},{6,2},{7,3},{8,12},{9,13},{10,... | collective-permute-start | bytes 294920 | tf_op jit(solution)/shard_map/ppermute | solution.py:55
  173.2 5.7 %collective-permute-start.7 = (f32[2,2,16,6,128]{4,2,3,1,0:T(8,128)S(1)}, f32[2,2,16,6,128]{4,2,3,1,0:T(8,128)S(1)}, u32[]{:S(2)}, u32[]{:S(2)}) collective-permute-start(f32[2,2,16,6,128]{4,2,3,1,0:T(8,128)S(1)} %pad_maximum_fusion.8), channel_id=1, source_target_pairs={{0,2},{1,3},{2,0},{3,1},{4,6},{5,7},{6,4},{7,5},{8,10},{9,11},{10,... | collective-permute-start | bytes 589832 | tf_op jit(solution)/shard_map/ppermute | solution.py:55
  179.1 6.7 %collective-permute-start.8 = (f32[2,2,2,16,6,128]{5,3,4,2,1,0:T(8,128)S(1)}, f32[2,2,2,16,6,128]{5,3,4,2,1,0:T(8,128)S(1)}, u32[]{:S(2)}, u32[]{:S(2)}) collective-permute-start(f32[2,2,2,16,6,128]{5,3,4,2,1,0:T(8,128)S(1)} %pad_maximum_fusion.5), channel_id=1, source_target_pairs={{0,1},{1,0},{2,3},{3,2},{4,5},{5,4},{6,7},{7,6},{8,9},{9,8},{10,11... | collective-permute-start | bytes 1179656 | tf_op jit(solution)/shard_map/ppermute | solution.py:55
  180.2 3.7 copy-start.4
  185.8 1.9 copy-start.5
  187.7 0.9 copy-start.11
  197.3 102.3 %all-to-all-start.2 = ((f32[16,512,128]{2,1,0:T(8,128)}), f32[16,512,128]{2,1,0:T(8,128)}, u32[]{:S(2)}, u32[]{:S(2)}) async-start(f32[16,512,128]{2,1,0:T(8,128)} %pad_maximum_fusion), calls=%async_computation.2 | async-start | bytes 8388608 | tf_op jit(solution)/shard_map/all_to_all | solution.py:75
  201.9 48.1 %collective-permute-start.9 = (f32[1,16,16,16,128]{4,3,2,1,0:T(8,128)S(1)}, f32[1,16,16,16,128]{4,3,2,1,0:T(8,128)}, u32[]{:S(2)}, u32[]{:S(2)}) collective-permute-start(f32[1,16,16,16,128]{4,3,2,1,0:T(8,128)S(1)} %bitcast.294), channel_id=1, source_target_pairs={{0,16},{16,0},{1,17},{17,1},{2,18},{18,2},{3,19},{19,3},{4,20},{20... | collective-permute-start | bytes 6291464 | tf_op jit(solution)/shard_map/ppermute | solution.py:55
  204.7 2.2 copy-start.1
  206.9 4.6 %copy-start.13 = (f32[48,4,128]{2,0,1:T(8,128)S(1)}, f32[48,4,128]{2,0,1:T(8,128)}, u32[]{:S(2)}) copy-start(f32[48,4,128]{2,0,1:T(8,128)} %copy-done.12) | copy-start | bytes 294916
  266.8 1.3 copy-start.9
  284.7 1.3 copy-start.8
  299.6 2.9 copy-start.10
  308.6 58.4 %all-to-all-start.3 = ((f32[32,136,128]{2,1,0:T(8,128)}), f32[32,136,128]{2,1,0:T(8,128)}, u32[]{:S(2)}, u32[]{:S(2)}) async-start(f32[32,136,128]{2,1,0:T(8,128)} %bitcast.291), calls=%async_computation.3 | async-start | bytes 4456448 | tf_op jit(solution)/shard_map/all_to_all | solution.py:75
  367.0 53.3 %all-to-all-start.4 = ((f32[32,128,128]{2,1,0:T(8,128)}), f32[32,128,128]{2,1,0:T(8,128)}, u32[]{:S(2)}, u32[]{:S(2)}) async-start(f32[32,128,128]{2,1,0:T(8,128)} %bitcast.128), calls=%async_computation.4 | async-start | bytes 4194304 | tf_op jit(solution)/shard_map/all_to_all | solution.py:75
  376.6 2.4 copy-start.6
  389.7 33.7 %collective-permute-start.10 = (f32[1,16,16,8,128]{4,3,1,2,0:T(8,128)}, f32[1,16,16,8,128]{4,3,1,2,0:T(8,128)}, u32[]{:S(2)}, u32[]{:S(2)}) collective-permute-start(f32[1,16,16,8,128]{4,3,1,2,0:T(8,128)} %multiply_bitcast_fusion.1), channel_id=1, source_target_pairs={{0,16},{16,0},{1,17},{17,1},{2,18},{18,2},{3,19},{19,3},{4,20},{20... | collective-permute-start | bytes 3145736 | tf_op jit(solution)/shard_map/ppermute | solution.py:55
  422.4 24.7 %collective-permute-start.11 = (f32[1,16,16,8,128]{4,3,1,2,0:T(8,128)S(1)}, f32[1,16,16,8,128]{4,3,1,2,0:T(8,128)S(1)}, u32[]{:S(2)}, u32[]{:S(2)}) collective-permute-start(f32[1,16,16,8,128]{4,3,1,2,0:T(8,128)S(1)} %multiply_bitcast_fusion), channel_id=1, source_target_pairs={{0,16},{16,0},{1,17},{17,1},{2,18},{18,2},{3,19},{19,3},{4,20},{20... | collective-permute-start | bytes 3145736 | tf_op jit(solution)/shard_map/ppermute | solution.py:55

commit v5 on v4

--- a/solution.py
+++ b/solution.py
@@ -13,7 +13,6 @@
 STRIDE = 16
 PRECISE = lax.Precision.HIGHEST
 TOGETHER = 4
-EARLY = True
 
 
 def kinetic_table(length):
@@ -31,33 +30,19 @@
     return [(i, i ^ bit) for i in range(size)]
 
 
-def xor_bits(size):
-    bits = []
-    bit = size // 2
-    while bit:
-        bits.append(bit)
-        bit //= 2
-    return bits
-
-
-def after(value, *others):
-    return lax.optimization_barrier((value,) + others)[0]
-
-
-def gather_steps(block, axis, waits=()):
+def gather_part(block, axis, shift, size):
+    place = lax.axis_index(axis)
+    own = lax.rem(lax.shift_right_logical(place, shift), size)
+    out = jnp.broadcast_to(block, (size,) + block.shape)
+    for apart in range(1, size):
+        got = lax.ppermute(block, axis, xor_route(lax.axis_size(axis), apart << shift))
+        out = lax.dynamic_update_slice_in_dim(out, got[None], own ^ apart, 0)
+    return out
+
+
+def gather_over(block, axis):
     size = lax.axis_size(axis)
-    place = lax.axis_index(axis)
-    shape = block.shape
-    bits = xor_bits(size)
-    for i, bit in enumerate(bits):
-        if i < len(waits) and waits[i] is not None:
-            block = after(block, waits[i])
-        other = lax.ppermute(block, axis, xor_route(size, bit))
-        upper = (place & bit) != 0
-        block = jnp.stack([jnp.where(upper, other, block), jnp.where(upper, block, other)])
-    count = len(bits)
-    block = jnp.transpose(block, tuple(range(count))[::-1] + tuple(range(count, block.ndim)))
-    return block.reshape((size * shape[0],) + shape[1:])
+    return gather_part(block, axis, 0, size).reshape((size * block.shape[0],) + block.shape[1:])
 
 
 def trade(blocks, axis):
@@ -75,18 +60,23 @@
     return lax.all_to_all(block, axis, split_axis=0, concat_axis=0, tiled=True)
 
 
+def wrapped(number, size):
+    number = jnp.where(number < 0, number + size, number)
+    return jnp.where(number >= size, number - size, number)
+
+
 def listed(starts, corner, total, planes, tiles, listing):
     all_planes, all_tiles, _ = total
 
     def one(atom, count):
-        ahead = lax.rem(starts[atom, 0] - corner[0] + all_planes, all_planes)
-        behind = lax.rem(corner[0] - starts[atom, 0] + all_planes, all_planes)
-        tile = lax.rem(starts[atom, 1] // 8 - corner[1] + all_tiles, all_tiles)
-        here = ((ahead < planes) | (behind < WIDE)) & ((tile < tiles) | (tile == all_tiles - 1))
+        ahead = wrapped(starts[atom, 0] - corner[0], all_planes)
+        tile = wrapped(lax.shift_right_logical(starts[atom, 1], 3) - corner[1], all_tiles)
+        near = (ahead < planes) | (ahead > all_planes - WIDE)
+        here = near & ((tile < tiles) | (tile == all_tiles - 1))
         listing[count] = atom
         return count + here.astype(jnp.int32)
 
-    return lax.fori_loop(0, starts.shape[0], one, jnp.int32(0))
+    return lax.fori_loop(0, starts.shape[0], one, jnp.int32(0), unroll=8)
 
 
 def split3(block):
@@ -99,13 +89,14 @@
 def placed(starts, corner, total, atom, planes, tiles, lane):
     all_planes, all_tiles, all_groups = total
     z_start, y_start, x_start = starts[atom, 0], starts[atom, 1], starts[atom, 2]
-    ahead = lax.rem(z_start - corner[0] + all_planes, all_planes)
-    depth = [jnp.minimum(lax.rem(ahead + dz, all_planes), planes - 1) for dz in range(WIDE)]
-    z_in = lax.rem(ahead + lane // STRIDE, all_planes) < planes
-    first = lax.rem(y_start // 8 - corner[1] + all_tiles, all_tiles)
-    tile_pair = (first, lax.rem(first + 1, all_tiles))
-    lane_pair = (x_start // 128, lax.rem(x_start // 128 + 1, all_groups))
-    return depth, z_in, tile_pair, lane_pair, lax.rem(y_start, 8), lax.rem(x_start, 128)
+    ahead = wrapped(z_start - corner[0], all_planes)
+    depth = [jnp.minimum(wrapped(ahead + dz, all_planes), planes - 1) for dz in range(WIDE)]
+    z_in = wrapped(ahead + lane // STRIDE, all_planes) < planes
+    first = wrapped(lax.shift_right_logical(y_start, 3) - corner[1], all_tiles)
+    tile_pair = (first, wrapped(first + 1, all_tiles))
+    group = lax.shift_right_logical(x_start, 7)
+    lane_pair = (group, wrapped(group + 1, all_groups))
+    return depth, z_in, tile_pair, lane_pair, y_start & 7, x_start & 127
 
 
 def corner_of(z, tile, group):
@@ -136,9 +127,9 @@
                 upper = jnp.where(lane >= right, at(z, t0, groups[0]), at(z, t0, groups[1]))
                 lower = jnp.where(lane >= right, at(z, t1, groups[0]), at(z, t1, groups[1]))
                 met = jnp.where(row >= down, upper, lower)
-                met = pltpu.roll(met, lax.rem(STRIDE * dz - right + 128, 128), 1)
+                met = pltpu.roll(met, (STRIDE * dz - right) & 127, 1)
                 window = jnp.where(lane // STRIDE == dz, met, window)
-            window = pltpu.roll(window, lax.rem(8 - down, 8), 0)
+            window = pltpu.roll(window, (8 - down) & 7, 0)
             tile_of = jnp.where(row < 8 - down, tile_pair[0], tile_pair[1])
             window = jnp.where(z_in & (tile_of < tiles), window, 0.0)
             spot = spots[atom]
@@ -178,7 +169,7 @@
             window = pltpu.roll(window, down, 0)
             for dz, z in enumerate(depth):
                 part = jnp.where(lane // STRIDE == dz, window, 0.0)
-                part = pltpu.roll(part, lax.rem(right - STRIDE * dz + 128, 128), 1)
+                part = pltpu.roll(part, (right - STRIDE * dz) & 127, 1)
                 spans = range(field.shape[3] // 128)
                 places = [(i, g, corner_of(z, t, g)) for i, t in enumerate((t0, t1)) for g in spans]
                 before = [field[place] for _, _, place in places]
@@ -227,54 +218,41 @@
     return times(high_table[...], high) + (times(low_table[...], high) + times(high_table[...], low))
 
 
-def lines_of(ref, group, start, rows, planes, r):
-    line = pl.ds(start + group * planes * rows + r, planes, stride=rows)
-    return jnp.concatenate([ref[d, line, :] for d in range(ref.shape[0])], axis=0)
+def lines_of(ref, r, rows):
+    devices, lines = ref.shape[:2]
+    line = pl.ds(r, lines // rows, stride=rows)
+    return jnp.concatenate([ref[d, line, :] for d in range(devices)], axis=0)
+
+
+def side_by_side(rows):
+    return [(r, r + 1) for r in range(0, rows - 1, 2)] + [(rows - 1,)] * (rows % 2)
 
 
 def out_kernel(rows, weights, field, potential, high_table, low_table, a_out, c_out, b_out):
-    groups, everywhere = a_out.shape[0], high_table.shape[0]
-    planes = everywhere // field.shape[0]
-
-    def one(r, carry):
-        v = jnp.concatenate([lines_of(field, g, 0, rows, planes, r) for g in range(groups)], axis=1)
-        a = depth_times(high_table, low_table, v)
-        for g in range(groups):
-            cols = slice(128 * g, 128 * g + 128)
-            well = lines_of(potential.at[g], 0, 0, rows, planes, r) - 2.0
-            line = pl.ds(r, everywhere, stride=rows)
-            a_out[g, line, :] = a[:, cols]
-            c_out[g, line, :] = weights[0] * v[:, cols] + weights[1] * a[:, cols]
-            b_out[g, line, :] = weights[1] * well * a[:, cols]
-        return carry
-
-    lax.fori_loop(0, rows, one, 0)
-
-
-def back_kernel(rows, weights, g_in, c_in, b_in, high_table, low_table, *numbers_out):
-    out = numbers_out[-1]
-    groups, everywhere = c_in.shape[0], high_table.shape[0]
-    planes = everywhere // g_in.shape[0]
-    devices = out.shape[1]
+    everywhere = high_table.shape[0]
+    for pair in side_by_side(rows):
+        v = jnp.concatenate([lines_of(field, r, rows) for r in pair], axis=1)
+        both = depth_times(high_table, low_table, v)
+        for i, r in enumerate(pair):
+            a, line = both[:, 128 * i : 128 * i + 128], pl.ds(r, everywhere, stride=rows)
+            a_out[0, line, :] = a
+            c_out[0, line, :] = weights[0] * v[:, 128 * i : 128 * i + 128] + weights[1] * a
+            b_out[0, line, :] = weights[1] * (lines_of(potential.at[0], r, rows) - 2.0) * a
+
+
+def back_kernel(rows, cuts, weights, g_in, c_in, b_in, high_table, low_table, *outs):
+    everywhere = high_table.shape[0]
+    devices = outs[0].shape[1]
     mine = everywhere // devices
-
-    def one(r, carry):
-        line = pl.ds(r, everywhere, stride=rows)
-        parts = [
-            c_in[g, line, :] + weights[1] * lines_of(g_in, g, 0, rows, planes, r) for g in range(groups)
-        ]
-        m = depth_times(high_table, low_table, jnp.concatenate(parts, axis=1))
-        for g in range(groups):
-            m_g = m[:, 128 * g : 128 * g + 128] + b_in[g, line, :]
-            for d in range(devices):
-                out[g, d, pl.ds(r, mine, stride=rows), :] = m_g[mine * d : mine * d + mine]
-        return carry
-
-    lax.fori_loop(0, rows, one, 0)
-    for numbers in numbers_out[:-1]:
-        for g in range(groups):
-            for d in range(devices):
-                out[g, d, mine * rows :, :] = numbers[...]
+    for pair in side_by_side(rows):
+        lines = [pl.ds(r, everywhere, stride=rows) for r in pair]
+        parts = [c_in[0, line, :] + weights[1] * lines_of(g_in, r, rows) for r, line in zip(pair, lines)]
+        both = depth_times(high_table, low_table, jnp.concatenate(parts, axis=1))
+        for i, (r, line) in enumerate(zip(pair, lines)):
+            m = both[:, 128 * i : 128 * i + 128] + b_in[0, line, :]
+            for out, (start, stop) in zip(outs, cuts):
+                for d in range(devices):
+                    out[0, d, pl.ds(r, stop - start, stride=rows), :] = m[mine * d + start : mine * d + stop]
 
 
 def tiled(field):
@@ -284,6 +262,16 @@
 SMEM = pl.BlockSpec(memory_space=pltpu.SMEM)
 VMEM = pl.BlockSpec(memory_space=pltpu.VMEM)
 PARAMS = pltpu.CompilerParams(vmem_limit_bytes=48 * 2**20)
+
+
+def ordered(kernel, count, others):
+    def run(*refs):
+        kernel(*refs[:count], *refs[count + others :])
+
+    return run
+
+
+ANY = pl.BlockSpec(memory_space=pl.ANY)
 
 
 def pick(total, starts, corner, spots, field, grouped=False):
@@ -327,18 +315,18 @@
     return pl.CostEstimate(flops=flops, bytes_accessed=4 * numbers, transcendentals=0)
 
 
-def planar_first(field, potential, tables):
+def planar_first(field, potential, tables, *others):
     plane, pair = plane_specs(field.shape)
     return pl.pallas_call(
-        first_kernel,
+        ordered(first_kernel, 4, len(others)),
         grid=field.shape[:1],
         out_shape=[jax.ShapeDtypeStruct(field.shape, jnp.float32)] * 2,
-        in_specs=[plane, plane, pair, pair],
+        in_specs=[plane, plane, pair, pair] + [ANY] * len(others),
         out_specs=[plane, plane],
         compiler_params=PARAMS,
         cost_estimate=cost(12 * field.shape[2] * field.size, 4 * field.size),
         name="planar_first",
-    )(field, potential, *tables)
+    )(field, potential, *tables, *others)
 
 
 def planar_second(weights, field, extra, potential, tables, parts):
@@ -357,32 +345,146 @@
     )(weights, field, extra, potential, *tables)
 
 
-def depth_out(weights, field, potential, rows, tables):
-    groups = potential.shape[0]
-    lines = tables[0].shape[0] * rows
+def tie(block, *others):
+    return pl.pallas_call(
+        lambda *refs: None,
+        out_shape=jax.ShapeDtypeStruct(block.shape, block.dtype),
+        in_specs=[ANY] * (1 + len(others)),
+        out_specs=ANY,
+        input_output_aliases={0: 0},
+        cost_estimate=cost(0, 0),
+        name="tie",
+    )(block, *others)
+
+
+def append_kernel(first, others, numbers, block, *refs):
+    out, sem = refs[others], refs[others + 1]
+    copies = [
+        pltpu.make_async_copy(numbers, out.at[d, pl.ds(first, numbers.shape[0]), :], sem.at[d])
+        for d in range(out.shape[0])
+    ]
+    for copy in copies:
+        copy.start()
+    for copy in copies:
+        copy.wait()
+
+
+def append(block, numbers, *others):
+    devices, lines, wide = block.shape
+    return pl.pallas_call(
+        functools.partial(append_kernel, lines - numbers.shape[0], len(others)),
+        out_shape=jax.ShapeDtypeStruct(block.shape, block.dtype),
+        in_specs=[VMEM, ANY] + [ANY] * len(others),
+        out_specs=ANY,
+        scratch_shapes=[pltpu.SemaphoreType.DMA((devices,))],
+        input_output_aliases={1: 0},
+        cost_estimate=cost(0, devices * numbers.size),
+        name="append",
+    )(numbers, block, *others)
+
+
+def pack_kernel(count, chunks, chosen, together, *refs):
+    fields, out = refs[:count], refs[-1]
+    planes, rows, cols = fields[0].shape
+    some = rows // chunks // together
+    lines = planes * some
+    for d in range(together):
+        at = 0
+        for i in chosen:
+            start = (d * chunks + i) * some
+            for g in range(cols // 128):
+                cells = (slice(None), slice(start, start + some), slice(128 * g, 128 * g + 128))
+                part = fields[0][cells]
+                for field in fields[1:]:
+                    part = part + field[cells]
+                out[d, at : at + lines, :] = part.reshape(lines, 128)
+                at += lines
+
+
+def pack(fields, devices, chunks, chosen, spare, *others):
+    planes, rows_y, cols = fields[0].shape
+    rows = rows_y // devices
+    together = math.gcd(devices, 4)
+    lines = planes * rows * cols // 128 * len(chosen) // chunks
+    block = pl.BlockSpec((planes, rows * together, cols), lambda d: (0, d, 0))
+    return pl.pallas_call(
+        ordered(functools.partial(pack_kernel, len(fields), chunks, chosen, together), len(fields), len(others)),
+        grid=(devices // together,),
+        out_shape=jax.ShapeDtypeStruct((devices, lines + spare, 128), jnp.float32),
+        in_specs=[block] * len(fields) + [ANY] * len(others),
+        out_specs=pl.BlockSpec((together, lines, 128), lambda d: (d, 0, 0)),
+        compiler_params=PARAMS,
+        cost_estimate=cost(devices * lines * 128, 2 * devices * lines * 128),
+        name="pack",
+    )(*fields, *others)
+
+
+def pack_part_kernel(place, field, out):
+    planes, rows, _ = field.shape
+    each = rows // out.shape[0]
+    for d in range(out.shape[0]):
+        out[d] = field[:, d * each : (d + 1) * each, :].reshape(planes * each, 128)
+
+
+def pack_part(field, devices, place):
+    planes, rows_y, _ = field.shape
+    together = math.gcd(devices, 4)
+    lines = planes * rows_y // devices
+    return pl.pallas_call(
+        pack_part_kernel,
+        grid_spec=pltpu.PrefetchScalarGridSpec(
+            num_scalar_prefetch=1,
+            grid=(devices // together,),
+            in_specs=[pl.BlockSpec((planes, rows_y // devices * together, 128), lambda d, place: (0, d, place[0]))],
+            out_specs=pl.BlockSpec((together, lines, 128), lambda d, place: (d, 0, 0)),
+        ),
+        out_shape=jax.ShapeDtypeStruct((devices, lines, 128), jnp.float32),
+        compiler_params=PARAMS,
+        cost_estimate=cost(0, 2 * devices * lines * 128),
+        name="pack_part",
+    )(place, field)
+
+
+def depth_specs(field, potential_shape, rows, chunk):
+    groups, lines = potential_shape[0], potential_shape[1] * potential_shape[2]
+    devices = field.shape[0]
+    got = pl.BlockSpec((devices, lines // devices, 128), lambda g: (0, chunk * groups + g, 0))
+    flat = pl.BlockSpec((1, lines, 128), lambda g: (g, 0, 0))
+    table = pl.BlockSpec((lines // rows, lines // rows), lambda g: (0, 0))
+    return got, flat, table
+
+
+def depth_out(weights, field, potential, rows, chunk, tables):
+    groups, devices, lines = potential.shape[:3]
+    got, flat, table = depth_specs(field, potential.shape, rows, chunk)
+    well = pl.BlockSpec((1, devices, lines, 128), lambda g: (g, 0, 0, 0))
+    lines = devices * lines
     return pl.pallas_call(
         functools.partial(out_kernel, rows),
+        grid=(groups,),
         out_shape=[jax.ShapeDtypeStruct((groups, lines, 128), jnp.float32)] * 3,
-        in_specs=[SMEM, VMEM, VMEM, VMEM, VMEM],
-        out_specs=[VMEM] * 3,
+        in_specs=[SMEM, got, well, table, table],
+        out_specs=[flat] * 3,
         compiler_params=PARAMS,
         cost_estimate=cost(6 * tables[0].size * rows * groups * 128, 5 * groups * lines * 128),
         name="depth_out",
     )(weights, field, potential, *tables)
 
 
-def depth_back(weights, g, c, b, rows, devices, tables, *numbers):
+def depth_back(weights, g, c, b, rows, devices, cuts, tables, *others):
     groups, lines = c.shape[:2]
-    shape = (groups, devices, lines // devices + sum(n.shape[0] for n in numbers), 128)
-    return pl.pallas_call(
-        functools.partial(back_kernel, rows),
-        out_shape=jax.ShapeDtypeStruct(shape, jnp.float32),
-        in_specs=[SMEM] + [VMEM] * (5 + len(numbers)),
-        out_specs=VMEM,
+    got, flat, table = depth_specs(g, (groups, 1, lines), rows, 0)
+    each = [(stop - start) * rows for start, stop in cuts]
+    return pl.pallas_call(
+        ordered(functools.partial(back_kernel, rows, cuts), 6, len(others)),
+        grid=(groups,),
+        out_shape=[jax.ShapeDtypeStruct((groups, devices, n, 128), jnp.float32) for n in each],
+        in_specs=[SMEM, got, flat, flat, table, table] + [ANY] * len(others),
+        out_specs=[pl.BlockSpec((1, devices, n, 128), lambda g: (g, 0, 0, 0)) for n in each],
         compiler_params=PARAMS,
         cost_estimate=cost(6 * tables[0].shape[0] * c.size, 4 * c.size),
         name="depth_back",
-    )(weights, g, c, b, *tables, *numbers)
+    )(weights, g, c, b, *tables, *others)
 
 
 def atom_windows(cells, all_planes, rows_y, cols_x):
@@ -428,26 +530,37 @@
     lines = groups * planes * some
     whole_tiles = planes % 8 == 0 and some % 8 == 0
 
-    def pieces(field):
-        field = field.reshape(planes, grid_count, chunks, some, groups, 128)
-        return [field[:, :, i].transpose(1, 3, 0, 2, 4).reshape(grid_count, lines, 128) for i in range(chunks)]
-
-    def exchange_after(piece, *others):
-        return exchange(after(piece, *others), "grid")
+    def packed(fields, chosen, spare, *others):
+        if whole_tiles:
+            return pack(fields, grid_count, chunks, chosen, spare, *others)
+        field = sum(fields[1:], fields[0]).reshape(planes, grid_count, chunks, some, groups, 128)
+        sent = [field[:, :, i].transpose(1, 3, 0, 2, 4).reshape(grid_count, lines, 128) for i in chosen]
+        return jnp.concatenate(sent + [jnp.zeros((grid_count, spare, 128), jnp.float32)], axis=1)
 
     def joined(got):
         if whole_tiles:
             return got
-        got = got[:, :lines].reshape(grid_count, groups, planes * some, 128)
-        return got.transpose(1, 0, 2, 3).reshape(1, grid_count * lines, 128)
-
-    raw = jnp.concatenate([sphere_cells.astype(jnp.float32), projectors], axis=1)
+        got = got.reshape(grid_count, -1, planes * some, 128)
+        return got.transpose(1, 0, 2, 3).reshape(1, -1, 128)
+
+    if part == 128 and rows % 8 == 0:
+        mine = pack_part(potential, grid_count, orb_pos[None])
+        mine = mine.reshape(grid_count, planes, rows, part)
+    else:
+        mine = lax.dynamic_slice_in_dim(potential, orb_pos * part, part, axis=2)
+        mine = mine.reshape(planes, grid_count, rows, part).transpose(1, 0, 2, 3)
+
+    raw = tie(jnp.concatenate([sphere_cells.astype(jnp.float32), projectors], axis=1), mine)
     here = [(grid_pos + grid_count + step) % grid_count for step in (-1, 0, 1)]
 
     def shifted(block, step):
         return lax.ppermute(block, "grid", [(i, (i + step) % grid_count) for i in range(grid_count)])
 
-    near = jnp.concatenate([shifted(raw, 1), raw, shifted(raw, -1)])
+    low = 1 << ((grid_count.bit_length() - 1) // 2)
+    high = grid_count // low
+    column = gather_part(raw, "grid", low.bit_length() - 1, high)
+    gots = [shifted(raw, 1), shifted(raw, -1)]
+    near = jnp.concatenate([gots[0], raw, gots[1]])
     near_projs = near[:, 2:]
     near_starts, near_spots = atom_windows(near[:, :2].astype(jnp.int32), all_planes, rows_y, cols_x)
     zero = jnp.zeros_like(grid_pos)
@@ -484,12 +597,8 @@
         spread = jnp.einsum("ap,apj->aj", coeffs * kb_energy, near_projs, precision=PRECISE)
         return put(total, near_starts, corner, near_spots, spread[:, None], base)
 
-    mine = lax.dynamic_slice_in_dim(potential, orb_pos * part, part, axis=2)
-    mine = mine.reshape(planes, grid_count, rows, part).transpose(1, 0, 2, 3)
-    if EARLY:
-        mine = after(mine, near_starts)
-    got_potential = exchange(mine, "grid")
-    shared = gather_steps(got_potential[None], "orb")
+    got_potential = exchange(tie(mine, *gots), "grid")
+    shared = gather_over(got_potential[None], "orb")
     shared = jnp.moveaxis(shared.reshape(orb_groups, all_planes, rows, part), 0, 2)
     shared = jnp.moveaxis(shared.reshape(all_planes, rows, groups, 128), 2, 0)
     shared = shared.reshape(groups, grid_count, planes, chunks, some, 128)
@@ -497,34 +606,35 @@
     if not whole_tiles:
         wells = [well.reshape(groups, 1, all_planes * some, 128) for well in wells]
 
-    every = None
-    sums = [0.0] * chunks
+    halves = [(0, planes // 2), (planes // 2, planes)] if planes % 16 == 0 else [(0, planes)]
+    cuts = [[(0, planes)]] * (chunks - 1) + [halves]
+    sums = [[0.0] * len(cut) for cut in cuts]
     weights = jnp.stack([c1_4, c2_8])
     for orb in range(orb_count):
         v = random_orbitals[orb]
         first = whole_near(partial_near(v))
-        pv, t = planar_first(v, potential, planar_tables)
-        v_send = jnp.concatenate(pieces(v), axis=1)
-        v_got = exchange_after(v_send, got_potential, pv, t, first)
-        v_blocks = [v_got[:, i * lines : (i + 1) * lines] for i in range(chunks)]
-        if every is None:
-            every = gather_steps(raw, "grid", (None, mine, got_potential, got_potential))
+        pv, t = planar_first(v, potential, planar_tables, mine)
+        v_send = packed([v], range(chunks), 0, mine)
+        if orb == 0:
+            every = gather_part(column, "grid", 0, low)
+            every = jnp.swapaxes(every, 0, 1).reshape((atoms,) + raw.shape[1:])
             every_projs = every[:, 2:]
             every_starts, every_spots = atom_windows(every[:, :2].astype(jnp.int32), all_planes, rows_y, cols_x)
+        v_got = exchange(tie(v_send, first, column), "grid")
         u = put_near(first, t)
-        g_send = jnp.concatenate(pieces(pv + u), axis=1)
         base = planar_second(
             jnp.stack([c2_8, c1_4, c0 - c2]), u, v, potential, planar_tables, orb_groups
         )
         second = everywhere(partial_near(u))
         if put_late:
-            base = trade(base, "orb")
-        g_got = exchange_after(g_send, v_got, base, second, every_starts, every_spots)
-        g_blocks = [g_got[:, i * lines : (i + 1) * lines] for i in range(chunks)]
+            mixed = trade(base, "orb")
+        g_gots = []
+        for i in range(chunks - 1):
+            g_gots.append(exchange(tie(packed([pv, u], [i], 0, base), every, *wells), "grid"))
 
         cb = []
         for i in range(chunks):
-            a, c, b = depth_out(weights, joined(v_blocks[i]), wells[i], some, depth_tables)
+            a, c, b = depth_out(weights, joined(v_got), wells[i], some, i, depth_tables)
             cb.append((c, b))
             field = a.reshape(groups, all_planes, some, 128)
             first_row = grid_pos * rows + i * some
@@ -534,47 +644,53 @@
             corner = jnp.stack([zero, first_row // 8, zero])
             values = pick(total, every_starts, corner, every_spots, field, grouped=True)
             second = second + jnp.einsum("aj,apj->ap", values[:, 0], every_projs, precision=PRECISE)
-        second = (c2_8 * second).reshape(-1)
-        more = -(-second.size // 1024) * 8
+        more = -(-orb_groups * second.size // 1024) * 8
+        g_last = packed([pv, u], [chunks - 1], more, base)
+        second = gather_over(c2_8 * second[None], "orb").reshape(-1)
         extra = jnp.pad(second, (0, more * 128 - second.size)).reshape(more, 128)
-
-        last = None
+        g_last = exchange(append(g_last, extra, *([mixed] if put_late else [])), "grid")
+        second = jnp.sum(g_last[:, lines:], axis=0).reshape(-1)[: second.size]
+        second = second.reshape(orb_groups, atoms, projs_each)
+        g_gots.append(g_last if whole_tiles else g_last[:, :lines])
+        if put_late:
+            corner = slab_corner + jnp.stack([zero, zero, orb_pos * (part // 128)])
+            q_all = jnp.stack([put_near(nearby(second[o]), mixed[o], corner) for o in range(orb_groups)])
+        else:
+            base = jnp.moveaxis(base, 0, 2).reshape(planes, rows_y, cols_x)
+            own = lax.dynamic_index_in_dim(second, orb_pos, 0, keepdims=False)
+            q = put_near(nearby(own), base).reshape(planes, rows_y, orb_groups, part)
+            q_all = trade(jnp.moveaxis(q, 2, 0), "orb")
+        q_all = q_all.reshape(orb_groups, planes, grid_count, chunks, some, part)
+
+        sends = []
         for i in range(chunks):
             if part == 128:
-                tail = [extra] if i == 0 else []
-                m = depth_back(weights, joined(g_blocks[i]), *cb[i], some, grid_count, depth_tables, *tail)
-                m = m.reshape(orb_groups * grid_count, -1, 128)
+                later = [q_all] if i > 0 else []
+                ms = depth_back(weights, joined(g_gots[i]), *cb[i], some, grid_count, cuts[i], depth_tables, *later)
+                sends.append([m.reshape(orb_groups * grid_count, -1, 128) for m in ms])
             else:
-                m = depth_back(weights, joined(g_blocks[i]), *cb[i], some, 1, depth_tables)
+                whole = [(0, all_planes)]
+                (m,) = depth_back(weights, joined(g_gots[i]), *cb[i], some, 1, whole, depth_tables)
                 m = jnp.moveaxis(m.reshape(groups, all_planes * some, 128), 0, 1)
                 m = jnp.moveaxis(m.reshape(all_planes * some, orb_groups, part), 1, 0)
-                m = m.reshape(orb_groups * grid_count, planes * some * part // 128, 128)
-                if i == 0:
-                    tail = jnp.broadcast_to(extra, (orb_groups * grid_count, more, 128))
-                    m = jnp.concatenate([m, tail], axis=1)
-            if last is not None:
-                m = after(m, last)
-            last = exchange(m, ("orb", "grid"))
-            length = planes * some * part // 128
-            m = last[:, :length].reshape(orb_groups, grid_count, planes, some, part)
-            if i == 0:
-                sent = last[:, length:].reshape(orb_groups, grid_count, more * 128)
-                second = jnp.sum(sent, axis=1)[:, : atoms * projs_each]
-                if put_late:
-                    corner = slab_corner + jnp.stack([zero, zero, orb_pos * (part // 128)])
-                    q_all = jnp.stack([put_near(nearby(second[o]), base[o], corner) for o in range(orb_groups)])
-                else:
-                    base = jnp.moveaxis(base, 0, 2).reshape(planes, rows_y, cols_x)
-                    own = lax.dynamic_index_in_dim(second, orb_pos, 0, keepdims=False)
-                    q = put_near(nearby(own), base).reshape(planes, rows_y, orb_groups, part)
-                    q_all = trade(jnp.moveaxis(q, 2, 0), "orb")
-                q_all = q_all.reshape(orb_groups, planes, grid_count, chunks, some, part)
-            filtered = q_all[:, :, :, i] + m.transpose(0, 2, 1, 3, 4)
-            sums[i] = sums[i] + jnp.sum(filtered * filtered, axis=0)
-    out = []
-    for own in sums:
-        own = own * (1.0 / (orb_count * orb_groups))
-        out.append(jnp.moveaxis(gather_steps(own[None], "orb"), 0, 3))
+                m = m.reshape(orb_groups * grid_count, planes, some * part)
+                sends.append([m[:, p:q].reshape(orb_groups * grid_count, -1, 128) for p, q in cuts[i]])
+        done, kept = [], []
+        for i in range(chunks):
+            for k, (start, stop) in enumerate(cuts[i]):
+                send = sends[i][k]
+                if len(kept) > 1:
+                    send = tie(send, kept[-2])
+                got = exchange(send, ("orb", "grid"))
+                if done:
+                    got = tie(got, *done[-2:])
+                m = got.reshape(orb_groups, grid_count, stop - start, some, part)
+                filtered = q_all[:, start:stop, :, i] + m.transpose(0, 2, 1, 3, 4)
+                own = jnp.sum(filtered * filtered, axis=0) * (1.0 / (orb_count * orb_groups))
+                kept.append(own)
+                done.append(gather_over(own[None], "orb"))
+                sums[i][k] = sums[i][k] + done[-1]
+    out = [jnp.moveaxis(jnp.concatenate(shares, axis=1), 0, 3) for shares in sums]
     return jnp.stack(out, axis=2).reshape(planes, rows_y, cols_x)
 
 

time: 452 us -> 423 us (0.936)
  waiting for transfers between devices: 209 us -> 151 us
  starting transfers between devices: 48.8 us -> 87.4 us
  other arithmetic: 36.4 us -> 25.5 us
    ppermute x7 -> x11, waiting for transfers between devices: 127 us -> 39.8 us  [gather_part(): lax.ppermute(block, axis, xor_route(lax.axis_size(axis), apart << shift))]
    all_to_all x5 -> x7, starting transfers between devices: 28.9 us -> 61.6 us  [exchange(): return lax.all_to_all(block, axis, split_axis=0, concat_axis=0, tiled=True)]
    ppermute x4, waiting for transfers between devices: 5.81 us -> 26.1 us  [shifted(): lax.ppermute(block, 'grid', [(i, (i + step) % grid_count) for i in range(...]
    slice x7 -> x2, local copies, waits for them, and re-layouts: 14.5 us -> 0.21 us  [the longest x1 0.2 us: atom_windows(): cells[:, 0]]
    all_to_all x5 -> x7, waiting for transfers between devices: 75.4 us -> 85.3 us  [exchange(): return lax.all_to_all(block, axis, split_axis=0, concat_axis=0, tiled=True)]
    pallas_call x5 -> x17, Pallas kernels: 41.3 us -> 49.7 us  [the longest x1 14.3 us: planar_first(): pl.pallas_call(ordered(first_kernel, 4, len(others)), grid=field.shape[:1...]
    ppermute x7 -> x11, starting transfers between devices: 8.54 us -> 16.2 us  [gather_part(): lax.ppermute(block, axis, xor_route(lax.axis_size(axis), apart << shift))]
    dynamic_update_slice x0 -> x11, local copies, waits for them, and re-layouts: none -> 7.38 us  [gather_part(): out = lax.dynamic_update_slice_in_dim(out, got[None], own ^ apart, 0)]
  transfers between devices with their start and end apart: 17 -> 23, of which waited for: 11 -> 11; matrix products, arithmetic and copies ran while one was open for 15% -> 14% of each run, Pallas kernels for 20% -> 23%
where the time goes in v5:
time: 423 us; the launch traced here: 420 us
  waiting for transfers between devices  151 us (36%)
  Pallas kernels  98.6 us (23%)
  starting transfers between devices  87.4 us (21%)
  local copies, waits for them, and re-layouts  47.5 us (11%)
  other arithmetic  25.5 us (6%)
  matrix products  5.89 us (1%)
    all_to_all x7, waiting for transfers between devices, exchange(): return lax.all_to_all(block, axis, split_axis=0, concat_axis=0, tiled=True)  85.3 us
    all_to_all x7, starting transfers between devices, exchange(): return lax.all_to_all(block, axis, split_axis=0, concat_axis=0, tiled=True)  61.6 us
    ppermute x11, waiting for transfers between devices, gather_part(): lax.ppermute(block, axis, xor_route(lax.axis_size(axis), apart << shift))  39.8 us
    ppermute x4, waiting for transfers between devices, shifted(): lax.ppermute(block, 'grid', [(i, (i + step) % grid_count) for i in range(...  26.1 us
    pallas_call x4, Pallas kernels, pick(): pl.pallas_call(functools.partial(pick_kernel, total, grouped), out_shape=...  21.7 us
    ppermute x11, starting transfers between devices, gather_part(): lax.ppermute(block, axis, xor_route(lax.axis_size(axis), apart << shift))  16.2 us
    pallas_call x1, Pallas kernels, planar_second(): pl.pallas_call(second_kernel, grid=field.shape[:1], out_shape=jax.ShapeDt...  14.5 us
    pallas_call x1, Pallas kernels, planar_first(): pl.pallas_call(ordered(first_kernel, 4, len(others)), grid=field.shape[:1...  14.3 us
  transfers between devices with their start and end apart: 23, of which 11 were waited for; matrix products, arithmetic and copies ran while one was open for 14% of the time, Pallas kernels for 23%

profile of v5, /device:TPU:0, one launch (start us, length us, event | category | flops | bytes accessed | tf_op | source)
XLA Modules:
  0.0 419.8 jit_solution(6526438367655403702)
XLA Ops:
  0.7 2.4 pack_part.1
  6.7 2.6 collective-permute-start.4
  9.3 2.6 collective-permute-start.5
  11.9 3.8 collective-permute-start.1
  17.1 4.8 %pack.3.refs_0_ = f32[16,512,128]{2,1,0:T(8,128)} custom-call(f32[16,256,256]{2,1,0:T(8,128)} %bitcast.239, f32[16,16,16,128]{3,2,1,0:T(8,128)S(1)} %bitcast.245), custom_call_target="tpu_custom_call" | custom-call | flops 1048576 | bytes 8388608 | tf_op jit(solution)/shard_map/pack/pallas_call | solution.py:410
  23.2 4.4 %all-to-all-start.1 = ((f32[16,16,16,128]{3,2,1,0:T(8,128)}), f32[16,16,16,128]{3,2,1,0:T(8,128)}, u32[]{:S(2)}, u32[]{:S(2)}) async-start(f32[16,16,16,128]{3,2,1,0:T(8,128)} %tie.9), calls=%async_computation.1 | async-start | bytes 4194304 | tf_op jit(solution)/shard_map/all_to_all | solution.py:60
  29.8 2.2 copy-done.2
  31.9 4.1 pick.4
  36.5 4.8 %collective-permute-start.2 = (f32[3,16,4]{2,1,0:T(8,128)S(1)}, f32[3,16,4]{2,1,0:T(8,128)S(1)}, u32[]{:S(2)}, u32[]{:S(2)}) collective-permute-start(f32[3,16,4]{2,1,0:T(8,128)S(1)} %bitcast.278), channel_id=1, source_target_pairs={{0,15},{1,0},{2,1},{3,2},{4,3},{5,4},{6,5},{7,6},{8,7},{9,8},{10,9... | collective-permute-start | bytes 2312 | tf_op jit(solution)/shard_map/ppermute | solution.py:557
  41.4 21.2 %collective-permute-done.2 = f32[3,16,4]{2,1,0:T(8,128)S(1)} collective-permute-done((f32[3,16,4]{2,1,0:T(8,128)S(1)}, f32[3,16,4]{2,1,0:T(8,128)S(1)}, u32[]{:S(2)}, u32[]{:S(2)}) %collective-permute-start.2) | collective-permute-done | bytes 800 | tf_op jit(solution)/shard_map/ppermute | solution.py:557
  62.6 4.9 %collective-permute-done.3 = f32[3,16,4]{2,1,0:T(8,128)S(1)} collective-permute-done((f32[3,16,4]{2,1,0:T(8,128)S(1)}, f32[3,16,4]{2,1,0:T(8,128)S(1)}, u32[]{:S(2)}, u32[]{:S(2)}) %collective-permute-start.3) | collective-permute-done | bytes 800 | tf_op jit(solution)/shard_map/ppermute | solution.py:557
  69.0 11.2 %all-to-all-start = ((f32[16,512,128]{2,1,0:T(8,128)}), f32[16,512,128]{2,1,0:T(8,128)}, u32[]{:S(2)}, u32[]{:S(2)}) async-start(f32[16,512,128]{2,1,0:T(8,128)} %tie.8), calls=%async_computation | async-start | bytes 8388608 | tf_op jit(solution)/shard_map/all_to_all | solution.py:60
  86.9 14.3 %planar_first.1 = (f32[16,256,256]{2,1,0:T(8,128)}, f32[16,256,256]{2,1,0:T(8,128)}) custom-call(f32[16,256,256]{2,1,0:T(8,128)} %bitcast.240, f32[16,256,256]{2,1,0:T(8,128)} %potential.1, bf16[2,256,256]{2,1,0:T(8,128)(2,1)S(1)} %get-tuple-element.126.refs_2_.high_tables, bf16[2,256,256]{2,1,0:T(8,128)(2,1)S(1)} %get-tuple-element.127.refs_3_.low_tables, ...), custom_call_target="tpu_custom_call" | custom-call | flops 3221225472 | bytes 16777216 | tf_op jit(solution)/shard_map/planar_first/pallas_call | solution.py:320
  101.6 1.7 collective-permute-start.8
  103.3 1.6 collective-permute-start.10
  105.3 5.2 %put.3.field = f32[16,32,8,256]{3,2,1,0:T(8,128)S(1)} custom-call(s32[48,3]{1,0:T(8,128)S(1)} %pad_add_fusion.3.starts, s32[3]{0:T(128)S(1)} %stack.70.corner, s32[48,2,128]{2,1,0:T(2,128)S(1)} %pad_add_fusion.2.spots, f32[48,1,128]{2,1,0:T(1,128)S(1)} %fusion.74.spread, f32[16,32,8,256]{3,2,1,0:T(8,128)} %bitcast.256), custom_call_target="tpu_custom_call" | custom-call | flops 16777216 | bytes 16777216 | tf_op jit(solution)/shard_map/put/pallas_call | solution.py:292
  110.5 4.1 pick.5
  115.5 14.5 %planar_second.1.refs_2_ = f32[2,16,256,128]{3,2,1,0:T(8,128)} custom-call(f32[3]{0:T(128)S(1)} %pad_maximum_fusion.6.weights, f32[16,256,256]{2,1,0:T(8,128)} %bitcast.228, f32[16,256,256]{2,1,0:T(8,128)} %bitcast.241, f32[16,256,256]{2,1,0:T(8,128)} %potential.1, bf16[2,256,256]{2,1,0:T(8,128)(2,1)S(1)} %get-tuple-element.126.refs_2_.high_tables, ...), custom_call_target="tpu_custom_call" | custom-call | flops 3221225472 | bytes 16777216 | tf_op jit(solution)/shard_map/planar_second/pallas_call | solution.py:336
  129.9 3.2 constant_dynamic-slice_fusion.6
  133.6 4.0 pack.5.refs_0_
  137.6 4.9 %pack.4.block = f32[16,272,128]{2,1,0:T(8,128)S(1)} custom-call(f32[16,256,256]{2,1,0:T(8,128)} %get-tuple-element.66.refs_0_, f32[16,256,256]{2,1,0:T(8,128)} %bitcast.230, f32[2,16,256,128]{3,2,1,0:T(8,128)} %planar_second.1.refs_2_), custom_call_target="tpu_custom_call" | custom-call | flops 524288 | bytes 4194304 | tf_op jit(solution)/shard_map/pack/pallas_call | solution.py:410
  145.9 6.2 %collective-permute-done.10 = f32[1,16,16,16,128]{4,3,2,1,0:T(8,128)} collective-permute-done((f32[1,16,16,16,128]{4,3,2,1,0:T(8,128)}, f32[1,16,16,16,128]{4,3,2,1,0:T(8,128)}, u32[]{:S(2)}, u32[]{:S(2)}) %collective-permute-start.10) | collective-permute-done | bytes 2097184 | tf_op jit(solution)/shard_map/ppermute | solution.py:38
  152.1 2.2 broadcast_in_dim.141
  154.3 1.8 bitcast_dynamic-update-slice_fusion
  156.1 2.6 slice_bitcast_fusion.3
  158.8 18.9 %all-to-all-start.3 = ((f32[16,256,128]{2,1,0:T(8,128)}), f32[16,256,128]{2,1,0:T(8,128)}, u32[]{:S(2)}, u32[]{:S(2)}) async-start(f32[16,256,128]{2,1,0:T(8,128)} %tie.10), calls=%async_computation.3 | async-start | bytes 4194304 | tf_op jit(solution)/shard_map/all_to_all | solution.py:60
  181.1 3.2 fusion.63
  184.5 4.9 %depth_out.2 = (f32[2,2048,128]{2,1,0:T(8,128)S(1)}, f32[2,2048,128]{2,1,0:T(8,128)S(1)}, f32[2,2048,128]{2,1,0:T(8,128)}) custom-call(f32[2]{0:T(128)S(1)} %pad_maximum_fusion.5.weights.refs_0_, f32[16,512,128]{2,1,0:T(8,128)} %all-to-all-done.field, f32[2,16,128,128]{3,2,1,0:T(8,128)} %get-tuple-element.82.potential.refs_2_, ...), custom_call_target="tpu_custom_call" | custom-call | flops 805306368 | bytes 10485760 | tf_op jit(solution)/shard_map/depth_out/pallas_call | solution.py:462
  189.4 1.4 copy-done.11
  190.8 6.8 %pick.6 = f32[256,1,128]{2,1,0:T(1,128)S(1)} custom-call(s32[256,3]{1,0:T(8,128)S(1)} %pad_add_fusion.1.starts, s32[3]{0:T(128)S(1)} %get-tuple-element.120.corner, s32[256,2,128]{2,1,0:T(2,128)S(1)} %pad_add_fusion.spots, f32[2,256,8,128]{3,2,1,0:T(8,128)S(1)} %bitcast.250), custom_call_target="tpu_custom_call" | custom-call | flops 16777216 | bytes 16777216 | tf_op jit(solution)/shard_map/pick/pallas_call | solution.py:278
  197.6 4.9 %depth_out.3 = (f32[2,2048,128]{2,1,0:T(8,128)S(1)}, f32[2,2048,128]{2,1,0:T(8,128)S(1)}, f32[2,2048,128]{2,1,0:T(8,128)}) custom-call(f32[2]{0:T(128)S(1)} %pad_maximum_fusion.5.weights.refs_0_, f32[16,512,128]{2,1,0:T(8,128)} %all-to-all-done.field, f32[2,16,128,128]{3,2,1,0:T(8,128)} %get-tuple-element.83.potential.refs_3_, ...), custom_call_target="tpu_custom_call" | custom-call | flops 805306368 | bytes 10485760 | tf_op jit(solution)/shard_map/depth_out/pallas_call | solution.py:462
  203.8 6.8 %pick.7 = f32[256,1,128]{2,1,0:T(1,128)S(1)} custom-call(s32[256,3]{1,0:T(8,128)S(1)} %pad_add_fusion.1.starts, s32[3]{0:T(128)S(1)} %get-tuple-element.119.corner, s32[256,2,128]{2,1,0:T(2,128)S(1)} %pad_add_fusion.spots, f32[2,256,8,128]{3,2,1,0:T(8,128)S(1)} %bitcast.249), custom_call_target="tpu_custom_call" | custom-call | flops 16777216 | bytes 16777216 | tf_op jit(solution)/shard_map/pick/pallas_call | solution.py:278
  210.6 1.8 fusion.17
  212.4 1.8 fusion.15
  214.3 1.6 collective-permute-start.11
  215.8 3.2 constant_dynamic-update-slice_fusion.6.refs_0_
  220.2 1.5 append.1
  221.7 8.3 %all-to-all-start.2 = ((f32[16,272,128]{2,1,0:T(8,128)}), f32[16,272,128]{2,1,0:T(8,128)}, u32[]{:S(2)}, u32[]{:S(2)}) async-start(f32[16,272,128]{2,1,0:T(8,128)} %append.1), calls=%async_computation.2 | async-start | bytes 4456448 | tf_op jit(solution)/shard_map/all_to_all | solution.py:60
  230.1 3.8 depth_back.2
  235.1 38.4 %all-to-all-done.2.refs_1_ = f32[16,272,128]{2,1,0:T(8,128)} async-done(((f32[16,272,128]{2,1,0:T(8,128)}), f32[16,272,128]{2,1,0:T(8,128)}, u32[]{:S(2)}, u32[]{:S(2)}) %all-to-all-start.2) | async-done | bytes 2228256 | tf_op jit(solution)/shard_map/all_to_all | solution.py:60
  273.5 12.0 %all-to-all-start.4 = ((f32[32,128,128]{2,1,0:T(8,128)}), f32[32,128,128]{2,1,0:T(8,128)}, u32[]{:S(2)}, u32[]{:S(2)}) async-start(f32[32,128,128]{2,1,0:T(8,128)} %bitcast.247), calls=%async_computation.4 | async-start | bytes 4194304 | tf_op jit(solution)/shard_map/all_to_all | solution.py:60
  285.6 4.7 %slice_bitcast_fusion = (f32[16,32,8,128]{3,2,1,0:T(8,128)}, f32[16,32,8,128]{3,2,1,0:T(8,128)}) fusion(f32[2,16,256,128]{3,2,1,0:T(8,128)} %constant_dynamic-update-slice_fusion.6.refs_0_), kind=kLoop, calls=%fused_computation.13 | loop fusion | bytes 8388608 | tf_op jit(solution)/shard_map/reshape;squeeze | solution.py:259
  292.8 1.6 copy-done.9
  294.4 3.8 put.5
  298.6 3.8 put.4
  302.4 2.5 pad_maximum_fusion.refs_6_
  305.5 4.2 %depth_back.3 = (f32[2,16,64,128]{3,2,1,0:T(8,128)}, f32[2,16,64,128]{3,2,1,0:T(8,128)S(1)}) custom-call(f32[2]{0:T(128)S(1)} %pad_maximum_fusion.5.weights.refs_0_, f32[16,272,128]{2,1,0:T(8,128)} %all-to-all-done.2.refs_1_, f32[2,2048,128]{2,1,0:T(8,128)S(1)} %copy-done.13, f32[2,2048,128]{2,1,0:T(8,128)} %get-tuple-element.70.refs_3_, ...), custom_call_target="tpu_custom_call" | custom-call | flops 805306368 | bytes 8388608 | tf_op jit(solution)/shard_map/depth_back/pallas_call | solution.py:478
  310.7 24.3 %all-to-all-done.4 = f32[32,128,128]{2,1,0:T(8,128)} async-done(((f32[32,128,128]{2,1,0:T(8,128)}), f32[32,128,128]{2,1,0:T(8,128)}, u32[]{:S(2)}, u32[]{:S(2)}) %all-to-all-start.4) | async-done | bytes 2097184 | tf_op jit(solution)/shard_map/all_to_all | solution.py:60
  335.0 3.4 all-to-all-start.5
  338.4 2.3 fusion.4
  340.7 1.6 fusion.106
  342.3 1.6 collective-permute-start.13
  343.9 21.8 %all-to-all-done.5.refs_0_ = f32[32,64,128]{2,1,0:T(8,128)} async-done(((f32[32,64,128]{2,1,0:T(8,128)}), f32[32,64,128]{2,1,0:T(8,128)}, u32[]{:S(2)}, u32[]{:S(2)}) %all-to-all-start.5) | async-done | bytes 1048608 | tf_op jit(solution)/shard_map/all_to_all | solution.py:60
  365.7 3.4 all-to-all-start.6
  369.1 10.2 %collective-permute-done.13 = f32[1,16,16,8,128]{4,3,2,1,0:T(8,128)} collective-permute-done((f32[1,16,16,8,128]{4,3,2,1,0:T(8,128)}, f32[1,16,16,8,128]{4,3,2,1,0:T(8,128)}, u32[]{:S(2)}, u32[]{:S(2)}) %collective-permute-start.13) | collective-permute-done | bytes 1048608 | tf_op jit(solution)/shard_map/ppermute | solution.py:38
  379.3 1.6 reshape.422
  380.9 2.3 constant_dynamic-update-slice_fusion.5.refs_1_
  383.2 1.6 fusion.9
  384.9 3.0 collective-permute-start.14
  387.9 12.6 %collective-permute-done.14 = f32[1,8,16,8,128]{4,3,2,1,0:T(8,128)S(1)} collective-permute-done((f32[1,8,16,8,128]{4,3,2,1,0:T(8,128)S(1)}, f32[1,8,16,8,128]{4,3,2,1,0:T(8,128)S(1)}, u32[]{:S(2)}, u32[]{:S(2)}) %collective-permute-start.14) | collective-permute-done | bytes 524320 | tf_op jit(solution)/shard_map/ppermute | solution.py:38
  401.6 1.6 fusion.14
  404.6 10.4 %collective-permute-done.15 = f32[1,8,16,8,128]{4,3,2,1,0:T(8,128)S(1)} collective-permute-done((f32[1,8,16,8,128]{4,3,2,1,0:T(8,128)S(1)}, f32[1,8,16,8,128]{4,3,2,1,0:T(8,128)S(1)}, u32[]{:S(2)}, u32[]{:S(2)}) %collective-permute-start.15) | collective-permute-done | bytes 524320 | tf_op jit(solution)/shard_map/ppermute | solution.py:38
  415.3 2.0 pad_maximum_fusion.1
  417.3 2.6 copy.205
  (193 shorter events, 35.2 us)
Async XLA Ops:
  0.7 3.8 copy-start.23
  3.2 1.3 copy-start.3
  5.1 10.6 %copy-start.4 = (f32[16,256,128]{2,1,0:T(8,128)S(1)}, f32[16,256,128]{2,1,0:T(8,128)}, u32[]{:S(2)}) copy-start(f32[16,256,128]{2,1,0:T(8,128)} %copy-done.3) | copy-start | bytes 6291460
  6.2 15.7 %collective-permute-start = (f32[16,6,128]{2,0,1:T(8,128)S(1)}, f32[16,6,128]{2,0,1:T(8,128)S(1)}, u32[]{:S(2)}, u32[]{:S(2)}) collective-permute-start(f32[16,6,128]{2,0,1:T(8,128)S(1)} %copy.156), channel_id=1, source_target_pairs={{0,1},{1,2},{2,3},{3,4},{4,5},{5,6},{6,7},{7,8},{8,9},{9,10},{10,1... | collective-permute-start | bytes 147464 | tf_op jit(solution)/shard_map/ppermute | solution.py:557
  6.7 34.6 %collective-permute-start.4 = (f32[16,6,128]{2,1,0:T(8,128)}, f32[16,6,128]{2,1,0:T(8,128)S(1)}, u32[]{:S(2)}, u32[]{:S(2)}) collective-permute-start(f32[16,6,128]{2,1,0:T(8,128)} %tie.7), channel_id=1, source_target_pairs={{0,4},{1,5},{2,6},{3,7},{4,0},{5,1},{6,2},{7,3},{8,12},{9,13},{10,... | collective-permute-start | bytes 147464 | tf_op jit(solution)/shard_map/ppermute | solution.py:38
  9.3 32.0 %collective-permute-start.5 = (f32[16,6,128]{2,1,0:T(8,128)}, f32[16,6,128]{2,1,0:T(8,128)S(1)}, u32[]{:S(2)}, u32[]{:S(2)}) collective-permute-start(f32[16,6,128]{2,1,0:T(8,128)} %tie.7), channel_id=1, source_target_pairs={{0,8},{1,9},{2,10},{3,11},{4,12},{5,13},{6,14},{7,15},{8,0},{9,1},... | collective-permute-start | bytes 147464 | tf_op jit(solution)/shard_map/ppermute | solution.py:38
  11.9 29.4 %collective-permute-start.6 = (f32[16,6,128]{2,1,0:T(8,128)}, f32[16,6,128]{2,1,0:T(8,128)S(1)}, u32[]{:S(2)}, u32[]{:S(2)}) collective-permute-start(f32[16,6,128]{2,1,0:T(8,128)} %tie.7), channel_id=1, source_target_pairs={{0,12},{1,13},{2,14},{3,15},{4,8},{5,9},{6,10},{7,11},{8,4},{9,5},... | collective-permute-start | bytes 147464 | tf_op jit(solution)/shard_map/ppermute | solution.py:38
  11.9 10.0 %collective-permute-start.1 = (f32[16,6,128]{2,0,1:T(8,128)S(1)}, f32[16,6,128]{2,0,1:T(8,128)S(1)}, u32[]{:S(2)}, u32[]{:S(2)}) collective-permute-start(f32[16,6,128]{2,0,1:T(8,128)S(1)} %copy.156), channel_id=1, source_target_pairs={{0,15},{1,0},{2,1},{3,2},{4,3},{5,4},{6,5},{7,6},{8,7},{9,8},{10,9... | collective-permute-start | bytes 147464 | tf_op jit(solution)/shard_map/ppermute | solution.py:557
  17.1 4.8 %copy-start.21 = (f32[16,6,128]{2,1,0:T(8,128)S(1)}, f32[16,6,128]{2,1,0:T(8,128)}, u32[]{:S(2)}) copy-start(f32[16,6,128]{2,1,0:T(8,128)} %tie.7) | copy-start | bytes 147460
  23.2 45.8 %all-to-all-start.1 = ((f32[16,16,16,128]{3,2,1,0:T(8,128)}), f32[16,16,16,128]{3,2,1,0:T(8,128)}, u32[]{:S(2)}, u32[]{:S(2)}) async-start(f32[16,16,16,128]{3,2,1,0:T(8,128)} %tie.9), calls=%async_computation.1 | async-start | bytes 4194304 | tf_op jit(solution)/shard_map/all_to_all | solution.py:60
  29.8 2.2 copy-start.2
  36.5 26.1 %collective-permute-start.2 = (f32[3,16,4]{2,1,0:T(8,128)S(1)}, f32[3,16,4]{2,1,0:T(8,128)S(1)}, u32[]{:S(2)}, u32[]{:S(2)}) collective-permute-start(f32[3,16,4]{2,1,0:T(8,128)S(1)} %bitcast.278), channel_id=1, source_target_pairs={{0,15},{1,0},{2,1},{3,2},{4,3},{5,4},{6,5},{7,6},{8,7},{9,8},{10,9... | collective-permute-start | bytes 2312 | tf_op jit(solution)/shard_map/ppermute | solution.py:557
  41.2 26.2 %collective-permute-start.3 = (f32[3,16,4]{2,1,0:T(8,128)S(1)}, f32[3,16,4]{2,1,0:T(8,128)S(1)}, u32[]{:S(2)}, u32[]{:S(2)}) collective-permute-start(f32[3,16,4]{2,1,0:T(8,128)S(1)} %bitcast.279), channel_id=1, source_target_pairs={{0,1},{1,2},{2,3},{3,4},{4,5},{5,6},{6,7},{7,8},{8,9},{9,10},{10,1... | collective-permute-start | bytes 2312 | tf_op jit(solution)/shard_map/ppermute | solution.py:557
  41.3 26.7 %copy-start.19 = (f32[4,16,6,128]{3,2,1,0:T(8,128)}, f32[4,16,6,128]{3,2,1,0:T(8,128)S(1)}, u32[]{:S(2)}) copy-start(f32[4,16,6,128]{3,2,1,0:T(8,128)S(1)} %bitcast_dynamic-update-slice_fusion.5.refs_2_) | copy-start | bytes 589828
  68.1 12.2 %copy-start.24 = (f32[3]{0:T(128)S(1)}, f32[3]{0:T(128)}, u32[]{:S(2)}) copy-start(f32[3]{0:T(128)} %param.19) | copy-start | bytes 40
  69.0 89.8 %all-to-all-start = ((f32[16,512,128]{2,1,0:T(8,128)}), f32[16,512,128]{2,1,0:T(8,128)}, u32[]{:S(2)}, u32[]{:S(2)}) async-start(f32[16,512,128]{2,1,0:T(8,128)} %tie.8), calls=%async_computation | async-start | bytes 8388608 | tf_op jit(solution)/shard_map/all_to_all | solution.py:60
  86.9 14.4 %copy-start.20 = (f32[4,16,6,128]{3,2,1,0:T(8,128)S(1)}, f32[4,16,6,128]{3,2,1,0:T(8,128)}, u32[]{:S(2)}) copy-start(f32[4,16,6,128]{3,2,1,0:T(8,128)} %copy-done.19) | copy-start | bytes 589828
  86.9 16.3 %copy-start.22 = (f32[3,16,4]{2,1,0:T(8,128)S(1)}, f32[3,16,4]{2,1,0:T(8,128)}, u32[]{:S(2)}) copy-start(f32[3,16,4]{2,1,0:T(8,128)} %add_add_fusion) | copy-start | bytes 2308
  86.9 16.3 %copy-start.25 = (f32[4]{0:T(128)S(1)}, f32[4]{0:T(128)}, u32[]{:S(2)}) copy-start(f32[4]{0:T(128)} %param.18) | copy-start | bytes 52
  101.3 41.3 %collective-permute-start.7 = (f32[4,16,6,128]{3,2,1,0:T(8,128)S(1)}, f32[4,16,6,128]{3,2,1,0:T(8,128)}, u32[]{:S(2)}, u32[]{:S(2)}) collective-permute-start(f32[4,16,6,128]{3,2,1,0:T(8,128)S(1)} %copy-done.20), channel_id=1, source_target_pairs={{0,1},{1,0},{2,3},{3,2},{4,5},{5,4},{6,7},{7,6},{8,9},{9,8},{10,11... | collective-permute-start | bytes 589832 | tf_op jit(solution)/shard_map/ppermute | solution.py:38
  101.6 42.3 %collective-permute-start.8 = (f32[4,16,6,128]{3,2,1,0:T(8,128)S(1)}, f32[4,16,6,128]{3,2,1,0:T(8,128)}, u32[]{:S(2)}, u32[]{:S(2)}) collective-permute-start(f32[4,16,6,128]{3,2,1,0:T(8,128)S(1)} %copy-done.20), channel_id=1, source_target_pairs={{0,2},{1,3},{2,0},{3,1},{4,6},{5,7},{6,4},{7,5},{8,10},{9,11},{10,... | collective-permute-start | bytes 589832 | tf_op jit(solution)/shard_map/ppermute | solution.py:38
  103.3 41.6 %collective-permute-start.9 = (f32[4,16,6,128]{3,2,1,0:T(8,128)S(1)}, f32[4,16,6,128]{3,2,1,0:T(8,128)}, u32[]{:S(2)}, u32[]{:S(2)}) collective-permute-start(f32[4,16,6,128]{3,2,1,0:T(8,128)S(1)} %copy-done.20), channel_id=1, source_target_pairs={{0,3},{1,2},{2,1},{3,0},{4,7},{5,6},{6,5},{7,4},{8,11},{9,10},{10,... | collective-permute-start | bytes 589832 | tf_op jit(solution)/shard_map/ppermute | solution.py:38
  103.3 48.8 %collective-permute-start.10 = (f32[1,16,16,16,128]{4,3,2,1,0:T(8,128)}, f32[1,16,16,16,128]{4,3,2,1,0:T(8,128)}, u32[]{:S(2)}, u32[]{:S(2)}) collective-permute-start(f32[1,16,16,16,128]{4,3,2,1,0:T(8,128)} %bitcast.64), channel_id=1, source_target_pairs={{0,16},{16,0},{1,17},{17,1},{2,18},{18,2},{3,19},{19,3},{4,20},{20... | collective-permute-start | bytes 6291464 | tf_op jit(solution)/shard_map/ppermute | solution.py:38
  110.5 4.1 copy-start
  133.1 82.8 %collective-permute-start.12 = (f32[1,16,256,128]{3,2,1,0:T(8,128)}, f32[1,16,256,128]{3,2,1,0:T(8,128)}, u32[]{:S(2)}, u32[]{:S(2)}) collective-permute-start(f32[1,16,256,128]{3,2,1,0:T(8,128)} %constant_dynamic-slice_fusion.6), channel_id=1, source_target_pairs={{0,16},{16,0},{1,17},{17,1},{2,18},{18,2},{3,19},{19,3},{4,20},{20... | collective-permute-start | bytes 6291464 | tf_op jit(solution)/shard_map/ppermute | solution.py:54
  137.6 4.9 %copy-start.6 = (f32[16,256,128]{2,1,0:T(8,128)}, f32[16,256,128]{2,1,0:T(8,128)S(1)}, u32[]{:S(2)}) copy-start(f32[16,256,128]{2,1,0:T(8,128)S(1)} %pack.5.refs_0_) | copy-start | bytes 6291460
  142.5 11.8 %copy-start.5 = (f32[16,272,128]{2,1,0:T(8,128)}, f32[16,272,128]{2,1,0:T(8,128)S(1)}, u32[]{:S(2)}) copy-start(f32[16,272,128]{2,1,0:T(8,128)S(1)} %pack.4.block) | copy-start | bytes 6684676
  145.9 8.4 %copy-start.14 = (f32[4,4,16,6,128]{4,3,2,0,1:T(8,128)}, f32[4,4,16,6,128]{4,3,2,0,1:T(8,128)S(1)}, u32[]{:S(2)}) copy-start(f32[4,4,16,6,128]{4,3,2,0,1:T(8,128)S(1)} %bitcast_dynamic-update-slice_fusion.1) | copy-start | bytes 2359300
  158.8 63.0 %all-to-all-start.3 = ((f32[16,256,128]{2,1,0:T(8,128)}), f32[16,256,128]{2,1,0:T(8,128)}, u32[]{:S(2)}, u32[]{:S(2)}) async-start(f32[16,256,128]{2,1,0:T(8,128)} %tie.10), calls=%async_computation.3 | async-start | bytes 4194304 | tf_op jit(solution)/shard_map/all_to_all | solution.py:60
  189.4 1.4 copy-start.11
  202.5 1.3 copy-start.12
  203.8 6.8 %copy-start.15 = (f32[4,4,16,6,128]{4,3,2,0,1:T(8,128)S(1)}, f32[4,4,16,6,128]{4,3,2,0,1:T(8,128)}, u32[]{:S(2)}) copy-start(f32[4,4,16,6,128]{4,3,2,0,1:T(8,128)} %copy-done.14) | copy-start | bytes 2359300
  214.3 5.1 %collective-permute-start.11 = (f32[1,256,4]{2,1,0:T(8,128)S(1)}, f32[1,256,4]{2,1,0:T(8,128)S(1)}, u32[]{:S(2)}, u32[]{:S(2)}) collective-permute-start(f32[1,256,4]{2,1,0:T(8,128)S(1)} %bitcast.260), channel_id=1, source_target_pairs={{0,16},{16,0},{1,17},{17,1},{2,18},{18,2},{3,19},{19,3},{4,20},{20... | collective-permute-start | bytes 12296 | tf_op jit(solution)/shard_map/ppermute | solution.py:38
  221.7 51.8 %all-to-all-start.2 = ((f32[16,272,128]{2,1,0:T(8,128)}), f32[16,272,128]{2,1,0:T(8,128)}, u32[]{:S(2)}, u32[]{:S(2)}) async-start(f32[16,272,128]{2,1,0:T(8,128)} %append.1), calls=%async_computation.2 | async-start | bytes 4456448 | tf_op jit(solution)/shard_map/all_to_all | solution.py:60
  233.8 1.3 copy-start.7
  273.5 61.5 %all-to-all-start.4 = ((f32[32,128,128]{2,1,0:T(8,128)}), f32[32,128,128]{2,1,0:T(8,128)}, u32[]{:S(2)}, u32[]{:S(2)}) async-start(f32[32,128,128]{2,1,0:T(8,128)} %bitcast.247), calls=%async_computation.4 | async-start | bytes 4194304 | tf_op jit(solution)/shard_map/all_to_all | solution.py:60
  292.8 1.6 copy-start.9
  294.4 4.2 %copy-start.8 = (f32[16,32,8,128]{3,2,1,0:T(8,128)S(1)}, f32[16,32,8,128]{3,2,1,0:T(8,128)}, u32[]{:S(2)}) copy-start(f32[16,32,8,128]{3,2,1,0:T(8,128)} %get-tuple-element.81.base) | copy-start | bytes 6291460
  302.4 2.8 copy-start.1
  302.4 3.1 copy-start.13
  309.8 1.0 copy-start.10
  335.0 30.7 %all-to-all-start.5 = ((f32[32,64,128]{2,1,0:T(8,128)}), f32[32,64,128]{2,1,0:T(8,128)}, u32[]{:S(2)}, u32[]{:S(2)}) async-start(f32[32,64,128]{2,1,0:T(8,128)} %bitcast.111), calls=%async_computation.5 | async-start | bytes 2097152 | tf_op jit(solution)/shard_map/all_to_all | solution.py:60
  342.3 37.0 %collective-permute-start.13 = (f32[1,16,16,8,128]{4,3,2,1,0:T(8,128)}, f32[1,16,16,8,128]{4,3,2,1,0:T(8,128)}, u32[]{:S(2)}, u32[]{:S(2)}) collective-permute-start(f32[1,16,16,8,128]{4,3,2,1,0:T(8,128)} %get-tuple-element.84), channel_id=1, source_target_pairs={{0,16},{16,0},{1,17},{17,1},{2,18},{18,2},{3,19},{19,3},{4,20},{20... | collective-permute-start | bytes 3145736 | tf_op jit(solution)/shard_map/ppermute | solution.py:38
  343.9 35.4 %copy-start.16 = (f32[16,16,8,128]{3,2,1,0:T(8,128)S(1)}, f32[16,16,8,128]{3,2,1,0:T(8,128)}, u32[]{:S(2)}) copy-start(f32[16,16,8,128]{3,2,1,0:T(8,128)} %get-tuple-element.85.refs_1_) | copy-start | bytes 3145732
  365.7 35.0 %all-to-all-start.6 = ((f32[32,64,128]{2,1,0:T(8,128)}), f32[32,64,128]{2,1,0:T(8,128)}, u32[]{:S(2)}, u32[]{:S(2)}) async-start(f32[32,64,128]{2,1,0:T(8,128)} %tie.12), calls=%async_computation.6 | async-start | bytes 2097152 | tf_op jit(solution)/shard_map/all_to_all | solution.py:60
  384.9 15.6 %collective-permute-start.14 = (f32[1,8,16,8,128]{4,3,2,1,0:T(8,128)S(1)}, f32[1,8,16,8,128]{4,3,2,1,0:T(8,128)S(1)}, u32[]{:S(2)}, u32[]{:S(2)}) collective-permute-start(f32[1,8,16,8,128]{4,3,2,1,0:T(8,128)S(1)} %get-tuple-element.88), channel_id=1, source_target_pairs={{0,16},{16,0},{1,17},{17,1},{2,18},{18,2},{3,19},{19,3},{4,20},{20... | collective-permute-start | bytes 1572872 | tf_op jit(solution)/shard_map/ppermute | solution.py:38
  400.7 1.0 copy-start.17
  403.2 11.9 %copy-start.18 = (f32[2,8,16,8,128]{4,3,2,1,0:T(8,128)S(1)}, f32[2,8,16,8,128]{4,3,2,1,0:T(8,128)}, u32[]{:S(2)}) copy-start(f32[2,8,16,8,128]{4,3,2,1,0:T(8,128)} %copy-done.17) | copy-start | bytes 3145732
  403.3 11.6 %collective-permute-start.15 = (f32[1,8,16,8,128]{4,3,2,1,0:T(8,128)S(1)}, f32[1,8,16,8,128]{4,3,2,1,0:T(8,128)S(1)}, u32[]{:S(2)}, u32[]{:S(2)}) collective-permute-start(f32[1,8,16,8,128]{4,3,2,1,0:T(8,128)S(1)} %get-tuple-element.86), channel_id=1, source_target_pairs={{0,16},{16,0},{1,17},{17,1},{2,18},{18,2},{3,19},{19,3},{4,20},{20... | collective-permute-start | bytes 1572872 | tf_op jit(solution)/shard_map/ppermute | solution.py:38

commit v6 on v5

--- a/solution.py
+++ b/solution.py
@@ -45,13 +45,15 @@
     return gather_part(block, axis, 0, size).reshape((size * block.shape[0],) + block.shape[1:])
 
 
-def trade(blocks, axis):
+def trade(blocks, axis, *others):
     size = lax.axis_size(axis)
     place = lax.axis_index(axis)
     out = blocks
     for apart in range(1, size):
         sent = lax.dynamic_index_in_dim(blocks, place ^ apart, 0)
         got = lax.ppermute(sent, axis, xor_route(size, apart))
+        if others:
+            got = tie(got, *others)
         out = lax.dynamic_update_slice_in_dim(out, got, place ^ apart, 0)
     return out
 
@@ -65,7 +67,7 @@
     return jnp.where(number >= size, number - size, number)
 
 
-def listed(starts, corner, total, planes, tiles, listing):
+def listed(starts, corner, total, planes, tiles, listing, one_group=False):
     all_planes, all_tiles, _ = total
 
     def one(atom, count):
@@ -73,6 +75,10 @@
         tile = wrapped(lax.shift_right_logical(starts[atom, 1], 3) - corner[1], all_tiles)
         near = (ahead < planes) | (ahead > all_planes - WIDE)
         here = near & ((tile < tiles) | (tile == all_tiles - 1))
+        if one_group:
+            group = lax.shift_right_logical(starts[atom, 2], 7)
+            crosses = ((starts[atom, 2] & 127) > 128 - WIDE) & (wrapped(group + 1, total[2]) == corner[2])
+            here = here & ((group == corner[2]) | crosses)
         listing[count] = atom
         return count + here.astype(jnp.int32)
 
@@ -103,12 +109,12 @@
     return z, tile, slice(None), pl.ds(pl.multiple_of(group * 128, 128), 128)
 
 
-def pick_kernel(total, grouped, starts, corner, spots, field, values, listing):
+def pick_kernel(total, starts, corner, spots, field, values, listing):
     values[...] = jnp.zeros_like(values)
-    planes, tiles = (field.shape[1], 1) if grouped else field.shape[:2]
+    planes, tiles = field.shape[:2]
 
     def at(z, tile, group):
-        return field[group, z] if grouped else field[corner_of(z, tile, group)]
+        return field[corner_of(z, tile, group)]
 
     lane = lax.broadcasted_iota(jnp.int32, (8, 128), 1)
     row = lax.broadcasted_iota(jnp.int32, (8, 128), 0)
@@ -138,6 +144,40 @@
             found = found[0:8] + found[8:16] + found[16:24]
             found = jnp.where(row == spot[0:1], found, 0.0)
             values[pl.ds(atom, 1)] = jnp.sum(found, axis=0, keepdims=True)[None]
+        return carry
+
+    lax.fori_loop(0, (count + TOGETHER - 1) // TOGETHER, some, 0)
+
+
+def pick_block_kernel(total, starts, corner, spots, field, values, listing):
+    values[...] = jnp.zeros_like(values)
+    orbitals, planes = field.shape[:2]
+    lane = lax.broadcasted_iota(jnp.int32, (8, 128), 1)
+    row = lax.broadcasted_iota(jnp.int32, (8, 128), 0)
+    slot = lax.broadcasted_iota(jnp.int32, (128, 128), 0)
+    count = listed(starts, corner, total, planes, 1, listing, one_group=True)
+
+    def some(group, carry):
+        for k in range(TOGETHER):
+            atom = listing[jnp.minimum(group * TOGETHER + k, count - 1)]
+            depth, z_in, tile_pair, groups, down, right = placed(
+                starts, corner, total, atom, planes, 1, lane
+            )
+            inside = jnp.where(row >= down, tile_pair[0], tile_pair[1]) == 0
+            inside = inside & (jnp.where(lane >= right, groups[0], groups[1]) == corner[2])
+            spot = spots[atom]
+            chosen = (slot == spot[1:2]).astype(jnp.float32).astype(jnp.bfloat16)
+            for o in range(orbitals):
+                window = jnp.zeros((8, 128), jnp.float32)
+                for dz, z in enumerate(depth):
+                    met = jnp.where(inside, field[o, z], 0.0)
+                    met = pltpu.roll(met, (STRIDE * dz - right) & 127, 1)
+                    window = jnp.where(lane // STRIDE == dz, met, window)
+                window = jnp.where(z_in, pltpu.roll(window, (8 - down) & 7, 0), 0.0)
+                found = jnp.dot(split3(window), chosen, preferred_element_type=jnp.float32)
+                found = found[0:8] + found[8:16] + found[16:24]
+                found = jnp.where(row == spot[0:1], found, 0.0)
+                values[o, pl.ds(atom, 1)] = jnp.sum(found, axis=0, keepdims=True)[None]
         return carry
 
     lax.fori_loop(0, (count + TOGETHER - 1) // TOGETHER, some, 0)
@@ -224,35 +264,31 @@
     return jnp.concatenate([ref[d, line, :] for d in range(devices)], axis=0)
 
 
-def side_by_side(rows):
-    return [(r, r + 1) for r in range(0, rows - 1, 2)] + [(rows - 1,)] * (rows % 2)
-
-
-def out_kernel(rows, weights, field, potential, high_table, low_table, a_out, c_out, b_out):
+def out_kernel(some, rows, chunk, weights, field, potential, high_table, low_table, a_out, c_out, b_out):
     everywhere = high_table.shape[0]
-    for pair in side_by_side(rows):
-        v = jnp.concatenate([lines_of(field, r, rows) for r in pair], axis=1)
+    for pair in [(r, r + 1) for r in range(0, some, 2)]:
+        v = jnp.concatenate([lines_of(field, r, some) for r in pair], axis=1)
         both = depth_times(high_table, low_table, v)
         for i, r in enumerate(pair):
-            a, line = both[:, 128 * i : 128 * i + 128], pl.ds(r, everywhere, stride=rows)
+            a, line = both[:, 128 * i : 128 * i + 128], pl.ds(r, everywhere, stride=some)
             a_out[0, line, :] = a
             c_out[0, line, :] = weights[0] * v[:, 128 * i : 128 * i + 128] + weights[1] * a
-            b_out[0, line, :] = weights[1] * (lines_of(potential.at[0], r, rows) - 2.0) * a
-
-
-def back_kernel(rows, cuts, weights, g_in, c_in, b_in, high_table, low_table, *outs):
+            b_out[0, line, :] = weights[1] * (lines_of(potential, chunk * some + r, rows) - 2.0) * a
+
+
+def back_kernel(some, cuts, weights, g_in, c_in, b_in, high_table, low_table, *outs):
     everywhere = high_table.shape[0]
-    devices = outs[0].shape[1]
+    devices = outs[0].shape[0]
     mine = everywhere // devices
-    for pair in side_by_side(rows):
-        lines = [pl.ds(r, everywhere, stride=rows) for r in pair]
-        parts = [c_in[0, line, :] + weights[1] * lines_of(g_in, r, rows) for r, line in zip(pair, lines)]
+    for pair in [(r, r + 1) for r in range(0, some, 2)]:
+        lines = [pl.ds(r, everywhere, stride=some) for r in pair]
+        parts = [c_in[0, line, :] + weights[1] * lines_of(g_in, r, some) for r, line in zip(pair, lines)]
         both = depth_times(high_table, low_table, jnp.concatenate(parts, axis=1))
         for i, (r, line) in enumerate(zip(pair, lines)):
             m = both[:, 128 * i : 128 * i + 128] + b_in[0, line, :]
             for out, (start, stop) in zip(outs, cuts):
                 for d in range(devices):
-                    out[0, d, pl.ds(r, stop - start, stride=rows), :] = m[mine * d + start : mine * d + stop]
+                    out[d, 0, pl.ds(r, stop - start, stride=some), :] = m[mine * d + start : mine * d + stop]
 
 
 def tiled(field):
@@ -274,9 +310,9 @@
 ANY = pl.BlockSpec(memory_space=pl.ANY)
 
 
-def pick(total, starts, corner, spots, field, grouped=False):
-    return pl.pallas_call(
-        functools.partial(pick_kernel, total, grouped),
+def pick(total, starts, corner, spots, field):
+    return pl.pallas_call(
+        functools.partial(pick_kernel, total),
         out_shape=jax.ShapeDtypeStruct((starts.shape[0], 1, 128), jnp.float32),
         in_specs=[SMEM, SMEM, VMEM, VMEM],
         out_specs=VMEM,
@@ -284,7 +320,20 @@
         compiler_params=PARAMS,
         cost_estimate=pl.CostEstimate(flops=1 << 24, bytes_accessed=1 << 24, transcendentals=0),
         name="pick",
-    )(starts, corner, spots, field if grouped else tiled(field))
+    )(starts, corner, spots, tiled(field))
+
+
+def pick_block(total, starts, corner, spots, field):
+    return pl.pallas_call(
+        functools.partial(pick_block_kernel, total),
+        out_shape=jax.ShapeDtypeStruct((field.shape[0], starts.shape[0], 1, 128), jnp.float32),
+        in_specs=[SMEM, SMEM, VMEM, VMEM],
+        out_specs=VMEM,
+        scratch_shapes=[pltpu.SMEM((starts.shape[0] + 1,), jnp.int32)],
+        compiler_params=PARAMS,
+        cost_estimate=pl.CostEstimate(flops=1 << 24, bytes_accessed=1 << 24, transcendentals=0),
+        name="pick_block",
+    )(starts, corner, spots, field)
 
 
 def put(total, starts, corner, spots, spread, base):
@@ -360,7 +409,9 @@
 def append_kernel(first, others, numbers, block, *refs):
     out, sem = refs[others], refs[others + 1]
     copies = [
-        pltpu.make_async_copy(numbers, out.at[d, pl.ds(first, numbers.shape[0]), :], sem.at[d])
+        pltpu.make_async_copy(
+            numbers.at[d % numbers.shape[0]], out.at[d, pl.ds(first, numbers.shape[1]), :], sem.at[d]
+        )
         for d in range(out.shape[0])
     ]
     for copy in copies:
@@ -372,51 +423,50 @@
 def append(block, numbers, *others):
     devices, lines, wide = block.shape
     return pl.pallas_call(
-        functools.partial(append_kernel, lines - numbers.shape[0], len(others)),
+        functools.partial(append_kernel, lines - numbers.shape[1], len(others)),
         out_shape=jax.ShapeDtypeStruct(block.shape, block.dtype),
         in_specs=[VMEM, ANY] + [ANY] * len(others),
         out_specs=ANY,
         scratch_shapes=[pltpu.SemaphoreType.DMA((devices,))],
         input_output_aliases={1: 0},
-        cost_estimate=cost(0, devices * numbers.size),
+        cost_estimate=cost(0, 2 * numbers.size),
         name="append",
     )(numbers, block, *others)
 
 
 def pack_kernel(count, chunks, chosen, together, *refs):
     fields, out = refs[:count], refs[-1]
-    planes, rows, cols = fields[0].shape
+    planes, rows, _ = fields[0].shape
     some = rows // chunks // together
     lines = planes * some
     for d in range(together):
-        at = 0
-        for i in chosen:
-            start = (d * chunks + i) * some
-            for g in range(cols // 128):
+        for g in range(out.shape[0]):
+            for at, i in enumerate(chosen):
+                start = (d * chunks + i) * some
                 cells = (slice(None), slice(start, start + some), slice(128 * g, 128 * g + 128))
                 part = fields[0][cells]
                 for field in fields[1:]:
                     part = part + field[cells]
-                out[d, at : at + lines, :] = part.reshape(lines, 128)
-                at += lines
+                out[g, d, at * lines : at * lines + lines, :] = part.reshape(lines, 128)
 
 
 def pack(fields, devices, chunks, chosen, spare, *others):
     planes, rows_y, cols = fields[0].shape
-    rows = rows_y // devices
+    rows, groups = rows_y // devices, cols // 128
     together = math.gcd(devices, 4)
-    lines = planes * rows * cols // 128 * len(chosen) // chunks
+    lines = planes * rows * len(chosen) // chunks
     block = pl.BlockSpec((planes, rows * together, cols), lambda d: (0, d, 0))
-    return pl.pallas_call(
+    got = pl.pallas_call(
         ordered(functools.partial(pack_kernel, len(fields), chunks, chosen, together), len(fields), len(others)),
         grid=(devices // together,),
-        out_shape=jax.ShapeDtypeStruct((devices, lines + spare, 128), jnp.float32),
+        out_shape=jax.ShapeDtypeStruct((groups, devices, lines + spare, 128), jnp.float32),
         in_specs=[block] * len(fields) + [ANY] * len(others),
-        out_specs=pl.BlockSpec((together, lines, 128), lambda d: (d, 0, 0)),
-        compiler_params=PARAMS,
-        cost_estimate=cost(devices * lines * 128, 2 * devices * lines * 128),
+        out_specs=pl.BlockSpec((groups, together, lines, 128), lambda d: (0, d, 0, 0)),
+        compiler_params=PARAMS,
+        cost_estimate=cost(groups * devices * lines * 128, 2 * groups * devices * lines * 128),
         name="pack",
     )(*fields, *others)
+    return got.reshape(groups * devices, lines + spare, 128)
 
 
 def pack_part_kernel(place, field, out):
@@ -445,44 +495,85 @@
     )(place, field)
 
 
-def depth_specs(field, potential_shape, rows, chunk):
-    groups, lines = potential_shape[0], potential_shape[1] * potential_shape[2]
-    devices = field.shape[0]
-    got = pl.BlockSpec((devices, lines // devices, 128), lambda g: (0, chunk * groups + g, 0))
-    flat = pl.BlockSpec((1, lines, 128), lambda g: (g, 0, 0))
-    table = pl.BlockSpec((lines // rows, lines // rows), lambda g: (0, 0))
-    return got, flat, table
-
-
-def depth_out(weights, field, potential, rows, chunk, tables):
-    groups, devices, lines = potential.shape[:3]
-    got, flat, table = depth_specs(field, potential.shape, rows, chunk)
-    well = pl.BlockSpec((1, devices, lines, 128), lambda g: (g, 0, 0, 0))
-    lines = devices * lines
-    return pl.pallas_call(
-        functools.partial(out_kernel, rows),
-        grid=(groups,),
-        out_shape=[jax.ShapeDtypeStruct((groups, lines, 128), jnp.float32)] * 3,
+def join_kernel(spans, planes, begin, place, *refs):
+    out = refs[-1]
+    devices, some = refs[0].shape[1:3]
+    rows = out.shape[1] // devices
+    first = begin + pl.program_id(0) * planes
+    mine = place[0] == 0
+    for (chunk, start, stop), own, other in zip(spans, refs[0::2], refs[1::2]):
+
+        @pl.when((first >= start) & (first < stop))
+        def _(chunk=chunk, own=own, other=other):
+            a, b = own[...], other[...]
+            left, right = jnp.where(mine, a, b), jnp.where(mine, b, a)
+            for d in range(devices):
+                lines = slice(d * rows + chunk * some, d * rows + (chunk + 1) * some)
+                out[:, lines, 0:128] = left[:, d]
+                out[:, lines, 128:256] = right[:, d]
+
+
+def join(shape, spans, place, pairs, begin, end, before):
+    planes = end - begin
+    for _, start, stop in spans:
+        planes = math.gcd(planes, start, stop)
+    planes = math.gcd(planes, begin, 4)
+    specs, blocks = [SMEM], []
+    for (_, start, stop), pair in zip(spans, pairs):
+        shift, count = (begin - start) // planes, (stop - start) // planes
+        block = (planes,) + pair[0].shape[1:]
+        spec = pl.BlockSpec(block, lambda z, shift=shift, count=count: (jnp.clip(z + shift, 0, count - 1), 0, 0, 0))
+        specs += [spec, spec]
+        blocks += pair
+    return pl.pallas_call(
+        ordered(functools.partial(join_kernel, spans, planes, begin), 1 + len(blocks), len(before)),
+        grid=((end - begin) // planes,),
+        out_shape=jax.ShapeDtypeStruct(shape, jnp.float32),
+        in_specs=specs + [ANY] * len(before),
+        out_specs=pl.BlockSpec((planes,) + shape[1:], lambda z: (z + begin // planes, 0, 0)),
+        input_output_aliases={1 + len(blocks): 0} if before else {},
+        compiler_params=PARAMS,
+        cost_estimate=cost(0, 2 * math.prod(shape) * (end - begin) // shape[0]),
+        name="join",
+    )(place, *blocks, *before)
+
+
+def depth_specs(planes, some, devices, chunk):
+    got = pl.BlockSpec((devices, planes // devices * some, 128), lambda o: (o, chunk, 0))
+    flat = pl.BlockSpec((1, planes * some, 128), lambda o: (o, 0, 0))
+    return got, flat, pl.BlockSpec((planes, planes), lambda o: (0, 0))
+
+
+def depth_out(weights, field, potential, some, chunk, orbitals, tables):
+    devices, planes = potential.shape[0], tables[0].shape[0]
+    rows = potential.shape[1] * devices // planes
+    got, flat, table = depth_specs(planes, some, devices, chunk)
+    well = pl.BlockSpec(potential.shape, lambda o: (0, 0, 0))
+    size = orbitals * planes * some * 128
+    return pl.pallas_call(
+        functools.partial(out_kernel, some, rows, chunk),
+        grid=(orbitals,),
+        out_shape=[jax.ShapeDtypeStruct((orbitals, planes * some, 128), jnp.float32)] * 3,
         in_specs=[SMEM, got, well, table, table],
         out_specs=[flat] * 3,
         compiler_params=PARAMS,
-        cost_estimate=cost(6 * tables[0].size * rows * groups * 128, 5 * groups * lines * 128),
+        cost_estimate=cost(6 * planes * size, 5 * size),
         name="depth_out",
     )(weights, field, potential, *tables)
 
 
-def depth_back(weights, g, c, b, rows, devices, cuts, tables, *others):
-    groups, lines = c.shape[:2]
-    got, flat, table = depth_specs(g, (groups, 1, lines), rows, 0)
-    each = [(stop - start) * rows for start, stop in cuts]
-    return pl.pallas_call(
-        ordered(functools.partial(back_kernel, rows, cuts), 6, len(others)),
-        grid=(groups,),
-        out_shape=[jax.ShapeDtypeStruct((groups, devices, n, 128), jnp.float32) for n in each],
+def depth_back(weights, g, c, b, some, devices, cuts, tables, *others):
+    orbitals, planes = c.shape[0], tables[0].shape[0]
+    got, flat, table = depth_specs(planes, some, devices, 0)
+    each = [(stop - start) * some for start, stop in cuts]
+    return pl.pallas_call(
+        ordered(functools.partial(back_kernel, some, cuts), 6, len(others)),
+        grid=(orbitals,),
+        out_shape=[jax.ShapeDtypeStruct((devices, orbitals, n, 128), jnp.float32) for n in each],
         in_specs=[SMEM, got, flat, flat, table, table] + [ANY] * len(others),
-        out_specs=[pl.BlockSpec((1, devices, n, 128), lambda g: (g, 0, 0, 0)) for n in each],
-        compiler_params=PARAMS,
-        cost_estimate=cost(6 * tables[0].shape[0] * c.size, 4 * c.size),
+        out_specs=[pl.BlockSpec((devices, 1, n, 128), lambda o: (0, o, 0, 0)) for n in each],
+        compiler_params=PARAMS,
+        cost_estimate=cost(6 * planes * c.size, 4 * c.size),
         name="depth_back",
     )(weights, g, c, b, *tables, *others)
 
@@ -519,38 +610,41 @@
     some = rows // chunks
     part = cols_x // orb_groups
     put_late = part % 128 == 0
+    joint = orb_groups == 2 and part == 128
     c0, c1, c2 = cheb_coef[0], cheb_coef[1], cheb_coef[2]
     c1_4 = c1 / 4.0
     c2_8 = c2 / 8.0
     planar_tables = [jnp.stack(pair) for pair in zip(halves_of(kinetic_table(cols_x)), halves_of(kinetic_table(rows_y)))]
-    depth_tables = halves_of(kinetic_table(all_planes))
+    kinetic_z = kinetic_table(all_planes)
+    depth_tables = halves_of(kinetic_z)
     total = (all_planes, rows_y // 8, cols_x // 128)
 
-    groups = cols_x // 128
-    lines = groups * planes * some
-    whole_tiles = planes % 8 == 0 and some % 8 == 0
+    lines = planes * some
+    fast = part == 128 and planes % 8 == 0 and some % 8 == 0
+    orbitals = orb_groups
 
     def packed(fields, chosen, spare, *others):
-        if whole_tiles:
+        if fast:
             return pack(fields, grid_count, chunks, chosen, spare, *others)
-        field = sum(fields[1:], fields[0]).reshape(planes, grid_count, chunks, some, groups, 128)
-        sent = [field[:, :, i].transpose(1, 3, 0, 2, 4).reshape(grid_count, lines, 128) for i in chosen]
-        return jnp.concatenate(sent + [jnp.zeros((grid_count, spare, 128), jnp.float32)], axis=1)
-
-    def joined(got):
-        if whole_tiles:
-            return got
-        got = got.reshape(grid_count, -1, planes * some, 128)
-        return got.transpose(1, 0, 2, 3).reshape(1, -1, 128)
-
-    if part == 128 and rows % 8 == 0:
+        field = sum(fields[1:], fields[0]).reshape(planes, grid_count, chunks, some, orb_groups, part)
+        field = jnp.stack([field[:, :, i] for i in chosen]).transpose(4, 2, 0, 1, 3, 5)
+        field = field.reshape(orb_groups * grid_count, len(chosen) * lines, part)
+        return jnp.concatenate([field, jnp.zeros((field.shape[0], spare, part), jnp.float32)], axis=1)
+
+    def along_z(field):
+        return jnp.einsum("wz,ozyx->owyx", kinetic_z, field, precision=PRECISE)
+
+    def everyones(block):
+        return exchange(block, ("orb", "grid"))
+
+    if fast:
         mine = pack_part(potential, grid_count, orb_pos[None])
         mine = mine.reshape(grid_count, planes, rows, part)
     else:
         mine = lax.dynamic_slice_in_dim(potential, orb_pos * part, part, axis=2)
         mine = mine.reshape(planes, grid_count, rows, part).transpose(1, 0, 2, 3)
 
-    raw = tie(jnp.concatenate([sphere_cells.astype(jnp.float32), projectors], axis=1), mine)
+    raw = jnp.concatenate([sphere_cells.astype(jnp.float32), projectors], axis=1)
     here = [(grid_pos + grid_count + step) % grid_count for step in (-1, 0, 1)]
 
     def shifted(block, step):
@@ -598,99 +692,123 @@
         return put(total, near_starts, corner, near_spots, spread[:, None], base)
 
     got_potential = exchange(tie(mine, *gots), "grid")
-    shared = gather_over(got_potential[None], "orb")
-    shared = jnp.moveaxis(shared.reshape(orb_groups, all_planes, rows, part), 0, 2)
-    shared = jnp.moveaxis(shared.reshape(all_planes, rows, groups, 128), 2, 0)
-    shared = shared.reshape(groups, grid_count, planes, chunks, some, 128)
-    wells = [shared[:, :, :, i].reshape(groups, grid_count, planes * some, 128) for i in range(chunks)]
-    if not whole_tiles:
-        wells = [well.reshape(groups, 1, all_planes * some, 128) for well in wells]
-
-    halves = [(0, planes // 2), (planes // 2, planes)] if planes % 16 == 0 else [(0, planes)]
-    cuts = [[(0, planes)]] * (chunks - 1) + [halves]
+    got_potential = got_potential.reshape(grid_count, planes * rows, part)
+
+    late = planes // 4 * 3
+    cuts = [[(0, planes)]] * (chunks - 1) + [[(0, late), (late, planes)] if planes % 16 == 0 else [(0, planes)]]
     sums = [[0.0] * len(cut) for cut in cuts]
     weights = jnp.stack([c1_4, c2_8])
     for orb in range(orb_count):
         v = random_orbitals[orb]
         first = whole_near(partial_near(v))
-        pv, t = planar_first(v, potential, planar_tables, mine)
-        v_send = packed([v], range(chunks), 0, mine)
+        pv, t = planar_first(v, potential, planar_tables, near_spots)
+        v_send = packed([v], range(chunks), 0, near_spots)
         if orb == 0:
             every = gather_part(column, "grid", 0, low)
             every = jnp.swapaxes(every, 0, 1).reshape((atoms,) + raw.shape[1:])
             every_projs = every[:, 2:]
             every_starts, every_spots = atom_windows(every[:, :2].astype(jnp.int32), all_planes, rows_y, cols_x)
-        v_got = exchange(tie(v_send, first, column), "grid")
+        v_got = everyones(tie(v_send, first, column))
         u = put_near(first, t)
         base = planar_second(
             jnp.stack([c2_8, c1_4, c0 - c2]), u, v, potential, planar_tables, orb_groups
         )
-        second = everywhere(partial_near(u))
-        if put_late:
-            mixed = trade(base, "orb")
+        second = jnp.zeros((orbitals, atoms, projs_each), jnp.float32)
+        second = lax.dynamic_update_slice_in_dim(second, everywhere(partial_near(u))[None], orb_pos, 0)
         g_gots = []
         for i in range(chunks - 1):
-            g_gots.append(exchange(tie(packed([pv, u], [i], 0, base), every, *wells), "grid"))
+            g_gots.append(everyones(tie(packed([pv, u], [i], 0, base), every)))
 
         cb = []
         for i in range(chunks):
-            a, c, b = depth_out(weights, joined(v_got), wells[i], some, i, depth_tables)
+            first_row = grid_pos * rows + i * some
+            if fast:
+                a, c, b = depth_out(weights, v_got, got_potential, some, i, orbitals, depth_tables)
+                corner = jnp.stack([zero, first_row // 8, orb_pos])
+                values = pick_block(total, every_starts, corner, every_spots, a.reshape(orbitals, all_planes, some, 128))
+            else:
+                v_i = v_got.reshape(orbitals, grid_count, chunks, planes, some, part)[:, :, i]
+                v_i = v_i.reshape(orbitals, all_planes, some, part)
+                well = got_potential.reshape(all_planes, rows, part)[:, i * some : (i + 1) * some]
+                a = along_z(v_i)
+                c, b = c1_4 * v_i + c2_8 * a, c2_8 * (well - 2.0) * a
+                corner = jnp.stack([zero, first_row // 8, zero])
+                values = []
+                for o in range(orbitals):
+                    padded = jnp.zeros((all_planes, -(-some // 8) * 8, cols_x), jnp.float32)
+                    padded = lax.dynamic_update_slice(padded, a[o], (0, first_row % 8, orb_pos * part))
+                    values.append(pick(total, every_starts, corner, every_spots, padded))
+                values = jnp.stack(values)
             cb.append((c, b))
-            field = a.reshape(groups, all_planes, some, 128)
-            first_row = grid_pos * rows + i * some
-            if some % 8:
-                padded = jnp.zeros((groups, all_planes, 8, 128), jnp.float32)
-                field = lax.dynamic_update_slice(padded, field, (0, 0, first_row % 8, 0))
-            corner = jnp.stack([zero, first_row // 8, zero])
-            values = pick(total, every_starts, corner, every_spots, field, grouped=True)
-            second = second + jnp.einsum("aj,apj->ap", values[:, 0], every_projs, precision=PRECISE)
-        more = -(-orb_groups * second.size // 1024) * 8
-        g_last = packed([pv, u], [chunks - 1], more, base)
-        second = gather_over(c2_8 * second[None], "orb").reshape(-1)
-        extra = jnp.pad(second, (0, more * 128 - second.size)).reshape(more, 128)
-        g_last = exchange(append(g_last, extra, *([mixed] if put_late else [])), "grid")
-        second = jnp.sum(g_last[:, lines:], axis=0).reshape(-1)[: second.size]
-        second = second.reshape(orb_groups, atoms, projs_each)
-        g_gots.append(g_last if whole_tiles else g_last[:, :lines])
+            second = second + jnp.einsum("oaj,apj->oap", values[:, :, 0], every_projs, precision=PRECISE)
+        if put_late:
+            mixed = trade(base, "orb", values)
+        second = c2_8 * second
+        if fast:
+            each = second.reshape(orbitals, grid_count, per_dev, projs_each)
+            each = jnp.stack([jnp.roll(each, 1, axis=1), each, jnp.roll(each, -1, axis=1)], axis=2)
+            each = jnp.moveaxis(each, 1, 0).reshape(grid_count, -1)
+            size = each.shape[1]
+            more = -(-size // 1024) * 8
+            each = jnp.pad(each, ((0, 0), (0, more * 128 - size))).reshape(grid_count, more, 128)
+            g_last = everyones(append(packed([pv, u], [chunks - 1], more, base), each, mixed))
+            second = jnp.sum(g_last[:, lines:], axis=0).reshape(-1)[:size]
+            second = second.reshape(orbitals, 3 * per_dev, projs_each)
+        else:
+            g_last = everyones(packed([pv, u], [chunks - 1], 0, base))
+            second = lax.psum(second, ("orb", "grid"))
+            second = jnp.stack([nearby(second[o]) for o in range(orbitals)])
+        g_gots.append(g_last)
         if put_late:
             corner = slab_corner + jnp.stack([zero, zero, orb_pos * (part // 128)])
-            q_all = jnp.stack([put_near(nearby(second[o]), mixed[o], corner) for o in range(orb_groups)])
+            q_all = jnp.stack([put_near(second[o], mixed[o], corner) for o in range(orb_groups)])
         else:
             base = jnp.moveaxis(base, 0, 2).reshape(planes, rows_y, cols_x)
             own = lax.dynamic_index_in_dim(second, orb_pos, 0, keepdims=False)
-            q = put_near(nearby(own), base).reshape(planes, rows_y, orb_groups, part)
+            q = put_near(own, base).reshape(planes, rows_y, orb_groups, part)
             q_all = trade(jnp.moveaxis(q, 2, 0), "orb")
         q_all = q_all.reshape(orb_groups, planes, grid_count, chunks, some, part)
 
         sends = []
         for i in range(chunks):
-            if part == 128:
+            if fast:
                 later = [q_all] if i > 0 else []
-                ms = depth_back(weights, joined(g_gots[i]), *cb[i], some, grid_count, cuts[i], depth_tables, *later)
-                sends.append([m.reshape(orb_groups * grid_count, -1, 128) for m in ms])
+                ms = depth_back(weights, g_gots[i], *cb[i], some, grid_count, cuts[i], depth_tables, *later)
             else:
-                whole = [(0, all_planes)]
-                (m,) = depth_back(weights, joined(g_gots[i]), *cb[i], some, 1, whole, depth_tables)
-                m = jnp.moveaxis(m.reshape(groups, all_planes * some, 128), 0, 1)
-                m = jnp.moveaxis(m.reshape(all_planes * some, orb_groups, part), 1, 0)
-                m = m.reshape(orb_groups * grid_count, planes, some * part)
-                sends.append([m[:, p:q].reshape(orb_groups * grid_count, -1, 128) for p, q in cuts[i]])
-        done, kept = [], []
+                c, b = cb[i]
+                g = g_gots[i][:, :lines].reshape(orbitals, all_planes, some, part)
+                m = (along_z(c + c2_8 * g) + b).reshape(orbitals, grid_count, planes, some, part)
+                m = jnp.moveaxis(m, 1, 0)
+                ms = [m[:, :, p:q].reshape(grid_count, orbitals, -1, part) for p, q in cuts[i]]
+            sends.append(ms)
+        kept, pairs, spans = [], [], []
         for i in range(chunks):
             for k, (start, stop) in enumerate(cuts[i]):
                 send = sends[i][k]
                 if len(kept) > 1:
-                    send = tie(send, kept[-2])
-                got = exchange(send, ("orb", "grid"))
-                if done:
-                    got = tie(got, *done[-2:])
-                m = got.reshape(orb_groups, grid_count, stop - start, some, part)
-                filtered = q_all[:, start:stop, :, i] + m.transpose(0, 2, 1, 3, 4)
+                    send = tie(send, *([pairs[0][1]] if pairs else kept[:1]), kept[-1])
+                got = exchange(send, "grid")
+                m = got.reshape(grid_count, orbitals, stop - start, some, part)
+                filtered = q_all[:, start:stop, :, i] + m.transpose(1, 2, 0, 3, 4)
                 own = jnp.sum(filtered * filtered, axis=0) * (1.0 / (orb_count * orb_groups))
                 kept.append(own)
-                done.append(gather_over(own[None], "orb"))
-                sums[i][k] = sums[i][k] + done[-1]
-    out = [jnp.moveaxis(jnp.concatenate(shares, axis=1), 0, 3) for shares in sums]
+                sums[i][k] = sums[i][k] + own
+                if orb == orb_count - 1 and joint:
+                    own = sums[i][k]
+                    spans.append((i, start, stop))
+                    pairs.append((own, lax.ppermute(own, "orb", [(0, 1), (1, 0)])))
+    if joint:
+        out, begin = [], 0
+        for end in sorted({stop for _, _, stop in spans}):
+            some = [i for i, (_, start, stop) in enumerate(spans) if start < end and stop > begin]
+            parts = [[each[i] for i in some] for each in (spans, pairs)]
+            out = [join(potential.shape, parts[0], orb_pos[None], parts[1], begin, end, out)]
+            begin = end
+        return out[0]
+    out = []
+    for parts in sums:
+        shares = [gather_over(own[None], "orb") for own in parts]
+        out.append(jnp.moveaxis(jnp.concatenate(shares, axis=1), 0, 3))
     return jnp.stack(out, axis=2).reshape(planes, rows_y, cols_x)
 
 

time: 423 us -> 413 us (0.976)
  starting transfers between devices: 87.4 us -> 70.9 us
  waiting for transfers between devices: 151 us -> 162 us
    all_to_all x7, waiting for transfers between devices: 85.3 us -> 136 us  [exchange(): return lax.all_to_all(block, axis, split_axis=0, concat_axis=0, tiled=True)]
    ppermute x11 -> x6, waiting for transfers between devices: 39.8 us -> 0.02 us  [gather_part(): lax.ppermute(block, axis, xor_route(lax.axis_size(axis), apart << shift))]
    all_to_all x7, starting transfers between devices: 61.6 us -> 49.8 us  [exchange(): return lax.all_to_all(block, axis, split_axis=0, concat_axis=0, tiled=True)]
    unnamed x55 -> x65, local copies, waits for them, and re-layouts: 13.1 us -> 24.8 us
    ppermute x11 -> x6, starting transfers between devices: 16.2 us -> 6.31 us  [gather_part(): lax.ppermute(block, axis, xor_route(lax.axis_size(axis), apart << shift))]
    dynamic_update_slice x11 -> x6, local copies, waits for them, and re-layouts: 7.38 us -> 0.17 us  [gather_part(): out = lax.dynamic_update_slice_in_dim(out, got[None], own ^ apart, 0)]
    pallas_call x9 -> x11, Pallas kernels: 41 us -> 47.4 us  [the longest x2 13.8 us: pick_block(): pl.pallas_call(functools.partial(pick_block_kernel, total), out_shape=jax...]
    ppermute x4, waiting for transfers between devices: 26.1 us -> 20.9 us  [shifted(): lax.ppermute(block, 'grid', [(i, (i + step) % grid_count) for i in range(...]
  transfers between devices with their start and end apart: 23 -> 21, of which waited for: 11 -> 9; matrix products, arithmetic and copies ran while one was open for 14% -> 12% of each run, Pallas kernels for 23% -> 24%
where the time goes in v6:
time: 413 us; the launch traced here: 411 us
  waiting for transfers between devices  162 us (39%)
  Pallas kernels  101 us (24%)
  starting transfers between devices  70.9 us (17%)
  local copies, waits for them, and re-layouts  44.5 us (11%)
  other arithmetic  23.6 us (6%)
  matrix products  6.03 us (1%)
    all_to_all x7, waiting for transfers between devices, exchange(): return lax.all_to_all(block, axis, split_axis=0, concat_axis=0, tiled=True)  136 us
    all_to_all x7, starting transfers between devices, exchange(): return lax.all_to_all(block, axis, split_axis=0, concat_axis=0, tiled=True)  49.8 us
    unnamed x65, local copies, waits for them, and re-layouts  24.8 us
    ppermute x4, waiting for transfers between devices, shifted(): lax.ppermute(block, 'grid', [(i, (i + step) % grid_count) for i in range(...  20.9 us
    pallas_call x2, Pallas kernels, pick_block(): pl.pallas_call(functools.partial(pick_block_kernel, total), out_shape=jax...  13.8 us
    pallas_call x1, Pallas kernels, planar_first(): pl.pallas_call(ordered(first_kernel, 4, len(others)), grid=field.shape[:1...  13.6 us
    pallas_call x1, Pallas kernels, planar_second(): pl.pallas_call(second_kernel, grid=field.shape[:1], out_shape=jax.ShapeDt...  13 us
    pallas_call x3, Pallas kernels, put(): pl.pallas_call(functools.partial(put_kernel, total), out_shape=jax.ShapeD...  12.7 us
  transfers between devices with their start and end apart: 21, of which 9 were waited for; matrix products, arithmetic and copies ran while one was open for 12% of the time, Pallas kernels for 24%

profile of v6, /device:TPU:0, one launch (start us, length us, event | category | flops | bytes accessed | tf_op | source)
XLA Modules:
  0.0 411.0 jit_solution(11626643670034201874)
XLA Ops:
  1.9 5.0 %collective-permute-start.1 = (f32[16,6,128]{2,0,1:T(8,128)S(1)}, f32[16,6,128]{2,0,1:T(8,128)S(1)}, u32[]{:S(2)}, u32[]{:S(2)}) collective-permute-start(f32[16,6,128]{2,0,1:T(8,128)S(1)} %pad_maximum_fusion.7), channel_id=1, source_target_pairs={{0,15},{1,0},{2,1},{3,2},{4,3},{5,4},{6,5},{7,6},{8,7},{9,8},{10,9... | collective-permute-start | bytes 147464 | tf_op jit(solution)/shard_map/ppermute | solution.py:651
  8.2 1.6 collective-permute-start.2
  9.7 1.6 collective-permute-start.4
  11.4 2.4 pack_part.1
  13.9 1.3 copy-done.7
  16.5 3.7 all-to-all-start.1
  22.6 2.2 copy-done.3
  24.7 4.1 pick.2
  29.6 4.1 %collective-permute-start.8 = (f32[3,16,4]{2,1,0:T(8,128)S(1)}, f32[3,16,4]{2,1,0:T(8,128)S(1)}, u32[]{:S(2)}, u32[]{:S(2)}) collective-permute-start(f32[3,16,4]{2,1,0:T(8,128)S(1)} %bitcast.264), channel_id=1, source_target_pairs={{0,15},{1,0},{2,1},{3,2},{4,3},{5,4},{6,5},{7,6},{8,7},{9,8},{10,9... | collective-permute-start | bytes 2312 | tf_op jit(solution)/shard_map/ppermute | solution.py:651
  33.9 3.3 pack.3
  37.2 2.0 copy-done.4
  39.2 20.9 %collective-permute-done.9 = f32[3,16,4]{2,1,0:T(8,128)S(1)} collective-permute-done((f32[3,16,4]{2,1,0:T(8,128)S(1)}, f32[3,16,4]{2,1,0:T(8,128)S(1)}, u32[]{:S(2)}, u32[]{:S(2)}) %collective-permute-start.9) | collective-permute-done | bytes 800 | tf_op jit(solution)/shard_map/ppermute | solution.py:651
  61.5 1.4 copy-done.22
  62.9 11.7 %all-to-all-start = ((f32[32,256,128]{2,1,0:T(8,128)}), f32[32,256,128]{2,1,0:T(8,128)}, u32[]{:S(2)}, u32[]{:S(2)}) async-start(f32[32,256,128]{2,1,0:T(8,128)} %tie.5), calls=%async_computation | async-start | bytes 8388608 | tf_op jit(solution)/shard_map/all_to_all | solution.py:62
  81.4 1.5 collective-permute-start.7
  83.4 13.6 %planar_first.1 = (f32[16,256,256]{2,1,0:T(8,128)S(1)}, f32[16,256,256]{2,1,0:T(8,128)}) custom-call(f32[16,256,256]{2,1,0:T(8,128)} %bitcast.217, f32[16,256,256]{2,1,0:T(8,128)} %potential.1, bf16[2,256,256]{2,1,0:T(8,128)(2,1)S(1)} %get-tuple-element.115.refs_2_.high_tables, bf16[2,256,256]{2,1,0:T(8,128)(2,1)S(1)} %get-tuple-element.116.refs_3_.low_tables, ...), custom_call_target="tpu_custom_call" | custom-call | flops 3221225472 | bytes 16777216 | tf_op jit(solution)/shard_map/planar_first/pallas_call | solution.py:369
  97.0 2.0 copy-done.8
  99.4 5.2 %put.3.field = f32[16,32,8,256]{3,2,1,0:T(8,128)S(1)} custom-call(s32[48,3]{1,0:T(8,128)S(1)} %pad_add_fusion.3.starts, s32[3]{0:T(128)S(1)} %stack.72.corner, s32[48,2,128]{2,1,0:T(2,128)S(1)} %pad_add_fusion.2.refs_1_.spots.refs_4_, f32[48,1,128]{2,1,0:T(1,128)S(1)} %fusion.73.spread, f32[16,32,8,256]{3,2,1,0:T(8,128)} %bitcast.234), custom_call_target="tpu_custom_call" | custom-call | flops 16777216 | bytes 16777216 | tf_op jit(solution)/shard_map/put/pallas_call | solution.py:341
  104.6 4.1 pick.3
  109.5 13.0 %planar_second.1.refs_2_ = f32[2,16,256,128]{3,2,1,0:T(8,128)S(1)} custom-call(f32[3]{0:T(128)S(1)} %pad_maximum_fusion.9.weights, f32[16,256,256]{2,1,0:T(8,128)} %bitcast.205, f32[16,256,256]{2,1,0:T(8,128)} %bitcast.218, f32[16,256,256]{2,1,0:T(8,128)} %potential.1, bf16[2,256,256]{2,1,0:T(8,128)(2,1)S(1)} %get-tuple-element.115.refs_2_.high_tables, ...), custom_call_target="tpu_custom_call" | custom-call | flops 3221225472 | bytes 16777216 | tf_op jit(solution)/shard_map/planar_second/pallas_call | solution.py:385
  122.6 1.7 constant_dynamic-slice_fusion
  125.4 1.7 collective-permute-start.10
  127.0 4.1 pack.5
  131.2 1.3 copy-done.6
  132.5 4.1 pack.4
  136.6 1.4 copy-done.5
  139.3 1.3 slice_convert_fusion
  141.0 28.9 %all-to-all-done.field = f32[32,256,128]{2,1,0:T(8,128)} async-done(((f32[32,256,128]{2,1,0:T(8,128)}), f32[32,256,128]{2,1,0:T(8,128)}, u32[]{:S(2)}, u32[]{:S(2)}) %all-to-all-start) | async-done | bytes 4194336 | tf_op jit(solution)/shard_map/all_to_all | solution.py:62
  169.9 2.9 all-to-all-start.3
  176.0 3.2 fusion.62
  179.6 5.4 %depth_out.2 = (f32[2,2048,128]{2,1,0:T(8,128)S(1)}, f32[2,2048,128]{2,1,0:T(8,128)S(1)}, f32[2,2048,128]{2,1,0:T(8,128)}) custom-call(f32[2]{0:T(128)S(1)} %pad_maximum_fusion.8.weights.refs_0_, f32[32,256,128]{2,1,0:T(8,128)} %all-to-all-done.field, f32[16,256,128]{2,1,0:T(8,128)} %bitcast.232, bf16[256,256]{1,0:T(8,128)(2,1)S(1)} %get-tuple-element.113.high_table.refs_4_, ...), custom_call_target="tpu_custom_call" | custom-call | flops 805306368 | bytes 10485760 | tf_op jit(solution)/shard_map/depth_out/pallas_call | solution.py:553
  185.0 1.3 copy-done.14
  186.4 6.9 %pick_block.2 = f32[2,256,1,128]{3,2,1,0:T(1,128)S(1)} custom-call(s32[256,3]{1,0:T(8,128)S(1)} %pad_add_fusion.1.starts, s32[3]{0:T(128)S(1)} %get-tuple-element.107.corner, s32[256,2,128]{2,1,0:T(2,128)S(1)} %pad_add_fusion.spots, f32[2,256,8,128]{3,2,1,0:T(8,128)S(1)} %bitcast.226), custom_call_target="tpu_custom_call" | custom-call | flops 16777216 | bytes 16777216 | tf_op jit(solution)/shard_map/pick_block/pallas_call | solution.py:327
  193.3 1.9 fusion.18
  195.4 3.0 add.386
  198.4 5.4 %depth_out.3 = (f32[2,2048,128]{2,1,0:T(8,128)S(1)}, f32[2,2048,128]{2,1,0:T(8,128)S(1)}, f32[2,2048,128]{2,1,0:T(8,128)}) custom-call(f32[2]{0:T(128)S(1)} %pad_maximum_fusion.8.weights.refs_0_, f32[32,256,128]{2,1,0:T(8,128)} %all-to-all-done.field, f32[16,256,128]{2,1,0:T(8,128)} %bitcast.233, bf16[256,256]{1,0:T(8,128)(2,1)S(1)} %get-tuple-element.113.high_table.refs_4_, ...), custom_call_target="tpu_custom_call" | custom-call | flops 805306368 | bytes 10485760 | tf_op jit(solution)/shard_map/depth_out/pallas_call | solution.py:553
  203.8 1.3 copy-done.16
  205.1 6.9 %pick_block.3.refs_1_ = f32[2,256,1,128]{3,2,1,0:T(1,128)S(1)} custom-call(s32[256,3]{1,0:T(8,128)S(1)} %pad_add_fusion.1.starts, s32[3]{0:T(128)S(1)} %get-tuple-element.108.corner, s32[256,2,128]{2,1,0:T(2,128)S(1)} %pad_add_fusion.spots, f32[2,256,8,128]{3,2,1,0:T(8,128)S(1)} %bitcast.225), custom_call_target="tpu_custom_call" | custom-call | flops 16777216 | bytes 16777216 | tf_op jit(solution)/shard_map/pick_block/pallas_call | solution.py:327
  212.1 1.9 fusion.11
  215.7 1.2 copy.212
  218.4 3.2 constant_dynamic-update-slice_fusion.refs_0_
  221.6 1.8 append.1
  223.5 6.7 %all-to-all-start.2 = ((f32[32,136,128]{2,1,0:T(8,128)}), f32[32,136,128]{2,1,0:T(8,128)}, u32[]{:S(2)}, u32[]{:S(2)}) async-start(f32[32,136,128]{2,1,0:T(8,128)} %append.1), calls=%async_computation.2 | async-start | bytes 4456448 | tf_op jit(solution)/shard_map/all_to_all | solution.py:62
  230.1 3.5 depth_back.2
  233.7 1.3 copy-done.9
  235.0 47.4 %all-to-all-done.2.refs_1_ = f32[32,136,128]{2,1,0:T(8,128)} async-done(((f32[32,136,128]{2,1,0:T(8,128)}), f32[32,136,128]{2,1,0:T(8,128)}, u32[]{:S(2)}, u32[]{:S(2)}) %all-to-all-start.2) | async-done | bytes 2228256 | tf_op jit(solution)/shard_map/all_to_all | solution.py:62
  282.4 4.4 %all-to-all-start.4 = ((f32[16,2,128,128]{3,2,1,0:T(8,128)}), f32[16,2,128,128]{3,2,1,0:T(8,128)}, u32[]{:S(2)}, u32[]{:S(2)}) async-start(f32[16,2,128,128]{3,2,1,0:T(8,128)} %copy-done.9), calls=%async_computation.4 | async-start | bytes 4194304 | tf_op jit(solution)/shard_map/all_to_all | solution.py:62
  286.9 4.8 %slice_bitcast_fusion = (f32[16,32,8,128]{3,2,1,0:T(8,128)}, f32[16,32,8,128]{3,2,1,0:T(8,128)}) fusion(f32[2,16,256,128]{3,2,1,0:T(8,128)} %constant_dynamic-update-slice_fusion.refs_0_), kind=kLoop, calls=%fused_computation.12 | loop fusion | bytes 8388608 | tf_op jit(solution)/shard_map/reshape;squeeze | solution.py:295
  293.3 1.6 copy-done.11
  294.8 3.8 put.5
  299.1 3.8 put.4
  302.9 2.4 pad_maximum_fusion.refs_6_
  306.0 3.6 depth_back.3
  311.5 16.5 %all-to-all-done.4 = f32[16,2,128,128]{3,2,1,0:T(8,128)} async-done(((f32[16,2,128,128]{3,2,1,0:T(8,128)}), f32[16,2,128,128]{3,2,1,0:T(8,128)}, u32[]{:S(2)}, u32[]{:S(2)}) %all-to-all-start.4) | async-done | bytes 2097184 | tf_op jit(solution)/shard_map/all_to_all | solution.py:62
  327.9 11.2 %all-to-all-start.5 = ((f32[16,2,96,128]{3,2,1,0:T(8,128)}), f32[16,2,96,128]{3,2,1,0:T(8,128)}, u32[]{:S(2)}, u32[]{:S(2)}) async-start(f32[16,2,96,128]{3,2,1,0:T(8,128)} %copy-done.18), calls=%async_computation.5 | async-start | bytes 3145728 | tf_op jit(solution)/shard_map/all_to_all | solution.py:62
  339.2 2.3 fusion.4
  342.7 28.6 %all-to-all-done.5 = f32[16,2,96,128]{3,2,1,0:T(8,128)} async-done(((f32[16,2,96,128]{3,2,1,0:T(8,128)}), f32[16,2,96,128]{3,2,1,0:T(8,128)}, u32[]{:S(2)}, u32[]{:S(2)}) %all-to-all-start.5) | async-done | bytes 1572896 | tf_op jit(solution)/shard_map/all_to_all | solution.py:62
  371.2 2.0 fusion.9
  374.1 9.2 %all-to-all-start.6 = ((f32[16,2,32,128]{3,2,1,0:T(8,128)}), f32[16,2,32,128]{3,2,1,0:T(8,128)}, u32[]{:S(2)}, u32[]{:S(2)}) async-start(f32[16,2,32,128]{3,2,1,0:T(8,128)} %tie.9), calls=%async_computation.6 | async-start | bytes 1048576 | tf_op jit(solution)/shard_map/all_to_all | solution.py:62
  384.3 13.5 %all-to-all-done.6 = f32[16,2,32,128]{3,2,1,0:T(8,128)} async-done(((f32[16,2,32,128]{3,2,1,0:T(8,128)}), f32[16,2,32,128]{3,2,1,0:T(8,128)}, u32[]{:S(2)}, u32[]{:S(2)}) %all-to-all-start.6) | async-done | bytes 524320 | tf_op jit(solution)/shard_map/all_to_all | solution.py:62
  397.8 1.3 fusion.16
  400.2 3.9 collective-permute-done.13.refs_4_
  404.1 3.7 join.2.refs_5_
  408.9 2.0 join.3
  (181 shorter events, 34.3 us)
Async XLA Ops:
  1.5 13.7 %collective-permute-start = (f32[16,6,128]{2,0,1:T(8,128)S(1)}, f32[16,6,128]{2,0,1:T(8,128)S(1)}, u32[]{:S(2)}, u32[]{:S(2)}) collective-permute-start(f32[16,6,128]{2,0,1:T(8,128)S(1)} %pad_maximum_fusion.7), channel_id=1, source_target_pairs={{0,1},{1,2},{2,3},{3,4},{4,5},{5,6},{6,7},{7,8},{8,9},{9,10},{10,1... | collective-permute-start | bytes 147464 | tf_op jit(solution)/shard_map/ppermute | solution.py:651
  1.9 13.9 %collective-permute-start.1 = (f32[16,6,128]{2,0,1:T(8,128)S(1)}, f32[16,6,128]{2,0,1:T(8,128)S(1)}, u32[]{:S(2)}, u32[]{:S(2)}) collective-permute-start(f32[16,6,128]{2,0,1:T(8,128)S(1)} %pad_maximum_fusion.7), channel_id=1, source_target_pairs={{0,15},{1,0},{2,1},{3,2},{4,3},{5,4},{6,5},{7,6},{8,7},{9,8},{10,9... | collective-permute-start | bytes 147464 | tf_op jit(solution)/shard_map/ppermute | solution.py:651
  7.0 26.9 %collective-permute-start.3 = (f32[16,6,128]{2,0,1:T(8,128)S(1)}, f32[16,6,128]{2,0,1:T(8,128)S(1)}, u32[]{:S(2)}, u32[]{:S(2)}) collective-permute-start(f32[16,6,128]{2,0,1:T(8,128)S(1)} %pad_maximum_fusion.7), channel_id=1, source_target_pairs={{0,8},{1,9},{2,10},{3,11},{4,12},{5,13},{6,14},{7,15},{8,0},{9,1},... | collective-permute-start | bytes 147464 | tf_op jit(solution)/shard_map/ppermute | solution.py:38
  8.2 25.6 %collective-permute-start.2 = (f32[16,6,128]{2,0,1:T(8,128)S(1)}, f32[16,6,128]{2,0,1:T(8,128)S(1)}, u32[]{:S(2)}, u32[]{:S(2)}) collective-permute-start(f32[16,6,128]{2,0,1:T(8,128)S(1)} %pad_maximum_fusion.7), channel_id=1, source_target_pairs={{0,4},{1,5},{2,6},{3,7},{4,0},{5,1},{6,2},{7,3},{8,12},{9,13},{10,... | collective-permute-start | bytes 147464 | tf_op jit(solution)/shard_map/ppermute | solution.py:38
  9.7 24.1 %collective-permute-start.4 = (f32[16,6,128]{2,0,1:T(8,128)S(1)}, f32[16,6,128]{2,0,1:T(8,128)S(1)}, u32[]{:S(2)}, u32[]{:S(2)}) collective-permute-start(f32[16,6,128]{2,0,1:T(8,128)S(1)} %pad_maximum_fusion.7), channel_id=1, source_target_pairs={{0,12},{1,13},{2,14},{3,15},{4,8},{5,9},{6,10},{7,11},{8,4},{9,5},... | collective-permute-start | bytes 147464 | tf_op jit(solution)/shard_map/ppermute | solution.py:38
  13.9 1.4 copy-start.7
  16.5 45.0 %all-to-all-start.1 = ((f32[16,16,16,128]{3,2,1,0:T(8,128)}), f32[16,16,16,128]{3,2,1,0:T(8,128)S(1)}, u32[]{:S(2)}, u32[]{:S(2)}) async-start(f32[16,16,16,128]{3,2,1,0:T(8,128)} %tie.6), calls=%async_computation.1 | async-start | bytes 4194304 | tf_op jit(solution)/shard_map/all_to_all | solution.py:62
  22.5 2.2 copy-start.3
  28.8 79.9 %copy-start.26 = (f32[48,4,128]{2,0,1:T(8,128)}, f32[48,4,128]{2,0,1:T(8,128)S(1)}, u32[]{:S(2)}) copy-start(f32[48,4,128]{2,0,1:T(8,128)S(1)} %pad_maximum_fusion.4) | copy-start | bytes 294916
  29.3 30.8 %collective-permute-start.9 = (f32[3,16,4]{2,1,0:T(8,128)S(1)}, f32[3,16,4]{2,1,0:T(8,128)S(1)}, u32[]{:S(2)}, u32[]{:S(2)}) collective-permute-start(f32[3,16,4]{2,1,0:T(8,128)S(1)} %bitcast.263), channel_id=1, source_target_pairs={{0,1},{1,2},{2,3},{3,4},{4,5},{5,6},{6,7},{7,8},{8,9},{9,10},{10,1... | collective-permute-start | bytes 2312 | tf_op jit(solution)/shard_map/ppermute | solution.py:651
  29.6 30.5 %collective-permute-start.8 = (f32[3,16,4]{2,1,0:T(8,128)S(1)}, f32[3,16,4]{2,1,0:T(8,128)S(1)}, u32[]{:S(2)}, u32[]{:S(2)}) collective-permute-start(f32[3,16,4]{2,1,0:T(8,128)S(1)} %bitcast.264), channel_id=1, source_target_pairs={{0,15},{1,0},{2,1},{3,2},{4,3},{5,4},{6,5},{7,6},{8,7},{9,8},{10,9... | collective-permute-start | bytes 2312 | tf_op jit(solution)/shard_map/ppermute | solution.py:651
  33.9 3.3 copy-start.23
  37.2 2.0 copy-start.4
  60.8 13.9 %copy-start.28 = (f32[3]{0:T(128)S(1)}, f32[3]{0:T(128)}, u32[]{:S(2)}) copy-start(f32[3]{0:T(128)} %param.19) | copy-start | bytes 40
  60.8 20.6 %copy-start.24 = (f32[4,16,6,128]{3,2,1,0:T(8,128)S(1)}, f32[4,16,6,128]{3,2,1,0:T(8,128)}, u32[]{:S(2)}) copy-start(f32[4,16,6,128]{3,2,1,0:T(8,128)} %copy-done.23) | copy-start | bytes 589828
  61.5 1.4 copy-start.22
  62.9 107.0 %all-to-all-start = ((f32[32,256,128]{2,1,0:T(8,128)}), f32[32,256,128]{2,1,0:T(8,128)}, u32[]{:S(2)}, u32[]{:S(2)}) async-start(f32[32,256,128]{2,1,0:T(8,128)} %tie.5), calls=%async_computation | async-start | bytes 8388608 | tf_op jit(solution)/shard_map/all_to_all | solution.py:62
  81.4 56.9 %collective-permute-start.7 = (f32[4,16,6,128]{3,2,1,0:T(8,128)S(1)}, f32[4,16,6,128]{3,2,1,0:T(8,128)S(1)}, u32[]{:S(2)}, u32[]{:S(2)}) collective-permute-start(f32[4,16,6,128]{3,2,1,0:T(8,128)S(1)} %copy-done.24), channel_id=1, source_target_pairs={{0,3},{1,2},{2,1},{3,0},{4,7},{5,6},{6,5},{7,4},{8,11},{9,10},{10,... | collective-permute-start | bytes 589832 | tf_op jit(solution)/shard_map/ppermute | solution.py:38
  82.9 55.3 %collective-permute-start.6 = (f32[4,16,6,128]{3,2,1,0:T(8,128)S(1)}, f32[4,16,6,128]{3,2,1,0:T(8,128)S(1)}, u32[]{:S(2)}, u32[]{:S(2)}) collective-permute-start(f32[4,16,6,128]{3,2,1,0:T(8,128)S(1)} %copy-done.24), channel_id=1, source_target_pairs={{0,2},{1,3},{2,0},{3,1},{4,6},{5,7},{6,4},{7,5},{8,10},{9,11},{10,... | collective-permute-start | bytes 589832 | tf_op jit(solution)/shard_map/ppermute | solution.py:38
  83.3 54.8 %collective-permute-start.5 = (f32[4,16,6,128]{3,2,1,0:T(8,128)S(1)}, f32[4,16,6,128]{3,2,1,0:T(8,128)S(1)}, u32[]{:S(2)}, u32[]{:S(2)}) collective-permute-start(f32[4,16,6,128]{3,2,1,0:T(8,128)S(1)} %copy-done.24), channel_id=1, source_target_pairs={{0,1},{1,0},{2,3},{3,2},{4,5},{5,4},{6,7},{7,6},{8,9},{9,8},{10,11... | collective-permute-start | bytes 589832 | tf_op jit(solution)/shard_map/ppermute | solution.py:38
  83.3 15.6 %copy-start.25 = (f32[3,16,4]{2,1,0:T(8,128)S(1)}, f32[3,16,4]{2,1,0:T(8,128)}, u32[]{:S(2)}) copy-start(f32[3,16,4]{2,1,0:T(8,128)} %add_add_fusion) | copy-start | bytes 2308
  83.3 15.6 %copy-start.29 = (f32[4]{0:T(128)S(1)}, f32[4]{0:T(128)}, u32[]{:S(2)}) copy-start(f32[4]{0:T(128)} %param.18) | copy-start | bytes 52
  97.0 2.0 copy-start.8
  104.6 4.1 copy-start.1
  122.6 2.8 copy-start
  125.4 93.1 %collective-permute-start.10 = (f32[1,16,256,128]{3,2,1,0:T(8,128)}, f32[1,16,256,128]{3,2,1,0:T(8,128)}, u32[]{:S(2)}, u32[]{:S(2)}) collective-permute-start(f32[1,16,256,128]{3,2,1,0:T(8,128)} %constant_dynamic-slice_fusion), channel_id=1, source_target_pairs={{0,16},{16,0},{1,17},{17,1},{2,18},{18,2},{3,19},{19,3},{4,20},{20... | collective-permute-start | bytes 6291464 | tf_op jit(solution)/shard_map/ppermute | solution.py:54
  131.1 1.4 copy-start.6
  136.6 1.4 copy-start.5
  138.4 1.0 copy-start.19
  169.9 53.5 %all-to-all-start.3 = ((f32[32,128,128]{2,1,0:T(8,128)}), f32[32,128,128]{2,1,0:T(8,128)S(1)}, u32[]{:S(2)}, u32[]{:S(2)}) async-start(f32[32,128,128]{2,1,0:T(8,128)} %tie.8), calls=%async_computation.3 | async-start | bytes 4194304 | tf_op jit(solution)/shard_map/all_to_all | solution.py:62
  185.0 1.3 copy-start.14
  186.4 6.9 %copy-start.20 = (f32[4,4,16,6,128]{4,3,2,0,1:T(8,128)S(1)}, f32[4,4,16,6,128]{4,3,2,0,1:T(8,128)}, u32[]{:S(2)}) copy-start(f32[4,4,16,6,128]{4,3,2,0,1:T(8,128)} %copy-done.19) | copy-start | bytes 2359300
  203.8 1.3 copy-start.16
  205.1 6.9 %copy-start.21 = (f32[4,4,16,6,128]{4,3,2,0,1:T(8,128)S(1)}, f32[4,4,16,6,128]{4,3,2,0,1:T(8,128)}, u32[]{:S(2)}) copy-start(f32[4,4,16,6,128]{4,3,2,0,1:T(8,128)} %copy-done.19) | copy-start | bytes 2359300
  212.1 5.3 %copy-start.13 = (f32[2,256,1,128]{3,2,1,0:T(1,128)}, f32[2,256,1,128]{3,2,1,0:T(1,128)S(1)}, u32[]{:S(2)}) copy-start(f32[2,256,1,128]{3,2,1,0:T(1,128)S(1)} %pick_block.3.refs_1_) | copy-start | bytes 786436
  223.5 59.0 %all-to-all-start.2 = ((f32[32,136,128]{2,1,0:T(8,128)}), f32[32,136,128]{2,1,0:T(8,128)}, u32[]{:S(2)}, u32[]{:S(2)}) async-start(f32[32,136,128]{2,1,0:T(8,128)} %append.1), calls=%async_computation.2 | async-start | bytes 4456448 | tf_op jit(solution)/shard_map/all_to_all | solution.py:62
  233.7 1.3 copy-start.9
  282.4 45.5 %all-to-all-start.4 = ((f32[16,2,128,128]{3,2,1,0:T(8,128)}), f32[16,2,128,128]{3,2,1,0:T(8,128)}, u32[]{:S(2)}, u32[]{:S(2)}) async-start(f32[16,2,128,128]{3,2,1,0:T(8,128)} %copy-done.9), calls=%async_computation.4 | async-start | bytes 4194304 | tf_op jit(solution)/shard_map/all_to_all | solution.py:62
  286.9 5.8 %copy-start.27 = (f32[48,4,128]{2,0,1:T(8,128)S(1)}, f32[48,4,128]{2,0,1:T(8,128)}, u32[]{:S(2)}) copy-start(f32[48,4,128]{2,0,1:T(8,128)} %copy-done.26) | copy-start | bytes 294916
  293.2 1.6 copy-start.11
  294.8 4.2 %copy-start.10 = (f32[16,32,8,128]{3,2,1,0:T(8,128)S(1)}, f32[16,32,8,128]{3,2,1,0:T(8,128)}, u32[]{:S(2)}) copy-start(f32[16,32,8,128]{3,2,1,0:T(8,128)} %get-tuple-element.81.base) | copy-start | bytes 6291460
  302.9 2.8 copy-start.2
  302.9 3.1 copy-start.17
  309.5 0.8 copy-start.15
  310.3 1.1 copy-start.18
  327.9 43.3 %all-to-all-start.5 = ((f32[16,2,96,128]{3,2,1,0:T(8,128)}), f32[16,2,96,128]{3,2,1,0:T(8,128)}, u32[]{:S(2)}, u32[]{:S(2)}) async-start(f32[16,2,96,128]{3,2,1,0:T(8,128)} %copy-done.18), calls=%async_computation.5 | async-start | bytes 3145728 | tf_op jit(solution)/shard_map/all_to_all | solution.py:62
  341.6 32.5 %collective-permute-start.11 = (f32[16,16,8,128]{3,2,1,0:T(8,128)S(1)}, f32[16,16,8,128]{3,2,1,0:T(8,128)}, u32[]{:S(2)}, u32[]{:S(2)}) collective-permute-start(f32[16,16,8,128]{3,2,1,0:T(8,128)S(1)} %broadcast_multiply_fusion.refs_1_), channel_id=1, source_target_pairs={{0,16},{16,0},{1,17},{17,1},{2,18},{18,2},{3,19},{19,3},{4,20},{20... | collective-permute-start | bytes 3145736 | tf_op jit(solution)/shard_map/ppermute | solution.py:799
  374.1 23.7 %all-to-all-start.6 = ((f32[16,2,32,128]{3,2,1,0:T(8,128)}), f32[16,2,32,128]{3,2,1,0:T(8,128)}, u32[]{:S(2)}, u32[]{:S(2)}) async-start(f32[16,2,32,128]{3,2,1,0:T(8,128)} %tie.9), calls=%async_computation.6 | async-start | bytes 1048576 | tf_op jit(solution)/shard_map/all_to_all | solution.py:62
  383.3 20.7 %collective-permute-start.13 = (f32[12,16,8,128]{3,2,1,0:T(8,128)}, f32[12,16,8,128]{3,2,1,0:T(8,128)}, u32[]{:S(2)}, u32[]{:S(2)}) collective-permute-start(f32[12,16,8,128]{3,2,1,0:T(8,128)} %broadcast_multiply_fusion.1.refs_2_.refs_3_), channel_id=1, source_target_pairs={{0,16},{16,0},{1,17},{17,1},{2,18},{18,2},{3,19},{19,3},{4,20},{20... | collective-permute-start | bytes 2359304 | tf_op jit(solution)/shard_map/ppermute | solution.py:799
  397.8 6.2 %copy-start.12 = (f32[12,16,8,128]{3,2,1,0:T(8,128)S(1)}, f32[12,16,8,128]{3,2,1,0:T(8,128)}, u32[]{:S(2)}) copy-start(f32[12,16,8,128]{3,2,1,0:T(8,128)} %broadcast_multiply_fusion.1.refs_2_.refs_3_) | copy-start | bytes 2359300
  399.1 9.8 %collective-permute-start.12 = (f32[4,16,8,128]{3,2,1,0:T(8,128)S(1)}, f32[4,16,8,128]{3,2,1,0:T(8,128)S(1)}, u32[]{:S(2)}, u32[]{:S(2)}) collective-permute-start(f32[4,16,8,128]{3,2,1,0:T(8,128)S(1)} %broadcast_multiply_fusion.2.refs_3_), channel_id=1, source_target_pairs={{0,16},{16,0},{1,17},{17,1},{2,18},{18,2},{3,19},{19,3},{4,20},{20... | collective-permute-start | bytes 786440 | tf_op jit(solution)/shard_map/ppermute | solution.py:799

commit v7 on v6

--- a/solution.py
+++ b/solution.py
@@ -55,7 +55,7 @@
         if others:
             got = tie(got, *others)
         out = lax.dynamic_update_slice_in_dim(out, got, place ^ apart, 0)
-    return out
+    return out, got
 
 
 def exchange(block, axis):
@@ -719,7 +719,7 @@
         for i in range(chunks - 1):
             g_gots.append(everyones(tie(packed([pv, u], [i], 0, base), every)))
 
-        cb = []
+        cb, picked = [], []
         for i in range(chunks):
             first_row = grid_pos * rows + i * some
             if fast:
@@ -740,10 +740,11 @@
                     values.append(pick(total, every_starts, corner, every_spots, padded))
                 values = jnp.stack(values)
             cb.append((c, b))
-            second = second + jnp.einsum("oaj,apj->oap", values[:, :, 0], every_projs, precision=PRECISE)
+            picked.append(values)
         if put_late:
-            mixed = trade(base, "orb", values)
-        second = c2_8 * second
+            mixed, _ = trade(base, "orb", values)
+        values = jnp.einsum("oaj,apj->oap", functools.reduce(jnp.add, picked)[:, :, 0], every_projs, precision=PRECISE)
+        second = c2_8 * (second + values)
         if fast:
             each = second.reshape(orbitals, grid_count, per_dev, projs_each)
             each = jnp.stack([jnp.roll(each, 1, axis=1), each, jnp.roll(each, -1, axis=1)], axis=2)
@@ -766,7 +767,7 @@
             base = jnp.moveaxis(base, 0, 2).reshape(planes, rows_y, cols_x)
             own = lax.dynamic_index_in_dim(second, orb_pos, 0, keepdims=False)
             q = put_near(own, base).reshape(planes, rows_y, orb_groups, part)
-            q_all = trade(jnp.moveaxis(q, 2, 0), "orb")
+            q_all, _ = trade(jnp.moveaxis(q, 2, 0), "orb")
         q_all = q_all.reshape(orb_groups, planes, grid_count, chunks, some, part)
 
         sends = []
@@ -786,7 +787,7 @@
             for k, (start, stop) in enumerate(cuts[i]):
                 send = sends[i][k]
                 if len(kept) > 1:
-                    send = tie(send, *([pairs[0][1]] if pairs else kept[:1]), kept[-1])
+                    send = tie(send, *([pairs[0][1]] if pairs else kept[:1]))
                 got = exchange(send, "grid")
                 m = got.reshape(grid_count, orbitals, stop - start, some, part)
                 filtered = q_all[:, start:stop, :, i] + m.transpose(1, 2, 0, 3, 4)

time: 413 us -> 409 us (level)
    all_to_all x7, waiting for transfers between devices: 136 us -> 107 us  [exchange(): return lax.all_to_all(block, axis, split_axis=0, concat_axis=0, tiled=True)]
    ppermute x3, waiting for transfers between devices: 5.12 us -> 32.5 us  [local(): pairs.append((own, lax.ppermute(own, 'orb', [(0, 1), (1, 0)])))]
  transfers between devices with their start and end apart: 21 -> 21, of which waited for: 9 -> 11; matrix products, arithmetic and copies ran while one was open for 12% -> 12% of each run, Pallas kernels for 24% -> 25%
where the time goes in v7:
time: 409 us; the launch traced here: 406 us
  waiting for transfers between devices  160 us (39%)
  Pallas kernels  103 us (25%)
  starting transfers between devices  68.3 us (17%)
  local copies, waits for them, and re-layouts  44 us (11%)
  other arithmetic  23.9 us (6%)
  matrix products  4.14 us (1%)
    all_to_all x7, waiting for transfers between devices, exchange(): return lax.all_to_all(block, axis, split_axis=0, concat_axis=0, tiled=True)  107 us
    all_to_all x7, starting transfers between devices, exchange(): return lax.all_to_all(block, axis, split_axis=0, concat_axis=0, tiled=True)  47.3 us
    ppermute x3, waiting for transfers between devices, local(): pairs.append((own, lax.ppermute(own, 'orb', [(0, 1), (1, 0)])))  32.5 us
    unnamed x65, local copies, waits for them, and re-layouts  24.9 us
    ppermute x4, waiting for transfers between devices, shifted(): lax.ppermute(block, 'grid', [(i, (i + step) % grid_count) for i in range(...  20.5 us
    pallas_call x2, Pallas kernels, pick_block(): pl.pallas_call(functools.partial(pick_block_kernel, total), out_shape=jax...  14.9 us
    pallas_call x3, Pallas kernels, put(): pl.pallas_call(functools.partial(put_kernel, total), out_shape=jax.ShapeD...  14 us
    pallas_call x1, Pallas kernels, planar_first(): pl.pallas_call(ordered(first_kernel, 4, len(others)), grid=field.shape[:1...  13.6 us
  transfers between devices with their start and end apart: 21, of which 11 were waited for; matrix products, arithmetic and copies ran while one was open for 12% of the time, Pallas kernels for 25%

profile of v7, /device:TPU:0, one launch (start us, length us, event | category | flops | bytes accessed | tf_op | source)
XLA Modules:
  0.0 406.5 jit_solution(13599892553339270100)
XLA Ops:
  1.9 5.0 %collective-permute-start.1 = (f32[16,6,128]{2,0,1:T(8,128)S(1)}, f32[16,6,128]{2,0,1:T(8,128)S(1)}, u32[]{:S(2)}, u32[]{:S(2)}) collective-permute-start(f32[16,6,128]{2,0,1:T(8,128)S(1)} %pad_maximum_fusion.7), channel_id=1, source_target_pairs={{0,15},{1,0},{2,1},{3,2},{4,3},{5,4},{6,5},{7,6},{8,7},{9,8},{10,9... | collective-permute-start | bytes 147464 | tf_op jit(solution)/shard_map/ppermute | solution.py:651
  7.0 1.2 collective-permute-start.3
  8.2 1.6 collective-permute-start.2
  9.7 1.6 collective-permute-start.4
  11.4 2.4 pack_part.1
  13.9 1.3 copy-done.7
  16.5 3.7 all-to-all-start.1
  22.6 2.2 copy-done.3
  24.7 4.5 %pick.2 = f32[48,1,128]{2,1,0:T(1,128)S(1)} custom-call(s32[48,3]{1,0:T(8,128)S(1)} %pad_add_fusion.3.starts, s32[3]{0:T(128)S(1)} %stack.72.corner, s32[48,2,128]{2,1,0:T(2,128)S(1)} %pad_add_fusion.2.refs_1_.spots.refs_4_, f32[16,32,8,256]{3,2,1,0:T(8,128)S(1)} %bitcast.214), custom_call_target="tpu_custom_call" | custom-call | flops 16777216 | bytes 16777216 | tf_op jit(solution)/shard_map/pick/pallas_call | solution.py:314
  29.8 4.4 %collective-permute-start.8 = (f32[3,16,4]{2,1,0:T(8,128)S(1)}, f32[3,16,4]{2,1,0:T(8,128)S(1)}, u32[]{:S(2)}, u32[]{:S(2)}) collective-permute-start(f32[3,16,4]{2,1,0:T(8,128)S(1)} %bitcast.258), channel_id=1, source_target_pairs={{0,15},{1,0},{2,1},{3,2},{4,3},{5,4},{6,5},{7,6},{8,7},{9,8},{10,9... | collective-permute-start | bytes 2312 | tf_op jit(solution)/shard_map/ppermute | solution.py:651
  34.4 3.3 pack.3
  37.6 2.0 copy-done.4
  39.6 20.5 %collective-permute-done.9 = f32[3,16,4]{2,1,0:T(8,128)S(1)} collective-permute-done((f32[3,16,4]{2,1,0:T(8,128)S(1)}, f32[3,16,4]{2,1,0:T(8,128)S(1)}, u32[]{:S(2)}, u32[]{:S(2)}) %collective-permute-start.9) | collective-permute-done | bytes 800 | tf_op jit(solution)/shard_map/ppermute | solution.py:651
  61.5 1.4 copy-done.20
  62.9 11.7 %all-to-all-start = ((f32[32,256,128]{2,1,0:T(8,128)}), f32[32,256,128]{2,1,0:T(8,128)}, u32[]{:S(2)}, u32[]{:S(2)}) async-start(f32[32,256,128]{2,1,0:T(8,128)} %tie.5), calls=%async_computation | async-start | bytes 8388608 | tf_op jit(solution)/shard_map/all_to_all | solution.py:62
  81.4 1.5 collective-permute-start.7
  83.4 13.6 %planar_first.1 = (f32[16,256,256]{2,1,0:T(8,128)S(1)}, f32[16,256,256]{2,1,0:T(8,128)}) custom-call(f32[16,256,256]{2,1,0:T(8,128)} %bitcast.212, f32[16,256,256]{2,1,0:T(8,128)} %potential.1, bf16[2,256,256]{2,1,0:T(8,128)(2,1)S(1)} %get-tuple-element.115.refs_2_.high_tables, bf16[2,256,256]{2,1,0:T(8,128)(2,1)S(1)} %get-tuple-element.116.refs_3_.low_tables, ...), custom_call_target="tpu_custom_call" | custom-call | flops 3221225472 | bytes 16777216 | tf_op jit(solution)/shard_map/planar_first/pallas_call | solution.py:369
  97.0 2.0 copy-done.8
  99.4 5.6 %put.3.field = f32[16,32,8,256]{3,2,1,0:T(8,128)S(1)} custom-call(s32[48,3]{1,0:T(8,128)S(1)} %pad_add_fusion.3.starts, s32[3]{0:T(128)S(1)} %stack.72.corner, s32[48,2,128]{2,1,0:T(2,128)S(1)} %pad_add_fusion.2.refs_1_.spots.refs_4_, f32[48,1,128]{2,1,0:T(1,128)S(1)} %fusion.69.spread, f32[16,32,8,256]{3,2,1,0:T(8,128)} %bitcast.229), custom_call_target="tpu_custom_call" | custom-call | flops 16777216 | bytes 16777216 | tf_op jit(solution)/shard_map/put/pallas_call | solution.py:341
  105.0 4.5 %pick.3 = f32[48,1,128]{2,1,0:T(1,128)S(1)} custom-call(s32[48,3]{1,0:T(8,128)S(1)} %pad_add_fusion.3.starts, s32[3]{0:T(128)S(1)} %stack.72.corner, s32[48,2,128]{2,1,0:T(2,128)S(1)} %pad_add_fusion.2.refs_1_.spots.refs_4_, f32[16,32,8,256]{3,2,1,0:T(8,128)S(1)} %put.3.field), custom_call_target="tpu_custom_call" | custom-call | flops 16777216 | bytes 16777216 | tf_op jit(solution)/shard_map/pick/pallas_call | solution.py:314
  110.4 13.0 %planar_second.1.refs_2_ = f32[2,16,256,128]{3,2,1,0:T(8,128)S(1)} custom-call(f32[3]{0:T(128)S(1)} %pad_maximum_fusion.9.weights, f32[16,256,256]{2,1,0:T(8,128)} %bitcast.200, f32[16,256,256]{2,1,0:T(8,128)} %bitcast.213, f32[16,256,256]{2,1,0:T(8,128)} %potential.1, bf16[2,256,256]{2,1,0:T(8,128)(2,1)S(1)} %get-tuple-element.115.refs_2_.high_tables, ...), custom_call_target="tpu_custom_call" | custom-call | flops 3221225472 | bytes 16777216 | tf_op jit(solution)/shard_map/planar_second/pallas_call | solution.py:385
  123.4 1.7 constant_dynamic-slice_fusion
  126.1 1.7 collective-permute-start.10
  127.8 4.1 %pack.5 = f32[2,16,128,128]{3,2,1,0:T(8,128)S(1)} custom-call(f32[16,256,256]{2,1,0:T(8,128)} %copy-done.8, f32[16,256,256]{2,1,0:T(8,128)} %bitcast.201, f32[2,16,256,128]{3,2,1,0:T(8,128)} %copy-done), custom_call_target="tpu_custom_call" | custom-call | flops 524288 | bytes 4194304 | tf_op jit(solution)/shard_map/pack/pallas_call | solution.py:459
  131.9 1.4 copy-done.6
  133.3 4.1 %pack.4 = f32[2,16,136,128]{3,2,1,0:T(8,128)S(1)} custom-call(f32[16,256,256]{2,1,0:T(8,128)} %copy-done.8, f32[16,256,256]{2,1,0:T(8,128)} %bitcast.202, f32[2,16,256,128]{3,2,1,0:T(8,128)} %copy-done), custom_call_target="tpu_custom_call" | custom-call | flops 524288 | bytes 4194304 | tf_op jit(solution)/shard_map/pack/pallas_call | solution.py:459
  137.4 1.4 copy-done.5
  140.2 1.3 slice_convert_fusion
  141.9 28.1 %all-to-all-done.field = f32[32,256,128]{2,1,0:T(8,128)} async-done(((f32[32,256,128]{2,1,0:T(8,128)}), f32[32,256,128]{2,1,0:T(8,128)}, u32[]{:S(2)}, u32[]{:S(2)}) %all-to-all-start) | async-done | bytes 4194336 | tf_op jit(solution)/shard_map/all_to_all | solution.py:62
  169.9 2.9 all-to-all-start.3
  176.0 3.2 fusion.58
  179.6 5.4 %depth_out.3 = (f32[2,2048,128]{2,1,0:T(8,128)S(1)}, f32[2,2048,128]{2,1,0:T(8,128)S(1)}, f32[2,2048,128]{2,1,0:T(8,128)}) custom-call(f32[2]{0:T(128)S(1)} %pad_maximum_fusion.8.weights.refs_0_, f32[32,256,128]{2,1,0:T(8,128)} %all-to-all-done.field, f32[16,256,128]{2,1,0:T(8,128)} %bitcast.221, bf16[256,256]{1,0:T(8,128)(2,1)S(1)} %get-tuple-element.113.high_table.refs_4_, ...), custom_call_target="tpu_custom_call" | custom-call | flops 805306368 | bytes 10485760 | tf_op jit(solution)/shard_map/depth_out/pallas_call | solution.py:553
  185.1 1.3 copy-done.17
  186.4 7.6 %pick_block.3.refs_1_ = f32[2,256,1,128]{3,2,1,0:T(1,128)S(1)} custom-call(s32[256,3]{1,0:T(8,128)S(1)} %pad_add_fusion.1.starts, s32[3]{0:T(128)S(1)} %get-tuple-element.108.corner, s32[256,2,128]{2,1,0:T(2,128)S(1)} %pad_add_fusion.spots, f32[2,256,8,128]{3,2,1,0:T(8,128)S(1)} %bitcast.220), custom_call_target="tpu_custom_call" | custom-call | flops 16777216 | bytes 16777216 | tf_op jit(solution)/shard_map/pick_block/pallas_call | solution.py:327
  194.0 5.5 %depth_out.2 = (f32[2,2048,128]{2,1,0:T(8,128)S(1)}, f32[2,2048,128]{2,1,0:T(8,128)S(1)}, f32[2,2048,128]{2,1,0:T(8,128)}) custom-call(f32[2]{0:T(128)S(1)} %pad_maximum_fusion.8.weights.refs_0_, f32[32,256,128]{2,1,0:T(8,128)} %all-to-all-done.field, f32[16,256,128]{2,1,0:T(8,128)} %bitcast.222, bf16[256,256]{1,0:T(8,128)(2,1)S(1)} %get-tuple-element.113.high_table.refs_4_, ...), custom_call_target="tpu_custom_call" | custom-call | flops 805306368 | bytes 10485760 | tf_op jit(solution)/shard_map/depth_out/pallas_call | solution.py:553
  199.5 1.3 copy-done.15
  200.8 7.3 %pick_block.2 = f32[2,256,1,128]{3,2,1,0:T(1,128)S(1)} custom-call(s32[256,3]{1,0:T(8,128)S(1)} %pad_add_fusion.1.starts, s32[3]{0:T(128)S(1)} %get-tuple-element.107.corner, s32[256,2,128]{2,1,0:T(2,128)S(1)} %pad_add_fusion.spots, f32[2,256,8,128]{3,2,1,0:T(8,128)S(1)} %bitcast.219), custom_call_target="tpu_custom_call" | custom-call | flops 16777216 | bytes 16777216 | tf_op jit(solution)/shard_map/pick_block/pallas_call | solution.py:327
  208.4 1.9 fusion.15
  210.4 3.0 add.388
  216.4 3.2 constant_dynamic-update-slice_fusion.refs_0_
  219.6 1.8 append.1
  222.4 4.0 all-to-all-start.2
  226.4 3.5 depth_back.2
  229.9 1.3 copy-done.11
  231.2 47.6 %all-to-all-done.2.refs_1_ = f32[32,136,128]{2,1,0:T(8,128)} async-done(((f32[32,136,128]{2,1,0:T(8,128)}), f32[32,136,128]{2,1,0:T(8,128)}, u32[]{:S(2)}, u32[]{:S(2)}) %all-to-all-start.2) | async-done | bytes 2228256 | tf_op jit(solution)/shard_map/all_to_all | solution.py:62
  278.9 4.7 %all-to-all-start.4 = ((f32[16,2,128,128]{3,2,1,0:T(8,128)}), f32[16,2,128,128]{3,2,1,0:T(8,128)}, u32[]{:S(2)}, u32[]{:S(2)}) async-start(f32[16,2,128,128]{3,2,1,0:T(8,128)} %copy-done.11), calls=%async_computation.4 | async-start | bytes 4194304 | tf_op jit(solution)/shard_map/all_to_all | solution.py:62
  283.6 4.8 %slice_bitcast_fusion = (f32[16,32,8,128]{3,2,1,0:T(8,128)}, f32[16,32,8,128]{3,2,1,0:T(8,128)}) fusion(f32[2,16,256,128]{3,2,1,0:T(8,128)} %constant_dynamic-update-slice_fusion.refs_0_), kind=kLoop, calls=%fused_computation.12 | loop fusion | bytes 8388608 | tf_op jit(solution)/shard_map/reshape;squeeze | solution.py:295
  289.9 1.6 copy-done.13
  291.5 4.2 %put.5 = f32[16,32,8,128]{3,2,1,0:T(8,128)S(1)} custom-call(s32[48,3]{1,0:T(8,128)S(1)} %pad_add_fusion.3.starts, s32[3]{0:T(128)S(1)} %pad_add_fusion.6.corner, s32[48,2,128]{2,1,0:T(2,128)S(1)} %pad_add_fusion.2.refs_1_.spots.refs_4_, f32[48,1,128]{2,1,0:T(1,128)S(1)} %fusion.63.spread, f32[16,32,8,128]{3,2,1,0:T(8,128)S(1)} %copy-done.13), custom_call_target="tpu_custom_call" | custom-call | flops 16777216 | bytes 16777216 | tf_op jit(solution)/shard_map/put/pallas_call | solution.py:341
  296.2 4.2 %put.4 = f32[16,32,8,128]{3,2,1,0:T(8,128)S(1)} custom-call(s32[48,3]{1,0:T(8,128)S(1)} %pad_add_fusion.3.starts, s32[3]{0:T(128)S(1)} %pad_add_fusion.6.corner, s32[48,2,128]{2,1,0:T(2,128)S(1)} %pad_add_fusion.2.refs_1_.spots.refs_4_, f32[48,1,128]{2,1,0:T(1,128)S(1)} %fusion.65.spread, f32[16,32,8,128]{3,2,1,0:T(8,128)S(1)} %copy-done.12), custom_call_target="tpu_custom_call" | custom-call | flops 16777216 | bytes 16777216 | tf_op jit(solution)/shard_map/put/pallas_call | solution.py:341
  300.3 2.4 pad_maximum_fusion.refs_6_
  303.5 3.6 depth_back.3
  309.0 15.4 %all-to-all-done.4 = f32[16,2,128,128]{3,2,1,0:T(8,128)} async-done(((f32[16,2,128,128]{3,2,1,0:T(8,128)}), f32[16,2,128,128]{3,2,1,0:T(8,128)}, u32[]{:S(2)}, u32[]{:S(2)}) %all-to-all-start.4) | async-done | bytes 2097184 | tf_op jit(solution)/shard_map/all_to_all | solution.py:62
  324.4 11.2 %all-to-all-start.6 = ((f32[16,2,96,128]{3,2,1,0:T(8,128)}), f32[16,2,96,128]{3,2,1,0:T(8,128)}, u32[]{:S(2)}, u32[]{:S(2)}) async-start(f32[16,2,96,128]{3,2,1,0:T(8,128)} %copy-done.19), calls=%async_computation.6 | async-start | bytes 3145728 | tf_op jit(solution)/shard_map/all_to_all | solution.py:62
  335.6 2.3 fusion.4
  339.1 24.5 %collective-permute-done.11.refs_1_.refs_2_ = f32[16,16,8,128]{3,2,1,0:T(8,128)S(1)} collective-permute-done((f32[16,16,8,128]{3,2,1,0:T(8,128)S(1)}, f32[16,16,8,128]{3,2,1,0:T(8,128)S(1)}, u32[]{:S(2)}, u32[]{:S(2)}) %collective-permute-start.11) | collective-permute-done | bytes 1048608 | tf_op jit(solution)/shard_map/ppermute | solution.py:800
  364.6 3.1 all-to-all-done.6
  367.7 9.2 %all-to-all-start.5 = ((f32[16,2,32,128]{3,2,1,0:T(8,128)}), f32[16,2,32,128]{3,2,1,0:T(8,128)}, u32[]{:S(2)}, u32[]{:S(2)}) async-start(f32[16,2,32,128]{3,2,1,0:T(8,128)} %tie.9), calls=%async_computation.5 | async-start | bytes 1048576 | tf_op jit(solution)/shard_map/all_to_all | solution.py:62
  376.8 2.0 fusion.9
  380.8 10.6 %all-to-all-done.5 = f32[16,2,32,128]{3,2,1,0:T(8,128)} async-done(((f32[16,2,32,128]{3,2,1,0:T(8,128)}), f32[16,2,32,128]{3,2,1,0:T(8,128)}, u32[]{:S(2)}, u32[]{:S(2)}) %all-to-all-start.5) | async-done | bytes 524320 | tf_op jit(solution)/shard_map/all_to_all | solution.py:62
  391.4 1.3 fusion.14
  393.7 6.8 %collective-permute-done.13.refs_4_ = f32[12,16,8,128]{3,2,1,0:T(8,128)} collective-permute-done((f32[12,16,8,128]{3,2,1,0:T(8,128)}, f32[12,16,8,128]{3,2,1,0:T(8,128)}, u32[]{:S(2)}, u32[]{:S(2)}) %collective-permute-start.13) | collective-permute-done | bytes 786464 | tf_op jit(solution)/shard_map/ppermute | solution.py:800
  400.5 3.7 join.2.refs_5_
  404.1 1.3 collective-permute-done.12.refs_4_
  (182 shorter events, 34.5 us)
Async XLA Ops:
  1.5 13.7 %collective-permute-start = (f32[16,6,128]{2,0,1:T(8,128)S(1)}, f32[16,6,128]{2,0,1:T(8,128)S(1)}, u32[]{:S(2)}, u32[]{:S(2)}) collective-permute-start(f32[16,6,128]{2,0,1:T(8,128)S(1)} %pad_maximum_fusion.7), channel_id=1, source_target_pairs={{0,1},{1,2},{2,3},{3,4},{4,5},{5,6},{6,7},{7,8},{8,9},{9,10},{10,1... | collective-permute-start | bytes 147464 | tf_op jit(solution)/shard_map/ppermute | solution.py:651
  1.9 13.9 %collective-permute-start.1 = (f32[16,6,128]{2,0,1:T(8,128)S(1)}, f32[16,6,128]{2,0,1:T(8,128)S(1)}, u32[]{:S(2)}, u32[]{:S(2)}) collective-permute-start(f32[16,6,128]{2,0,1:T(8,128)S(1)} %pad_maximum_fusion.7), channel_id=1, source_target_pairs={{0,15},{1,0},{2,1},{3,2},{4,3},{5,4},{6,5},{7,6},{8,7},{9,8},{10,9... | collective-permute-start | bytes 147464 | tf_op jit(solution)/shard_map/ppermute | solution.py:651
  7.0 27.3 %collective-permute-start.3 = (f32[16,6,128]{2,0,1:T(8,128)S(1)}, f32[16,6,128]{2,0,1:T(8,128)S(1)}, u32[]{:S(2)}, u32[]{:S(2)}) collective-permute-start(f32[16,6,128]{2,0,1:T(8,128)S(1)} %pad_maximum_fusion.7), channel_id=1, source_target_pairs={{0,8},{1,9},{2,10},{3,11},{4,12},{5,13},{6,14},{7,15},{8,0},{9,1},... | collective-permute-start | bytes 147464 | tf_op jit(solution)/shard_map/ppermute | solution.py:38
  8.2 26.0 %collective-permute-start.2 = (f32[16,6,128]{2,0,1:T(8,128)S(1)}, f32[16,6,128]{2,0,1:T(8,128)S(1)}, u32[]{:S(2)}, u32[]{:S(2)}) collective-permute-start(f32[16,6,128]{2,0,1:T(8,128)S(1)} %pad_maximum_fusion.7), channel_id=1, source_target_pairs={{0,4},{1,5},{2,6},{3,7},{4,0},{5,1},{6,2},{7,3},{8,12},{9,13},{10,... | collective-permute-start | bytes 147464 | tf_op jit(solution)/shard_map/ppermute | solution.py:38
  9.7 24.6 %collective-permute-start.4 = (f32[16,6,128]{2,0,1:T(8,128)S(1)}, f32[16,6,128]{2,0,1:T(8,128)S(1)}, u32[]{:S(2)}, u32[]{:S(2)}) collective-permute-start(f32[16,6,128]{2,0,1:T(8,128)S(1)} %pad_maximum_fusion.7), channel_id=1, source_target_pairs={{0,12},{1,13},{2,14},{3,15},{4,8},{5,9},{6,10},{7,11},{8,4},{9,5},... | collective-permute-start | bytes 147464 | tf_op jit(solution)/shard_map/ppermute | solution.py:38
  13.9 1.4 copy-start.7
  16.5 45.0 %all-to-all-start.1 = ((f32[16,16,16,128]{3,2,1,0:T(8,128)}), f32[16,16,16,128]{3,2,1,0:T(8,128)S(1)}, u32[]{:S(2)}, u32[]{:S(2)}) async-start(f32[16,16,16,128]{3,2,1,0:T(8,128)} %tie.6), calls=%async_computation.1 | async-start | bytes 4194304 | tf_op jit(solution)/shard_map/all_to_all | solution.py:62
  22.5 2.2 copy-start.3
  29.3 80.3 %copy-start.26 = (f32[48,4,128]{2,0,1:T(8,128)}, f32[48,4,128]{2,0,1:T(8,128)S(1)}, u32[]{:S(2)}) copy-start(f32[48,4,128]{2,0,1:T(8,128)S(1)} %pad_maximum_fusion.4) | copy-start | bytes 294916
  29.7 30.4 %collective-permute-start.9 = (f32[3,16,4]{2,1,0:T(8,128)S(1)}, f32[3,16,4]{2,1,0:T(8,128)S(1)}, u32[]{:S(2)}, u32[]{:S(2)}) collective-permute-start(f32[3,16,4]{2,1,0:T(8,128)S(1)} %bitcast.257), channel_id=1, source_target_pairs={{0,1},{1,2},{2,3},{3,4},{4,5},{5,6},{6,7},{7,8},{8,9},{9,10},{10,1... | collective-permute-start | bytes 2312 | tf_op jit(solution)/shard_map/ppermute | solution.py:651
  29.8 30.3 %collective-permute-start.8 = (f32[3,16,4]{2,1,0:T(8,128)S(1)}, f32[3,16,4]{2,1,0:T(8,128)S(1)}, u32[]{:S(2)}, u32[]{:S(2)}) collective-permute-start(f32[3,16,4]{2,1,0:T(8,128)S(1)} %bitcast.258), channel_id=1, source_target_pairs={{0,15},{1,0},{2,1},{3,2},{4,3},{5,4},{6,5},{7,6},{8,7},{9,8},{10,9... | collective-permute-start | bytes 2312 | tf_op jit(solution)/shard_map/ppermute | solution.py:651
  34.4 3.3 copy-start.23
  37.6 2.0 copy-start.4
  60.8 13.9 %copy-start.28 = (f32[3]{0:T(128)S(1)}, f32[3]{0:T(128)}, u32[]{:S(2)}) copy-start(f32[3]{0:T(128)} %param.19) | copy-start | bytes 40
  60.8 20.6 %copy-start.24 = (f32[4,16,6,128]{3,2,1,0:T(8,128)S(1)}, f32[4,16,6,128]{3,2,1,0:T(8,128)}, u32[]{:S(2)}) copy-start(f32[4,16,6,128]{3,2,1,0:T(8,128)} %copy-done.23) | copy-start | bytes 589828
  61.5 1.4 copy-start.20
  62.9 107.0 %all-to-all-start = ((f32[32,256,128]{2,1,0:T(8,128)}), f32[32,256,128]{2,1,0:T(8,128)}, u32[]{:S(2)}, u32[]{:S(2)}) async-start(f32[32,256,128]{2,1,0:T(8,128)} %tie.5), calls=%async_computation | async-start | bytes 8388608 | tf_op jit(solution)/shard_map/all_to_all | solution.py:62
  81.4 57.7 %collective-permute-start.7 = (f32[4,16,6,128]{3,2,1,0:T(8,128)S(1)}, f32[4,16,6,128]{3,2,1,0:T(8,128)S(1)}, u32[]{:S(2)}, u32[]{:S(2)}) collective-permute-start(f32[4,16,6,128]{3,2,1,0:T(8,128)S(1)} %copy-done.24), channel_id=1, source_target_pairs={{0,3},{1,2},{2,1},{3,0},{4,7},{5,6},{6,5},{7,4},{8,11},{9,10},{10,... | collective-permute-start | bytes 589832 | tf_op jit(solution)/shard_map/ppermute | solution.py:38
  82.9 56.2 %collective-permute-start.6 = (f32[4,16,6,128]{3,2,1,0:T(8,128)S(1)}, f32[4,16,6,128]{3,2,1,0:T(8,128)S(1)}, u32[]{:S(2)}, u32[]{:S(2)}) collective-permute-start(f32[4,16,6,128]{3,2,1,0:T(8,128)S(1)} %copy-done.24), channel_id=1, source_target_pairs={{0,2},{1,3},{2,0},{3,1},{4,6},{5,7},{6,4},{7,5},{8,10},{9,11},{10,... | collective-permute-start | bytes 589832 | tf_op jit(solution)/shard_map/ppermute | solution.py:38
  83.3 55.6 %collective-permute-start.5 = (f32[4,16,6,128]{3,2,1,0:T(8,128)S(1)}, f32[4,16,6,128]{3,2,1,0:T(8,128)S(1)}, u32[]{:S(2)}, u32[]{:S(2)}) collective-permute-start(f32[4,16,6,128]{3,2,1,0:T(8,128)S(1)} %copy-done.24), channel_id=1, source_target_pairs={{0,1},{1,0},{2,3},{3,2},{4,5},{5,4},{6,7},{7,6},{8,9},{9,8},{10,11... | collective-permute-start | bytes 589832 | tf_op jit(solution)/shard_map/ppermute | solution.py:38
  83.3 15.6 %copy-start.25 = (f32[3,16,4]{2,1,0:T(8,128)S(1)}, f32[3,16,4]{2,1,0:T(8,128)}, u32[]{:S(2)}) copy-start(f32[3,16,4]{2,1,0:T(8,128)} %add_add_fusion) | copy-start | bytes 2308
  83.3 15.6 %copy-start.29 = (f32[4]{0:T(128)S(1)}, f32[4]{0:T(128)}, u32[]{:S(2)}) copy-start(f32[4]{0:T(128)} %param.18) | copy-start | bytes 52
  97.0 2.0 copy-start.8
  105.0 4.5 %copy-start.1 = (f32[16,32,8,256]{3,2,1,0:T(8,128)}, f32[16,32,8,256]{3,2,1,0:T(8,128)S(1)}, u32[]{:S(2)}) copy-start(f32[16,32,8,256]{3,2,1,0:T(8,128)S(1)} %put.3.field) | copy-start | bytes 12582916
  123.4 2.7 copy-start
  126.1 90.2 %collective-permute-start.10 = (f32[1,16,256,128]{3,2,1,0:T(8,128)}, f32[1,16,256,128]{3,2,1,0:T(8,128)}, u32[]{:S(2)}, u32[]{:S(2)}) collective-permute-start(f32[1,16,256,128]{3,2,1,0:T(8,128)} %constant_dynamic-slice_fusion), channel_id=1, source_target_pairs={{0,16},{16,0},{1,17},{17,1},{2,18},{18,2},{3,19},{19,3},{4,20},{20... | collective-permute-start | bytes 6291464 | tf_op jit(solution)/shard_map/ppermute | solution.py:54
  131.9 1.4 copy-start.6
  137.4 1.4 copy-start.5
  139.2 1.0 copy-start.21
  169.9 52.4 %all-to-all-start.3 = ((f32[32,128,128]{2,1,0:T(8,128)}), f32[32,128,128]{2,1,0:T(8,128)S(1)}, u32[]{:S(2)}, u32[]{:S(2)}) async-start(f32[32,128,128]{2,1,0:T(8,128)} %tie.8), calls=%async_computation.3 | async-start | bytes 4194304 | tf_op jit(solution)/shard_map/all_to_all | solution.py:62
  185.1 1.3 copy-start.17
  194.0 14.0 %copy-start.14 = (f32[2,256,1,128]{3,2,1,0:T(1,128)}, f32[2,256,1,128]{3,2,1,0:T(1,128)S(1)}, u32[]{:S(2)}) copy-start(f32[2,256,1,128]{3,2,1,0:T(1,128)S(1)} %pick_block.3.refs_1_) | copy-start | bytes 786436
  199.5 1.3 copy-start.15
  200.8 7.6 %copy-start.22 = (f32[4,4,16,6,128]{4,3,2,0,1:T(8,128)S(1)}, f32[4,4,16,6,128]{4,3,2,0,1:T(8,128)}, u32[]{:S(2)}) copy-start(f32[4,4,16,6,128]{4,3,2,0,1:T(8,128)} %copy-done.21) | copy-start | bytes 2359300
  222.4 56.5 %all-to-all-start.2 = ((f32[32,136,128]{2,1,0:T(8,128)}), f32[32,136,128]{2,1,0:T(8,128)}, u32[]{:S(2)}, u32[]{:S(2)}) async-start(f32[32,136,128]{2,1,0:T(8,128)} %append.1), calls=%async_computation.2 | async-start | bytes 4456448 | tf_op jit(solution)/shard_map/all_to_all | solution.py:62
  229.9 1.3 copy-start.11
  278.9 45.5 %all-to-all-start.4 = ((f32[16,2,128,128]{3,2,1,0:T(8,128)}), f32[16,2,128,128]{3,2,1,0:T(8,128)}, u32[]{:S(2)}, u32[]{:S(2)}) async-start(f32[16,2,128,128]{3,2,1,0:T(8,128)} %copy-done.11), calls=%async_computation.4 | async-start | bytes 4194304 | tf_op jit(solution)/shard_map/all_to_all | solution.py:62
  283.6 5.8 %copy-start.27 = (f32[48,4,128]{2,0,1:T(8,128)S(1)}, f32[48,4,128]{2,0,1:T(8,128)}, u32[]{:S(2)}) copy-start(f32[48,4,128]{2,0,1:T(8,128)} %copy-done.26) | copy-start | bytes 294916
  289.9 1.6 copy-start.13
  291.5 4.6 %copy-start.12 = (f32[16,32,8,128]{3,2,1,0:T(8,128)S(1)}, f32[16,32,8,128]{3,2,1,0:T(8,128)}, u32[]{:S(2)}) copy-start(f32[16,32,8,128]{3,2,1,0:T(8,128)} %get-tuple-element.81.base) | copy-start | bytes 6291460
  300.3 2.8 copy-start.2
  300.3 3.1 copy-start.18
  307.0 0.8 copy-start.16
  307.8 1.1 copy-start.19
  324.4 43.3 %all-to-all-start.6 = ((f32[16,2,96,128]{3,2,1,0:T(8,128)}), f32[16,2,96,128]{3,2,1,0:T(8,128)}, u32[]{:S(2)}, u32[]{:S(2)}) async-start(f32[16,2,96,128]{3,2,1,0:T(8,128)} %copy-done.19), calls=%async_computation.6 | async-start | bytes 3145728 | tf_op jit(solution)/shard_map/all_to_all | solution.py:62
  338.1 25.5 %collective-permute-start.11 = (f32[16,16,8,128]{3,2,1,0:T(8,128)S(1)}, f32[16,16,8,128]{3,2,1,0:T(8,128)S(1)}, u32[]{:S(2)}, u32[]{:S(2)}) collective-permute-start(f32[16,16,8,128]{3,2,1,0:T(8,128)S(1)} %broadcast_multiply_fusion.refs_1_), channel_id=1, source_target_pairs={{0,16},{16,0},{1,17},{17,1},{2,18},{18,2},{3,19},{19,3},{4,20},{20... | collective-permute-start | bytes 3145736 | tf_op jit(solution)/shard_map/ppermute | solution.py:800
  363.6 1.0 copy-start.9
  367.7 23.7 %all-to-all-start.5 = ((f32[16,2,32,128]{3,2,1,0:T(8,128)}), f32[16,2,32,128]{3,2,1,0:T(8,128)}, u32[]{:S(2)}, u32[]{:S(2)}) async-start(f32[16,2,32,128]{3,2,1,0:T(8,128)} %tie.9), calls=%async_computation.5 | async-start | bytes 1048576 | tf_op jit(solution)/shard_map/all_to_all | solution.py:62
  379.8 20.7 %collective-permute-start.13 = (f32[12,16,8,128]{3,2,1,0:T(8,128)}, f32[12,16,8,128]{3,2,1,0:T(8,128)}, u32[]{:S(2)}, u32[]{:S(2)}) collective-permute-start(f32[12,16,8,128]{3,2,1,0:T(8,128)} %broadcast_multiply_fusion.1.refs_3_), channel_id=1, source_target_pairs={{0,16},{16,0},{1,17},{17,1},{2,18},{18,2},{3,19},{19,3},{4,20},{20... | collective-permute-start | bytes 2359304 | tf_op jit(solution)/shard_map/ppermute | solution.py:800
  391.4 9.1 %copy-start.10 = (f32[16,16,8,128]{3,2,1,0:T(8,128)S(1)}, f32[16,16,8,128]{3,2,1,0:T(8,128)}, u32[]{:S(2)}) copy-start(f32[16,16,8,128]{3,2,1,0:T(8,128)} %copy-done.9) | copy-start | bytes 3145732
  392.7 12.7 %collective-permute-start.12 = (f32[4,16,8,128]{3,2,1,0:T(8,128)S(1)}, f32[4,16,8,128]{3,2,1,0:T(8,128)S(1)}, u32[]{:S(2)}, u32[]{:S(2)}) collective-permute-start(f32[4,16,8,128]{3,2,1,0:T(8,128)S(1)} %broadcast_multiply_fusion.2.refs_3_), channel_id=1, source_target_pairs={{0,16},{16,0},{1,17},{17,1},{2,18},{18,2},{3,19},{19,3},{4,20},{20... | collective-permute-start | bytes 786440 | tf_op jit(solution)/shard_map/ppermute | solution.py:800

commit v8 on v7

--- a/solution.py
+++ b/solution.py
@@ -694,7 +694,7 @@
     got_potential = exchange(tie(mine, *gots), "grid")
     got_potential = got_potential.reshape(grid_count, planes * rows, part)
 
-    late = planes // 4 * 3
+    late = planes // 8 * 5
     cuts = [[(0, planes)]] * (chunks - 1) + [[(0, late), (late, planes)] if planes % 16 == 0 else [(0, planes)]]
     sums = [[0.0] * len(cut) for cut in cuts]
     weights = jnp.stack([c1_4, c2_8])

time: 409 us -> 407 us (level)
    all_to_all x7, waiting for transfers between devices: 107 us -> 111 us  [exchange(): return lax.all_to_all(block, axis, split_axis=0, concat_axis=0, tiled=True)]
  transfers between devices with their start and end apart: 21 -> 21, of which waited for: 11 -> 9; matrix products, arithmetic and copies ran while one was open for 12% -> 12% of each run, Pallas kernels for 25% -> 25%
where the time goes in v8:
time: 407 us; the launch traced here: 405 us
  waiting for transfers between devices  162 us (40%)
  Pallas kernels  101 us (25%)
  starting transfers between devices  66 us (16%)
  local copies, waits for them, and re-layouts  44 us (11%)
  other arithmetic  23.8 us (6%)
  matrix products  4.14 us (1%)
    all_to_all x7, waiting for transfers between devices, exchange(): return lax.all_to_all(block, axis, split_axis=0, concat_axis=0, tiled=True)  111 us
    all_to_all x7, starting transfers between devices, exchange(): return lax.all_to_all(block, axis, split_axis=0, concat_axis=0, tiled=True)  45 us
    ppermute x3, waiting for transfers between devices, local(): pairs.append((own, lax.ppermute(own, 'orb', [(0, 1), (1, 0)])))  30.3 us
    unnamed x65, local copies, waits for them, and re-layouts  25 us
    ppermute x4, waiting for transfers between devices, shifted(): lax.ppermute(block, 'grid', [(i, (i + step) % grid_count) for i in range(...  20.9 us
    pallas_call x1, Pallas kernels, planar_first(): pl.pallas_call(ordered(first_kernel, 4, len(others)), grid=field.shape[:1...  13.6 us
    pallas_call x2, Pallas kernels, pick_block(): pl.pallas_call(functools.partial(pick_block_kernel, total), out_shape=jax...  13.5 us
    pallas_call x1, Pallas kernels, planar_second(): pl.pallas_call(second_kernel, grid=field.shape[:1], out_shape=jax.ShapeDt...  13 us
  transfers between devices with their start and end apart: 21, of which 9 were waited for; matrix products, arithmetic and copies ran while one was open for 12% of the time, Pallas kernels for 25%

profile of v8, /device:TPU:0, one launch (start us, length us, event | category | flops | bytes accessed | tf_op | source)
XLA Modules:
  0.0 404.7 jit_solution(2530170158304588915)
XLA Ops:
  1.9 5.0 %collective-permute-start.1 = (f32[16,6,128]{2,0,1:T(8,128)S(1)}, f32[16,6,128]{2,0,1:T(8,128)S(1)}, u32[]{:S(2)}, u32[]{:S(2)}) collective-permute-start(f32[16,6,128]{2,0,1:T(8,128)S(1)} %pad_maximum_fusion.7), channel_id=1, source_target_pairs={{0,15},{1,0},{2,1},{3,2},{4,3},{5,4},{6,5},{7,6},{8,7},{9,8},{10,9... | collective-permute-start | bytes 147464 | tf_op jit(solution)/shard_map/ppermute | solution.py:651
  7.0 1.2 collective-permute-start.3
  8.2 1.6 collective-permute-start.2
  9.7 1.6 collective-permute-start.4
  11.4 2.4 pack_part.1
  13.9 1.3 copy-done.7
  16.5 3.7 all-to-all-start.1
  22.6 2.2 copy-done.3
  24.7 4.1 %pick.2 = f32[48,1,128]{2,1,0:T(1,128)S(1)} custom-call(s32[48,3]{1,0:T(8,128)S(1)} %pad_add_fusion.3.starts, s32[3]{0:T(128)S(1)} %stack.72.corner, s32[48,2,128]{2,1,0:T(2,128)S(1)} %pad_add_fusion.2.refs_1_.spots.refs_4_, f32[16,32,8,256]{3,2,1,0:T(8,128)S(1)} %bitcast.214), custom_call_target="tpu_custom_call" | custom-call | flops 16777216 | bytes 16777216 | tf_op jit(solution)/shard_map/pick/pallas_call | solution.py:314
  29.6 4.1 %collective-permute-start.8 = (f32[3,16,4]{2,1,0:T(8,128)S(1)}, f32[3,16,4]{2,1,0:T(8,128)S(1)}, u32[]{:S(2)}, u32[]{:S(2)}) collective-permute-start(f32[3,16,4]{2,1,0:T(8,128)S(1)} %bitcast.258), channel_id=1, source_target_pairs={{0,15},{1,0},{2,1},{3,2},{4,3},{5,4},{6,5},{7,6},{8,7},{9,8},{10,9... | collective-permute-start | bytes 2312 | tf_op jit(solution)/shard_map/ppermute | solution.py:651
  33.9 3.3 pack.3
  37.2 2.0 copy-done.4
  39.2 20.9 %collective-permute-done.9 = f32[3,16,4]{2,1,0:T(8,128)S(1)} collective-permute-done((f32[3,16,4]{2,1,0:T(8,128)S(1)}, f32[3,16,4]{2,1,0:T(8,128)S(1)}, u32[]{:S(2)}, u32[]{:S(2)}) %collective-permute-start.9) | collective-permute-done | bytes 800 | tf_op jit(solution)/shard_map/ppermute | solution.py:651
  61.5 1.4 copy-done.20
  62.9 11.7 %all-to-all-start = ((f32[32,256,128]{2,1,0:T(8,128)}), f32[32,256,128]{2,1,0:T(8,128)}, u32[]{:S(2)}, u32[]{:S(2)}) async-start(f32[32,256,128]{2,1,0:T(8,128)} %tie.5), calls=%async_computation | async-start | bytes 8388608 | tf_op jit(solution)/shard_map/all_to_all | solution.py:62
  81.4 1.5 collective-permute-start.7
  83.4 13.6 %planar_first.1 = (f32[16,256,256]{2,1,0:T(8,128)S(1)}, f32[16,256,256]{2,1,0:T(8,128)}) custom-call(f32[16,256,256]{2,1,0:T(8,128)} %bitcast.212, f32[16,256,256]{2,1,0:T(8,128)} %potential.1, bf16[2,256,256]{2,1,0:T(8,128)(2,1)S(1)} %get-tuple-element.115.refs_2_.high_tables, bf16[2,256,256]{2,1,0:T(8,128)(2,1)S(1)} %get-tuple-element.116.refs_3_.low_tables, ...), custom_call_target="tpu_custom_call" | custom-call | flops 3221225472 | bytes 16777216 | tf_op jit(solution)/shard_map/planar_first/pallas_call | solution.py:369
  97.0 2.0 copy-done.8
  99.4 5.2 %put.3.field = f32[16,32,8,256]{3,2,1,0:T(8,128)S(1)} custom-call(s32[48,3]{1,0:T(8,128)S(1)} %pad_add_fusion.3.starts, s32[3]{0:T(128)S(1)} %stack.72.corner, s32[48,2,128]{2,1,0:T(2,128)S(1)} %pad_add_fusion.2.refs_1_.spots.refs_4_, f32[48,1,128]{2,1,0:T(1,128)S(1)} %fusion.69.spread, f32[16,32,8,256]{3,2,1,0:T(8,128)} %bitcast.229), custom_call_target="tpu_custom_call" | custom-call | flops 16777216 | bytes 16777216 | tf_op jit(solution)/shard_map/put/pallas_call | solution.py:341
  104.6 4.1 %pick.3 = f32[48,1,128]{2,1,0:T(1,128)S(1)} custom-call(s32[48,3]{1,0:T(8,128)S(1)} %pad_add_fusion.3.starts, s32[3]{0:T(128)S(1)} %stack.72.corner, s32[48,2,128]{2,1,0:T(2,128)S(1)} %pad_add_fusion.2.refs_1_.spots.refs_4_, f32[16,32,8,256]{3,2,1,0:T(8,128)S(1)} %put.3.field), custom_call_target="tpu_custom_call" | custom-call | flops 16777216 | bytes 16777216 | tf_op jit(solution)/shard_map/pick/pallas_call | solution.py:314
  109.6 13.0 %planar_second.1.refs_2_ = f32[2,16,256,128]{3,2,1,0:T(8,128)S(1)} custom-call(f32[3]{0:T(128)S(1)} %pad_maximum_fusion.9.weights, f32[16,256,256]{2,1,0:T(8,128)} %bitcast.200, f32[16,256,256]{2,1,0:T(8,128)} %bitcast.213, f32[16,256,256]{2,1,0:T(8,128)} %potential.1, bf16[2,256,256]{2,1,0:T(8,128)(2,1)S(1)} %get-tuple-element.115.refs_2_.high_tables, ...), custom_call_target="tpu_custom_call" | custom-call | flops 3221225472 | bytes 16777216 | tf_op jit(solution)/shard_map/planar_second/pallas_call | solution.py:385
  122.6 1.7 constant_dynamic-slice_fusion
  125.3 1.7 collective-permute-start.10
  127.0 4.1 %pack.5 = f32[2,16,128,128]{3,2,1,0:T(8,128)S(1)} custom-call(f32[16,256,256]{2,1,0:T(8,128)} %copy-done.8, f32[16,256,256]{2,1,0:T(8,128)} %bitcast.201, f32[2,16,256,128]{3,2,1,0:T(8,128)} %copy-done), custom_call_target="tpu_custom_call" | custom-call | flops 524288 | bytes 4194304 | tf_op jit(solution)/shard_map/pack/pallas_call | solution.py:459
  131.1 1.4 copy-done.6
  132.5 4.1 %pack.4 = f32[2,16,136,128]{3,2,1,0:T(8,128)S(1)} custom-call(f32[16,256,256]{2,1,0:T(8,128)} %copy-done.8, f32[16,256,256]{2,1,0:T(8,128)} %bitcast.202, f32[2,16,256,128]{3,2,1,0:T(8,128)} %copy-done), custom_call_target="tpu_custom_call" | custom-call | flops 524288 | bytes 4194304 | tf_op jit(solution)/shard_map/pack/pallas_call | solution.py:459
  136.6 1.4 copy-done.5
  139.4 1.3 slice_convert_fusion
  141.0 28.9 %all-to-all-done.field = f32[32,256,128]{2,1,0:T(8,128)} async-done(((f32[32,256,128]{2,1,0:T(8,128)}), f32[32,256,128]{2,1,0:T(8,128)}, u32[]{:S(2)}, u32[]{:S(2)}) %all-to-all-start) | async-done | bytes 4194336 | tf_op jit(solution)/shard_map/all_to_all | solution.py:62
  169.9 2.9 all-to-all-start.3
  176.0 3.2 fusion.58
  179.6 5.4 %depth_out.3 = (f32[2,2048,128]{2,1,0:T(8,128)S(1)}, f32[2,2048,128]{2,1,0:T(8,128)S(1)}, f32[2,2048,128]{2,1,0:T(8,128)}) custom-call(f32[2]{0:T(128)S(1)} %pad_maximum_fusion.8.weights.refs_0_, f32[32,256,128]{2,1,0:T(8,128)} %all-to-all-done.field, f32[16,256,128]{2,1,0:T(8,128)} %bitcast.221, bf16[256,256]{1,0:T(8,128)(2,1)S(1)} %get-tuple-element.113.high_table.refs_4_, ...), custom_call_target="tpu_custom_call" | custom-call | flops 805306368 | bytes 10485760 | tf_op jit(solution)/shard_map/depth_out/pallas_call | solution.py:553
  185.1 1.3 copy-done.17
  186.4 6.6 %pick_block.3.refs_1_ = f32[2,256,1,128]{3,2,1,0:T(1,128)S(1)} custom-call(s32[256,3]{1,0:T(8,128)S(1)} %pad_add_fusion.1.starts, s32[3]{0:T(128)S(1)} %get-tuple-element.108.corner, s32[256,2,128]{2,1,0:T(2,128)S(1)} %pad_add_fusion.spots, f32[2,256,8,128]{3,2,1,0:T(8,128)S(1)} %bitcast.220), custom_call_target="tpu_custom_call" | custom-call | flops 16777216 | bytes 16777216 | tf_op jit(solution)/shard_map/pick_block/pallas_call | solution.py:327
  193.0 5.5 %depth_out.2 = (f32[2,2048,128]{2,1,0:T(8,128)S(1)}, f32[2,2048,128]{2,1,0:T(8,128)S(1)}, f32[2,2048,128]{2,1,0:T(8,128)}) custom-call(f32[2]{0:T(128)S(1)} %pad_maximum_fusion.8.weights.refs_0_, f32[32,256,128]{2,1,0:T(8,128)} %all-to-all-done.field, f32[16,256,128]{2,1,0:T(8,128)} %bitcast.222, bf16[256,256]{1,0:T(8,128)(2,1)S(1)} %get-tuple-element.113.high_table.refs_4_, ...), custom_call_target="tpu_custom_call" | custom-call | flops 805306368 | bytes 10485760 | tf_op jit(solution)/shard_map/depth_out/pallas_call | solution.py:553
  198.4 1.3 copy-done.16
  199.7 6.9 %pick_block.2 = f32[2,256,1,128]{3,2,1,0:T(1,128)S(1)} custom-call(s32[256,3]{1,0:T(8,128)S(1)} %pad_add_fusion.1.starts, s32[3]{0:T(128)S(1)} %get-tuple-element.107.corner, s32[256,2,128]{2,1,0:T(2,128)S(1)} %pad_add_fusion.spots, f32[2,256,8,128]{3,2,1,0:T(8,128)S(1)} %bitcast.219), custom_call_target="tpu_custom_call" | custom-call | flops 16777216 | bytes 16777216 | tf_op jit(solution)/shard_map/pick_block/pallas_call | solution.py:327
  207.0 1.9 fusion.15
  209.0 3.0 add.388
  215.0 3.2 constant_dynamic-update-slice_fusion.refs_0_
  218.2 1.8 append.1
  220.0 2.3 all-to-all-done.3.refs_1_
  222.4 4.2 %all-to-all-start.2 = ((f32[32,136,128]{2,1,0:T(8,128)}), f32[32,136,128]{2,1,0:T(8,128)}, u32[]{:S(2)}, u32[]{:S(2)}) async-start(f32[32,136,128]{2,1,0:T(8,128)} %append.1), calls=%async_computation.2 | async-start | bytes 4456448 | tf_op jit(solution)/shard_map/all_to_all | solution.py:62
  226.6 3.5 depth_back.2
  230.2 1.3 copy-done.11
  231.5 47.6 %all-to-all-done.2.refs_1_ = f32[32,136,128]{2,1,0:T(8,128)} async-done(((f32[32,136,128]{2,1,0:T(8,128)}), f32[32,136,128]{2,1,0:T(8,128)}, u32[]{:S(2)}, u32[]{:S(2)}) %all-to-all-start.2) | async-done | bytes 2228256 | tf_op jit(solution)/shard_map/all_to_all | solution.py:62
  279.1 4.7 %all-to-all-start.4 = ((f32[16,2,128,128]{3,2,1,0:T(8,128)}), f32[16,2,128,128]{3,2,1,0:T(8,128)}, u32[]{:S(2)}, u32[]{:S(2)}) async-start(f32[16,2,128,128]{3,2,1,0:T(8,128)} %copy-done.11), calls=%async_computation.4 | async-start | bytes 4194304 | tf_op jit(solution)/shard_map/all_to_all | solution.py:62
  283.9 4.8 %slice_bitcast_fusion = (f32[16,32,8,128]{3,2,1,0:T(8,128)}, f32[16,32,8,128]{3,2,1,0:T(8,128)}) fusion(f32[2,16,256,128]{3,2,1,0:T(8,128)} %constant_dynamic-update-slice_fusion.refs_0_), kind=kLoop, calls=%fused_computation.12 | loop fusion | bytes 8388608 | tf_op jit(solution)/shard_map/reshape;squeeze | solution.py:295
  290.2 1.6 copy-done.13
  291.7 3.8 put.5
  296.0 3.8 put.4
  299.8 2.4 pad_maximum_fusion.refs_6_
  302.9 3.6 depth_back.3
  308.5 16.2 %all-to-all-done.4 = f32[16,2,128,128]{3,2,1,0:T(8,128)} async-done(((f32[16,2,128,128]{3,2,1,0:T(8,128)}), f32[16,2,128,128]{3,2,1,0:T(8,128)}, u32[]{:S(2)}, u32[]{:S(2)}) %all-to-all-start.4) | async-done | bytes 2097184 | tf_op jit(solution)/shard_map/all_to_all | solution.py:62
  324.6 11.2 %all-to-all-start.6 = ((f32[16,2,80,128]{3,2,1,0:T(8,128)}), f32[16,2,80,128]{3,2,1,0:T(8,128)}, u32[]{:S(2)}, u32[]{:S(2)}) async-start(f32[16,2,80,128]{3,2,1,0:T(8,128)} %copy-done.19), calls=%async_computation.6 | async-start | bytes 2621440 | tf_op jit(solution)/shard_map/all_to_all | solution.py:62
  335.9 2.3 fusion.4
  339.4 24.5 %collective-permute-done.11.refs_1_.refs_2_ = f32[16,16,8,128]{3,2,1,0:T(8,128)S(1)} collective-permute-done((f32[16,16,8,128]{3,2,1,0:T(8,128)S(1)}, f32[16,16,8,128]{3,2,1,0:T(8,128)S(1)}, u32[]{:S(2)}, u32[]{:S(2)}) %collective-permute-start.11) | collective-permute-done | bytes 1048608 | tf_op jit(solution)/shard_map/ppermute | solution.py:800
  364.8 6.6 %all-to-all-start.5 = ((f32[16,2,48,128]{3,2,1,0:T(8,128)}), f32[16,2,48,128]{3,2,1,0:T(8,128)}, u32[]{:S(2)}, u32[]{:S(2)}) async-start(f32[16,2,48,128]{3,2,1,0:T(8,128)} %tie.9), calls=%async_computation.5 | async-start | bytes 1572864 | tf_op jit(solution)/shard_map/all_to_all | solution.py:62
  371.4 1.8 fusion.9
  375.1 15.1 %all-to-all-done.5 = f32[16,2,48,128]{3,2,1,0:T(8,128)} async-done(((f32[16,2,48,128]{3,2,1,0:T(8,128)}), f32[16,2,48,128]{3,2,1,0:T(8,128)}, u32[]{:S(2)}, u32[]{:S(2)}) %all-to-all-start.5) | async-done | bytes 786464 | tf_op jit(solution)/shard_map/all_to_all | solution.py:62
  390.2 1.5 fusion.14
  392.7 4.5 %join.2.refs_5_ = f32[16,256,256]{2,1,0:T(8,128)} custom-call(s32[1]{0:T(128)} %bitcast.place.refs_0_, f32[16,16,8,128]{3,2,1,0:T(8,128)S(1)} %broadcast_multiply_fusion.refs_1_, f32[16,16,8,128]{3,2,1,0:T(8,128)S(1)} %copy-done.10, f32[10,16,8,128]{3,2,1,0:T(8,128)} %broadcast_multiply_fusion.1.refs_3_, f32[10,16,8,128]{3,2,1,0:T(8,128)} %collective-permute-done.13.refs_4_), custom_call_target="tpu_custom_call" | custom-call | bytes 5242880 | tf_op jit(solution)/shard_map/join/pallas_call | solution.py:528
  397.2 5.8 %collective-permute-done.12.refs_4_ = f32[6,16,8,128]{3,2,1,0:T(8,128)S(1)} collective-permute-done((f32[6,16,8,128]{3,2,1,0:T(8,128)S(1)}, f32[6,16,8,128]{3,2,1,0:T(8,128)S(1)}, u32[]{:S(2)}, u32[]{:S(2)}) %collective-permute-start.12) | collective-permute-done | bytes 393248 | tf_op jit(solution)/shard_map/ppermute | solution.py:800
  403.0 1.7 join.3
  (182 shorter events, 32.8 us)
Async XLA Ops:
  1.5 13.7 %collective-permute-start = (f32[16,6,128]{2,0,1:T(8,128)S(1)}, f32[16,6,128]{2,0,1:T(8,128)S(1)}, u32[]{:S(2)}, u32[]{:S(2)}) collective-permute-start(f32[16,6,128]{2,0,1:T(8,128)S(1)} %pad_maximum_fusion.7), channel_id=1, source_target_pairs={{0,1},{1,2},{2,3},{3,4},{4,5},{5,6},{6,7},{7,8},{8,9},{9,10},{10,1... | collective-permute-start | bytes 147464 | tf_op jit(solution)/shard_map/ppermute | solution.py:651
  1.9 13.9 %collective-permute-start.1 = (f32[16,6,128]{2,0,1:T(8,128)S(1)}, f32[16,6,128]{2,0,1:T(8,128)S(1)}, u32[]{:S(2)}, u32[]{:S(2)}) collective-permute-start(f32[16,6,128]{2,0,1:T(8,128)S(1)} %pad_maximum_fusion.7), channel_id=1, source_target_pairs={{0,15},{1,0},{2,1},{3,2},{4,3},{5,4},{6,5},{7,6},{8,7},{9,8},{10,9... | collective-permute-start | bytes 147464 | tf_op jit(solution)/shard_map/ppermute | solution.py:651
  7.0 26.9 %collective-permute-start.3 = (f32[16,6,128]{2,0,1:T(8,128)S(1)}, f32[16,6,128]{2,0,1:T(8,128)S(1)}, u32[]{:S(2)}, u32[]{:S(2)}) collective-permute-start(f32[16,6,128]{2,0,1:T(8,128)S(1)} %pad_maximum_fusion.7), channel_id=1, source_target_pairs={{0,8},{1,9},{2,10},{3,11},{4,12},{5,13},{6,14},{7,15},{8,0},{9,1},... | collective-permute-start | bytes 147464 | tf_op jit(solution)/shard_map/ppermute | solution.py:38
  8.2 25.6 %collective-permute-start.2 = (f32[16,6,128]{2,0,1:T(8,128)S(1)}, f32[16,6,128]{2,0,1:T(8,128)S(1)}, u32[]{:S(2)}, u32[]{:S(2)}) collective-permute-start(f32[16,6,128]{2,0,1:T(8,128)S(1)} %pad_maximum_fusion.7), channel_id=1, source_target_pairs={{0,4},{1,5},{2,6},{3,7},{4,0},{5,1},{6,2},{7,3},{8,12},{9,13},{10,... | collective-permute-start | bytes 147464 | tf_op jit(solution)/shard_map/ppermute | solution.py:38
  9.7 24.1 %collective-permute-start.4 = (f32[16,6,128]{2,0,1:T(8,128)S(1)}, f32[16,6,128]{2,0,1:T(8,128)S(1)}, u32[]{:S(2)}, u32[]{:S(2)}) collective-permute-start(f32[16,6,128]{2,0,1:T(8,128)S(1)} %pad_maximum_fusion.7), channel_id=1, source_target_pairs={{0,12},{1,13},{2,14},{3,15},{4,8},{5,9},{6,10},{7,11},{8,4},{9,5},... | collective-permute-start | bytes 147464 | tf_op jit(solution)/shard_map/ppermute | solution.py:38
  13.9 1.4 copy-start.7
  16.5 45.0 %all-to-all-start.1 = ((f32[16,16,16,128]{3,2,1,0:T(8,128)}), f32[16,16,16,128]{3,2,1,0:T(8,128)S(1)}, u32[]{:S(2)}, u32[]{:S(2)}) async-start(f32[16,16,16,128]{3,2,1,0:T(8,128)} %tie.6), calls=%async_computation.1 | async-start | bytes 4194304 | tf_op jit(solution)/shard_map/all_to_all | solution.py:62
  22.5 2.2 copy-start.3
  28.8 79.9 %copy-start.26 = (f32[48,4,128]{2,0,1:T(8,128)}, f32[48,4,128]{2,0,1:T(8,128)S(1)}, u32[]{:S(2)}) copy-start(f32[48,4,128]{2,0,1:T(8,128)S(1)} %pad_maximum_fusion.4) | copy-start | bytes 294916
  29.3 30.8 %collective-permute-start.9 = (f32[3,16,4]{2,1,0:T(8,128)S(1)}, f32[3,16,4]{2,1,0:T(8,128)S(1)}, u32[]{:S(2)}, u32[]{:S(2)}) collective-permute-start(f32[3,16,4]{2,1,0:T(8,128)S(1)} %bitcast.257), channel_id=1, source_target_pairs={{0,1},{1,2},{2,3},{3,4},{4,5},{5,6},{6,7},{7,8},{8,9},{9,10},{10,1... | collective-permute-start | bytes 2312 | tf_op jit(solution)/shard_map/ppermute | solution.py:651
  29.6 30.5 %collective-permute-start.8 = (f32[3,16,4]{2,1,0:T(8,128)S(1)}, f32[3,16,4]{2,1,0:T(8,128)S(1)}, u32[]{:S(2)}, u32[]{:S(2)}) collective-permute-start(f32[3,16,4]{2,1,0:T(8,128)S(1)} %bitcast.258), channel_id=1, source_target_pairs={{0,15},{1,0},{2,1},{3,2},{4,3},{5,4},{6,5},{7,6},{8,7},{9,8},{10,9... | collective-permute-start | bytes 2312 | tf_op jit(solution)/shard_map/ppermute | solution.py:651
  33.9 3.3 copy-start.23
  37.2 2.0 copy-start.4
  60.8 13.9 %copy-start.28 = (f32[3]{0:T(128)S(1)}, f32[3]{0:T(128)}, u32[]{:S(2)}) copy-start(f32[3]{0:T(128)} %param.19) | copy-start | bytes 40
  60.8 20.6 %copy-start.24 = (f32[4,16,6,128]{3,2,1,0:T(8,128)S(1)}, f32[4,16,6,128]{3,2,1,0:T(8,128)}, u32[]{:S(2)}) copy-start(f32[4,16,6,128]{3,2,1,0:T(8,128)} %copy-done.23) | copy-start | bytes 589828
  61.5 1.4 copy-start.20
  62.9 107.0 %all-to-all-start = ((f32[32,256,128]{2,1,0:T(8,128)}), f32[32,256,128]{2,1,0:T(8,128)}, u32[]{:S(2)}, u32[]{:S(2)}) async-start(f32[32,256,128]{2,1,0:T(8,128)} %tie.5), calls=%async_computation | async-start | bytes 8388608 | tf_op jit(solution)/shard_map/all_to_all | solution.py:62
  81.4 56.9 %collective-permute-start.7 = (f32[4,16,6,128]{3,2,1,0:T(8,128)S(1)}, f32[4,16,6,128]{3,2,1,0:T(8,128)S(1)}, u32[]{:S(2)}, u32[]{:S(2)}) collective-permute-start(f32[4,16,6,128]{3,2,1,0:T(8,128)S(1)} %copy-done.24), channel_id=1, source_target_pairs={{0,3},{1,2},{2,1},{3,0},{4,7},{5,6},{6,5},{7,4},{8,11},{9,10},{10,... | collective-permute-start | bytes 589832 | tf_op jit(solution)/shard_map/ppermute | solution.py:38
  82.9 55.3 %collective-permute-start.6 = (f32[4,16,6,128]{3,2,1,0:T(8,128)S(1)}, f32[4,16,6,128]{3,2,1,0:T(8,128)S(1)}, u32[]{:S(2)}, u32[]{:S(2)}) collective-permute-start(f32[4,16,6,128]{3,2,1,0:T(8,128)S(1)} %copy-done.24), channel_id=1, source_target_pairs={{0,2},{1,3},{2,0},{3,1},{4,6},{5,7},{6,4},{7,5},{8,10},{9,11},{10,... | collective-permute-start | bytes 589832 | tf_op jit(solution)/shard_map/ppermute | solution.py:38
  83.3 54.8 %collective-permute-start.5 = (f32[4,16,6,128]{3,2,1,0:T(8,128)S(1)}, f32[4,16,6,128]{3,2,1,0:T(8,128)S(1)}, u32[]{:S(2)}, u32[]{:S(2)}) collective-permute-start(f32[4,16,6,128]{3,2,1,0:T(8,128)S(1)} %copy-done.24), channel_id=1, source_target_pairs={{0,1},{1,0},{2,3},{3,2},{4,5},{5,4},{6,7},{7,6},{8,9},{9,8},{10,11... | collective-permute-start | bytes 589832 | tf_op jit(solution)/shard_map/ppermute | solution.py:38
  83.3 15.6 %copy-start.25 = (f32[3,16,4]{2,1,0:T(8,128)S(1)}, f32[3,16,4]{2,1,0:T(8,128)}, u32[]{:S(2)}) copy-start(f32[3,16,4]{2,1,0:T(8,128)} %add_add_fusion) | copy-start | bytes 2308
  83.3 15.6 %copy-start.29 = (f32[4]{0:T(128)S(1)}, f32[4]{0:T(128)}, u32[]{:S(2)}) copy-start(f32[4]{0:T(128)} %param.18) | copy-start | bytes 52
  97.0 2.0 copy-start.8
  104.6 4.1 %copy-start.1 = (f32[16,32,8,256]{3,2,1,0:T(8,128)}, f32[16,32,8,256]{3,2,1,0:T(8,128)S(1)}, u32[]{:S(2)}) copy-start(f32[16,32,8,256]{3,2,1,0:T(8,128)S(1)} %put.3.field) | copy-start | bytes 12582916
  122.6 2.7 copy-start
  125.3 89.7 %collective-permute-start.10 = (f32[1,16,256,128]{3,2,1,0:T(8,128)}, f32[1,16,256,128]{3,2,1,0:T(8,128)}, u32[]{:S(2)}, u32[]{:S(2)}) collective-permute-start(f32[1,16,256,128]{3,2,1,0:T(8,128)} %constant_dynamic-slice_fusion), channel_id=1, source_target_pairs={{0,16},{16,0},{1,17},{17,1},{2,18},{18,2},{3,19},{19,3},{4,20},{20... | collective-permute-start | bytes 6291464 | tf_op jit(solution)/shard_map/ppermute | solution.py:54
  131.1 1.4 copy-start.6
  136.6 1.4 copy-start.5
  138.3 1.0 copy-start.21
  169.9 52.4 %all-to-all-start.3 = ((f32[32,128,128]{2,1,0:T(8,128)}), f32[32,128,128]{2,1,0:T(8,128)S(1)}, u32[]{:S(2)}, u32[]{:S(2)}) async-start(f32[32,128,128]{2,1,0:T(8,128)} %tie.8), calls=%async_computation.3 | async-start | bytes 4194304 | tf_op jit(solution)/shard_map/all_to_all | solution.py:62
  185.1 1.3 copy-start.17
  193.0 13.7 %copy-start.15 = (f32[2,256,1,128]{3,2,1,0:T(1,128)}, f32[2,256,1,128]{3,2,1,0:T(1,128)S(1)}, u32[]{:S(2)}) copy-start(f32[2,256,1,128]{3,2,1,0:T(1,128)S(1)} %pick_block.3.refs_1_) | copy-start | bytes 786436
  198.4 1.3 copy-start.16
  199.7 7.2 %copy-start.22 = (f32[4,4,16,6,128]{4,3,2,0,1:T(8,128)S(1)}, f32[4,4,16,6,128]{4,3,2,0,1:T(8,128)}, u32[]{:S(2)}) copy-start(f32[4,4,16,6,128]{4,3,2,0,1:T(8,128)} %copy-done.21) | copy-start | bytes 2359300
  222.4 56.7 %all-to-all-start.2 = ((f32[32,136,128]{2,1,0:T(8,128)}), f32[32,136,128]{2,1,0:T(8,128)}, u32[]{:S(2)}, u32[]{:S(2)}) async-start(f32[32,136,128]{2,1,0:T(8,128)} %append.1), calls=%async_computation.2 | async-start | bytes 4456448 | tf_op jit(solution)/shard_map/all_to_all | solution.py:62
  230.2 1.3 copy-start.11
  279.1 45.5 %all-to-all-start.4 = ((f32[16,2,128,128]{3,2,1,0:T(8,128)}), f32[16,2,128,128]{3,2,1,0:T(8,128)}, u32[]{:S(2)}, u32[]{:S(2)}) async-start(f32[16,2,128,128]{3,2,1,0:T(8,128)} %copy-done.11), calls=%async_computation.4 | async-start | bytes 4194304 | tf_op jit(solution)/shard_map/all_to_all | solution.py:62
  283.9 5.8 %copy-start.27 = (f32[48,4,128]{2,0,1:T(8,128)S(1)}, f32[48,4,128]{2,0,1:T(8,128)}, u32[]{:S(2)}) copy-start(f32[48,4,128]{2,0,1:T(8,128)} %copy-done.26) | copy-start | bytes 294916
  290.2 1.6 copy-start.13
  291.7 4.2 %copy-start.12 = (f32[16,32,8,128]{3,2,1,0:T(8,128)S(1)}, f32[16,32,8,128]{3,2,1,0:T(8,128)}, u32[]{:S(2)}) copy-start(f32[16,32,8,128]{3,2,1,0:T(8,128)} %get-tuple-element.81.base) | copy-start | bytes 6291460
  299.8 2.8 copy-start.2
  299.8 3.1 copy-start.18
  306.5 0.9 copy-start.14
  307.4 1.1 copy-start.19
  324.6 40.2 %all-to-all-start.6 = ((f32[16,2,80,128]{3,2,1,0:T(8,128)}), f32[16,2,80,128]{3,2,1,0:T(8,128)}, u32[]{:S(2)}, u32[]{:S(2)}) async-start(f32[16,2,80,128]{3,2,1,0:T(8,128)} %copy-done.19), calls=%async_computation.6 | async-start | bytes 2621440 | tf_op jit(solution)/shard_map/all_to_all | solution.py:62
  338.3 25.5 %collective-permute-start.11 = (f32[16,16,8,128]{3,2,1,0:T(8,128)S(1)}, f32[16,16,8,128]{3,2,1,0:T(8,128)S(1)}, u32[]{:S(2)}, u32[]{:S(2)}) collective-permute-start(f32[16,16,8,128]{3,2,1,0:T(8,128)S(1)} %broadcast_multiply_fusion.refs_1_), channel_id=1, source_target_pairs={{0,16},{16,0},{1,17},{17,1},{2,18},{18,2},{3,19},{19,3},{4,20},{20... | collective-permute-start | bytes 3145736 | tf_op jit(solution)/shard_map/ppermute | solution.py:800
  363.8 1.0 copy-start.9
  364.8 25.4 %all-to-all-start.5 = ((f32[16,2,48,128]{3,2,1,0:T(8,128)}), f32[16,2,48,128]{3,2,1,0:T(8,128)}, u32[]{:S(2)}, u32[]{:S(2)}) async-start(f32[16,2,48,128]{3,2,1,0:T(8,128)} %tie.9), calls=%async_computation.5 | async-start | bytes 1572864 | tf_op jit(solution)/shard_map/all_to_all | solution.py:62
  374.1 18.6 %collective-permute-start.13 = (f32[10,16,8,128]{3,2,1,0:T(8,128)}, f32[10,16,8,128]{3,2,1,0:T(8,128)}, u32[]{:S(2)}, u32[]{:S(2)}) collective-permute-start(f32[10,16,8,128]{3,2,1,0:T(8,128)} %broadcast_multiply_fusion.1.refs_3_), channel_id=1, source_target_pairs={{0,16},{16,0},{1,17},{17,1},{2,18},{18,2},{3,19},{19,3},{4,20},{20... | collective-permute-start | bytes 1966088 | tf_op jit(solution)/shard_map/ppermute | solution.py:800
  390.2 2.5 copy-start.10
  391.7 11.3 %collective-permute-start.12 = (f32[6,16,8,128]{3,2,1,0:T(8,128)S(1)}, f32[6,16,8,128]{3,2,1,0:T(8,128)S(1)}, u32[]{:S(2)}, u32[]{:S(2)}) collective-permute-start(f32[6,16,8,128]{3,2,1,0:T(8,128)S(1)} %broadcast_multiply_fusion.2.refs_3_), channel_id=1, source_target_pairs={{0,16},{16,0},{1,17},{17,1},{2,18},{18,2},{3,19},{19,3},{4,20},{20... | collective-permute-start | bytes 1179656 | tf_op jit(solution)/shard_map/ppermute | solution.py:800
